TPU v7x, 32 devices: a whole 2x2x4 slice. The times are simulated.
32 devices in a mesh: groups: 2 (over x), ep: 16 (over z, y, core).
Axes of the slice: x: 2, y: 2, z: 4, core: 2. Of those that a mesh axis runs over, the one named last changes fastest.
Arguments:
- residual: bfloat16 [2048, 7168], P('groups', 'ep'), parts along dimension 0, may hold values from -6 to 6
- attn_out: bfloat16 [2048, 7168], P('groups', 'ep'), parts along dimension 0, may hold values from -6 to 6
- norm_gain: float32 [7168], replicated, may hold values from 0.5 to 1.5
- expert_routes: int32 [2048, 2], P(('groups', 'ep')), parts along dimension 0, may hold values from 0 to 2, as said below
- route_gain: float32 [2048, 2], P(('groups', 'ep')), parts along dimension 0, may hold values from 0.1 to 1
- w_gate: bfloat16 [7168, 4096], P(None, 'ep'), may hold values from -0.0625 to 0.0625
- w_up: bfloat16 [7168, 4096], P(None, 'ep'), may hold values from -0.0625 to 0.0625
- w_down: bfloat16 [4096, 7168], P('ep'), may hold values from -0.125 to 0.125
Outputs:
- mixed: bfloat16 [2048, 7168], P(('groups', 'ep')), parts along dimension 0
There are 2 independent parts, one for each index of `groups`. A program takes and returns all parts, laid end to end along the dimension named above; an argument that names none is the same for every part. Nothing has to cross between parts.
Inputs may be any that keep to these rules, and one draw needn't show every extreme that they name: `expert_routes`: value 2 marks a route to an expert outside this wave; a token names each expert of the wave at most once. Among the tokens of one block of 64, at most 64 routes name one expert, and in every draw some expert is named exactly 64 times by every block.
All inputs are finite; a program needn't handle non-finite values.
Results may differ from a plain program's by a relative error of at most 0.0055.
Values may be sent and summed in bfloat16 or wider, within the bound.
No kernel may reach another device: no remote copies, remote signals or barrier semaphores. Data moves between devices by JAX's collectives and lax.ppermute only.
A program may use at most 192 MiB of HBM per device.

v0:
```python
import jax
import jax.numpy as jnp
from jax import lax
from jax.sharding import PartitionSpec as P

FSPLIT = 8


epsilon = 1e-06


def normalize(stream_rows, norm_gain):
    values = stream_rows.astype(jnp.float32)
    inv_rms = lax.rsqrt(jnp.mean(values * values, axis=-1, keepdims=True) + epsilon)
    return (values * inv_rms * norm_gain).astype(jnp.bfloat16)


def route_match(routes, experts, capacity):
    flat_ids = routes.reshape(-1)
    onehot = (flat_ids[:, None] == jnp.arange(experts, dtype=jnp.int32)[None, :]).astype(jnp.int32)
    earlier = jnp.cumsum(onehot, axis=0) - onehot
    slot_pos = jnp.sum(earlier * onehot, axis=1)
    slot_code = jnp.where(flat_ids < experts, flat_ids * capacity + slot_pos, -1)
    target = jnp.arange(experts * capacity, dtype=jnp.int32)
    return slot_code[None, :] == target[:, None]


def selection(routes, experts, capacity):
    matched = route_match(routes, experts, capacity).astype(jnp.int32)
    return matched.reshape(experts * capacity, routes.shape[0], routes.shape[1]).sum(axis=2)


def gain_table(routes, route_gain, experts, capacity):
    matched = route_match(routes, experts, capacity)
    weighted = jnp.where(matched, route_gain.reshape(-1)[None, :], 0.0)
    return weighted.reshape(experts * capacity, routes.shape[0], routes.shape[1]).sum(axis=2).T


def expert_rows(normed, w_gate, w_up, w_down):
    gate_act = jnp.dot(normed, w_gate, preferred_element_type=jnp.float32)
    up_act = jnp.dot(normed, w_up, preferred_element_type=jnp.float32)
    hidden = (jax.nn.silu(gate_act) * up_act).astype(jnp.bfloat16)
    return jnp.dot(hidden, w_down, preferred_element_type=jnp.float32).astype(jnp.bfloat16)


def body(residual, attn_out, norm_gain, expert_routes, route_gain, w_gate, w_up, w_down):
    devices = lax.axis_size("ep")
    tok_here = expert_routes.shape[0]
    route_slots = expert_routes.shape[1]
    experts = devices // FSPLIT
    capacity = route_slots * tok_here // experts
    model_width = w_gate.shape[0]
    stream_feat = (residual.astype(jnp.float32) + attn_out.astype(jnp.float32)).astype(jnp.bfloat16)
    stream_rows = lax.all_to_all(stream_feat, "ep", split_axis=0, concat_axis=1, tiled=True)
    combine_weights = gain_table(expert_routes, route_gain, experts, capacity)
    normed_rows = normalize(stream_rows, norm_gain)
    select = selection(expert_routes, experts, capacity).astype(jnp.bfloat16)
    per_expert = jnp.dot(select, normed_rows, preferred_element_type=jnp.float32).astype(
        jnp.bfloat16
    )
    per_expert = per_expert.reshape(experts, 1, capacity, model_width)
    outgoing = jnp.broadcast_to(per_expert, (experts, FSPLIT, capacity, model_width))
    outgoing = outgoing.reshape(devices, capacity, model_width)
    received = lax.all_to_all(outgoing, "ep", split_axis=0, concat_axis=0, tiled=True)
    slot_count = received.shape[1]
    partial_value = expert_rows(received.reshape(-1, model_width), w_gate, w_up, w_down)
    partial_value = partial_value.reshape(devices, slot_count, model_width)
    returned = lax.all_to_all(partial_value, "ep", split_axis=0, concat_axis=0, tiled=True)
    summed = (
        returned.reshape(experts, FSPLIT, capacity, model_width).astype(jnp.float32).sum(axis=1)
    )
    summed = summed.reshape(experts * capacity, model_width)
    routed_sum = jnp.dot(combine_weights, summed, precision=lax.Precision.HIGHEST)
    return (stream_rows.astype(jnp.float32) + routed_sum).astype(jnp.bfloat16)


def solution(mesh):
    in_specs = (
        P("groups", "ep"),
        P("groups", "ep"),
        P(),
        P(("groups", "ep"), None),
        P(("groups", "ep"), None),
        P(None, "ep"),
        P(None, "ep"),
        P("ep", None),
    )
    out_specs = P(("groups", "ep"), None)
    return jax.shard_map(body, mesh=mesh, in_specs=in_specs, out_specs=out_specs, check_vma=False)
```

profile of v0, /device:TPU:15, one launch (start us, length us, event | category | flops | bytes accessed | tf_op | source)
XLA Modules:
  0.0 732.4 jit_solution(11290937489123675443)
XLA Ops:
  0.0 0.0 copy-start.2
  0.0 1.8 add_convert_fusion
  1.8 1.3 copy.34
  3.1 6.6 all-to-all-start
  9.7 0.0 copy-done.2
  9.7 0.1 copy.36
  9.8 0.1 eq.16
  9.9 0.1 fusion.11
  10.0 0.2 reduce_window_sum.12
  10.2 0.2 select_reduce_fusion.1
  10.4 0.1 reduce_sum.52
  10.5 0.1 copy.37
  10.6 0.1 convert_reduce_fusion.1
  10.7 23.9 %all-to-all-done = bf16[16,64,448]{2,1,0:T(8,128)(2,1)S(1)} async-done(((bf16[16,64,448]{2,1,0:T(8,128)(2,1)}), bf16[16,64,448]{2,1,0:T(8,128)(2,1)S(1)}, u32[]{:S(2)}, u32[]{:S(2)}) %all-to-all-start) | async-done | bytes 917536 | tf_op jit(solution)/shard_map/all_to_all | solution.py:54
  34.6 0.3 convert_bitcast_fusion
  34.9 0.0 copy-start.1
  34.9 2.6 copy.35
  37.4 2.2 reshape.74
  39.6 0.3 fusion.1
  40.0 0.0 copy-done.1
  40.0 0.7 convolution_convert_fusion.1
  40.7 1.9 broadcast_in_dim.36
  42.6 0.0 copy-start.4
  42.6 322.0 %all_to_all.23 = bf16[16,64,7168]{2,1,0:T(8,128)(2,1)S(1)} all-to-all(bf16[16,64,7168]{2,1,0:T(8,128)(2,1)S(1)} %bitcast.21), channel_id=1, replica_groups=mesh['groups'=2,'ep'=16] {'ep'}, dimensions={0} | all-to-all | bytes 29360128 | tf_op jit(solution)/shard_map/all_to_all | solution.py:64
  364.6 0.0 copy-start
  364.6 5.2 copy-done
  369.8 0.0 copy-done.4
  369.8 3.9 fusion.14
  373.7 23.7 %convolution_convert_fusion = bf16[1024,7168]{1,0:T(8,128)(2,1)} fusion(bf16[256,7168]{1,0:T(8,128)(2,1)} %param.15, bf16[1024,7168]{1,0:T(8,128)(2,1)} %bitcast.20, bf16[7168,256]{1,0:T(8,128)(2,1)} %param.14, f32[1024,256]{1,0:T(8,128)S(1)} %fusion.14), kind=kOutput, calls=%fused_computation.1 | convolution fusion | flops 7525105664 | bytes 37748736 | tf_op jit(solution)/shard_map/dot_general | solution.py:43
  397.4 0.0 copy-start.3
  397.4 6.4 all-to-all-start.2
  403.8 0.0 copy-done.3
  403.9 0.1 select_reduce_fusion
  404.0 317.1 %all-to-all-done.2 = bf16[16,64,7168]{2,1,0:T(8,128)(2,1)} async-done(((bf16[16,64,7168]{2,1,0:T(8,128)(2,1)}), bf16[16,64,7168]{2,1,0:T(8,128)(2,1)}, u32[]{:S(2)}, u32[]{:S(2)}) %all-to-all-start.2) | async-done | bytes 14680096 | tf_op jit(solution)/shard_map/all_to_all | solution.py:68
  721.0 8.4 %convert_reduce_fusion = f32[2,64,7168]{2,1,0:T(8,128)S(1)} fusion(bf16[16,64,7168]{2,1,0:T(8,128)(2,1)} %all-to-all-done.2), kind=kLoop, calls=%fused_computation | loop fusion | flops 13762560 | bytes 18350080 | tf_op jit(solution)/shard_map/reduce_sum | solution.py:70
  729.4 3.0 fusion
  (2 shorter events, 0.0 us)
Async XLA Ops:
  0.0 9.7 %copy-start.2 = (s32[64,2]{0,1:T(2,128)S(1)}, s32[64,2]{0,1:T(2,128)}, u32[]{:S(2)}) copy-start(s32[64,2]{0,1:T(2,128)} %param.11) | copy-start | bytes 1540
  3.1 31.4 %all-to-all-start = ((bf16[16,64,448]{2,1,0:T(8,128)(2,1)}), bf16[16,64,448]{2,1,0:T(8,128)(2,1)S(1)}, u32[]{:S(2)}, u32[]{:S(2)}) async-start(bf16[16,64,448]{2,1,0:T(8,128)(2,1)} %bitcast), calls=%async_computation | async-start | bytes 2097152 | tf_op jit(solution)/shard_map/all_to_all | solution.py:54
  34.9 5.1 copy-start.1
  42.6 327.2 %copy-start.4 = (bf16[7168,256]{1,0:T(8,128)(2,1)S(1)}, bf16[7168,256]{1,0:T(8,128)(2,1)}, u32[]{:S(2)}) copy-start(bf16[7168,256]{1,0:T(8,128)(2,1)} %param.13) | copy-start | bytes 11010052
  364.6 5.2 copy-start
  397.4 6.4 copy-start.3
  397.4 323.6 %all-to-all-start.2 = ((bf16[16,64,7168]{2,1,0:T(8,128)(2,1)}), bf16[16,64,7168]{2,1,0:T(8,128)(2,1)}, u32[]{:S(2)}, u32[]{:S(2)}) async-start(bf16[16,64,7168]{2,1,0:T(8,128)(2,1)} %bitcast.18), calls=%async_computation.2 | async-start | bytes 29360128 | tf_op jit(solution)/shard_map/all_to_all | solution.py:68
where the time goes:
time: 733 us; the launch traced here: 732 us
  waiting for transfers between devices  341 us (47%)
  blocking collectives  322 us (44%)
  matrix products  31.3 us (4%)
  local copies, waits for them, and re-layouts  13.6 us (2%)
  starting transfers between devices  13 us (2%)
  other arithmetic  11.5 us (2%)
    all_to_all x1, blocking collectives, body(): lax.all_to_all(outgoing, 'ep', split_axis=0, concat_axis=0, tiled=True)  322 us
    all_to_all x1, waiting for transfers between devices, body(): lax.all_to_all(partial_value, 'ep', split_axis=0, concat_axis=0, tiled=True)  317 us
    all_to_all x1, waiting for transfers between devices, body(): lax.all_to_all(stream_feat, 'ep', split_axis=0, concat_axis=1, tiled=True)  23.9 us
    dot_general x1, matrix products, expert_rows(): jnp.dot(hidden, w_down, preferred_element_type=jnp.float32)  23.7 us
  transfers between devices with their start and end apart: 2, of which 2 were waited for; matrix products, arithmetic and copies ran while one was open for 0% of the time, Pallas kernels for 0%

commit v1 on v0

--- a/solution.py
+++ b/solution.py
@@ -43,7 +43,7 @@
     return jnp.dot(hidden, w_down, preferred_element_type=jnp.float32).astype(jnp.bfloat16)
 
 
-def body(residual, attn_out, norm_gain, expert_routes, route_gain, w_gate, w_up, w_down):
+def routed_body(residual, attn_out, norm_gain, expert_routes, route_gain, w_gate, w_up, w_down):
     devices = lax.axis_size("ep")
     tok_here = expert_routes.shape[0]
     route_slots = expert_routes.shape[1]
@@ -74,6 +74,41 @@
     return (stream_rows.astype(jnp.float32) + routed_sum).astype(jnp.bfloat16)
 
 
+def token_gains(routes, route_gain, experts):
+    named = routes[:, :, None] == jnp.arange(experts, dtype=jnp.int32)
+    return jnp.where(named, route_gain[:, :, None], 0.0).sum(axis=1)
+
+
+def dense_body(residual, attn_out, norm_gain, expert_routes, route_gain, w_gate, w_up, w_down):
+    experts = lax.axis_size("ep") // FSPLIT
+    tok_here = expert_routes.shape[0]
+    me = lax.axis_index("ep")
+    stream_feat = (residual.astype(jnp.float32) + attn_out.astype(jnp.float32)).astype(jnp.bfloat16)
+    stream = lax.all_gather(stream_feat.T, "ep", axis=0, tiled=True)
+    gains = lax.all_gather(token_gains(expert_routes, route_gain, experts), "ep", axis=0, tiled=True)
+    gain_here = lax.dynamic_slice_in_dim(gains, me // FSPLIT, 1, axis=1)
+    scaled_gate = (w_gate.astype(jnp.float32) * norm_gain[:, None]).astype(jnp.bfloat16)
+    scaled_up = (w_up.astype(jnp.float32) * norm_gain[:, None]).astype(jnp.bfloat16)
+    values = stream.astype(jnp.float32)
+    inv_rms = lax.rsqrt(jnp.mean(values * values, axis=0) + epsilon)[:, None]
+    over_features = (((0,), (0,)), ((), ()))
+    gate_act = lax.dot_general(stream, scaled_gate, over_features, preferred_element_type=jnp.float32)
+    up_act = lax.dot_general(stream, scaled_up, over_features, preferred_element_type=jnp.float32)
+    hidden = (jax.nn.silu(gate_act * inv_rms) * (up_act * inv_rms)).astype(jnp.bfloat16)
+    partial_value = jnp.dot(hidden, w_down, preferred_element_type=jnp.float32)
+    partial_value = (partial_value * gain_here).astype(jnp.bfloat16)
+    routed_sum = lax.psum_scatter(partial_value, "ep", scatter_dimension=0, tiled=True)
+    stream_rows = lax.dynamic_slice_in_dim(stream, me * tok_here, tok_here, axis=1).T
+    return (stream_rows.astype(jnp.float32) + routed_sum.astype(jnp.float32)).astype(jnp.bfloat16)
+
+
+def body(residual, attn_out, norm_gain, expert_routes, route_gain, w_gate, w_up, w_down):
+    tok_here, route_slots = expert_routes.shape
+    capacity = route_slots * tok_here // (lax.axis_size("ep") // FSPLIT)
+    chosen = dense_body if capacity >= tok_here else routed_body
+    return chosen(residual, attn_out, norm_gain, expert_routes, route_gain, w_gate, w_up, w_down)
+
+
 def solution(mesh):
     in_specs = (
         P("groups", "ep"),

time: 733 us -> 318 us (0.43)
  the two profiles are of different devices: /device:TPU:15 before, /device:TPU:0 now
where the time goes in v1:
time: 318 us
  waiting for transfers between devices  238 us (75%)
  matrix products  26.5 us (8%)
  blocking collectives  23.3 us (7%)
  other arithmetic  13.8 us (4%)
  between operations  13.5 us (4%)
    reduce_scatter x1, waiting for transfers between devices, dense_body(): lax.psum_scatter(partial_value, 'ep', scatter_dimension=0, tiled=True)  145 us
    all_gather x1, waiting for transfers between devices, dense_body(): stream = lax.all_gather(stream_feat.T, 'ep', axis=0, tiled=True)  92.8 us
    all_gather x1, blocking collectives, dense_body(): lax.all_gather(token_gains(expert_routes, route_gain, experts), 'ep', axi...  23.3 us
    dot_general x1, matrix products, dense_body(): lax.dot_general(stream, scaled_gate, over_features, preferred_element_typ...  11.7 us
    dot_general x1, matrix products, dense_body(): partial_value = jnp.dot(hidden, w_down, preferred_element_type=jnp.float32)  9.33 us
    reduce_sum x1, other arithmetic, dense_body(): inv_rms = lax.rsqrt(jnp.mean(values * values, axis=0) + epsilon)[:, None]  8.08 us
  transfers between devices with their start and end apart: 2, of which 2 were waited for; matrix products, arithmetic and copies ran while one was open for 1% of the time, Pallas kernels for 0%

profile of v1, /device:TPU:0, one launch (start us, length us, event | category | flops | bytes accessed | tf_op | source)
XLA Modules:
  0.0 318.0 jit_solution(12832006984992876961)
XLA Ops:
  6.5 0.0 all-gather.3.cloned.1.call-start
  6.5 2.7 fusion.9
  9.3 0.0 all-gather.3.cloned.1.call-update
  9.3 0.0 reduce-scatter.2.cloned.1.call-start
  9.4 0.7 fusion.12
  10.1 23.3 %all-gather = f32[16,64,2]{1,2,0:T(2,128)S(1)} all-gather(f32[1,64,2]{1,2,0:T(2,128)S(1)} %bitcast.18), channel_id=1, replica_groups=mesh['groups'=2,'ep'=16] {'ep'}, dimensions={0}, use_global_device_ids=true | all-gather | bytes 8704 | tf_op jit(solution)/shard_map/all_gather | solution.py:88
  33.4 0.1 reshape.9
  33.5 0.0 copy-start.2
  33.5 92.8 %all-gather.3.cloned.1.call-done = bf16[7168,1024]{1,0:T(8,128)(2,1)} async-done(((bf16[448,1024]{1,0:T(8,128)(2,1)}), bf16[7168,1024]{1,0:T(8,128)(2,1)}) %all-gather.3.cloned.1.call-update) | async-done | bytes 14680080 | tf_op jit(solution)/shard_map/all_gather | solution.py:87
  126.2 8.1 %multiply_reduce_fusion = f32[1024]{0:T(1024)S(1)} fusion(bf16[7168,1024]{1,0:T(8,128)(2,1)} %all-gather.3.cloned.1.call-done), kind=kLoop, calls=%fused_computation.1 | loop fusion | flops 22019072 | bytes 14684160 | tf_op jit(solution)/shard_map/reduce_sum | solution.py:93
  134.3 0.0 copy-done.2
  134.3 0.0 copy-start
  134.4 0.0 copy-start.1
  134.4 11.7 %fusion.7 = f32[1024,256]{1,0:T(8,128)S(1)} fusion(bf16[7168,1024]{1,0:T(8,128)(2,1)} %all-gather.3.cloned.1.call-done, bf16[7168,256]{1,0:T(8,128)(2,1)} %param.13, f32[7168]{0:T(1024)S(1)} %copy-done.2, f32[1024]{0:T(1024)S(1)} %add_rsqrt_fusion), kind=kOutput, calls=%fused_computation.13 | convolution fusion | flops 3763863552 | bytes 19431424 | tf_op jit(solution)/shard_map/dot_general | solution.py:95
  146.0 0.0 copy-done
  146.0 0.0 copy-done.1
  146.0 5.5 %fusion.8.clone.4 = bf16[1024,256]{1,0:T(8,128)(2,1)S(1)} fusion(bf16[7168,1024]{1,0:T(8,128)(2,1)S(1)} %copy-done, bf16[7168,256]{1,0:T(8,128)(2,1)S(1)} %copy-done.1, f32[7168]{0:T(1024)S(1)} %copy-done.2, f32[1024,256]{1,0:T(8,128)S(1)} %fusion.7, f32[1024]{0:T(1024)S(1)} %add_rsqrt_fusion), kind=kOutput, calls=%fused_computation.14.clone.clone.clone.1 | convolution fusion | flops 3765436416 | bytes 19955712 | tf_op jit(solution)/shard_map/dot_general | solution.py:96
  151.6 9.3 %multiply_convert_fusion = bf16[1024,7168]{1,0:T(8,128)(2,1)} fusion(f32[1024]{0:T(1024)S(1)} %bitcast.19, bf16[256,7168]{1,0:T(8,128)(2,1)} %param.15, bf16[1024,256]{1,0:T(8,128)(2,1)S(1)} %fusion.8.clone.4), kind=kOutput, calls=%fused_computation | convolution fusion | flops 3772776448 | bytes 18878464 | tf_op jit(solution)/shard_map/dot_general | solution.py:98
  160.9 0.0 reduce-scatter.2.cloned.1.call-update
  160.9 2.1 constant_dynamic-slice_fusion.1
  163.0 0.8 copy.24
  163.8 145.1 %reduce-scatter.2.cloned.1.call-done = bf16[64,7168]{1,0:T(8,128)(2,1)} async-done(((bf16[1024,7168]{1,0:T(8,128)(2,1)}), bf16[64,7168]{1,0:T(8,128)(2,1)}) %reduce-scatter.2.cloned.1.call-update) | async-done | bytes 917520 | tf_op jit(solution)/shard_map/reduce_scatter | solution.py:100
  308.9 2.3 fusion.4
  (3 shorter events, 0.0 us)
Async XLA Ops:
  6.5 119.7 %all-gather.3.cloned.1.call-start = ((), (), s32[]{:S(2)}) async-start(), calls=%async_computation.1 | async-start | bytes 15597568 | tf_op jit(solution)/shard_map/all_gather | solution.py:87
  9.3 299.6 %reduce-scatter.2.cloned.1.call-start = ((), (), s32[]{:S(2)}) async-start(), calls=%async_computation.2 | async-start | bytes 15597568 | tf_op jit(solution)/shard_map/reduce_scatter | solution.py:100
  33.5 100.9 %copy-start.2 = (f32[7168]{0:T(1024)S(1)}, f32[7168]{0:T(1024)}, u32[]{:S(2)}) copy-start(f32[7168]{0:T(1024)} %param.10) | copy-start | bytes 86020
  134.3 11.7 %copy-start = (bf16[7168,1024]{1,0:T(8,128)(2,1)S(1)}, bf16[7168,1024]{1,0:T(8,128)(2,1)}, u32[]{:S(2)}) copy-start(bf16[7168,1024]{1,0:T(8,128)(2,1)} %all-gather.3.cloned.1.call-done) | copy-start | bytes 44040196
  134.4 11.7 %copy-start.1 = (bf16[7168,256]{1,0:T(8,128)(2,1)S(1)}, bf16[7168,256]{1,0:T(8,128)(2,1)}, u32[]{:S(2)}) copy-start(bf16[7168,256]{1,0:T(8,128)(2,1)} %param.14) | copy-start | bytes 11010052
Sparse Core Ops, SparseCore 0:
  9.6 116.5 all-gather.2
  161.0 147.7 reduce-scatter.1

commit v2 on v0

--- a/solution.py
+++ b/solution.py
@@ -43,7 +43,7 @@
     return jnp.dot(hidden, w_down, preferred_element_type=jnp.float32).astype(jnp.bfloat16)
 
 
-def body(residual, attn_out, norm_gain, expert_routes, route_gain, w_gate, w_up, w_down):
+def routed_body(residual, attn_out, norm_gain, expert_routes, route_gain, w_gate, w_up, w_down):
     devices = lax.axis_size("ep")
     tok_here = expert_routes.shape[0]
     route_slots = expert_routes.shape[1]
@@ -74,6 +74,174 @@
     return (stream_rows.astype(jnp.float32) + routed_sum).astype(jnp.bfloat16)
 
 
+def token_gains(routes, route_gain, experts):
+    named = routes[:, :, None] == jnp.arange(experts, dtype=jnp.int32)
+    return jnp.where(named, route_gain[:, :, None], 0.0).sum(axis=1)
+
+
+def ring_order(chips):
+    return list(range(0, chips, 2)) + list(reversed(range(1, chips, 2)))
+
+
+def ring_shift(value, ring, step):
+    chips = len(ring)
+    pairs = [
+        (2 * ring[i] + core, 2 * ring[(i + step) % chips] + core)
+        for i in range(chips)
+        for core in range(2)
+    ]
+    return lax.ppermute(value, "ep", pairs)
+
+
+def swap_cores(value):
+    return lax.ppermute(value, "ep", [(i, i ^ 1) for i in range(lax.axis_size("ep"))])
+
+
+def gather_small(value, chips, chip):
+    width = 1
+    while width < chips:
+        pairs = [
+            (2 * i + core, 2 * (i ^ width) + core) for i in range(chips) for core in range(2)
+        ]
+        other = lax.ppermute(value, "ep", pairs)
+        upper = (chip // width) % 2 == 1
+        value = jnp.concatenate(
+            [jnp.where(upper, other, value), jnp.where(upper, value, other)], axis=0
+        )
+        width *= 2
+    return value
+
+
+def dense_body(residual, attn_out, norm_gain, expert_routes, route_gain, w_gate, w_up, w_down):
+    devices = lax.axis_size("ep")
+    experts = devices // FSPLIT
+    chips = devices // 2
+    far = chips // 2
+    tok_here = expert_routes.shape[0]
+    feat_here = residual.shape[1]
+    model_width = w_gate.shape[0]
+    hidden_here = w_gate.shape[1]
+    ring = ring_order(chips)
+    me = lax.axis_index("ep")
+    chip, core = me // 2, me % 2
+    spot = jnp.asarray([ring.index(i) for i in range(chips)], jnp.int32)[chip]
+    chip_at = jnp.asarray(ring, jnp.int32)
+
+    def chip_by_distance(distance):
+        return chip_at[(spot + distance) % chips]
+
+    stream_feat = (residual.astype(jnp.float32) + attn_out.astype(jnp.float32)).astype(jnp.bfloat16)
+    by_core = stream_feat.reshape(chips, 2, tok_here, feat_here)
+    mine = lax.dynamic_index_in_dim(by_core, core, 1, keepdims=False)
+    theirs = lax.dynamic_index_in_dim(by_core, 1 - core, 1, keepdims=False)
+    swapped = swap_cores(theirs)
+    block = jnp.concatenate(
+        [jnp.where(core == 0, mine, swapped), jnp.where(core == 0, swapped, mine)], axis=2
+    )
+    block = block.reshape(2, far * tok_here, 2 * feat_here)
+    blocks = {0: [block[0], block[1]]}
+
+    scaled = jnp.concatenate([w_gate, w_up], axis=1).astype(jnp.float32) * norm_gain[:, None]
+    scaled = scaled.astype(jnp.bfloat16)
+    weights = [scaled, swap_cores(scaled)]
+    down = jnp.concatenate([w_down, swap_cores(w_down)], axis=0)
+    gains = gather_small(token_gains(expert_routes, route_gain, experts), chips, chip)
+    gain_here = lax.dynamic_slice_in_dim(gains, me // FSPLIT, 1, axis=1)
+
+    for distance in range(1, far):
+        for sign, order in ((-1, (0, 1)), (1, (1, 0))):
+            came = [None, None]
+            for part in order:
+                came[part] = ring_shift(blocks[sign * (distance - 1)][part], ring, -sign)
+            blocks[sign * distance] = came
+    blocks[far] = [
+        ring_shift(blocks[1 - far][0], ring, 1),
+        ring_shift(blocks[far - 1][1], ring, -1),
+    ]
+
+    sums = [[0.0, 0.0], [0.0, 0.0]]
+    squares = [0.0, 0.0]
+    stream_rows = jnp.zeros((tok_here, model_width), jnp.bfloat16)
+    for distance in sorted(blocks, key=abs):
+        source = chip_by_distance(distance)
+        for part in range(2):
+            rows = blocks[distance][part]
+            values = rows.astype(jnp.float32)
+            squares[part] += jnp.sum(values * values, axis=1, keepdims=True)
+            for which in range(2):
+                piece = lax.dynamic_slice_in_dim(
+                    weights[which], source * 2 * feat_here, 2 * feat_here, axis=0
+                )
+                sums[part][which] += jnp.dot(rows, piece, preferred_element_type=jnp.float32)
+        row = (chip % far) * tok_here
+        own = jnp.where(
+            chip < far,
+            lax.dynamic_slice_in_dim(blocks[distance][0], row, tok_here, axis=0),
+            lax.dynamic_slice_in_dim(blocks[distance][1], row, tok_here, axis=0),
+        )
+        stream_rows = lax.dynamic_update_slice_in_dim(
+            stream_rows, own, source * 2 * feat_here, axis=1
+        )
+
+    hidden = []
+    for part in range(2):
+        inv_rms = lax.rsqrt(squares[part] / model_width + epsilon)
+        acts = [act * inv_rms for act in sums[part]]
+        hidden.append(
+            jnp.concatenate(
+                [jax.nn.silu(act[:, :hidden_here]) * act[:, hidden_here:] for act in acts], axis=1
+            )
+        )
+    hidden = jnp.concatenate(hidden, axis=0).astype(jnp.bfloat16)
+
+    def contribution(rows, row_gain):
+        out = jnp.dot(rows, down, preferred_element_type=jnp.float32)
+        return (out * row_gain).astype(jnp.bfloat16)
+
+    half = model_width // 2
+
+    def of_chip(table, distance):
+        return lax.dynamic_slice_in_dim(
+            table, chip_by_distance(distance) * tok_here, tok_here, axis=0
+        )
+
+    first = contribution(of_chip(hidden, far), of_chip(gain_here, far))
+    moving = {
+        1: [ring_shift(first[:, :half], ring, 1), None],
+        -1: [None, ring_shift(first[:, half:], ring, -1)],
+    }
+    everything = contribution(hidden, gain_here)
+    for distance in range(far - 1, 0, -1):
+        for sign, order in ((1, (1, 0)), (-1, (0, 1))):
+            add = of_chip(everything, sign * distance)
+            sent = [None, None]
+            for part in order:
+                value = add[:, part * half : (part + 1) * half]
+                if moving[sign][part] is not None:
+                    value = value.astype(jnp.float32) + moving[sign][part].astype(jnp.float32)
+                    value = value.astype(jnp.bfloat16)
+                sent[part] = ring_shift(value, ring, sign)
+            moving[sign] = sent
+    out = stream_rows.astype(jnp.float32) + of_chip(everything, 0).astype(jnp.float32)
+    outs = []
+    for part in range(2):
+        total = out[:, part * half : (part + 1) * half]
+        for sign in (1, -1):
+            if moving[sign][part] is not None:
+                total = total + moving[sign][part].astype(jnp.float32)
+        outs.append(total)
+    return jnp.concatenate(outs, axis=1).astype(jnp.bfloat16)
+
+
+def body(residual, attn_out, norm_gain, expert_routes, route_gain, w_gate, w_up, w_down):
+    tok_here, route_slots = expert_routes.shape
+    devices = lax.axis_size("ep")
+    capacity = route_slots * tok_here // (devices // FSPLIT)
+    dense = capacity >= tok_here and devices % 4 == 0 and devices & (devices - 1) == 0
+    chosen = dense_body if dense else routed_body
+    return chosen(residual, attn_out, norm_gain, expert_routes, route_gain, w_gate, w_up, w_down)
+
+
 def solution(mesh):
     in_specs = (
         P("groups", "ep"),

time: 733 us -> 236 us (0.32)
  the two profiles are of different devices: /device:TPU:15 before, /device:TPU:0 now
where the time goes in v2:
time: 236 us; the launch traced here: 234 us
  waiting for transfers between devices  84.7 us (36%)
  matrix products  59.2 us (25%)
  starting transfers between devices  37 us (16%)
  other arithmetic  26.9 us (11%)
  between operations  17.7 us (8%)
  local copies, waits for them, and re-layouts  8.36 us (4%)
    ppermute x28, waiting for transfers between devices, ring_shift(): return lax.ppermute(value, 'ep', pairs)  82.7 us
    dot_general x32, matrix products, dense_body(): jnp.dot(rows, piece, preferred_element_type=jnp.float32)  53.6 us
    ppermute x28, starting transfers between devices, ring_shift(): return lax.ppermute(value, 'ep', pairs)  29.2 us
    convert_element_type x1, other arithmetic, dense_body(): scaled = scaled.astype(jnp.bfloat16)  7.54 us
    ppermute x3, starting transfers between devices, gather_small(): other = lax.ppermute(value, 'ep', pairs)  7.2 us
    convert_element_type x5, other arithmetic, dense_body(): value = value.astype(jnp.bfloat16)  6.14 us
    dot_general x2, matrix products, contribution(): out = jnp.dot(rows, down, preferred_element_type=jnp.float32)  5.61 us
    dynamic_update_slice x8, other arithmetic, dense_body(): lax.dynamic_update_slice_in_dim(stream_rows, own, source * 2 * feat_here,...  5.06 us
  transfers between devices with their start and end apart: 34, of which 21 were waited for; matrix products, arithmetic and copies ran while one was open for 25% of the time, Pallas kernels for 0%

profile of v2, /device:TPU:0, one launch (start us, length us, event | category | flops | bytes accessed | tf_op | source)
XLA Modules:
  0.0 233.9 jit_solution(13656894367177697378)
XLA Ops:
  0.0 1.8 add_convert_fusion
  3.0 7.5 %multiply_convert_fusion.1 = bf16[7168,512]{1,0:T(8,128)(2,1)} fusion(bf16[7168,256]{1,0:T(8,128)(2,1)} %param.16, bf16[7168,256]{1,0:T(8,128)(2,1)} %param.15, f32[7168]{0:T(1024)} %param.12), kind=kLoop, calls=%fused_computation.1 | loop fusion | flops 22020096 | bytes 14708736 | tf_op jit(solution)/shard_map/convert_element_type | solution.py:145
  10.6 3.0 %collective-permute-start.17 = (f32[64,2]{0,1:T(2,128)S(1)}, f32[64,2]{0,1:T(2,128)S(1)}, u32[]{:S(2)}, u32[]{:S(2)}) collective-permute-start(f32[64,2]{0,1:T(2,128)S(1)} %fusion.104), channel_id=1, source_target_pairs={{0,2},{1,3},{2,0},{3,1},{4,6},{5,7},{6,4},{7,5},{8,10},{9,11},{10,... | collective-permute-start | bytes 1544 | tf_op jit(solution)/shard_map/ppermute | solution.py:106
  26.6 4.1 %constant_dynamic-update-slice_fusion.1 = bf16[512,7168]{1,0:T(8,128)(2,1)} fusion(bf16[256,7168]{1,0:T(8,128)(2,1)} %param.17), kind=kLoop, calls=%fused_computation.179 | loop fusion | bytes 7340032
  30.8 1.6 collective-permute-start.18
  32.4 2.0 collective-permute-done.18
  34.5 2.6 %collective-permute-start.19 = (f32[256,2]{0,1:T(2,128)S(1)}, f32[256,2]{0,1:T(2,128)S(1)}, u32[]{:S(2)}, u32[]{:S(2)}) collective-permute-start(f32[256,2]{0,1:T(2,128)S(1)} %pad_maximum_fusion.2), channel_id=1, source_target_pairs={{0,8},{1,9},{2,10},{3,11},{4,12},{5,13},{6,14},{7,15},{8,0},{9,1},... | collective-permute-start | bytes 6152 | tf_op jit(solution)/shard_map/ppermute | solution.py:106
  42.6 1.6 collective-permute-start.1
  44.6 2.4 %fusion.63 = f32[256,512]{1,0:T(8,128)} fusion(bf16[256,896]{1,0:T(8,128)(2,1)S(1)} %bitcast.66, bf16[7168,512]{1,0:T(8,128)(2,1)} %multiply_convert_fusion.1, s32[]{:T(128)S(6)} %select_n.352), kind=kOutput, calls=%fused_computation.117 | convolution fusion | flops 234881024 | bytes 1900548 | tf_op jit(solution)/shard_map/dot_general | solution.py:175
  47.2 6.7 %collective-permute-done.3 = bf16[256,896]{1,0:T(8,128)(2,1)S(1)} collective-permute-done((bf16[256,896]{1,0:T(8,128)(2,1)S(1)}, bf16[256,896]{1,0:T(8,128)(2,1)S(1)}, u32[]{:S(2)}, u32[]{:S(2)}) %collective-permute-start.3) | collective-permute-done | bytes 458784 | tf_op jit(solution)/shard_map/ppermute | solution.py:93
  54.4 1.6 collective-permute-start.7
  56.0 1.6 fusion.59
  57.8 3.7 %collective-permute-done.1 = bf16[256,896]{1,0:T(8,128)(2,1)S(1)} collective-permute-done((bf16[256,896]{1,0:T(8,128)(2,1)S(1)}, bf16[256,896]{1,0:T(8,128)(2,1)S(1)}, u32[]{:S(2)}, u32[]{:S(2)}) %collective-permute-start.1) | collective-permute-done | bytes 458784 | tf_op jit(solution)/shard_map/ppermute | solution.py:93
  64.4 1.6 convolution_add_fusion.8
  66.0 1.8 convolution_add_fusion.17
  67.8 1.6 convolution_add_fusion.16
  69.8 1.6 convolution_add_fusion.7
  71.4 2.2 collective-permute-done.7
  75.2 1.6 fusion.53
  77.3 6.1 %collective-permute-done.8 = bf16[256,896]{1,0:T(8,128)(2,1)S(1)} collective-permute-done((bf16[256,896]{1,0:T(8,128)(2,1)S(1)}, bf16[256,896]{1,0:T(8,128)(2,1)S(1)}, u32[]{:S(2)}, u32[]{:S(2)}) %collective-permute-start.8) | collective-permute-done | bytes 458784 | tf_op jit(solution)/shard_map/ppermute | solution.py:93
  85.0 1.6 fusion.51
  86.6 1.6 fusion.1
  88.8 1.6 fusion.8
  91.1 2.9 %collective-permute-done.9 = bf16[256,896]{1,0:T(8,128)(2,1)S(1)} collective-permute-done((bf16[256,896]{1,0:T(8,128)(2,1)S(1)}, bf16[256,896]{1,0:T(8,128)(2,1)S(1)}, u32[]{:S(2)}, u32[]{:S(2)}) %collective-permute-start.9) | collective-permute-done | bytes 458784 | tf_op jit(solution)/shard_map/ppermute | solution.py:93
  96.2 1.6 fusion.47
  97.8 2.5 %collective-permute-done.12 = bf16[256,896]{1,0:T(8,128)(2,1)S(1)} collective-permute-done((bf16[256,896]{1,0:T(8,128)(2,1)S(1)}, bf16[256,896]{1,0:T(8,128)(2,1)S(1)}, u32[]{:S(2)}, u32[]{:S(2)}) %collective-permute-start.12) | collective-permute-done | bytes 458784 | tf_op jit(solution)/shard_map/ppermute | solution.py:93
  100.4 1.8 fusion.45
  103.1 2.0 fusion.2
  106.8 1.8 fusion.9
  108.6 2.9 %collective-permute-done.13 = bf16[256,896]{1,0:T(8,128)(2,1)S(1)} collective-permute-done((bf16[256,896]{1,0:T(8,128)(2,1)S(1)}, bf16[256,896]{1,0:T(8,128)(2,1)S(1)}, u32[]{:S(2)}, u32[]{:S(2)}) %collective-permute-start.13) | collective-permute-done | bytes 458784 | tf_op jit(solution)/shard_map/ppermute | solution.py:93
  112.6 1.7 fusion.3
  114.4 1.6 fusion.10
  116.4 1.6 fusion.35
  118.0 1.6 fusion.39
  119.7 1.6 fusion.29
  121.3 1.7 fusion.23
  123.0 1.7 fusion.4
  124.7 1.6 fusion.5
  126.3 1.7 fusion.6
  128.0 1.6 fusion.7
  129.7 1.6 fusion.33
  131.4 1.6 fusion.37
  133.0 1.6 fusion.27
  134.7 1.6 fusion.21
  136.3 1.6 fusion.11
  137.9 1.6 fusion.12
  139.6 1.6 fusion.13
  141.2 1.6 fusion.14
  145.2 1.6 collective-permute-start.20
  146.8 4.2 %multiply_convert_fusion = bf16[512,7168]{1,0:T(8,128)(2,1)S(1)} fusion(bf16[512,7168]{1,0:T(8,128)(2,1)S(1)} %constant_dynamic-update-slice_fusion, f32[512]{0:T(512)S(1)} %bitcast.76, bf16[256,256]{1,0:T(8,128)(2,1)S(1)} %fusion.66, bf16[256,256]{1,0:T(8,128)(2,1)S(1)} %fusion.67, bf16[256,256]{1,0:T(8,128)(2,1)S(1)} %fusion.68, bf16[256,256]{1,0:T(8,128)(2,1)S(1)} %fusion.69), kind=kOutput, calls=%fused_computation | convolution fusion | flops 3767533568 | bytes 15206400 | tf_op jit(solution)/shard_map/dot_general | solution.py:198
  151.0 4.7 %collective-permute-done.20 = bf16[64,3584]{1,0:T(8,128)(2,1)S(1)} collective-permute-done((bf16[64,3584]{1,0:T(8,128)(2,1)S(1)}, bf16[64,3584]{1,0:T(8,128)(2,1)S(1)}, u32[]{:S(2)}, u32[]{:S(2)}) %collective-permute-start.20) | collective-permute-done | bytes 458784 | tf_op jit(solution)/shard_map/ppermute | solution.py:93
  155.8 1.6 collective-permute-start.21
  158.9 1.6 collective-permute-start.27
  160.9 8.4 %collective-permute-done.21 = bf16[64,3584]{1,0:T(8,128)(2,1)S(1)} collective-permute-done((bf16[64,3584]{1,0:T(8,128)(2,1)S(1)}, bf16[64,3584]{1,0:T(8,128)(2,1)S(1)}, u32[]{:S(2)}, u32[]{:S(2)}) %collective-permute-start.21) | collective-permute-done | bytes 458784 | tf_op jit(solution)/shard_map/ppermute | solution.py:93
  170.2 1.6 collective-permute-start.22
  174.3 4.4 %collective-permute-done.27 = bf16[64,3584]{1,0:T(8,128)(2,1)} collective-permute-done((bf16[64,3584]{1,0:T(8,128)(2,1)}, bf16[64,3584]{1,0:T(8,128)(2,1)}, u32[]{:S(2)}, u32[]{:S(2)}) %collective-permute-start.27) | collective-permute-done | bytes 458784 | tf_op jit(solution)/shard_map/ppermute | solution.py:93
  178.8 4.9 %collective-permute-done.22 = bf16[64,3584]{1,0:T(8,128)(2,1)} collective-permute-done((bf16[64,3584]{1,0:T(8,128)(2,1)}, bf16[64,3584]{1,0:T(8,128)(2,1)}, u32[]{:S(2)}, u32[]{:S(2)}) %collective-permute-start.22) | collective-permute-done | bytes 458784 | tf_op jit(solution)/shard_map/ppermute | solution.py:93
  183.7 2.4 %add_convert_fusion.8 = (bf16[64,3584]{1,0:T(8,128)(2,1)S(1)}, bf16[64,3584]{1,0:T(8,128)(2,1)S(1)}, bf16[64,3584]{1,0:T(8,128)(2,1)S(1)}, bf16[64,3584]{1,0:T(8,128)(2,1)S(1)}) fusion(bf16[64,3584]{1,0:T(8,128)(2,1)} %collective-permute-done.22, bf16[512,7168]{1,0:T(8,128)(2,1)} %copy-done, s32[]{:T(128)S(6)} %select_n.399, ...), kind=kLoop, calls=%fused_computation.54 | loop fusion | flops 3670016 | bytes 5505044 | tf_op jit(solution)/shard_map/convert_element_type | solution.py:222
  191.8 6.4 %collective-permute-done.25 = bf16[64,3584]{1,0:T(8,128)(2,1)S(1)} collective-permute-done((bf16[64,3584]{1,0:T(8,128)(2,1)S(1)}, bf16[64,3584]{1,0:T(8,128)(2,1)S(1)}, u32[]{:S(2)}, u32[]{:S(2)}) %collective-permute-start.25) | collective-permute-done | bytes 458784 | tf_op jit(solution)/shard_map/ppermute | solution.py:93
  198.2 6.8 %collective-permute-done.31 = bf16[64,3584]{1,0:T(8,128)(2,1)S(1)} collective-permute-done((bf16[64,3584]{1,0:T(8,128)(2,1)S(1)}, bf16[64,3584]{1,0:T(8,128)(2,1)S(1)}, u32[]{:S(2)}, u32[]{:S(2)}) %collective-permute-start.31) | collective-permute-done | bytes 458784 | tf_op jit(solution)/shard_map/ppermute | solution.py:93
  205.0 1.6 add_convert_fusion.6
  212.8 7.3 %collective-permute-done.32 = bf16[64,3584]{1,0:T(8,128)(2,1)S(1)} collective-permute-done((bf16[64,3584]{1,0:T(8,128)(2,1)S(1)}, bf16[64,3584]{1,0:T(8,128)(2,1)S(1)}, u32[]{:S(2)}, u32[]{:S(2)}) %collective-permute-start.32) | collective-permute-done | bytes 458784 | tf_op jit(solution)/shard_map/ppermute | solution.py:93
  223.2 4.5 %collective-permute-done.26 = bf16[64,3584]{1,0:T(8,128)(2,1)S(1)} collective-permute-done((bf16[64,3584]{1,0:T(8,128)(2,1)S(1)}, bf16[64,3584]{1,0:T(8,128)(2,1)S(1)}, u32[]{:S(2)}, u32[]{:S(2)}) %collective-permute-start.26) | collective-permute-done | bytes 458784 | tf_op jit(solution)/shard_map/ppermute | solution.py:93
  227.7 4.9 %collective-permute-done.33 = bf16[64,3584]{1,0:T(8,128)(2,1)S(1)} collective-permute-done((bf16[64,3584]{1,0:T(8,128)(2,1)S(1)}, bf16[64,3584]{1,0:T(8,128)(2,1)S(1)}, u32[]{:S(2)}, u32[]{:S(2)}) %collective-permute-start.33) | collective-permute-done | bytes 458784 | tf_op jit(solution)/shard_map/ppermute | solution.py:93
  (143 shorter events, 42.8 us)
Async XLA Ops:
  2.4 8.2 %copy-start.17 = (f32[64,2]{0,1:T(2,128)S(1)}, f32[64,2]{0,1:T(2,128)}, u32[]{:S(2)}) copy-start(f32[64,2]{0,1:T(2,128)} %param.14) | copy-start | bytes 1540
  2.4 8.2 %copy-start.18 = (s32[64,2]{0,1:T(2,128)S(1)}, s32[64,2]{0,1:T(2,128)}, u32[]{:S(2)}) copy-start(s32[64,2]{0,1:T(2,128)} %param.13) | copy-start | bytes 1540
  2.4 11.2 %copy-start.19 = (s32[8]{0:T(128)S(1)}, s32[8]{0:T(128)}, u32[]{:S(2)}) copy-start(s32[8]{0:T(128)} %constant.232.clone) | copy-start | bytes 100
  2.4 18.4 %copy-start.16 = (s32[8]{0:T(128)S(1)}, s32[8]{0:T(128)}, u32[]{:S(2)}) copy-start(s32[8]{0:T(128)} %constant.233.clone) | copy-start | bytes 100
  2.4 37.3 %collective-permute-start = (bf16[8,64,448]{2,1,0:T(8,128)(2,1)S(1)}, bf16[8,64,448]{2,1,0:T(8,128)(2,1)S(1)}, u32[]{:S(2)}, u32[]{:S(2)}) collective-permute-start(bf16[8,64,448]{2,1,0:T(8,128)(2,1)S(1)} %dynamic-slice_bitcast_fusion), channel_id=1, source_target_pairs={{0,1},{1,0},{2,3},{3,2},{4,5},{5,4},{6,7},{7,6},{8,9},{9,8},{10,11... | collective-permute-start | bytes 1376264 | tf_op jit(solution)/shard_map/ppermute | solution.py:97
  10.5 105.9 %collective-permute-start.15 = (bf16[7168,512]{1,0:T(8,128)(2,1)}, bf16[7168,512]{1,0:T(8,128)(2,1)}, u32[]{:S(2)}, u32[]{:S(2)}) collective-permute-start(bf16[7168,512]{1,0:T(8,128)(2,1)} %multiply_convert_fusion.1), channel_id=1, source_target_pairs={{0,1},{1,0},{2,3},{3,2},{4,5},{5,4},{6,7},{7,6},{8,9},{9,8},{10,11... | collective-permute-start | bytes 22020104 | tf_op jit(solution)/shard_map/ppermute | solution.py:97
  10.6 20.1 %collective-permute-start.17 = (f32[64,2]{0,1:T(2,128)S(1)}, f32[64,2]{0,1:T(2,128)S(1)}, u32[]{:S(2)}, u32[]{:S(2)}) collective-permute-start(f32[64,2]{0,1:T(2,128)S(1)} %fusion.104), channel_id=1, source_target_pairs={{0,2},{1,3},{2,0},{3,1},{4,6},{5,7},{6,4},{7,5},{8,10},{9,11},{10,... | collective-permute-start | bytes 1544 | tf_op jit(solution)/shard_map/ppermute | solution.py:106
  30.8 3.6 %collective-permute-start.18 = (f32[128,2]{0,1:T(2,128)S(1)}, f32[128,2]{0,1:T(2,128)S(1)}, u32[]{:S(2)}, u32[]{:S(2)}) collective-permute-start(f32[128,2]{0,1:T(2,128)S(1)} %pad_maximum_fusion.3), channel_id=1, source_target_pairs={{0,4},{1,5},{2,6},{3,7},{4,0},{5,1},{6,2},{7,3},{8,12},{9,13},{10,... | collective-permute-start | bytes 3080 | tf_op jit(solution)/shard_map/ppermute | solution.py:106
  34.5 5.2 %collective-permute-start.19 = (f32[256,2]{0,1:T(2,128)S(1)}, f32[256,2]{0,1:T(2,128)S(1)}, u32[]{:S(2)}, u32[]{:S(2)}) collective-permute-start(f32[256,2]{0,1:T(2,128)S(1)} %pad_maximum_fusion.2), channel_id=1, source_target_pairs={{0,8},{1,9},{2,10},{3,11},{4,12},{5,13},{6,14},{7,15},{8,0},{9,1},... | collective-permute-start | bytes 6152 | tf_op jit(solution)/shard_map/ppermute | solution.py:106
  40.4 17.4 %copy-start.6 = (bf16[4,64,896]{2,1,0:T(8,128)(2,1)}, bf16[4,64,896]{2,1,0:T(8,128)(2,1)S(1)}, u32[]{:S(2)}) copy-start(bf16[4,64,896]{2,1,0:T(8,128)(2,1)S(1)} %get-tuple-element.6) | copy-start | bytes 1376260
  40.4 31.0 %copy-start.10 = (bf16[4,64,896]{2,1,0:T(8,128)(2,1)}, bf16[4,64,896]{2,1,0:T(8,128)(2,1)S(1)}, u32[]{:S(2)}) copy-start(bf16[4,64,896]{2,1,0:T(8,128)(2,1)S(1)} %get-tuple-element.23) | copy-start | bytes 1376260
  40.4 13.5 %collective-permute-start.3 = (bf16[256,896]{1,0:T(8,128)(2,1)S(1)}, bf16[256,896]{1,0:T(8,128)(2,1)S(1)}, u32[]{:S(2)}, u32[]{:S(2)}) collective-permute-start(bf16[256,896]{1,0:T(8,128)(2,1)S(1)} %bitcast.64), channel_id=1, source_target_pairs={{0,2},{1,3},{4,0},{5,1},{8,4},{9,5},{12,8},{13,9},{14,12},{15,13},... | collective-permute-start | bytes 1376264 | tf_op jit(solution)/shard_map/ppermute | solution.py:93
  41.0 13.5 %collective-permute-start.2 = (bf16[256,896]{1,0:T(8,128)(2,1)S(1)}, bf16[256,896]{1,0:T(8,128)(2,1)S(1)}, u32[]{:S(2)}, u32[]{:S(2)}) collective-permute-start(bf16[256,896]{1,0:T(8,128)(2,1)S(1)} %bitcast.69), channel_id=1, source_target_pairs={{0,4},{1,5},{4,8},{5,9},{8,12},{9,13},{12,14},{13,15},{14,10},{15,... | collective-permute-start | bytes 1376264 | tf_op jit(solution)/shard_map/ppermute | solution.py:93
  42.6 18.9 %collective-permute-start.1 = (bf16[256,896]{1,0:T(8,128)(2,1)S(1)}, bf16[256,896]{1,0:T(8,128)(2,1)S(1)}, u32[]{:S(2)}, u32[]{:S(2)}) collective-permute-start(bf16[256,896]{1,0:T(8,128)(2,1)S(1)} %bitcast.65), channel_id=1, source_target_pairs={{0,4},{1,5},{4,8},{5,9},{8,12},{9,13},{12,14},{13,15},{14,10},{15,... | collective-permute-start | bytes 1376264 | tf_op jit(solution)/shard_map/ppermute | solution.py:93
  44.2 19.5 %collective-permute-start.4 = (bf16[256,896]{1,0:T(8,128)(2,1)S(1)}, bf16[256,896]{1,0:T(8,128)(2,1)S(1)}, u32[]{:S(2)}, u32[]{:S(2)}) collective-permute-start(bf16[256,896]{1,0:T(8,128)(2,1)S(1)} %bitcast.70), channel_id=1, source_target_pairs={{0,2},{1,3},{4,0},{5,1},{8,4},{9,5},{12,8},{13,9},{14,12},{15,13},... | collective-permute-start | bytes 1376264 | tf_op jit(solution)/shard_map/ppermute | solution.py:93
  53.9 22.9 %copy-start.8 = (bf16[256,896]{1,0:T(8,128)(2,1)}, bf16[256,896]{1,0:T(8,128)(2,1)S(1)}, u32[]{:S(2)}) copy-start(bf16[256,896]{1,0:T(8,128)(2,1)S(1)} %collective-permute-done.3) | copy-start | bytes 1376260
  53.9 62.2 %collective-permute-start.16 = (bf16[256,7168]{1,0:T(8,128)(2,1)}, bf16[256,7168]{1,0:T(8,128)(2,1)S(1)}, u32[]{:S(2)}, u32[]{:S(2)}) collective-permute-start(bf16[256,7168]{1,0:T(8,128)(2,1)} %param.17), channel_id=1, source_target_pairs={{0,1},{1,0},{2,3},{3,2},{4,5},{5,4},{6,7},{7,6},{8,9},{9,8},{10,11... | collective-permute-start | bytes 11010056 | tf_op jit(solution)/shard_map/ppermute | solution.py:97
  54.4 22.4 %copy-start.1 = (bf16[256,896]{1,0:T(8,128)(2,1)}, bf16[256,896]{1,0:T(8,128)(2,1)S(1)}, u32[]{:S(2)}) copy-start(bf16[256,896]{1,0:T(8,128)(2,1)S(1)} %collective-permute-done.2) | copy-start | bytes 1376260
  54.4 19.2 %collective-permute-start.7 = (bf16[256,896]{1,0:T(8,128)(2,1)S(1)}, bf16[256,896]{1,0:T(8,128)(2,1)S(1)}, u32[]{:S(2)}, u32[]{:S(2)}) collective-permute-start(bf16[256,896]{1,0:T(8,128)(2,1)S(1)} %collective-permute-done.3), channel_id=1, source_target_pairs={{0,2},{1,3},{4,0},{5,1},{8,4},{9,5},{12,8},{13,9},{14,12},{15,13},... | collective-permute-start | bytes 1376264 | tf_op jit(solution)/shard_map/ppermute | solution.py:93
  61.5 25.1 %copy-start.14 = (bf16[256,896]{1,0:T(8,128)(2,1)}, bf16[256,896]{1,0:T(8,128)(2,1)S(1)}, u32[]{:S(2)}) copy-start(bf16[256,896]{1,0:T(8,128)(2,1)S(1)} %collective-permute-done.1) | copy-start | bytes 1376260
  61.5 15.3 %collective-permute-start.5 = (bf16[256,896]{1,0:T(8,128)(2,1)S(1)}, bf16[256,896]{1,0:T(8,128)(2,1)S(1)}, u32[]{:S(2)}, u32[]{:S(2)}) collective-permute-start(bf16[256,896]{1,0:T(8,128)(2,1)S(1)} %collective-permute-done.1), channel_id=1, source_target_pairs={{0,4},{1,5},{4,8},{5,9},{8,12},{9,13},{12,14},{13,15},{14,10},{15,... | collective-permute-start | bytes 1376264 | tf_op jit(solution)/shard_map/ppermute | solution.py:93
  63.7 22.9 %copy-start.12 = (bf16[256,896]{1,0:T(8,128)(2,1)}, bf16[256,896]{1,0:T(8,128)(2,1)S(1)}, u32[]{:S(2)}) copy-start(bf16[256,896]{1,0:T(8,128)(2,1)S(1)} %collective-permute-done.4) | copy-start | bytes 1376260
  63.7 19.7 %collective-permute-start.8 = (bf16[256,896]{1,0:T(8,128)(2,1)S(1)}, bf16[256,896]{1,0:T(8,128)(2,1)S(1)}, u32[]{:S(2)}, u32[]{:S(2)}) collective-permute-start(bf16[256,896]{1,0:T(8,128)(2,1)S(1)} %collective-permute-done.4), channel_id=1, source_target_pairs={{0,2},{1,3},{4,0},{5,1},{8,4},{9,5},{12,8},{13,9},{14,12},{15,13},... | collective-permute-start | bytes 1376264 | tf_op jit(solution)/shard_map/ppermute | solution.py:93
  73.6 14.7 %collective-permute-start.6 = (bf16[256,896]{1,0:T(8,128)(2,1)S(1)}, bf16[256,896]{1,0:T(8,128)(2,1)S(1)}, u32[]{:S(2)}, u32[]{:S(2)}) collective-permute-start(bf16[256,896]{1,0:T(8,128)(2,1)S(1)} %collective-permute-done.2), channel_id=1, source_target_pairs={{0,4},{1,5},{4,8},{5,9},{8,12},{9,13},{12,14},{13,15},{14,10},{15,... | collective-permute-start | bytes 1376264 | tf_op jit(solution)/shard_map/ppermute | solution.py:93
  76.8 19.0 %collective-permute-start.11 = (bf16[256,896]{1,0:T(8,128)(2,1)S(1)}, bf16[256,896]{1,0:T(8,128)(2,1)S(1)}, u32[]{:S(2)}, u32[]{:S(2)}) collective-permute-start(bf16[256,896]{1,0:T(8,128)(2,1)S(1)} %collective-permute-done.7), channel_id=1, source_target_pairs={{0,2},{1,3},{4,0},{5,1},{8,4},{9,5},{12,8},{13,9},{14,12},{15,13},... | collective-permute-start | bytes 1376264 | tf_op jit(solution)/shard_map/ppermute | solution.py:93
  83.4 49.6 %copy-start.3 = (bf16[256,896]{1,0:T(8,128)(2,1)}, bf16[256,896]{1,0:T(8,128)(2,1)S(1)}, u32[]{:S(2)}) copy-start(bf16[256,896]{1,0:T(8,128)(2,1)S(1)} %collective-permute-done.8) | copy-start | bytes 1376260
  83.4 10.6 %collective-permute-start.9 = (bf16[256,896]{1,0:T(8,128)(2,1)S(1)}, bf16[256,896]{1,0:T(8,128)(2,1)S(1)}, u32[]{:S(2)}, u32[]{:S(2)}) collective-permute-start(bf16[256,896]{1,0:T(8,128)(2,1)S(1)} %collective-permute-done.5), channel_id=1, source_target_pairs={{0,4},{1,5},{4,8},{5,9},{8,12},{9,13},{12,14},{13,15},{14,10},{15,... | collective-permute-start | bytes 1376264 | tf_op jit(solution)/shard_map/ppermute | solution.py:93
  88.3 12.1 %collective-permute-start.12 = (bf16[256,896]{1,0:T(8,128)(2,1)S(1)}, bf16[256,896]{1,0:T(8,128)(2,1)S(1)}, u32[]{:S(2)}, u32[]{:S(2)}) collective-permute-start(bf16[256,896]{1,0:T(8,128)(2,1)S(1)} %collective-permute-done.8), channel_id=1, source_target_pairs={{0,2},{1,3},{4,0},{5,1},{8,4},{9,5},{12,8},{13,9},{14,12},{15,13},... | collective-permute-start | bytes 1376264 | tf_op jit(solution)/shard_map/ppermute | solution.py:93
  94.0 12.6 %collective-permute-start.10 = (bf16[256,896]{1,0:T(8,128)(2,1)S(1)}, bf16[256,896]{1,0:T(8,128)(2,1)S(1)}, u32[]{:S(2)}, u32[]{:S(2)}) collective-permute-start(bf16[256,896]{1,0:T(8,128)(2,1)S(1)} %collective-permute-done.6), channel_id=1, source_target_pairs={{0,4},{1,5},{4,8},{5,9},{8,12},{9,13},{12,14},{13,15},{14,10},{15,... | collective-permute-start | bytes 1376264 | tf_op jit(solution)/shard_map/ppermute | solution.py:93
  95.8 25.5 %copy-start.4 = (bf16[256,896]{1,0:T(8,128)(2,1)}, bf16[256,896]{1,0:T(8,128)(2,1)S(1)}, u32[]{:S(2)}) copy-start(bf16[256,896]{1,0:T(8,128)(2,1)S(1)} %collective-permute-done.11) | copy-start | bytes 1376260
  95.8 15.8 %collective-permute-start.13 = (bf16[256,896]{1,0:T(8,128)(2,1)S(1)}, bf16[256,896]{1,0:T(8,128)(2,1)S(1)}, u32[]{:S(2)}, u32[]{:S(2)}) collective-permute-start(bf16[256,896]{1,0:T(8,128)(2,1)S(1)} %collective-permute-done.9), channel_id=1, source_target_pairs={{0,4},{1,5},{4,8},{5,9},{8,12},{9,13},{12,14},{13,15},{14,10},{15,... | collective-permute-start | bytes 1376264 | tf_op jit(solution)/shard_map/ppermute | solution.py:93
  100.4 34.3 %copy-start.5 = (bf16[256,896]{1,0:T(8,128)(2,1)}, bf16[256,896]{1,0:T(8,128)(2,1)S(1)}, u32[]{:S(2)}) copy-start(bf16[256,896]{1,0:T(8,128)(2,1)S(1)} %collective-permute-done.12) | copy-start | bytes 1376260
  102.1 14.0 %slice-start = ((s8[7340032]{0:T(1024)(128)(4,1)}), s8[4194304]{0:T(1024)(128)(4,1)S(1)}, s32[]{:S(2)}) async-start(s8[7340032]{0:T(1024)(128)(4,1)} %bitcast.62), calls=%async_computation | async-start | bytes 8388608
  102.3 10.1 %collective-permute-start.14 = (bf16[256,896]{1,0:T(8,128)(2,1)S(1)}, bf16[256,896]{1,0:T(8,128)(2,1)S(1)}, u32[]{:S(2)}, u32[]{:S(2)}) collective-permute-start(bf16[256,896]{1,0:T(8,128)(2,1)S(1)} %collective-permute-done.12), channel_id=1, source_target_pairs={{0,2},{1,3},{4,0},{5,1},{8,4},{9,5},{12,8},{13,9},{14,12},{15,13},... | collective-permute-start | bytes 1376264 | tf_op jit(solution)/shard_map/ppermute | solution.py:93
  106.8 9.3 %slice-start.1 = ((s8[7340032]{0:T(1024)(128)(4,1)}), s8[3145728]{0:T(1024)(128)(4,1)S(1)}, s32[]{:S(2)}) async-start(s8[7340032]{0:T(1024)(128)(4,1)} %bitcast.62), calls=%async_computation.1 | async-start | bytes 6291456
  108.6 7.8 %copy-start.9 = (bf16[256,896]{1,0:T(8,128)(2,1)S(1)}, bf16[256,896]{1,0:T(8,128)(2,1)}, u32[]{:S(2)}) copy-start(bf16[256,896]{1,0:T(8,128)(2,1)} %copy-done.8) | copy-start | bytes 1376260
  112.6 5.4 %copy-start.15 = (bf16[256,896]{1,0:T(8,128)(2,1)S(1)}, bf16[256,896]{1,0:T(8,128)(2,1)}, u32[]{:S(2)}) copy-start(bf16[256,896]{1,0:T(8,128)(2,1)} %copy-done.14) | copy-start | bytes 1376260
  116.1 6.9 %copy-start.7 = (bf16[4,64,896]{2,1,0:T(8,128)(2,1)S(1)}, bf16[4,64,896]{2,1,0:T(8,128)(2,1)}, u32[]{:S(2)}) copy-start(bf16[4,64,896]{2,1,0:T(8,128)(2,1)} %copy-done.6) | copy-start | bytes 1376260
  121.3 8.4 %copy-start.13 = (bf16[256,896]{1,0:T(8,128)(2,1)S(1)}, bf16[256,896]{1,0:T(8,128)(2,1)}, u32[]{:S(2)}) copy-start(bf16[256,896]{1,0:T(8,128)(2,1)} %copy-done.12) | copy-start | bytes 1376260
  123.0 8.4 %copy-start.2 = (bf16[256,896]{1,0:T(8,128)(2,1)S(1)}, bf16[256,896]{1,0:T(8,128)(2,1)}, u32[]{:S(2)}) copy-start(bf16[256,896]{1,0:T(8,128)(2,1)} %copy-done.1) | copy-start | bytes 1376260
  126.3 10.0 %copy-start.11 = (bf16[4,64,896]{2,1,0:T(8,128)(2,1)S(1)}, bf16[4,64,896]{2,1,0:T(8,128)(2,1)}, u32[]{:S(2)}) copy-start(bf16[4,64,896]{2,1,0:T(8,128)(2,1)} %copy-done.10) | copy-start | bytes 1376260
  145.2 10.5 %collective-permute-start.20 = (bf16[64,3584]{1,0:T(8,128)(2,1)S(1)}, bf16[64,3584]{1,0:T(8,128)(2,1)S(1)}, u32[]{:S(2)}, u32[]{:S(2)}) collective-permute-start(bf16[64,3584]{1,0:T(8,128)(2,1)S(1)} %get-tuple-element.24), channel_id=1, source_target_pairs={{0,4},{1,5},{4,8},{5,9},{8,12},{9,13},{12,14},{13,15},{14,10},{15,... | collective-permute-start | bytes 1376264 | tf_op jit(solution)/shard_map/ppermute | solution.py:93
  151.0 18.3 %copy-start = (bf16[512,7168]{1,0:T(8,128)(2,1)}, bf16[512,7168]{1,0:T(8,128)(2,1)S(1)}, u32[]{:S(2)}) copy-start(bf16[512,7168]{1,0:T(8,128)(2,1)S(1)} %multiply_convert_fusion) | copy-start | bytes 22020100
  155.8 13.5 %collective-permute-start.21 = (bf16[64,3584]{1,0:T(8,128)(2,1)S(1)}, bf16[64,3584]{1,0:T(8,128)(2,1)S(1)}, u32[]{:S(2)}, u32[]{:S(2)}) collective-permute-start(bf16[64,3584]{1,0:T(8,128)(2,1)S(1)} %add_convert_fusion.10), channel_id=1, source_target_pairs={{0,4},{1,5},{4,8},{5,9},{8,12},{9,13},{12,14},{13,15},{14,10},{15,... | collective-permute-start | bytes 1376264 | tf_op jit(solution)/shard_map/ppermute | solution.py:93
  158.5 15.9 %collective-permute-start.24 = (bf16[64,3584]{1,0:T(8,128)(2,1)}, bf16[64,3584]{1,0:T(8,128)(2,1)}, u32[]{:S(2)}, u32[]{:S(2)}) collective-permute-start(bf16[64,3584]{1,0:T(8,128)(2,1)} %get-tuple-element.16), channel_id=1, source_target_pairs={{0,2},{1,3},{4,0},{5,1},{8,4},{9,5},{12,8},{13,9},{14,12},{15,13},... | collective-permute-start | bytes 1376264 | tf_op jit(solution)/shard_map/ppermute | solution.py:93
  158.9 19.9 %collective-permute-start.27 = (bf16[64,3584]{1,0:T(8,128)(2,1)}, bf16[64,3584]{1,0:T(8,128)(2,1)}, u32[]{:S(2)}, u32[]{:S(2)}) collective-permute-start(bf16[64,3584]{1,0:T(8,128)(2,1)} %get-tuple-element.17), channel_id=1, source_target_pairs={{0,4},{1,5},{4,8},{5,9},{8,12},{9,13},{12,14},{13,15},{14,10},{15,... | collective-permute-start | bytes 1376264 | tf_op jit(solution)/shard_map/ppermute | solution.py:93
  160.5 18.3 %collective-permute-start.30 = (bf16[64,3584]{1,0:T(8,128)(2,1)}, bf16[64,3584]{1,0:T(8,128)(2,1)}, u32[]{:S(2)}, u32[]{:S(2)}) collective-permute-start(bf16[64,3584]{1,0:T(8,128)(2,1)} %get-tuple-element.25), channel_id=1, source_target_pairs={{0,2},{1,3},{4,0},{5,1},{8,4},{9,5},{12,8},{13,9},{14,12},{15,13},... | collective-permute-start | bytes 1376264 | tf_op jit(solution)/shard_map/ppermute | solution.py:93
  170.2 13.5 %collective-permute-start.22 = (bf16[64,3584]{1,0:T(8,128)(2,1)}, bf16[64,3584]{1,0:T(8,128)(2,1)}, u32[]{:S(2)}, u32[]{:S(2)}) collective-permute-start(bf16[64,3584]{1,0:T(8,128)(2,1)} %add_convert_fusion.9), channel_id=1, source_target_pairs={{0,4},{1,5},{4,8},{5,9},{8,12},{9,13},{12,14},{13,15},{14,10},{15,... | collective-permute-start | bytes 1376264 | tf_op jit(solution)/shard_map/ppermute | solution.py:93
  186.1 12.1 %collective-permute-start.25 = (bf16[64,3584]{1,0:T(8,128)(2,1)S(1)}, bf16[64,3584]{1,0:T(8,128)(2,1)S(1)}, u32[]{:S(2)}, u32[]{:S(2)}) collective-permute-start(bf16[64,3584]{1,0:T(8,128)(2,1)S(1)} %get-tuple-element.10), channel_id=1, source_target_pairs={{0,2},{1,3},{4,0},{5,1},{8,4},{9,5},{12,8},{13,9},{14,12},{15,13},... | collective-permute-start | bytes 1376264 | tf_op jit(solution)/shard_map/ppermute | solution.py:93
  186.7 11.5 %collective-permute-start.28 = (bf16[64,3584]{1,0:T(8,128)(2,1)S(1)}, bf16[64,3584]{1,0:T(8,128)(2,1)S(1)}, u32[]{:S(2)}, u32[]{:S(2)}) collective-permute-start(bf16[64,3584]{1,0:T(8,128)(2,1)S(1)} %get-tuple-element.12), channel_id=1, source_target_pairs={{0,4},{1,5},{4,8},{5,9},{8,12},{9,13},{12,14},{13,15},{14,10},{15,... | collective-permute-start | bytes 1376264 | tf_op jit(solution)/shard_map/ppermute | solution.py:93
  188.2 16.8 %collective-permute-start.31 = (bf16[64,3584]{1,0:T(8,128)(2,1)S(1)}, bf16[64,3584]{1,0:T(8,128)(2,1)S(1)}, u32[]{:S(2)}, u32[]{:S(2)}) collective-permute-start(bf16[64,3584]{1,0:T(8,128)(2,1)S(1)} %get-tuple-element.11), channel_id=1, source_target_pairs={{0,2},{1,3},{4,0},{5,1},{8,4},{9,5},{12,8},{13,9},{14,12},{15,13},... | collective-permute-start | bytes 1376264 | tf_op jit(solution)/shard_map/ppermute | solution.py:93
  206.6 13.5 %collective-permute-start.32 = (bf16[64,3584]{1,0:T(8,128)(2,1)S(1)}, bf16[64,3584]{1,0:T(8,128)(2,1)S(1)}, u32[]{:S(2)}, u32[]{:S(2)}) collective-permute-start(bf16[64,3584]{1,0:T(8,128)(2,1)S(1)} %get-tuple-element.14), channel_id=1, source_target_pairs={{0,2},{1,3},{4,0},{5,1},{8,4},{9,5},{12,8},{13,9},{14,12},{15,13},... | collective-permute-start | bytes 1376264 | tf_op jit(solution)/shard_map/ppermute | solution.py:93
  209.2 14.0 %collective-permute-start.23 = (bf16[64,3584]{1,0:T(8,128)(2,1)S(1)}, bf16[64,3584]{1,0:T(8,128)(2,1)S(1)}, u32[]{:S(2)}, u32[]{:S(2)}) collective-permute-start(bf16[64,3584]{1,0:T(8,128)(2,1)S(1)} %get-tuple-element.9), channel_id=1, source_target_pairs={{0,4},{1,5},{4,8},{5,9},{8,12},{9,13},{12,14},{13,15},{14,10},{15,... | collective-permute-start | bytes 1376264 | tf_op jit(solution)/shard_map/ppermute | solution.py:93
  210.8 16.9 %collective-permute-start.26 = (bf16[64,3584]{1,0:T(8,128)(2,1)S(1)}, bf16[64,3584]{1,0:T(8,128)(2,1)S(1)}, u32[]{:S(2)}, u32[]{:S(2)}) collective-permute-start(bf16[64,3584]{1,0:T(8,128)(2,1)S(1)} %get-tuple-element.13), channel_id=1, source_target_pairs={{0,2},{1,3},{4,0},{5,1},{8,4},{9,5},{12,8},{13,9},{14,12},{15,13},... | collective-permute-start | bytes 1376264 | tf_op jit(solution)/shard_map/ppermute | solution.py:93
  211.3 16.4 %collective-permute-start.29 = (bf16[64,3584]{1,0:T(8,128)(2,1)S(1)}, bf16[64,3584]{1,0:T(8,128)(2,1)S(1)}, u32[]{:S(2)}, u32[]{:S(2)}) collective-permute-start(bf16[64,3584]{1,0:T(8,128)(2,1)S(1)} %get-tuple-element.15), channel_id=1, source_target_pairs={{0,4},{1,5},{4,8},{5,9},{8,12},{9,13},{12,14},{13,15},{14,10},{15,... | collective-permute-start | bytes 1376264 | tf_op jit(solution)/shard_map/ppermute | solution.py:93
  221.3 11.3 %collective-permute-start.33 = (bf16[64,3584]{1,0:T(8,128)(2,1)S(1)}, bf16[64,3584]{1,0:T(8,128)(2,1)S(1)}, u32[]{:S(2)}, u32[]{:S(2)}) collective-permute-start(bf16[64,3584]{1,0:T(8,128)(2,1)S(1)} %add_convert_fusion.1), channel_id=1, source_target_pairs={{0,2},{1,3},{4,0},{5,1},{8,4},{9,5},{12,8},{13,9},{14,12},{15,13},... | collective-permute-start | bytes 1376264 | tf_op jit(solution)/shard_map/ppermute | solution.py:93

commit v3 on v0

--- a/solution.py
+++ b/solution.py
@@ -1,6 +1,8 @@
 import jax
 import jax.numpy as jnp
 from jax import lax
+from jax.experimental import pallas as pl
+from jax.experimental.pallas import tpu as pltpu
 from jax.sharding import PartitionSpec as P
 
 FSPLIT = 8
@@ -43,7 +45,7 @@
     return jnp.dot(hidden, w_down, preferred_element_type=jnp.float32).astype(jnp.bfloat16)
 
 
-def body(residual, attn_out, norm_gain, expert_routes, route_gain, w_gate, w_up, w_down):
+def routed_body(residual, attn_out, norm_gain, expert_routes, route_gain, w_gate, w_up, w_down):
     devices = lax.axis_size("ep")
     tok_here = expert_routes.shape[0]
     route_slots = expert_routes.shape[1]
@@ -74,6 +76,358 @@
     return (stream_rows.astype(jnp.float32) + routed_sum).astype(jnp.bfloat16)
 
 
+def token_gains(routes, route_gain, experts):
+    named = routes[:, :, None] == jnp.arange(experts, dtype=jnp.int32)
+    return jnp.where(named, route_gain[:, :, None], 0.0).sum(axis=1)
+
+
+def ring_order(chips):
+    return list(range(0, chips, 2)) + list(reversed(range(1, chips, 2)))
+
+
+def swap_cores(value):
+    return lax.ppermute(value, "ep", [(i, i ^ 1) for i in range(lax.axis_size("ep"))])
+
+
+def gather_small(value, chips, chip):
+    width = 1
+    while width < chips:
+        pairs = [
+            (2 * i + core, 2 * (i ^ width) + core) for i in range(chips) for core in range(2)
+        ]
+        other = lax.ppermute(value, "ep", pairs)
+        upper = (chip // width) % 2 == 1
+        value = jnp.concatenate(
+            [jnp.where(upper, other, value), jnp.where(upper, value, other)], axis=0
+        )
+        width *= 2
+    return value
+
+
+def ring_shift(value, ring, step):
+    chips = len(ring)
+    pairs = [
+        (2 * ring[i] + core, 2 * ring[(i + step) % chips] + core)
+        for i in range(chips)
+        for core in range(2)
+    ]
+    return lax.ppermute(value, "ep", pairs)
+
+
+VMEM_BYTES = 32 * 1024 * 1024
+
+
+def whole(shape):
+    return pl.BlockSpec(shape, lambda i, where: (0,) * len(shape))
+
+
+def accumulate(where, positions, parts, norm_gain, weights, carried, closing):
+    count = len(positions)
+    rows, width = parts[0][0].shape
+    hidden_here = weights[0].shape[1]
+    model_width = weights[0].shape[0]
+    tok_here = closing["tok_here"]
+    far = rows // tok_here
+    last = "gain" in closing
+    first = carried is None
+    side = closing["side"]
+
+    def kernel(where_ref, *refs):
+        refs = list(refs)
+        xs = [[refs.pop(0) for _ in range(2)] for _ in range(count)]
+        scales = [refs.pop(0) for _ in range(count)]
+        tables = [[refs.pop(0) for _ in range(len(weights))] for _ in range(count)]
+        acc_in, sq_in = (None, None) if first else (refs.pop(0), refs.pop(0))
+        gain_ref = refs.pop(0) if last else None
+        owns = [refs.pop(0) for _ in range(count)]
+        if last:
+            hidden_ref = refs.pop(0)
+        else:
+            acc_out, sq_out = refs.pop(0), refs.pop(0)
+        chip = where_ref[0]
+        for b in range(count):
+            start = pl.multiple_of(lax.rem(chip, far) * tok_here, tok_here)
+
+            @pl.when(chip < far)
+            def _():
+                owns[b][...] = xs[b][0][pl.ds(start, tok_here), :]
+
+            @pl.when(chip >= far)
+            def _():
+                owns[b][...] = xs[b][1][pl.ds(start, tok_here), :]
+
+        for part in range(2):
+            span = slice(part * rows, (part + 1) * rows)
+            scaled, squares = [], None if first else sq_in[span, :]
+            for b in range(count):
+                values = xs[b][part][...].astype(jnp.float32)
+                for lane in range(0, width, side):
+                    piece = values[:, lane : lane + side]
+                    squares = piece * piece if squares is None else squares + piece * piece
+                scaled.append((values * scales[b][0]).astype(jnp.bfloat16))
+            totals = []
+            for which in range(len(weights)):
+                cols = slice(which * hidden_here, (which + 1) * hidden_here)
+                total = None if first else acc_in[span, cols]
+                for b in range(count):
+                    product = jnp.dot(
+                        scaled[b], tables[b][which][...], preferred_element_type=jnp.float32
+                    )
+                    total = product if total is None else total + product
+                if last:
+                    totals.append(total)
+                else:
+                    acc_out[span, cols] = total
+            if last:
+                mean = jnp.sum(squares, axis=1, keepdims=True) / model_width
+                inv_rms = lax.rsqrt(mean + epsilon)
+                for core in range(len(weights) // 2):
+                    gate_act = totals[2 * core] * inv_rms
+                    up_act = totals[2 * core + 1] * inv_rms
+                    act = gate_act * jax.nn.sigmoid(gate_act) * up_act * gain_ref[span, :]
+                    cols = slice(core * hidden_here, (core + 1) * hidden_here)
+                    hidden_ref[span, cols] = act.astype(jnp.bfloat16)
+            else:
+                sq_out[span, :] = squares
+
+    def table_spec(position):
+        return pl.BlockSpec((width, hidden_here), lambda i, where: (where[position], 0))
+
+    operands = [half for block in parts for half in block]
+    in_specs = [whole((rows, width))] * (2 * count)
+    for position in positions:
+        operands.append(norm_gain)
+        in_specs.append(
+            pl.BlockSpec((1, 1, width), lambda i, where, p=position: (where[p], 0, 0))
+        )
+    for position in positions:
+        operands.extend(weights)
+        in_specs.extend([table_spec(position)] * len(weights))
+    sums = (2 * rows, len(weights) * hidden_here)
+    aliases = {}
+    if not first:
+        if not last:
+            aliases = {len(operands) + 1: count, len(operands) + 2: count + 1}
+        operands.extend(carried)
+        in_specs.extend([whole(sums), whole((2 * rows, side))])
+    out_shape = [jax.ShapeDtypeStruct((tok_here, width), jnp.bfloat16)] * count
+    out_specs = [whole((tok_here, width))] * count
+    if last:
+        operands.append(closing["gain"])
+        in_specs.append(whole((2 * rows, 1)))
+        shape = (2 * rows, len(weights) // 2 * hidden_here)
+        out_shape.append(jax.ShapeDtypeStruct(shape, jnp.bfloat16))
+        out_specs.append(whole(shape))
+    else:
+        out_shape.append(jax.ShapeDtypeStruct(sums, jnp.float32))
+        out_shape.append(jax.ShapeDtypeStruct((2 * rows, side), jnp.float32))
+        out_specs.extend([whole(sums), whole((2 * rows, side))])
+    flops = 2 * count * 2 * rows * width * sums[1]
+    return pl.pallas_call(
+        kernel,
+        grid_spec=pltpu.PrefetchScalarGridSpec(
+            num_scalar_prefetch=1, grid=(1,), in_specs=in_specs, out_specs=out_specs
+        ),
+        out_shape=out_shape,
+        input_output_aliases=aliases,
+        compiler_params=pltpu.CompilerParams(vmem_limit_bytes=VMEM_BYTES),
+        cost_estimate=pl.CostEstimate(
+            flops=flops,
+            bytes_accessed=count * width * (rows * 4 + sums[1] * 2) + sums[0] * sums[1] * 8,
+            transcendentals=0,
+        ),
+    )(where, *operands)
+
+
+def add_rows(where, position, table, moved):
+    rows, width = moved.shape
+    steps = 2
+
+    def kernel(where_ref, table_ref, moved_ref, out_ref):
+        total = table_ref[...].astype(jnp.float32) + moved_ref[...].astype(jnp.float32)
+        out_ref[...] = total.astype(jnp.bfloat16)
+
+    here = pl.BlockSpec((rows, width // steps), lambda i, where: (0, i))
+    return pl.pallas_call(
+        kernel,
+        grid_spec=pltpu.PrefetchScalarGridSpec(
+            num_scalar_prefetch=1,
+            grid=(steps,),
+            in_specs=[
+                pl.BlockSpec((rows, width // steps), lambda i, where: (where[position], i)),
+                here,
+            ],
+            out_specs=here,
+        ),
+        out_shape=jax.ShapeDtypeStruct((rows, width), jnp.bfloat16),
+        compiler_params=pltpu.CompilerParams(vmem_limit_bytes=VMEM_BYTES),
+        cost_estimate=pl.CostEstimate(
+            flops=rows * width, bytes_accessed=rows * width * 6, transcendentals=0
+        ),
+    )(where, table, moved)
+
+
+def own_rows(where, positions, pieces, tables):
+    rows, width = pieces[0].shape
+    chips = len(pieces)
+    model_width = chips * width
+    half = model_width // 2
+
+    def kernel(where_ref, *refs):
+        out_ref = refs[-1]
+        for part in range(2):
+            out_ref[:, part * half : (part + 1) * half] = refs[chips + part][...].astype(
+                jnp.float32
+            )
+        for k in range(chips):
+            start = pl.multiple_of(where_ref[positions[k]] * width, width)
+            out_ref[:, pl.ds(start, width)] += refs[k][...].astype(jnp.float32)
+
+    return pl.pallas_call(
+        kernel,
+        grid_spec=pltpu.PrefetchScalarGridSpec(
+            num_scalar_prefetch=1,
+            grid=(1,),
+            in_specs=[whole((rows, width))] * chips
+            + [pl.BlockSpec((rows, half), lambda i, where: (where[0], 0))] * 2,
+            out_specs=whole((rows, model_width)),
+        ),
+        out_shape=jax.ShapeDtypeStruct((rows, model_width), jnp.float32),
+        compiler_params=pltpu.CompilerParams(vmem_limit_bytes=VMEM_BYTES),
+        cost_estimate=pl.CostEstimate(
+            flops=rows * model_width, bytes_accessed=rows * model_width * 8, transcendentals=0
+        ),
+    )(where, *pieces, *tables)
+
+
+def final_sum(base, arrived):
+    rows, model_width = base.shape
+    half = model_width // 2
+
+    def kernel(base_ref, *refs):
+        out_ref = refs[-1]
+        for part in range(2):
+            cols = slice(part * half, (part + 1) * half)
+            total = base_ref[:, cols]
+            for k in range(len(arrived[part])):
+                total = total + refs[k + part * len(arrived[0])][...].astype(jnp.float32)
+            out_ref[:, cols] = total.astype(jnp.bfloat16)
+
+    return pl.pallas_call(
+        kernel,
+        out_shape=jax.ShapeDtypeStruct((rows, model_width), jnp.bfloat16),
+        compiler_params=pltpu.CompilerParams(vmem_limit_bytes=VMEM_BYTES),
+        cost_estimate=pl.CostEstimate(
+            flops=rows * model_width * 3, bytes_accessed=rows * model_width * 10, transcendentals=0
+        ),
+    )(base, *arrived[0], *arrived[1])
+
+
+def dense_body(residual, attn_out, norm_gain, expert_routes, route_gain, w_gate, w_up, w_down):
+    devices = lax.axis_size("ep")
+    experts = devices // FSPLIT
+    chips = devices // 2
+    far = chips // 2
+    tok_here = expert_routes.shape[0]
+    feat_here = residual.shape[1]
+    model_width = w_gate.shape[0]
+    half = model_width // 2
+    ring = ring_order(chips)
+    me = lax.axis_index("ep")
+    chip, core = me // 2, me % 2
+    seen = [[ring[(ring.index(i) + d) % chips] for d in range(chips)] for i in range(chips)]
+    where = lax.dynamic_index_in_dim(jnp.asarray(seen, jnp.int32), chip, 0, keepdims=False)
+
+    stream_feat = (residual.astype(jnp.float32) + attn_out.astype(jnp.float32)).astype(jnp.bfloat16)
+    by_core = stream_feat.reshape(chips, 2, tok_here, feat_here)
+    mine = lax.dynamic_index_in_dim(by_core, core, 1, keepdims=False)
+    theirs = lax.dynamic_index_in_dim(by_core, 1 - core, 1, keepdims=False)
+    swapped = swap_cores(theirs)
+    block = jnp.concatenate(
+        [jnp.where(core == 0, mine, swapped), jnp.where(core == 0, swapped, mine)], axis=2
+    )
+    block = block.reshape(2, far * tok_here, 2 * feat_here)
+    blocks = {0: [block[0], block[1]]}
+
+    own_gains = token_gains(expert_routes, route_gain, experts)
+    swapped, w_gate, w_up, w_down, own_gains = lax.optimization_barrier(
+        (swapped, w_gate, w_up, w_down, own_gains)
+    )
+    weights = [w_gate, w_up, swap_cores(w_gate), swap_cores(w_up)]
+    other_down = swap_cores(w_down)
+    down = [
+        jnp.concatenate([w_down[:, cols], other_down[:, cols]], axis=0)
+        for cols in (slice(0, half), slice(half, model_width))
+    ]
+    gains = gather_small(own_gains, chips, chip)
+    gain_here = lax.dynamic_slice_in_dim(gains, me // FSPLIT, 1, axis=1)
+
+    for distance in range(1, far):
+        for sign, order in ((-1, (0, 1)), (1, (1, 0))):
+            came = [None, None]
+            for part in order:
+                came[part] = ring_shift(blocks[sign * (distance - 1)][part], ring, -sign)
+            blocks[sign * distance] = came
+    blocks[far] = [
+        ring_shift(blocks[1 - far][0], ring, 1),
+        ring_shift(blocks[far - 1][1], ring, -1),
+    ]
+
+    gain_rows = norm_gain.reshape(chips, 1, 2 * feat_here)
+    closing = {"tok_here": tok_here, "side": 128}
+    carried, owns, positions = None, [], []
+    for distance in range(far + 1):
+        group = [distance] if distance in (0, far) else [distance, -distance]
+        at = [d % chips for d in group]
+        if distance == far:
+            closing["gain"] = gain_here
+        made = accumulate(
+            where, at, [blocks[d] for d in group], gain_rows, weights, carried, closing
+        )
+        owns.extend(made[: len(at)])
+        positions.extend(at)
+        carried = made[len(at) :]
+    hidden = carried[0]
+
+    def contribution(rows, part):
+        return jnp.dot(rows, down[part], preferred_element_type=jnp.float32).astype(jnp.bfloat16)
+
+    farthest = lax.dynamic_slice_in_dim(hidden, where[far] * tok_here, tok_here, axis=0)
+    moving = {
+        1: [ring_shift(contribution(farthest, 0), ring, 1), None],
+        -1: [None, ring_shift(contribution(farthest, 1), ring, -1)],
+    }
+    everything = [contribution(hidden, part) for part in range(2)]
+    base = own_rows(where, positions, owns, everything)
+    for distance in range(far - 1, 0, -1):
+        for sign, order in ((1, (1, 0)), (-1, (0, 1))):
+            position = (sign * distance) % chips
+            sent = [None, None]
+            for part in order:
+                if moving[sign][part] is None:
+                    value = lax.dynamic_slice_in_dim(
+                        everything[part], where[position] * tok_here, tok_here, axis=0
+                    )
+                else:
+                    value = add_rows(where, position, everything[part], moving[sign][part])
+                sent[part] = ring_shift(value, ring, sign)
+            moving[sign] = sent
+    arrived = [
+        [moving[sign][part] for sign in (1, -1) if moving[sign][part] is not None]
+        for part in range(2)
+    ]
+    return final_sum(base, arrived)
+
+
+def body(residual, attn_out, norm_gain, expert_routes, route_gain, w_gate, w_up, w_down):
+    tok_here, route_slots = expert_routes.shape
+    devices = lax.axis_size("ep")
+    capacity = route_slots * tok_here // (devices // FSPLIT)
+    dense = capacity >= tok_here and devices % 4 == 0 and devices & (devices - 1) == 0
+    chosen = dense_body if dense else routed_body
+    return chosen(residual, attn_out, norm_gain, expert_routes, route_gain, w_gate, w_up, w_down)
+
+
 def solution(mesh):
     in_specs = (
         P("groups", "ep"),

time: 733 us -> 188 us (0.26)
  the two profiles are of different devices: /device:TPU:15 before, /device:TPU:0 now
where the time goes in v3:
time: 188 us
  waiting for transfers between devices  98 us (52%)
  starting transfers between devices  40 us (21%)
  Pallas kernels  30.4 us (16%)
  local copies, waits for them, and re-layouts  9.35 us (5%)
  matrix products  5.63 us (3%)
  other arithmetic  2.4 us (1%)
  between operations  2.31 us (1%)
    ppermute x28, waiting for transfers between devices, ring_shift(): return lax.ppermute(value, 'ep', pairs)  79.7 us
    ppermute x28, starting transfers between devices, ring_shift(): return lax.ppermute(value, 'ep', pairs)  31.4 us
    pallas_call x5, Pallas kernels, accumulate(): pl.pallas_call(kernel, grid_spec=pltpu.PrefetchScalarGridSpec(num_scalar_...  20.2 us
    ppermute x3, waiting for transfers between devices, gather_small(): other = lax.ppermute(value, 'ep', pairs)  16.8 us
    pallas_call x10, Pallas kernels, add_rows(): pl.pallas_call(kernel, grid_spec=pltpu.PrefetchScalarGridSpec(num_scalar_...  8.17 us
    ppermute x3, starting transfers between devices, gather_small(): other = lax.ppermute(value, 'ep', pairs)  7.56 us
    dot_general x4, matrix products, contribution(): jnp.dot(rows, down[part], preferred_element_type=jnp.float32)  5.63 us
    slice x1, local copies, waits for them, and re-layouts, dense_body(): w_down[:, cols]  4.18 us
  transfers between devices with their start and end apart: 35, of which 18 were waited for; matrix products, arithmetic and copies ran while one was open for 5% of the time, Pallas kernels for 14%

profile of v3, /device:TPU:0, one launch (start us, length us, event | category | flops | bytes accessed | tf_op | source)
XLA Modules:
  0.0 188.1 jit_solution(4340255751053904769)
XLA Ops:
  0.0 1.8 add_convert_fusion
  3.0 1.5 collective-permute-done
  4.5 2.9 %collective-permute-start.17 = (f32[64,2]{0,1:T(2,128)S(1)}, f32[64,2]{0,1:T(2,128)S(1)}, u32[]{:S(2)}, u32[]{:S(2)}) collective-permute-start(f32[64,2]{0,1:T(2,128)S(1)} %fusion.3), channel_id=1, source_target_pairs={{0,2},{1,3},{2,0},{3,1},{4,6},{5,7},{6,4},{7,5},{8,10},{9,11},{10,... | collective-permute-start | bytes 1544 | tf_op jit(solution)/shard_map/ppermute | solution.py:98
  8.0 0.9 collective-permute-done.17
  9.0 2.1 %collective-permute-start.18 = (f32[128,2]{0,1:T(2,128)S(1)}, f32[128,2]{0,1:T(2,128)S(1)}, u32[]{:S(2)}, u32[]{:S(2)}) collective-permute-start(f32[128,2]{0,1:T(2,128)S(1)} %pad_maximum_fusion.8), channel_id=1, source_target_pairs={{0,4},{1,5},{2,6},{3,7},{4,0},{5,1},{6,2},{7,3},{8,12},{9,13},{10,... | collective-permute-start | bytes 3080 | tf_op jit(solution)/shard_map/ppermute | solution.py:98
  11.1 1.5 collective-permute-start.4
  13.1 8.1 %collective-permute-done.18 = f32[128,2]{0,1:T(2,128)S(1)} collective-permute-done((f32[128,2]{0,1:T(2,128)S(1)}, f32[128,2]{0,1:T(2,128)S(1)}, u32[]{:S(2)}, u32[]{:S(2)}) %collective-permute-start.18) | collective-permute-done | bytes 1056 | tf_op jit(solution)/shard_map/ppermute | solution.py:98
  21.3 2.6 %collective-permute-start.19 = (f32[256,2]{0,1:T(2,128)S(1)}, f32[256,2]{0,1:T(2,128)S(1)}, u32[]{:S(2)}, u32[]{:S(2)}) collective-permute-start(f32[256,2]{0,1:T(2,128)S(1)} %pad_maximum_fusion.7), channel_id=1, source_target_pairs={{0,8},{1,9},{2,10},{3,11},{4,12},{5,13},{6,14},{7,15},{8,0},{9,1},... | collective-permute-start | bytes 6152 | tf_op jit(solution)/shard_map/ppermute | solution.py:98
  23.9 7.8 %collective-permute-done.19 = f32[256,2]{0,1:T(2,128)S(1)} collective-permute-done((f32[256,2]{0,1:T(2,128)S(1)}, f32[256,2]{0,1:T(2,128)S(1)}, u32[]{:S(2)}, u32[]{:S(2)}) %collective-permute-start.19) | collective-permute-done | bytes 2080 | tf_op jit(solution)/shard_map/ppermute | solution.py:98
  32.2 1.6 collective-permute-start.5
  33.8 11.7 %collective-permute-done.5.refs_2_ = bf16[256,896]{1,0:T(8,128)(2,1)S(1)} collective-permute-done((bf16[256,896]{1,0:T(8,128)(2,1)S(1)}, bf16[256,896]{1,0:T(8,128)(2,1)S(1)}, u32[]{:S(2)}, u32[]{:S(2)}) %collective-permute-start.5) | collective-permute-done | bytes 458784 | tf_op jit(solution)/shard_map/ppermute | solution.py:114
  45.5 8.9 %collective-permute-done.10.refs_3_ = bf16[256,896]{1,0:T(8,128)(2,1)S(1)} collective-permute-done((bf16[256,896]{1,0:T(8,128)(2,1)S(1)}, bf16[256,896]{1,0:T(8,128)(2,1)S(1)}, u32[]{:S(2)}, u32[]{:S(2)}) %collective-permute-start.10) | collective-permute-done | bytes 458784 | tf_op jit(solution)/shard_map/ppermute | solution.py:114
  54.5 0.7 constant_dynamic-slice_fusion.2
  55.2 0.6 fusion.14
  57.8 2.1 %collective-permute-start.9 = (bf16[256,896]{1,0:T(8,128)(2,1)S(1)}, bf16[256,896]{1,0:T(8,128)(2,1)}, u32[]{:S(2)}, u32[]{:S(2)}) collective-permute-start(bf16[256,896]{1,0:T(8,128)(2,1)S(1)} %collective-permute-done.5.refs_2_), channel_id=1, source_target_pairs={{0,4},{1,5},{4,8},{5,9},{8,12},{9,13},{12,14},{13,15},{14,10},{15,... | collective-permute-start | bytes 1376264 | tf_op jit(solution)/shard_map/ppermute | solution.py:114
  59.8 6.5 %collective-permute-done.8.refs_1_ = bf16[256,896]{1,0:T(8,128)(2,1)} collective-permute-done((bf16[256,896]{1,0:T(8,128)(2,1)S(1)}, bf16[256,896]{1,0:T(8,128)(2,1)}, u32[]{:S(2)}, u32[]{:S(2)}) %collective-permute-start.8) | collective-permute-done | bytes 458784 | tf_op jit(solution)/shard_map/ppermute | solution.py:114
  66.6 4.2 %fusion.12 = (bf16[256,3584]{1,0:T(8,128)(2,1)}, bf16[256,3584]{1,0:T(8,128)(2,1)}) fusion(bf16[256,7168]{1,0:T(8,128)(2,1)} %param.16), kind=kLoop, calls=%fused_computation.39 | loop fusion | bytes 7340032 | tf_op jit(solution)/shard_map/slice | solution.py:359
  71.0 1.0 collective-permute-start.11
  72.0 8.1 %collective-permute-done.12.refs_1_ = bf16[256,896]{1,0:T(8,128)(2,1)} collective-permute-done((bf16[256,896]{1,0:T(8,128)(2,1)}, bf16[256,896]{1,0:T(8,128)(2,1)}, u32[]{:S(2)}, u32[]{:S(2)}) %collective-permute-start.12) | collective-permute-done | bytes 458784 | tf_op jit(solution)/shard_map/ppermute | solution.py:114
  80.1 1.6 collective-permute-start.13
  81.7 0.6 collective-permute-start.14
  82.3 2.3 %fusion.13 = (bf16[256,3584]{1,0:T(8,128)(2,1)S(1)}, bf16[256,3584]{1,0:T(8,128)(2,1)S(1)}) fusion(bf16[256,7168]{1,0:T(8,128)(2,1)} %collective-permute-done.20), kind=kLoop, calls=%fused_computation.40 | loop fusion | bytes 7340032 | tf_op jit(solution)/shard_map/slice | solution.py:359
  84.6 9.2 %collective-permute-done.13.refs_2_ = bf16[256,896]{1,0:T(8,128)(2,1)S(1)} collective-permute-done((bf16[256,896]{1,0:T(8,128)(2,1)}, bf16[256,896]{1,0:T(8,128)(2,1)S(1)}, u32[]{:S(2)}, u32[]{:S(2)}) %collective-permute-start.13) | collective-permute-done | bytes 458784 | tf_op jit(solution)/shard_map/ppermute | solution.py:114
  93.8 1.6 collective-permute-start.15
  95.8 3.0 %shard_map.91 = (bf16[64,896]{1,0:T(8,128)(2,1)S(1)}, f32[512,1024]{1,0:T(8,128)S(1)}, f32[512,128]{1,0:T(8,128)S(1)}) custom-call(s32[8]{0:T(128)S(1)} %get-tuple-element.56.where_ref, bf16[256,896]{1,0:T(8,128)(2,1)S(1)} %bitcast.21, bf16[256,896]{1,0:T(8,128)(2,1)S(1)} %bitcast.18, f32[8,1,896]{2,1,0:T(1,128)S(1)} %bitcast.22, ...), custom_call_target="tpu_custom_call" | custom-call | flops 939524096 | bytes 6946816 | tf_op jit(solution)/shard_map/pallas_call | solution.py:226
  98.8 4.5 %shard_map.92 = (bf16[64,896]{1,0:T(8,128)(2,1)S(1)}, bf16[64,896]{1,0:T(8,128)(2,1)S(1)}, f32[512,1024]{1,0:T(8,128)S(1)}, f32[512,128]{1,0:T(8,128)S(1)}) custom-call(s32[8]{0:T(128)S(1)} %get-tuple-element.56.where_ref, bf16[256,896]{1,0:T(8,128)(2,1)S(1)} %collective-permute-done.3.refs_0_, ...), custom_call_target="tpu_custom_call", output_to_operand_aliasing={{2}: (15, {}), {3}: (16, {})} | custom-call | flops 1879048192 | bytes 9699328 | tf_op jit(solution)/shard_map/pallas_call | solution.py:226
  103.3 4.9 %shard_map.93 = (bf16[64,896]{1,0:T(8,128)(2,1)S(1)}, bf16[64,896]{1,0:T(8,128)(2,1)S(1)}, f32[512,1024]{1,0:T(8,128)S(1)}, f32[512,128]{1,0:T(8,128)S(1)}) custom-call(s32[8]{0:T(128)S(1)} %get-tuple-element.56.where_ref, bf16[256,896]{1,0:T(8,128)(2,1)} %collective-permute-done.7.refs_0_, ...), custom_call_target="tpu_custom_call", output_to_operand_aliasing={{2}: (15, {}), {3}: (16, {})} | custom-call | flops 1879048192 | bytes 9699328 | tf_op jit(solution)/shard_map/pallas_call | solution.py:226
  108.2 4.6 %shard_map.94 = (bf16[64,896]{1,0:T(8,128)(2,1)S(1)}, bf16[64,896]{1,0:T(8,128)(2,1)S(1)}, f32[512,1024]{1,0:T(8,128)S(1)}, f32[512,128]{1,0:T(8,128)S(1)}) custom-call(s32[8]{0:T(128)S(1)} %get-tuple-element.56.where_ref, bf16[256,896]{1,0:T(8,128)(2,1)S(1)} %collective-permute-done.11.refs_0_, ...), custom_call_target="tpu_custom_call", output_to_operand_aliasing={{2}: (15, {}), {3}: (16, {})} | custom-call | flops 1879048192 | bytes 9699328 | tf_op jit(solution)/shard_map/pallas_call | solution.py:226
  112.8 3.3 %shard_map.95 = (bf16[64,896]{1,0:T(8,128)(2,1)S(1)}, bf16[512,512]{1,0:T(8,128)(2,1)S(1)}) custom-call(s32[8]{0:T(128)S(1)} %get-tuple-element.56.where_ref, bf16[256,896]{1,0:T(8,128)(2,1)S(1)} %collective-permute-done.15.refs_0_, bf16[256,896]{1,0:T(8,128)(2,1)S(1)} %collective-permute-done.16.refs_1_, f32[8,1,896]{2,1,0:T(1,128)S(1)} %bitcast.29, ...), custom_call_target="tpu_custom_call" | custom-call | flops 939524096 | bytes 6946816 | tf_op jit(solution)/shard_map/pallas_call | solution.py:226
  116.1 2.1 %convolution_convert_fusion.refs_9_.table_ref = bf16[512,3584]{1,0:T(8,128)(2,1)S(1)} fusion(bf16[512,512]{1,0:T(8,128)(2,1)S(1)} %get-tuple-element.45, bf16[256,3584]{1,0:T(8,128)(2,1)S(1)} %get-tuple-element.49, bf16[256,3584]{1,0:T(8,128)(2,1)S(1)} %copy-done.4), kind=kOutput, calls=%fused_computation | convolution fusion | flops 1888223232 | bytes 7864320 | tf_op jit(solution)/shard_map/dot_general | solution.py:393
  118.2 0.7 convolution_convert_fusion.2
  119.0 0.7 copy-done.3
  119.7 2.1 %convolution_convert_fusion.1.refs_8_.table_ref = bf16[512,3584]{1,0:T(8,128)(2,1)S(1)} fusion(bf16[512,512]{1,0:T(8,128)(2,1)S(1)} %get-tuple-element.45, bf16[256,3584]{1,0:T(8,128)(2,1)S(1)} %get-tuple-element.50, bf16[256,3584]{1,0:T(8,128)(2,1)S(1)} %copy-done.3), kind=kOutput, calls=%fused_computation.1 | convolution fusion | flops 1888223232 | bytes 7864320 | tf_op jit(solution)/shard_map/dot_general | solution.py:393
  121.8 0.7 convolution_convert_fusion.3
  122.9 1.8 collective-permute-start.28
  124.7 1.6 collective-permute-start.21
  126.8 8.3 %collective-permute-done.31.moved_ref = bf16[64,3584]{1,0:T(8,128)(2,1)S(1)} collective-permute-done((bf16[64,3584]{1,0:T(8,128)(2,1)S(1)}, bf16[64,3584]{1,0:T(8,128)(2,1)S(1)}, u32[]{:S(2)}, u32[]{:S(2)}) %collective-permute-start.31) | collective-permute-done | bytes 458784 | tf_op jit(solution)/shard_map/ppermute | solution.py:114
  135.1 0.8 shard_map.104
  135.9 1.3 collective-permute-start.32
  137.2 7.9 %collective-permute-done.21.moved_ref = bf16[64,3584]{1,0:T(8,128)(2,1)S(1)} collective-permute-done((bf16[64,3584]{1,0:T(8,128)(2,1)S(1)}, bf16[64,3584]{1,0:T(8,128)(2,1)S(1)}, u32[]{:S(2)}, u32[]{:S(2)}) %collective-permute-start.21) | collective-permute-done | bytes 458784 | tf_op jit(solution)/shard_map/ppermute | solution.py:114
  145.1 0.8 shard_map.97
  145.9 2.5 %collective-permute-start.22 = (bf16[64,3584]{1,0:T(8,128)(2,1)S(1)}, bf16[64,3584]{1,0:T(8,128)(2,1)S(1)}, u32[]{:S(2)}, u32[]{:S(2)}) collective-permute-start(bf16[64,3584]{1,0:T(8,128)(2,1)S(1)} %shard_map.97), channel_id=1, source_target_pairs={{0,4},{1,5},{4,8},{5,9},{8,12},{9,13},{12,14},{13,15},{14,10},{15,... | collective-permute-start | bytes 1376264 | tf_op jit(solution)/shard_map/ppermute | solution.py:114
  148.5 0.8 shard_map.102
  149.3 1.7 collective-permute-start.29
  151.0 0.8 shard_map.100
  152.3 1.5 collective-permute-done.32.moved_ref
  153.7 0.8 shard_map.105
  154.5 2.3 %collective-permute-start.33 = (bf16[64,3584]{1,0:T(8,128)(2,1)S(1)}, bf16[64,3584]{1,0:T(8,128)(2,1)S(1)}, u32[]{:S(2)}, u32[]{:S(2)}) collective-permute-start(bf16[64,3584]{1,0:T(8,128)(2,1)S(1)} %shard_map.105), channel_id=1, source_target_pairs={{0,2},{1,3},{4,0},{5,1},{8,4},{9,5},{12,8},{13,9},{14,12},{15,13},... | collective-permute-start | bytes 1376264 | tf_op jit(solution)/shard_map/ppermute | solution.py:114
  156.9 2.6 %collective-permute-done.22.moved_ref = bf16[64,3584]{1,0:T(8,128)(2,1)S(1)} collective-permute-done((bf16[64,3584]{1,0:T(8,128)(2,1)S(1)}, bf16[64,3584]{1,0:T(8,128)(2,1)S(1)}, u32[]{:S(2)}, u32[]{:S(2)}) %collective-permute-start.22) | collective-permute-done | bytes 458784 | tf_op jit(solution)/shard_map/ppermute | solution.py:114
  159.4 0.8 shard_map.98
  160.3 2.5 %collective-permute-start.23 = (bf16[64,3584]{1,0:T(8,128)(2,1)S(1)}, bf16[64,3584]{1,0:T(8,128)(2,1)S(1)}, u32[]{:S(2)}, u32[]{:S(2)}) collective-permute-start(bf16[64,3584]{1,0:T(8,128)(2,1)S(1)} %shard_map.98), channel_id=1, source_target_pairs={{0,4},{1,5},{4,8},{5,9},{8,12},{9,13},{12,14},{13,15},{14,10},{15,... | collective-permute-start | bytes 1376264 | tf_op jit(solution)/shard_map/ppermute | solution.py:114
  162.8 6.5 %collective-permute-done.29.moved_ref = bf16[64,3584]{1,0:T(8,128)(2,1)S(1)} collective-permute-done((bf16[64,3584]{1,0:T(8,128)(2,1)S(1)}, bf16[64,3584]{1,0:T(8,128)(2,1)S(1)}, u32[]{:S(2)}, u32[]{:S(2)}) %collective-permute-start.29) | collective-permute-done | bytes 458784 | tf_op jit(solution)/shard_map/ppermute | solution.py:114
  169.3 0.8 shard_map.103
  170.1 2.5 %collective-permute-start.30 = (bf16[64,3584]{1,0:T(8,128)(2,1)S(1)}, bf16[64,3584]{1,0:T(8,128)(2,1)S(1)}, u32[]{:S(2)}, u32[]{:S(2)}) collective-permute-start(bf16[64,3584]{1,0:T(8,128)(2,1)S(1)} %shard_map.103), channel_id=1, source_target_pairs={{0,4},{1,5},{4,8},{5,9},{8,12},{9,13},{12,14},{13,15},{14,10},{15,... | collective-permute-start | bytes 1376264 | tf_op jit(solution)/shard_map/ppermute | solution.py:114
  172.6 0.8 shard_map.101
  173.5 0.8 shard_map.106
  174.9 0.8 collective-permute-done.23.moved_ref
  175.7 0.8 shard_map.99
  176.5 1.8 collective-permute-start.24
  178.3 0.8 shard_map.96.base_ref
  179.1 1.5 collective-permute-done.30.refs_2_
  180.6 1.4 collective-permute-done.27.refs_1_
  182.0 4.9 %collective-permute-done.34.refs_3_ = bf16[64,3584]{1,0:T(8,128)(2,1)S(1)} collective-permute-done((bf16[64,3584]{1,0:T(8,128)(2,1)S(1)}, bf16[64,3584]{1,0:T(8,128)(2,1)S(1)}, u32[]{:S(2)}, u32[]{:S(2)}) %collective-permute-start.34) | collective-permute-done | bytes 458784 | tf_op jit(solution)/shard_map/ppermute | solution.py:114
  186.9 1.2 shard_map.107
  (60 shorter events, 5.8 us)
Async XLA Ops:
  0.0 2.9 %copy-start.6 = (s32[64,2]{0,1:T(2,128)S(1)}, s32[64,2]{0,1:T(2,128)}, u32[]{:S(2)}) copy-start(s32[64,2]{0,1:T(2,128)} %param.12) | copy-start | bytes 1540
  0.0 2.9 %copy-start.5 = (f32[64,2]{0,1:T(2,128)S(1)}, f32[64,2]{0,1:T(2,128)}, u32[]{:S(2)}) copy-start(f32[64,2]{0,1:T(2,128)} %param.13) | copy-start | bytes 1540
  2.4 2.1 %collective-permute-start = (bf16[8,64,448]{2,1,0:T(8,128)(2,1)S(1)}, bf16[8,64,448]{2,1,0:T(8,128)(2,1)S(1)}, u32[]{:S(2)}, u32[]{:S(2)}) collective-permute-start(bf16[8,64,448]{2,1,0:T(8,128)(2,1)S(1)} %dynamic-slice_bitcast_fusion), channel_id=1, source_target_pairs={{0,1},{1,0},{2,3},{3,2},{4,5},{5,4},{6,7},{7,6},{8,9},{9,8},{10,11... | collective-permute-start | bytes 1376264 | tf_op jit(solution)/shard_map/ppermute | solution.py:89
  4.5 4.4 %collective-permute-start.17 = (f32[64,2]{0,1:T(2,128)S(1)}, f32[64,2]{0,1:T(2,128)S(1)}, u32[]{:S(2)}, u32[]{:S(2)}) collective-permute-start(f32[64,2]{0,1:T(2,128)S(1)} %fusion.3), channel_id=1, source_target_pairs={{0,2},{1,3},{2,0},{3,1},{4,6},{5,7},{6,4},{7,5},{8,10},{9,11},{10,... | collective-permute-start | bytes 1544 | tf_op jit(solution)/shard_map/ppermute | solution.py:98
  7.4 74.3 %collective-permute-start.20 = (bf16[256,7168]{1,0:T(8,128)(2,1)}, bf16[256,7168]{1,0:T(8,128)(2,1)}, u32[]{:S(2)}, u32[]{:S(2)}) collective-permute-start(bf16[256,7168]{1,0:T(8,128)(2,1)} %param.16), channel_id=1, source_target_pairs={{0,1},{1,0},{2,3},{3,2},{4,5},{5,4},{6,7},{7,6},{8,9},{9,8},{10,11... | collective-permute-start | bytes 11010056 | tf_op jit(solution)/shard_map/ppermute | solution.py:89
  7.8 23.9 %collective-permute-start.3 = (bf16[256,896]{1,0:T(8,128)(2,1)S(1)}, bf16[256,896]{1,0:T(8,128)(2,1)S(1)}, u32[]{:S(2)}, u32[]{:S(2)}) collective-permute-start(bf16[256,896]{1,0:T(8,128)(2,1)S(1)} %bitcast.19), channel_id=1, source_target_pairs={{0,2},{1,3},{4,0},{5,1},{8,4},{9,5},{12,8},{13,9},{14,12},{15,13},... | collective-permute-start | bytes 1376264 | tf_op jit(solution)/shard_map/ppermute | solution.py:114
  9.0 12.2 %collective-permute-start.18 = (f32[128,2]{0,1:T(2,128)S(1)}, f32[128,2]{0,1:T(2,128)S(1)}, u32[]{:S(2)}, u32[]{:S(2)}) collective-permute-start(f32[128,2]{0,1:T(2,128)S(1)} %pad_maximum_fusion.8), channel_id=1, source_target_pairs={{0,4},{1,5},{2,6},{3,7},{4,0},{5,1},{6,2},{7,3},{8,12},{9,13},{10,... | collective-permute-start | bytes 3080 | tf_op jit(solution)/shard_map/ppermute | solution.py:98
  11.1 21.1 %collective-permute-start.4 = (bf16[256,896]{1,0:T(8,128)(2,1)S(1)}, bf16[256,896]{1,0:T(8,128)(2,1)S(1)}, u32[]{:S(2)}, u32[]{:S(2)}) collective-permute-start(bf16[256,896]{1,0:T(8,128)(2,1)S(1)} %bitcast.16), channel_id=1, source_target_pairs={{0,2},{1,3},{4,0},{5,1},{8,4},{9,5},{12,8},{13,9},{14,12},{15,13},... | collective-permute-start | bytes 1376264 | tf_op jit(solution)/shard_map/ppermute | solution.py:114
  12.6 21.2 %collective-permute-start.6 = (bf16[256,896]{1,0:T(8,128)(2,1)S(1)}, bf16[256,896]{1,0:T(8,128)(2,1)S(1)}, u32[]{:S(2)}, u32[]{:S(2)}) collective-permute-start(bf16[256,896]{1,0:T(8,128)(2,1)S(1)} %bitcast.17), channel_id=1, source_target_pairs={{0,4},{1,5},{4,8},{5,9},{8,12},{9,13},{12,14},{13,15},{14,10},{15,... | collective-permute-start | bytes 1376264 | tf_op jit(solution)/shard_map/ppermute | solution.py:114
  21.3 10.4 %collective-permute-start.19 = (f32[256,2]{0,1:T(2,128)S(1)}, f32[256,2]{0,1:T(2,128)S(1)}, u32[]{:S(2)}, u32[]{:S(2)}) collective-permute-start(f32[256,2]{0,1:T(2,128)S(1)} %pad_maximum_fusion.7), channel_id=1, source_target_pairs={{0,8},{1,9},{2,10},{3,11},{4,12},{5,13},{6,14},{7,15},{8,0},{9,1},... | collective-permute-start | bytes 6152 | tf_op jit(solution)/shard_map/ppermute | solution.py:98
  31.6 63.7 %collective-permute-start.1 = (bf16[7168,256]{1,0:T(8,128)(2,1)}, bf16[7168,256]{1,0:T(8,128)(2,1)}, u32[]{:S(2)}, u32[]{:S(2)}) collective-permute-start(bf16[7168,256]{1,0:T(8,128)(2,1)} %refs_3_.1), channel_id=1, source_target_pairs={{0,1},{1,0},{2,3},{3,2},{4,5},{5,4},{6,7},{7,6},{8,9},{9,8},{10,11... | collective-permute-start | bytes 11010056 | tf_op jit(solution)/shard_map/ppermute | solution.py:89
  31.6 64.1 %collective-permute-start.2 = (bf16[7168,256]{1,0:T(8,128)(2,1)}, bf16[7168,256]{1,0:T(8,128)(2,1)}, u32[]{:S(2)}, u32[]{:S(2)}) collective-permute-start(bf16[7168,256]{1,0:T(8,128)(2,1)} %refs_4_.1), channel_id=1, source_target_pairs={{0,1},{1,0},{2,3},{3,2},{4,5},{5,4},{6,7},{7,6},{8,9},{9,8},{10,11... | collective-permute-start | bytes 11010056 | tf_op jit(solution)/shard_map/ppermute | solution.py:89
  32.2 13.4 %collective-permute-start.5 = (bf16[256,896]{1,0:T(8,128)(2,1)S(1)}, bf16[256,896]{1,0:T(8,128)(2,1)S(1)}, u32[]{:S(2)}, u32[]{:S(2)}) collective-permute-start(bf16[256,896]{1,0:T(8,128)(2,1)S(1)} %bitcast.20), channel_id=1, source_target_pairs={{0,4},{1,5},{4,8},{5,9},{8,12},{9,13},{12,14},{13,15},{14,10},{15,... | collective-permute-start | bytes 1376264 | tf_op jit(solution)/shard_map/ppermute | solution.py:114
  33.8 20.7 %collective-permute-start.10 = (bf16[256,896]{1,0:T(8,128)(2,1)S(1)}, bf16[256,896]{1,0:T(8,128)(2,1)S(1)}, u32[]{:S(2)}, u32[]{:S(2)}) collective-permute-start(bf16[256,896]{1,0:T(8,128)(2,1)S(1)} %collective-permute-done.6.refs_3_), channel_id=1, source_target_pairs={{0,4},{1,5},{4,8},{5,9},{8,12},{9,13},{12,14},{13,15},{14,10},{15,... | collective-permute-start | bytes 1376264 | tf_op jit(solution)/shard_map/ppermute | solution.py:114
  45.5 12.2 %collective-permute-start.7 = (bf16[256,896]{1,0:T(8,128)(2,1)S(1)}, bf16[256,896]{1,0:T(8,128)(2,1)}, u32[]{:S(2)}, u32[]{:S(2)}) collective-permute-start(bf16[256,896]{1,0:T(8,128)(2,1)S(1)} %collective-permute-done.3.refs_0_), channel_id=1, source_target_pairs={{0,2},{1,3},{4,0},{5,1},{8,4},{9,5},{12,8},{13,9},{14,12},{15,13},... | collective-permute-start | bytes 1376264 | tf_op jit(solution)/shard_map/ppermute | solution.py:114
  54.5 11.9 %collective-permute-start.8 = (bf16[256,896]{1,0:T(8,128)(2,1)S(1)}, bf16[256,896]{1,0:T(8,128)(2,1)}, u32[]{:S(2)}, u32[]{:S(2)}) collective-permute-start(bf16[256,896]{1,0:T(8,128)(2,1)S(1)} %collective-permute-done.4.refs_1_), channel_id=1, source_target_pairs={{0,2},{1,3},{4,0},{5,1},{8,4},{9,5},{12,8},{13,9},{14,12},{15,13},... | collective-permute-start | bytes 1376264 | tf_op jit(solution)/shard_map/ppermute | solution.py:114
  57.8 13.2 %collective-permute-start.9 = (bf16[256,896]{1,0:T(8,128)(2,1)S(1)}, bf16[256,896]{1,0:T(8,128)(2,1)}, u32[]{:S(2)}, u32[]{:S(2)}) collective-permute-start(bf16[256,896]{1,0:T(8,128)(2,1)S(1)} %collective-permute-done.5.refs_2_), channel_id=1, source_target_pairs={{0,4},{1,5},{4,8},{5,9},{8,12},{9,13},{12,14},{13,15},{14,10},{15,... | collective-permute-start | bytes 1376264 | tf_op jit(solution)/shard_map/ppermute | solution.py:114
  66.3 13.8 %collective-permute-start.12 = (bf16[256,896]{1,0:T(8,128)(2,1)}, bf16[256,896]{1,0:T(8,128)(2,1)}, u32[]{:S(2)}, u32[]{:S(2)}) collective-permute-start(bf16[256,896]{1,0:T(8,128)(2,1)} %collective-permute-done.8.refs_1_), channel_id=1, source_target_pairs={{0,2},{1,3},{4,0},{5,1},{8,4},{9,5},{12,8},{13,9},{14,12},{15,13},... | collective-permute-start | bytes 1376264 | tf_op jit(solution)/shard_map/ppermute | solution.py:114
  70.8 25.0 %copy-start.2 = (f32[7168]{0:T(1024)S(1)}, f32[7168]{0:T(1024)}, u32[]{:S(2)}) copy-start(f32[7168]{0:T(1024)} %param.11) | copy-start | bytes 86020
  71.0 24.8 %copy-start = (bf16[7168,256]{1,0:T(8,128)(2,1)S(1)}, bf16[7168,256]{1,0:T(8,128)(2,1)}, u32[]{:S(2)}) copy-start(bf16[7168,256]{1,0:T(8,128)(2,1)} %refs_3_.1) | copy-start | bytes 11010052
  71.0 24.8 %copy-start.1 = (bf16[7168,256]{1,0:T(8,128)(2,1)S(1)}, bf16[7168,256]{1,0:T(8,128)(2,1)}, u32[]{:S(2)}) copy-start(bf16[7168,256]{1,0:T(8,128)(2,1)} %refs_4_.1) | copy-start | bytes 11010052
  71.0 37.2 %collective-permute-start.11 = (bf16[256,896]{1,0:T(8,128)(2,1)}, bf16[256,896]{1,0:T(8,128)(2,1)S(1)}, u32[]{:S(2)}, u32[]{:S(2)}) collective-permute-start(bf16[256,896]{1,0:T(8,128)(2,1)} %collective-permute-done.7.refs_0_), channel_id=1, source_target_pairs={{0,2},{1,3},{4,0},{5,1},{8,4},{9,5},{12,8},{13,9},{14,12},{15,13},... | collective-permute-start | bytes 1376264 | tf_op jit(solution)/shard_map/ppermute | solution.py:114
  80.1 13.7 %collective-permute-start.13 = (bf16[256,896]{1,0:T(8,128)(2,1)}, bf16[256,896]{1,0:T(8,128)(2,1)S(1)}, u32[]{:S(2)}, u32[]{:S(2)}) collective-permute-start(bf16[256,896]{1,0:T(8,128)(2,1)} %collective-permute-done.9.refs_2_), channel_id=1, source_target_pairs={{0,4},{1,5},{4,8},{5,9},{8,12},{9,13},{12,14},{13,15},{14,10},{15,... | collective-permute-start | bytes 1376264 | tf_op jit(solution)/shard_map/ppermute | solution.py:114
  81.7 26.5 %collective-permute-start.14 = (bf16[256,896]{1,0:T(8,128)(2,1)S(1)}, bf16[256,896]{1,0:T(8,128)(2,1)S(1)}, u32[]{:S(2)}, u32[]{:S(2)}) collective-permute-start(bf16[256,896]{1,0:T(8,128)(2,1)S(1)} %collective-permute-done.10.refs_3_), channel_id=1, source_target_pairs={{0,4},{1,5},{4,8},{5,9},{8,12},{9,13},{12,14},{13,15},{14,10},{15,... | collective-permute-start | bytes 1376264 | tf_op jit(solution)/shard_map/ppermute | solution.py:114
  93.8 19.0 %collective-permute-start.15 = (bf16[256,896]{1,0:T(8,128)(2,1)S(1)}, bf16[256,896]{1,0:T(8,128)(2,1)S(1)}, u32[]{:S(2)}, u32[]{:S(2)}) collective-permute-start(bf16[256,896]{1,0:T(8,128)(2,1)S(1)} %collective-permute-done.13.refs_2_), channel_id=1, source_target_pairs={{0,4},{1,5},{4,8},{5,9},{8,12},{9,13},{12,14},{13,15},{14,10},{15,... | collective-permute-start | bytes 1376264 | tf_op jit(solution)/shard_map/ppermute | solution.py:114
  95.4 17.4 %collective-permute-start.16 = (bf16[256,896]{1,0:T(8,128)(2,1)}, bf16[256,896]{1,0:T(8,128)(2,1)S(1)}, u32[]{:S(2)}, u32[]{:S(2)}) collective-permute-start(bf16[256,896]{1,0:T(8,128)(2,1)} %collective-permute-done.12.refs_1_), channel_id=1, source_target_pairs={{0,2},{1,3},{4,0},{5,1},{8,4},{9,5},{12,8},{13,9},{14,12},{15,13},... | collective-permute-start | bytes 1376264 | tf_op jit(solution)/shard_map/ppermute | solution.py:114
  112.8 3.3 %copy-start.4 = (bf16[256,3584]{1,0:T(8,128)(2,1)S(1)}, bf16[256,3584]{1,0:T(8,128)(2,1)}, u32[]{:S(2)}) copy-start(bf16[256,3584]{1,0:T(8,128)(2,1)} %get-tuple-element.47) | copy-start | bytes 5505028
  118.2 1.5 copy-start.3
  122.5 12.6 %collective-permute-start.31 = (bf16[64,3584]{1,0:T(8,128)(2,1)S(1)}, bf16[64,3584]{1,0:T(8,128)(2,1)S(1)}, u32[]{:S(2)}, u32[]{:S(2)}) collective-permute-start(bf16[64,3584]{1,0:T(8,128)(2,1)S(1)} %convolution_convert_fusion.2), channel_id=1, source_target_pairs={{0,2},{1,3},{4,0},{5,1},{8,4},{9,5},{12,8},{13,9},{14,12},{15,13},... | collective-permute-start | bytes 1376264 | tf_op jit(solution)/shard_map/ppermute | solution.py:114
  122.9 25.6 %collective-permute-start.28 = (bf16[64,3584]{1,0:T(8,128)(2,1)S(1)}, bf16[64,3584]{1,0:T(8,128)(2,1)S(1)}, u32[]{:S(2)}, u32[]{:S(2)}) collective-permute-start(bf16[64,3584]{1,0:T(8,128)(2,1)S(1)} %constant_dynamic-slice_fusion), channel_id=1, source_target_pairs={{0,4},{1,5},{4,8},{5,9},{8,12},{9,13},{12,14},{13,15},{14,10},{15,... | collective-permute-start | bytes 1376264 | tf_op jit(solution)/shard_map/ppermute | solution.py:114
  124.7 20.4 %collective-permute-start.21 = (bf16[64,3584]{1,0:T(8,128)(2,1)S(1)}, bf16[64,3584]{1,0:T(8,128)(2,1)S(1)}, u32[]{:S(2)}, u32[]{:S(2)}) collective-permute-start(bf16[64,3584]{1,0:T(8,128)(2,1)S(1)} %convolution_convert_fusion.3), channel_id=1, source_target_pairs={{0,4},{1,5},{4,8},{5,9},{8,12},{9,13},{12,14},{13,15},{14,10},{15,... | collective-permute-start | bytes 1376264 | tf_op jit(solution)/shard_map/ppermute | solution.py:114
  126.3 24.7 %collective-permute-start.25 = (bf16[64,3584]{1,0:T(8,128)(2,1)S(1)}, bf16[64,3584]{1,0:T(8,128)(2,1)S(1)}, u32[]{:S(2)}, u32[]{:S(2)}) collective-permute-start(bf16[64,3584]{1,0:T(8,128)(2,1)S(1)} %constant_dynamic-slice_fusion.1), channel_id=1, source_target_pairs={{0,2},{1,3},{4,0},{5,1},{8,4},{9,5},{12,8},{13,9},{14,12},{15,13},... | collective-permute-start | bytes 1376264 | tf_op jit(solution)/shard_map/ppermute | solution.py:114
  135.9 17.8 %collective-permute-start.32 = (bf16[64,3584]{1,0:T(8,128)(2,1)S(1)}, bf16[64,3584]{1,0:T(8,128)(2,1)S(1)}, u32[]{:S(2)}, u32[]{:S(2)}) collective-permute-start(bf16[64,3584]{1,0:T(8,128)(2,1)S(1)} %shard_map.104), channel_id=1, source_target_pairs={{0,2},{1,3},{4,0},{5,1},{8,4},{9,5},{12,8},{13,9},{14,12},{15,13},... | collective-permute-start | bytes 1376264 | tf_op jit(solution)/shard_map/ppermute | solution.py:114
  145.9 13.5 %collective-permute-start.22 = (bf16[64,3584]{1,0:T(8,128)(2,1)S(1)}, bf16[64,3584]{1,0:T(8,128)(2,1)S(1)}, u32[]{:S(2)}, u32[]{:S(2)}) collective-permute-start(bf16[64,3584]{1,0:T(8,128)(2,1)S(1)} %shard_map.97), channel_id=1, source_target_pairs={{0,4},{1,5},{4,8},{5,9},{8,12},{9,13},{12,14},{13,15},{14,10},{15,... | collective-permute-start | bytes 1376264 | tf_op jit(solution)/shard_map/ppermute | solution.py:114
  149.3 20.0 %collective-permute-start.29 = (bf16[64,3584]{1,0:T(8,128)(2,1)S(1)}, bf16[64,3584]{1,0:T(8,128)(2,1)S(1)}, u32[]{:S(2)}, u32[]{:S(2)}) collective-permute-start(bf16[64,3584]{1,0:T(8,128)(2,1)S(1)} %shard_map.102), channel_id=1, source_target_pairs={{0,4},{1,5},{4,8},{5,9},{8,12},{9,13},{12,14},{13,15},{14,10},{15,... | collective-permute-start | bytes 1376264 | tf_op jit(solution)/shard_map/ppermute | solution.py:114
  151.9 20.8 %collective-permute-start.26 = (bf16[64,3584]{1,0:T(8,128)(2,1)S(1)}, bf16[64,3584]{1,0:T(8,128)(2,1)S(1)}, u32[]{:S(2)}, u32[]{:S(2)}) collective-permute-start(bf16[64,3584]{1,0:T(8,128)(2,1)S(1)} %shard_map.100), channel_id=1, source_target_pairs={{0,2},{1,3},{4,0},{5,1},{8,4},{9,5},{12,8},{13,9},{14,12},{15,13},... | collective-permute-start | bytes 1376264 | tf_op jit(solution)/shard_map/ppermute | solution.py:114
  154.5 19.0 %collective-permute-start.33 = (bf16[64,3584]{1,0:T(8,128)(2,1)S(1)}, bf16[64,3584]{1,0:T(8,128)(2,1)S(1)}, u32[]{:S(2)}, u32[]{:S(2)}) collective-permute-start(bf16[64,3584]{1,0:T(8,128)(2,1)S(1)} %shard_map.105), channel_id=1, source_target_pairs={{0,2},{1,3},{4,0},{5,1},{8,4},{9,5},{12,8},{13,9},{14,12},{15,13},... | collective-permute-start | bytes 1376264 | tf_op jit(solution)/shard_map/ppermute | solution.py:114
  160.3 15.4 %collective-permute-start.23 = (bf16[64,3584]{1,0:T(8,128)(2,1)S(1)}, bf16[64,3584]{1,0:T(8,128)(2,1)S(1)}, u32[]{:S(2)}, u32[]{:S(2)}) collective-permute-start(bf16[64,3584]{1,0:T(8,128)(2,1)S(1)} %shard_map.98), channel_id=1, source_target_pairs={{0,4},{1,5},{4,8},{5,9},{8,12},{9,13},{12,14},{13,15},{14,10},{15,... | collective-permute-start | bytes 1376264 | tf_op jit(solution)/shard_map/ppermute | solution.py:114
  170.1 10.5 %collective-permute-start.30 = (bf16[64,3584]{1,0:T(8,128)(2,1)S(1)}, bf16[64,3584]{1,0:T(8,128)(2,1)S(1)}, u32[]{:S(2)}, u32[]{:S(2)}) collective-permute-start(bf16[64,3584]{1,0:T(8,128)(2,1)S(1)} %shard_map.103), channel_id=1, source_target_pairs={{0,4},{1,5},{4,8},{5,9},{8,12},{9,13},{12,14},{13,15},{14,10},{15,... | collective-permute-start | bytes 1376264 | tf_op jit(solution)/shard_map/ppermute | solution.py:114
  173.5 8.5 %collective-permute-start.27 = (bf16[64,3584]{1,0:T(8,128)(2,1)S(1)}, bf16[64,3584]{1,0:T(8,128)(2,1)S(1)}, u32[]{:S(2)}, u32[]{:S(2)}) collective-permute-start(bf16[64,3584]{1,0:T(8,128)(2,1)S(1)} %shard_map.101), channel_id=1, source_target_pairs={{0,2},{1,3},{4,0},{5,1},{8,4},{9,5},{12,8},{13,9},{14,12},{15,13},... | collective-permute-start | bytes 1376264 | tf_op jit(solution)/shard_map/ppermute | solution.py:114
  174.4 12.5 %collective-permute-start.34 = (bf16[64,3584]{1,0:T(8,128)(2,1)S(1)}, bf16[64,3584]{1,0:T(8,128)(2,1)S(1)}, u32[]{:S(2)}, u32[]{:S(2)}) collective-permute-start(bf16[64,3584]{1,0:T(8,128)(2,1)S(1)} %shard_map.106), channel_id=1, source_target_pairs={{0,2},{1,3},{4,0},{5,1},{8,4},{9,5},{12,8},{13,9},{14,12},{15,13},... | collective-permute-start | bytes 1376264 | tf_op jit(solution)/shard_map/ppermute | solution.py:114
  176.5 10.4 %collective-permute-start.24 = (bf16[64,3584]{1,0:T(8,128)(2,1)S(1)}, bf16[64,3584]{1,0:T(8,128)(2,1)S(1)}, u32[]{:S(2)}, u32[]{:S(2)}) collective-permute-start(bf16[64,3584]{1,0:T(8,128)(2,1)S(1)} %shard_map.99), channel_id=1, source_target_pairs={{0,4},{1,5},{4,8},{5,9},{8,12},{9,13},{12,14},{13,15},{14,10},{15,... | collective-permute-start | bytes 1376264 | tf_op jit(solution)/shard_map/ppermute | solution.py:114

commit v4 on v3

--- a/solution.py
+++ b/solution.py
@@ -89,19 +89,20 @@
     return lax.ppermute(value, "ep", [(i, i ^ 1) for i in range(lax.axis_size("ep"))])
 
 
-def gather_small(value, chips, chip):
-    width = 1
-    while width < chips:
-        pairs = [
-            (2 * i + core, 2 * (i ^ width) + core) for i in range(chips) for core in range(2)
-        ]
-        other = lax.ppermute(value, "ep", pairs)
-        upper = (chip // width) % 2 == 1
-        value = jnp.concatenate(
-            [jnp.where(upper, other, value), jnp.where(upper, value, other)], axis=0
-        )
-        width *= 2
-    return value
+def pair_gather(value):
+    pairs = [[i, i + 1] for i in range(0, lax.axis_size("ep"), 2)]
+    return lax.all_gather(value, "ep", axis_index_groups=pairs, axis=0, tiled=True)
+
+
+def gain_header(gains, width):
+    parts, left = [], gains.T
+    for _ in range(3):
+        part = lax.reduce_precision(left, exponent_bits=8, mantissa_bits=7)
+        parts.append(part)
+        left = left - part
+    rows = jnp.stack(parts, axis=1).reshape(3 * gains.shape[1], gains.shape[0])
+    pad = (-rows.shape[0]) % 16
+    return jnp.pad(rows, ((0, pad), (0, width - rows.shape[1]))).astype(jnp.bfloat16)
 
 
 def ring_shift(value, ring, step):
@@ -115,128 +116,212 @@
 
 
 VMEM_BYTES = 32 * 1024 * 1024
+COST_SCALE = 3
 
 
 def whole(shape):
     return pl.BlockSpec(shape, lambda i, where: (0,) * len(shape))
 
 
-def accumulate(where, positions, parts, norm_gain, weights, carried, closing):
+def accumulate(where, positions, parts, norm_gain, weights, carried, headers):
     count = len(positions)
-    rows, width = parts[0][0].shape
+    width = parts[0][0].shape[1]
+    chips = norm_gain.shape[0]
+    model_width = chips * width
     hidden_here = weights[0].shape[1]
-    model_width = weights[0].shape[0]
-    tok_here = closing["tok_here"]
-    far = rows // tok_here
-    last = "gain" in closing
+    both = 2 * hidden_here
+    head = parts[0][0].shape[0] - parts[0][1].shape[0]
+    sizes = [piece.shape[0] - (head if k == 0 else 0) for k, piece in enumerate(parts[0])]
+    starts = [sum(sizes[:k]) for k in range(len(sizes))]
+    offsets = [head if k == 0 else 0 for k in range(len(sizes))]
+    tokens = sum(sizes)
+    tok_here = tokens // chips
+    side = 128
+    last = headers is not None
     first = carried is None
-    side = closing["side"]
 
     def kernel(where_ref, *refs):
         refs = list(refs)
-        xs = [[refs.pop(0) for _ in range(2)] for _ in range(count)]
+        xs = [[refs.pop(0) for _ in sizes] for _ in range(count)]
         scales = [refs.pop(0) for _ in range(count)]
-        tables = [[refs.pop(0) for _ in range(len(weights))] for _ in range(count)]
+        stored = [refs.pop(0) for _ in weights]
         acc_in, sq_in = (None, None) if first else (refs.pop(0), refs.pop(0))
-        gain_ref = refs.pop(0) if last else None
+        tops = [refs.pop(0) for _ in headers] if last else []
         owns = [refs.pop(0) for _ in range(count)]
         if last:
             hidden_ref = refs.pop(0)
         else:
-            acc_out, sq_out = refs.pop(0), refs.pop(0)
-        chip = where_ref[0]
+            acc_out, sq_out, done_ref = refs.pop(0), refs.pop(0), refs.pop(0)
+            done_ref[0] = 0
+        table_ref, sems = refs.pop(0), refs.pop(0)
+        gain_ref = refs.pop(0) if last else None
+        copies = {}
+        for core in range(2):
+            for which in range(2):
+                for b in range(count):
+                    row = (core * chips + where_ref[positions[b]]) * width
+                    slot = (core * 2 + which) * count + b
+                    copies[core, which, b] = pltpu.make_async_copy(
+                        stored[which].at[pl.ds(pl.multiple_of(row, width), width), :],
+                        table_ref.at[slot],
+                        sems.at[slot],
+                    )
+                    copies[core, which, b].start()
+        begin = where_ref[0] * tok_here
         for b in range(count):
-            start = pl.multiple_of(lax.rem(chip, far) * tok_here, tok_here)
-
-            @pl.when(chip < far)
-            def _():
-                owns[b][...] = xs[b][0][pl.ds(start, tok_here), :]
-
-            @pl.when(chip >= far)
-            def _():
-                owns[b][...] = xs[b][1][pl.ds(start, tok_here), :]
-
-        for part in range(2):
-            span = slice(part * rows, (part + 1) * rows)
+            for k, size in enumerate(sizes):
+
+                @pl.when((begin >= starts[k]) & (begin < starts[k] + size))
+                def _():
+                    row = pl.multiple_of(begin - starts[k] + offsets[k], 16)
+                    owns[b][...] = xs[b][k][pl.ds(row, tok_here), :]
+
+        if last:
+            expert = where_ref[chips]
+            row_at = lax.broadcasted_iota(jnp.int32, (head, tok_here), 0)
+            diagonal = lax.broadcasted_iota(
+                jnp.int32, (tok_here, tok_here), 0
+            ) == lax.broadcasted_iota(jnp.int32, (tok_here, tok_here), 1)
+            for d in range(chips):
+                parts_of = tops[d][:, :tok_here].astype(jnp.float32)
+                named = (row_at >= 3 * expert) & (row_at < 3 * expert + 3)
+                along = jnp.sum(jnp.where(named, parts_of, 0.0), axis=0, keepdims=True)
+                down_rows = jnp.sum(jnp.where(diagonal, along, 0.0), axis=1, keepdims=True)
+                at = pl.multiple_of(where_ref[d] * tok_here, tok_here)
+                gain_ref[pl.ds(at, tok_here), :] = down_rows
+
+        for k, size in enumerate(sizes):
+            span = slice(starts[k], starts[k] + size)
             scaled, squares = [], None if first else sq_in[span, :]
             for b in range(count):
-                values = xs[b][part][...].astype(jnp.float32)
+                values = xs[b][k][offsets[k] : offsets[k] + size, :].astype(jnp.float32)
                 for lane in range(0, width, side):
                     piece = values[:, lane : lane + side]
                     squares = piece * piece if squares is None else squares + piece * piece
                 scaled.append((values * scales[b][0]).astype(jnp.bfloat16))
-            totals = []
-            for which in range(len(weights)):
-                cols = slice(which * hidden_here, (which + 1) * hidden_here)
-                total = None if first else acc_in[span, cols]
-                for b in range(count):
-                    product = jnp.dot(
-                        scaled[b], tables[b][which][...], preferred_element_type=jnp.float32
-                    )
-                    total = product if total is None else total + product
-                if last:
-                    totals.append(total)
-                else:
-                    acc_out[span, cols] = total
             if last:
                 mean = jnp.sum(squares, axis=1, keepdims=True) / model_width
                 inv_rms = lax.rsqrt(mean + epsilon)
-                for core in range(len(weights) // 2):
-                    gate_act = totals[2 * core] * inv_rms
-                    up_act = totals[2 * core + 1] * inv_rms
-                    act = gate_act * jax.nn.sigmoid(gate_act) * up_act * gain_ref[span, :]
+            else:
+                sq_out[span, :] = squares
+            for core in range(2):
+                acts = []
+                for which in range(2):
+                    at = core * both + which * hidden_here
+                    cols = slice(at, at + hidden_here)
+                    total = None if first else acc_in[span, cols]
+                    for b in range(count):
+                        if k == 0:
+                            copies[core, which, b].wait()
+                        product = jnp.dot(
+                            scaled[b],
+                            table_ref[(core * 2 + which) * count + b],
+                            preferred_element_type=jnp.float32,
+                        )
+                        total = product if total is None else total + product
+                    if last:
+                        acts.append(total * inv_rms)
+                    else:
+                        acc_out[span, cols] = total
+                if last:
+                    act = acts[0] * jax.nn.sigmoid(acts[0]) * acts[1] * gain_ref[span, :]
                     cols = slice(core * hidden_here, (core + 1) * hidden_here)
                     hidden_ref[span, cols] = act.astype(jnp.bfloat16)
-            else:
-                sq_out[span, :] = squares
-
-    def table_spec(position):
-        return pl.BlockSpec((width, hidden_here), lambda i, where: (where[position], 0))
-
-    operands = [half for block in parts for half in block]
-    in_specs = [whole((rows, width))] * (2 * count)
+
+    operands = [piece for block in parts for piece in block]
+    in_specs = [whole(piece.shape) for piece in operands]
     for position in positions:
         operands.append(norm_gain)
         in_specs.append(
             pl.BlockSpec((1, 1, width), lambda i, where, p=position: (where[p], 0, 0))
         )
-    for position in positions:
-        operands.extend(weights)
-        in_specs.extend([table_spec(position)] * len(weights))
-    sums = (2 * rows, len(weights) * hidden_here)
+    operands.extend(weights)
+    in_specs.extend([pl.BlockSpec(memory_space=pltpu.HBM)] * len(weights))
+    sums, squared = (tokens, 2 * both), (tokens, side)
     aliases = {}
     if not first:
         if not last:
             aliases = {len(operands) + 1: count, len(operands) + 2: count + 1}
-        operands.extend(carried)
-        in_specs.extend([whole(sums), whole((2 * rows, side))])
+        operands.extend(carried[:2])
+        in_specs.extend([whole(sums), whole(squared)])
     out_shape = [jax.ShapeDtypeStruct((tok_here, width), jnp.bfloat16)] * count
     out_specs = [whole((tok_here, width))] * count
     if last:
-        operands.append(closing["gain"])
-        in_specs.append(whole((2 * rows, 1)))
-        shape = (2 * rows, len(weights) // 2 * hidden_here)
-        out_shape.append(jax.ShapeDtypeStruct(shape, jnp.bfloat16))
-        out_specs.append(whole(shape))
+        operands.extend(headers)
+        in_specs.extend([whole((head, width))] * len(headers))
+        out_shape.append(jax.ShapeDtypeStruct((tokens, both), jnp.bfloat16))
+        out_specs.append(whole((tokens, both)))
     else:
         out_shape.append(jax.ShapeDtypeStruct(sums, jnp.float32))
-        out_shape.append(jax.ShapeDtypeStruct((2 * rows, side), jnp.float32))
-        out_specs.extend([whole(sums), whole((2 * rows, side))])
-    flops = 2 * count * 2 * rows * width * sums[1]
-    return pl.pallas_call(
+        out_shape.append(jax.ShapeDtypeStruct(squared, jnp.float32))
+        out_shape.append(jax.ShapeDtypeStruct((1,), jnp.int32))
+        out_specs.extend([whole(sums), whole(squared), pl.BlockSpec(memory_space=pltpu.SMEM)])
+    slots = 4 * count
+    scratch = [
+        pltpu.VMEM((slots, width, hidden_here), jnp.bfloat16),
+        pltpu.SemaphoreType.DMA((slots,)),
+    ]
+    if last:
+        scratch.append(pltpu.VMEM((tokens, 1), jnp.float32))
+    made = pl.pallas_call(
         kernel,
         grid_spec=pltpu.PrefetchScalarGridSpec(
-            num_scalar_prefetch=1, grid=(1,), in_specs=in_specs, out_specs=out_specs
+            num_scalar_prefetch=1,
+            grid=(1,),
+            in_specs=in_specs,
+            out_specs=out_specs,
+            scratch_shapes=scratch,
         ),
         out_shape=out_shape,
         input_output_aliases=aliases,
         compiler_params=pltpu.CompilerParams(vmem_limit_bytes=VMEM_BYTES),
         cost_estimate=pl.CostEstimate(
-            flops=flops,
-            bytes_accessed=count * width * (rows * 4 + sums[1] * 2) + sums[0] * sums[1] * 8,
+            flops=COST_SCALE * 2 * count * tokens * width * sums[1],
+            bytes_accessed=count * width * (tokens + sums[1]) * 2 + tokens * sums[1] * 8,
             transcendentals=0,
         ),
     )(where, *operands)
+    return made[:count], made[count:]
+
+
+def farthest_rows(where, position, hidden, down):
+    tokens, units = hidden.shape
+    half = down.shape[1] // 2
+    rows = tokens // (where.shape[0] - 1)
+    steps = 4
+
+    def kernel(where_ref, hidden_ref, lower_ref, upper_ref, kept_ref, *outs):
+        at = pl.multiple_of(where_ref[position] * rows, rows)
+        kept_ref[...] = hidden_ref[...]
+        for table_ref, out_ref in zip((lower_ref, upper_ref), outs):
+            out = jnp.dot(
+                hidden_ref[pl.ds(at, rows), :], table_ref[...], preferred_element_type=jnp.float32
+            )
+            out_ref[...] = out.astype(jnp.bfloat16)
+
+    made = pl.BlockSpec((rows, half // steps), lambda i, where: (0, i))
+    return pl.pallas_call(
+        kernel,
+        grid_spec=pltpu.PrefetchScalarGridSpec(
+            num_scalar_prefetch=1,
+            grid=(steps,),
+            in_specs=[
+                whole((tokens, units)),
+                pl.BlockSpec((units, half // steps), lambda i, where: (0, i)),
+                pl.BlockSpec((units, half // steps), lambda i, where: (0, steps + i)),
+            ],
+            out_specs=[whole((tokens, units)), made, made],
+        ),
+        out_shape=[
+            jax.ShapeDtypeStruct(hidden.shape, hidden.dtype),
+            jax.ShapeDtypeStruct((rows, half), jnp.bfloat16),
+            jax.ShapeDtypeStruct((rows, half), jnp.bfloat16),
+        ],
+        compiler_params=pltpu.CompilerParams(vmem_limit_bytes=VMEM_BYTES),
+        cost_estimate=pl.CostEstimate(
+            flops=4 * rows * units * half, bytes_accessed=4 * units * half, transcendentals=0
+        ),
+    )(where, hidden, down, down)
 
 
 def add_rows(where, position, table, moved):
@@ -336,6 +421,7 @@
     me = lax.axis_index("ep")
     chip, core = me // 2, me % 2
     seen = [[ring[(ring.index(i) + d) % chips] for d in range(chips)] for i in range(chips)]
+    seen = [row + [2 * i // FSPLIT] for i, row in enumerate(seen)]
     where = lax.dynamic_index_in_dim(jnp.asarray(seen, jnp.int32), chip, 0, keepdims=False)
 
     stream_feat = (residual.astype(jnp.float32) + attn_out.astype(jnp.float32)).astype(jnp.bfloat16)
@@ -347,56 +433,52 @@
         [jnp.where(core == 0, mine, swapped), jnp.where(core == 0, swapped, mine)], axis=2
     )
     block = block.reshape(2, far * tok_here, 2 * feat_here)
-    blocks = {0: [block[0], block[1]]}
-
-    own_gains = token_gains(expert_routes, route_gain, experts)
-    swapped, w_gate, w_up, w_down, own_gains = lax.optimization_barrier(
-        (swapped, w_gate, w_up, w_down, own_gains)
-    )
-    weights = [w_gate, w_up, swap_cores(w_gate), swap_cores(w_up)]
-    other_down = swap_cores(w_down)
-    down = [
-        jnp.concatenate([w_down[:, cols], other_down[:, cols]], axis=0)
-        for cols in (slice(0, half), slice(half, model_width))
+    header = gain_header(token_gains(expert_routes, route_gain, experts), 2 * feat_here)
+    blocks = {0: [jnp.concatenate([header, block[0]], axis=0), block[1]]}
+
+    swapped, w_gate, w_up, w_down = lax.optimization_barrier((swapped, w_gate, w_up, w_down))
+    weights = [
+        pltpu.with_memory_space_constraint(pair_gather(table), pltpu.HBM)
+        for table in (w_gate, w_up)
     ]
-    gains = gather_small(own_gains, chips, chip)
-    gain_here = lax.dynamic_slice_in_dim(gains, me // FSPLIT, 1, axis=1)
+    down = pair_gather(w_down)
+    width = 2 * feat_here
+    groups = [[0]] + [[d, chips - d] for d in range(1, far)] + [[far]]
 
     for distance in range(1, far):
-        for sign, order in ((-1, (0, 1)), (1, (1, 0))):
-            came = [None, None]
-            for part in order:
-                came[part] = ring_shift(blocks[sign * (distance - 1)][part], ring, -sign)
-            blocks[sign * distance] = came
-    blocks[far] = [
-        ring_shift(blocks[1 - far][0], ring, 1),
-        ring_shift(blocks[far - 1][1], ring, -1),
-    ]
-
-    gain_rows = norm_gain.reshape(chips, 1, 2 * feat_here)
-    closing = {"tok_here": tok_here, "side": 128}
+        for sign in (-1, 1):
+            blocks[sign * distance] = [
+                ring_shift(part, ring, -sign) for part in blocks[sign * (distance - 1)]
+            ]
+    gain_rows = norm_gain.reshape(chips, 1, width)
     carried, owns, positions = None, [], []
-    for distance in range(far + 1):
-        group = [distance] if distance in (0, far) else [distance, -distance]
-        at = [d % chips for d in group]
-        if distance == far:
-            closing["gain"] = gain_here
-        made = accumulate(
-            where, at, [blocks[d] for d in group], gain_rows, weights, carried, closing
+    for group in groups:
+        if group == [far]:
+            headers = [blocks[d if d <= far else d - chips][0] for d in range(chips)]
+        parts = [blocks[d if d <= far else d - chips] for d in group]
+        made, carried = accumulate(
+            where, group, parts, gain_rows, weights, carried, headers if group == [far] else None
         )
-        owns.extend(made[: len(at)])
-        positions.extend(at)
-        carried = made[len(at) :]
+        owns.extend(made)
+        positions.extend(group)
+        if group == groups[max(far - 2, 0)]:
+            zero = carried[2][0]
+            blocks[far] = []
+            for lower, upper in zip(blocks[1 - far], blocks[far - 1]):
+                size = far * tok_here // 2
+                cut = lower.shape[0] - size
+                first = lax.dynamic_slice_in_dim(lower, zero, cut, axis=0)
+                second = lax.dynamic_slice_in_dim(upper, cut + zero, size, axis=0)
+                blocks[far].append(ring_shift(first, ring, 1))
+                blocks[far].append(ring_shift(second, ring, -1))
     hidden = carried[0]
 
     def contribution(rows, part):
-        return jnp.dot(rows, down[part], preferred_element_type=jnp.float32).astype(jnp.bfloat16)
-
-    farthest = lax.dynamic_slice_in_dim(hidden, where[far] * tok_here, tok_here, axis=0)
-    moving = {
-        1: [ring_shift(contribution(farthest, 0), ring, 1), None],
-        -1: [None, ring_shift(contribution(farthest, 1), ring, -1)],
-    }
+        cols = down[:, part * half : (part + 1) * half]
+        return jnp.dot(rows, cols, preferred_element_type=jnp.float32).astype(jnp.bfloat16)
+
+    hidden, lower, upper = farthest_rows(where, far, hidden, down)
+    moving = {1: [ring_shift(lower, ring, 1), None], -1: [None, ring_shift(upper, ring, -1)]}
     everything = [contribution(hidden, part) for part in range(2)]
     base = own_rows(where, positions, owns, everything)
     for distance in range(far - 1, 0, -1):

time: 188 us -> 202 us (1.074)
  waiting for transfers between devices: 98 us -> 75.9 us
  between operations: 2.31 us -> 20.6 us
  local copies, waits for them, and re-layouts: 9.35 us -> 22.2 us
  Pallas kernels: 30.4 us -> 42.6 us
  starting transfers between devices: 40 us -> 33.4 us
    ppermute x3 -> x0, waiting for transfers between devices: 16.8 us -> none  [gather_small(): other = lax.ppermute(value, 'ep', pairs)]
    unnamed x15 -> x68, local copies, waits for them, and re-layouts: 0.91 us -> 15 us
    pallas_call x5, Pallas kernels: 20.2 us -> 29.1 us  [accumulate(): pl.pallas_call(kernel, grid_spec=pltpu.PrefetchScalarGridSpec(num_scalar_...]
    ppermute x3 -> x0, starting transfers between devices: 7.56 us -> none  [gather_small(): other = lax.ppermute(value, 'ep', pairs)]
    ppermute x28 -> x30, waiting for transfers between devices: 79.7 us -> 72.9 us  [ring_shift(): return lax.ppermute(value, 'ep', pairs)]
    slice x2 -> x0, local copies, waits for them, and re-layouts: 6.47 us -> none  [the longest x1 4.18 us: dense_body(): w_down[:, cols]]
    dynamic_slice x0 -> x4, local copies, waits for them, and re-layouts: none -> 5.21 us  [the longest x2 2.71 us: dense_body(): second = lax.dynamic_slice_in_dim(upper, cut + zero, size, axis=0)]
    pallas_call x0 -> x1, Pallas kernels: none -> 3.27 us  [farthest_rows(): pl.pallas_call(kernel, grid_spec=pltpu.PrefetchScalarGridSpec(num_scalar_...]
  transfers between devices with their start and end apart: 35 -> 34, of which waited for: 18 -> 14; matrix products, arithmetic and copies ran while one was open for 5% -> 6% of each run, Pallas kernels for 14% -> 19%
where the time goes in v4:
time: 202 us; the launch traced here: 201 us
  waiting for transfers between devices  75.9 us (38%)
  Pallas kernels  42.6 us (21%)
  starting transfers between devices  33.4 us (17%)
  local copies, waits for them, and re-layouts  22.2 us (11%)
  between operations  20.6 us (10%)
  matrix products  4.15 us (2%)
  other arithmetic  2.24 us (1%)
    ppermute x30, waiting for transfers between devices, ring_shift(): return lax.ppermute(value, 'ep', pairs)  72.9 us
    ppermute x30, starting transfers between devices, ring_shift(): return lax.ppermute(value, 'ep', pairs)  32.8 us
    pallas_call x5, Pallas kernels, accumulate(): pl.pallas_call(kernel, grid_spec=pltpu.PrefetchScalarGridSpec(num_scalar_...  29.1 us
    unnamed x68, local copies, waits for them, and re-layouts  15 us
    pallas_call x10, Pallas kernels, add_rows(): pl.pallas_call(kernel, grid_spec=pltpu.PrefetchScalarGridSpec(num_scalar_...  8.17 us
    dot_general x2, matrix products, contribution(): jnp.dot(rows, cols, preferred_element_type=jnp.float32).astype(jnp.bfloat16)  4.15 us
  transfers between devices with their start and end apart: 34, of which 14 were waited for; matrix products, arithmetic and copies ran while one was open for 6% of the time, Pallas kernels for 19%

profile of v4, /device:TPU:0, one launch (start us, length us, event | category | flops | bytes accessed | tf_op | source)
XLA Modules:
  0.0 201.1 jit_solution(15890624328030645085)
XLA Ops:
  6.5 1.8 add_convert_fusion
  9.5 1.5 collective-permute-done
  13.1 2.9 %collective-permute-start.1 = (bf16[272,896]{1,0:T(8,128)(2,1)S(1)}, bf16[272,896]{1,0:T(8,128)(2,1)S(1)}, u32[]{:S(2)}, u32[]{:S(2)}) collective-permute-start(bf16[272,896]{1,0:T(8,128)(2,1)S(1)} %fusion.3.refs_0_.refs_9_), channel_id=1, source_target_pairs={{0,2},{1,3},{4,0},{5,1},{8,4},{9,5},{12,8},{13,9},{14,12},{15,13},... | collective-permute-start | bytes 1462280 | tf_op jit(solution)/shard_map/ppermute | solution.py:115
  16.1 1.9 collective-permute-start.2
  18.2 9.8 %collective-permute-done.1.refs_0_.refs_10_ = bf16[272,896]{1,0:T(8,128)(2,1)S(1)} collective-permute-done((bf16[272,896]{1,0:T(8,128)(2,1)S(1)}, bf16[272,896]{1,0:T(8,128)(2,1)S(1)}, u32[]{:S(2)}, u32[]{:S(2)}) %collective-permute-start.1) | collective-permute-done | bytes 487456 | tf_op jit(solution)/shard_map/ppermute | solution.py:115
  28.0 2.0 collective-permute-start.5
  30.0 0.8 copy-done.4
  30.8 0.8 copy-done.7
  31.6 6.2 %collective-permute-done.2.refs_1_ = bf16[256,896]{1,0:T(8,128)(2,1)S(1)} collective-permute-done((bf16[256,896]{1,0:T(8,128)(2,1)S(1)}, bf16[256,896]{1,0:T(8,128)(2,1)S(1)}, u32[]{:S(2)}, u32[]{:S(2)}) %collective-permute-start.2) | collective-permute-done | bytes 458784 | tf_op jit(solution)/shard_map/ppermute | solution.py:115
  37.8 2.0 collective-permute-start.6
  39.8 0.8 copy-done.28
  40.7 0.8 copy-done.30
  41.5 0.7 constant_dynamic-slice_fusion.6
  44.1 13.6 %collective-permute-done.6.refs_1_ = bf16[256,896]{1,0:T(8,128)(2,1)} collective-permute-done((bf16[256,896]{1,0:T(8,128)(2,1)S(1)}, bf16[256,896]{1,0:T(8,128)(2,1)}, u32[]{:S(2)}, u32[]{:S(2)}) %collective-permute-start.6) | collective-permute-done | bytes 458784 | tf_op jit(solution)/shard_map/ppermute | solution.py:115
  57.7 1.7 collective-permute-start.10
  59.7 1.7 collective-permute-start.9
  61.8 0.8 copy-done.12
  62.5 4.2 %shard_map.91 = (bf16[64,896]{1,0:T(8,128)(2,1)S(1)}, f32[512,1024]{1,0:T(8,128)S(1)}, f32[512,128]{1,0:T(8,128)S(1)}, s32[1]{0:T(128)}) custom-call(s32[9]{0:T(128)S(1)} %get-tuple-element.58.where_ref, bf16[272,896]{1,0:T(8,128)(2,1)S(1)} %fusion.3.refs_0_.refs_9_, bf16[256,896]{1,0:T(8,128)(2,1)S(1)} %bitcast.37, f32[8,1,896]{2,1,0:T(1,128)S(1)} %bitcast.38, ...), custom_call_target="tpu_custom_call" | custom-call | flops 2818572288 | bytes 6946816 | tf_op jit(solution)/shard_map/pallas_call | solution.py:266
  67.4 5.8 %shard_map.92 = (bf16[64,896]{1,0:T(8,128)(2,1)S(1)}, bf16[64,896]{1,0:T(8,128)(2,1)S(1)}, f32[512,1024]{1,0:T(8,128)S(1)}, f32[512,128]{1,0:T(8,128)S(1)}, s32[1]{0:T(128)}) custom-call(s32[9]{0:T(128)S(1)} %get-tuple-element.58.where_ref, bf16[272,896]{1,0:T(8,128)(2,1)S(1)} %copy-done.5, ...), custom_call_target="tpu_custom_call", output_to_operand_aliasing={{2}: (9, {}), {3}: (10, {})} | custom-call | flops 5637144576 | bytes 9699328 | tf_op jit(solution)/shard_map/pallas_call | solution.py:266
  73.9 7.2 %shard_map.93 = (bf16[64,896]{1,0:T(8,128)(2,1)S(1)}, bf16[64,896]{1,0:T(8,128)(2,1)S(1)}, f32[512,1024]{1,0:T(8,128)S(1)}, f32[512,128]{1,0:T(8,128)S(1)}, s32[1]{0:T(128)}) custom-call(s32[9]{0:T(128)S(1)} %get-tuple-element.58.where_ref, bf16[272,896]{1,0:T(8,128)(2,1)} %collective-permute-done.5.refs_0_.refs_11_, ...), custom_call_target="tpu_custom_call", output_to_operand_aliasing={{2}: (9, {}), {3}: (10, {})} | custom-call | flops 5637144576 | bytes 9699328 | tf_op jit(solution)/shard_map/pallas_call | solution.py:266
  81.2 0.7 copy-done.10
  85.1 0.8 constant_dynamic-slice_fusion.5
  85.8 1.7 collective-permute-start.13
  88.9 1.7 constant_dynamic-slice_fusion.4
  92.1 1.7 constant_dynamic-slice_fusion.3
  93.9 1.7 collective-permute-start.15
  96.9 1.0 constant_dynamic-slice_fusion.2
  98.2 0.9 copy-done.11
  99.2 7.1 %shard_map.94 = (bf16[64,896]{1,0:T(8,128)(2,1)S(1)}, bf16[64,896]{1,0:T(8,128)(2,1)S(1)}, f32[512,1024]{1,0:T(8,128)S(1)}, f32[512,128]{1,0:T(8,128)S(1)}, s32[1]{0:T(128)}) custom-call(s32[9]{0:T(128)S(1)} %get-tuple-element.58.where_ref, bf16[272,896]{1,0:T(8,128)(2,1)} %collective-permute-done.9.refs_0_.refs_12_, ...), custom_call_target="tpu_custom_call", output_to_operand_aliasing={{2}: (9, {}), {3}: (10, {})} | custom-call | flops 5637144576 | bytes 9699328 | tf_op jit(solution)/shard_map/pallas_call | solution.py:266
  107.6 4.8 %shard_map.95 = (bf16[64,896]{1,0:T(8,128)(2,1)S(1)}, bf16[512,512]{1,0:T(8,128)(2,1)S(1)}) custom-call(s32[9]{0:T(128)S(1)} %get-tuple-element.58.where_ref, bf16[144,896]{1,0:T(8,128)(2,1)S(1)} %collective-permute-done.13.refs_0_.refs_13_, bf16[128,896]{1,0:T(8,128)(2,1)} %collective-permute-done.14.refs_1_, ...), custom_call_target="tpu_custom_call" | custom-call | flops 2818572288 | bytes 6946816 | tf_op jit(solution)/shard_map/pallas_call | solution.py:266
  112.4 0.8 copy-done.2
  113.8 3.1 %copy-done = bf16[512,7168]{1,0:T(8,128)(2,1)S(1)} copy-done((bf16[512,7168]{1,0:T(8,128)(2,1)S(1)}, bf16[512,7168]{1,0:T(8,128)(2,1)}, u32[]{:S(2)}) %copy-start) | copy-done | bytes 7340056
  116.9 1.0 copy-done.3
  118.0 3.3 %shard_map.96 = (bf16[512,512]{1,0:T(8,128)(2,1)S(1)}, bf16[64,3584]{1,0:T(8,128)(2,1)S(1)}, bf16[64,3584]{1,0:T(8,128)(2,1)S(1)}) custom-call(s32[9]{0:T(128)S(1)} %get-tuple-element.58.where_ref, bf16[512,512]{1,0:T(8,128)(2,1)S(1)} %copy-done.3, bf16[512,7168]{1,0:T(8,128)(2,1)S(1)} %copy-done, bf16[512,7168]{1,0:T(8,128)(2,1)S(1)} %copy-done), custom_call_target="tpu_custom_call" | custom-call | flops 469762048 | bytes 7340032 | tf_op jit(solution)/shard_map/pallas_call | solution.py:303
  121.3 1.8 collective-permute-start.17
  123.0 2.1 %convolution_convert_fusion.1.refs_8_.table_ref = bf16[512,3584]{1,0:T(8,128)(2,1)S(1)} fusion(bf16[512,512]{1,0:T(8,128)(2,1)S(1)} %get-tuple-element.50, bf16[512,7168]{1,0:T(8,128)(2,1)S(1)} %copy-done.1), kind=kOutput, calls=%fused_computation.1 | convolution fusion | flops 1880883200 | bytes 7864320 | tf_op jit(solution)/shard_map/dot_general | solution.py:478
  125.5 1.7 collective-permute-start.27
  127.2 2.1 %convolution_convert_fusion.refs_9_.table_ref = bf16[512,3584]{1,0:T(8,128)(2,1)S(1)} fusion(bf16[512,512]{1,0:T(8,128)(2,1)S(1)} %get-tuple-element.50, bf16[512,7168]{1,0:T(8,128)(2,1)S(1)} %copy-done.1), kind=kOutput, calls=%fused_computation | convolution fusion | flops 1880883200 | bytes 7864320 | tf_op jit(solution)/shard_map/dot_general | solution.py:478
  129.7 4.4 %collective-permute-done.17.moved_ref = bf16[64,3584]{1,0:T(8,128)(2,1)S(1)} collective-permute-done((bf16[64,3584]{1,0:T(8,128)(2,1)S(1)}, bf16[64,3584]{1,0:T(8,128)(2,1)S(1)}, u32[]{:S(2)}, u32[]{:S(2)}) %collective-permute-start.17) | collective-permute-done | bytes 458784 | tf_op jit(solution)/shard_map/ppermute | solution.py:115
  134.1 0.8 shard_map.98
  134.9 1.9 collective-permute-start.18
  136.9 8.0 %collective-permute-done.27.moved_ref = bf16[64,3584]{1,0:T(8,128)(2,1)S(1)} collective-permute-done((bf16[64,3584]{1,0:T(8,128)(2,1)S(1)}, bf16[64,3584]{1,0:T(8,128)(2,1)S(1)}, u32[]{:S(2)}, u32[]{:S(2)}) %collective-permute-start.27) | collective-permute-done | bytes 458784 | tf_op jit(solution)/shard_map/ppermute | solution.py:115
  144.9 0.8 shard_map.105
  146.0 0.8 shard_map.101
  146.9 1.7 collective-permute-start.22
  148.6 0.8 shard_map.103
  149.8 3.9 %collective-permute-done.18.moved_ref = bf16[64,3584]{1,0:T(8,128)(2,1)S(1)} collective-permute-done((bf16[64,3584]{1,0:T(8,128)(2,1)S(1)}, bf16[64,3584]{1,0:T(8,128)(2,1)S(1)}, u32[]{:S(2)}, u32[]{:S(2)}) %collective-permute-start.18) | collective-permute-done | bytes 458784 | tf_op jit(solution)/shard_map/ppermute | solution.py:115
  153.7 0.8 shard_map.99
  154.6 1.9 collective-permute-start.19
  156.5 2.7 %collective-permute-done.28.moved_ref = bf16[64,3584]{1,0:T(8,128)(2,1)S(1)} collective-permute-done((bf16[64,3584]{1,0:T(8,128)(2,1)S(1)}, bf16[64,3584]{1,0:T(8,128)(2,1)S(1)}, u32[]{:S(2)}, u32[]{:S(2)}) %collective-permute-start.28) | collective-permute-done | bytes 458784 | tf_op jit(solution)/shard_map/ppermute | solution.py:115
  159.2 0.8 shard_map.106
  160.4 8.6 %collective-permute-done.22.moved_ref = bf16[64,3584]{1,0:T(8,128)(2,1)S(1)} collective-permute-done((bf16[64,3584]{1,0:T(8,128)(2,1)S(1)}, bf16[64,3584]{1,0:T(8,128)(2,1)S(1)}, u32[]{:S(2)}, u32[]{:S(2)}) %collective-permute-start.22) | collective-permute-done | bytes 458784 | tf_op jit(solution)/shard_map/ppermute | solution.py:115
  169.0 0.8 shard_map.102
  170.2 0.8 shard_map.104
  171.1 1.8 collective-permute-start.26
  173.4 0.8 shard_map.100
  174.2 1.9 collective-permute-start.20
  176.2 2.7 %collective-permute-done.29.moved_ref = bf16[64,3584]{1,0:T(8,128)(2,1)S(1)} collective-permute-done((bf16[64,3584]{1,0:T(8,128)(2,1)S(1)}, bf16[64,3584]{1,0:T(8,128)(2,1)S(1)}, u32[]{:S(2)}, u32[]{:S(2)}) %collective-permute-start.29) | collective-permute-done | bytes 458784 | tf_op jit(solution)/shard_map/ppermute | solution.py:115
  178.9 0.8 shard_map.107
  180.1 0.8 shard_map.97.base_ref
  180.9 7.5 %collective-permute-done.23.refs_1_ = bf16[64,3584]{1,0:T(8,128)(2,1)S(1)} collective-permute-done((bf16[64,3584]{1,0:T(8,128)(2,1)S(1)}, bf16[64,3584]{1,0:T(8,128)(2,1)S(1)}, u32[]{:S(2)}, u32[]{:S(2)}) %collective-permute-start.23) | collective-permute-done | bytes 458784 | tf_op jit(solution)/shard_map/ppermute | solution.py:115
  188.4 1.7 collective-permute-done.20.refs_0_
  190.1 3.2 %collective-permute-done.30.refs_3_ = bf16[64,3584]{1,0:T(8,128)(2,1)S(1)} collective-permute-done((bf16[64,3584]{1,0:T(8,128)(2,1)S(1)}, bf16[64,3584]{1,0:T(8,128)(2,1)S(1)}, u32[]{:S(2)}, u32[]{:S(2)}) %collective-permute-start.30) | collective-permute-done | bytes 458784 | tf_op jit(solution)/shard_map/ppermute | solution.py:115
  193.3 1.2 shard_map.108
  (114 shorter events, 13.1 us)
Async XLA Ops:
  6.5 55.2 %all-gather.4.cloned.1.call-start = ((), (), s32[]{:S(2)}) async-start(), calls=%async_computation | async-start | bytes 11010048 | tf_op jit(solution)/shard_map/all_gather | solution.py:94
  8.9 2.1 %collective-permute-start = (bf16[8,64,448]{2,1,0:T(8,128)(2,1)S(1)}, bf16[8,64,448]{2,1,0:T(8,128)(2,1)S(1)}, u32[]{:S(2)}, u32[]{:S(2)}) collective-permute-start(bf16[8,64,448]{2,1,0:T(8,128)(2,1)S(1)} %dynamic-slice_bitcast_fusion), channel_id=1, source_target_pairs={{0,1},{1,0},{2,3},{3,2},{4,5},{5,4},{6,7},{7,6},{8,9},{9,8},{10,11... | collective-permute-start | bytes 1376264 | tf_op jit(solution)/shard_map/ppermute | solution.py:89
  11.0 1.5 copy-start.32
  11.0 1.5 copy-start.33
  11.0 50.7 %all-gather.6.cloned.1.call-start = ((), (), s32[]{:S(2)}) async-start(), calls=%async_computation.1 | async-start | bytes 11010048 | tf_op jit(solution)/shard_map/all_gather | solution.py:94
  11.8 102.0 %all-gather.8.cloned.1.call-start = ((), (), s32[]{:S(2)}) async-start(), calls=%async_computation.2 | async-start | bytes 11010048 | tf_op jit(solution)/shard_map/all_gather | solution.py:94
  13.1 14.9 %collective-permute-start.1 = (bf16[272,896]{1,0:T(8,128)(2,1)S(1)}, bf16[272,896]{1,0:T(8,128)(2,1)S(1)}, u32[]{:S(2)}, u32[]{:S(2)}) collective-permute-start(bf16[272,896]{1,0:T(8,128)(2,1)S(1)} %fusion.3.refs_0_.refs_9_), channel_id=1, source_target_pairs={{0,2},{1,3},{4,0},{5,1},{8,4},{9,5},{12,8},{13,9},{14,12},{15,13},... | collective-permute-start | bytes 1462280 | tf_op jit(solution)/shard_map/ppermute | solution.py:115
  16.0 14.8 %collective-permute-start.3 = (bf16[272,896]{1,0:T(8,128)(2,1)S(1)}, bf16[272,896]{1,0:T(8,128)(2,1)S(1)}, u32[]{:S(2)}, u32[]{:S(2)}) collective-permute-start(bf16[272,896]{1,0:T(8,128)(2,1)S(1)} %fusion.3.refs_0_.refs_9_), channel_id=1, source_target_pairs={{0,4},{1,5},{4,8},{5,9},{8,12},{9,13},{12,14},{13,15},{14,10},{15,... | collective-permute-start | bytes 1462280 | tf_op jit(solution)/shard_map/ppermute | solution.py:115
  16.1 21.7 %collective-permute-start.2 = (bf16[256,896]{1,0:T(8,128)(2,1)S(1)}, bf16[256,896]{1,0:T(8,128)(2,1)S(1)}, u32[]{:S(2)}, u32[]{:S(2)}) collective-permute-start(bf16[256,896]{1,0:T(8,128)(2,1)S(1)} %bitcast.35), channel_id=1, source_target_pairs={{0,2},{1,3},{4,0},{5,1},{8,4},{9,5},{12,8},{13,9},{14,12},{15,13},... | collective-permute-start | bytes 1376264 | tf_op jit(solution)/shard_map/ppermute | solution.py:115
  18.0 22.6 %collective-permute-start.4 = (bf16[256,896]{1,0:T(8,128)(2,1)S(1)}, bf16[256,896]{1,0:T(8,128)(2,1)S(1)}, u32[]{:S(2)}, u32[]{:S(2)}) collective-permute-start(bf16[256,896]{1,0:T(8,128)(2,1)S(1)} %bitcast.36), channel_id=1, source_target_pairs={{0,4},{1,5},{4,8},{5,9},{8,12},{9,13},{12,14},{13,15},{14,10},{15,... | collective-permute-start | bytes 1376264 | tf_op jit(solution)/shard_map/ppermute | solution.py:115
  28.0 31.8 %collective-permute-start.5 = (bf16[272,896]{1,0:T(8,128)(2,1)S(1)}, bf16[272,896]{1,0:T(8,128)(2,1)}, u32[]{:S(2)}, u32[]{:S(2)}) collective-permute-start(bf16[272,896]{1,0:T(8,128)(2,1)S(1)} %collective-permute-done.1.refs_0_.refs_10_), channel_id=1, source_target_pairs={{0,2},{1,3},{4,0},{5,1},{8,4},{9,5},{12,8},{13,9},{14,12},{15,13},... | collective-permute-start | bytes 1462280 | tf_op jit(solution)/shard_map/ppermute | solution.py:115
  30.0 0.8 copy-start.4
  30.8 30.7 %collective-permute-start.7 = (bf16[272,896]{1,0:T(8,128)(2,1)S(1)}, bf16[272,896]{1,0:T(8,128)(2,1)}, u32[]{:S(2)}, u32[]{:S(2)}) collective-permute-start(bf16[272,896]{1,0:T(8,128)(2,1)S(1)} %collective-permute-done.3.refs_2_.refs_16_), channel_id=1, source_target_pairs={{0,4},{1,5},{4,8},{5,9},{8,12},{9,13},{12,14},{13,15},{14,10},{15,... | collective-permute-start | bytes 1462280 | tf_op jit(solution)/shard_map/ppermute | solution.py:115
  30.8 0.8 copy-start.7
  37.8 19.9 %collective-permute-start.6 = (bf16[256,896]{1,0:T(8,128)(2,1)S(1)}, bf16[256,896]{1,0:T(8,128)(2,1)}, u32[]{:S(2)}, u32[]{:S(2)}) collective-permute-start(bf16[256,896]{1,0:T(8,128)(2,1)S(1)} %collective-permute-done.2.refs_1_), channel_id=1, source_target_pairs={{0,2},{1,3},{4,0},{5,1},{8,4},{9,5},{12,8},{13,9},{14,12},{15,13},... | collective-permute-start | bytes 1376264 | tf_op jit(solution)/shard_map/ppermute | solution.py:115
  39.8 0.8 copy-start.28
  40.6 18.8 %collective-permute-start.8 = (bf16[256,896]{1,0:T(8,128)(2,1)S(1)}, bf16[256,896]{1,0:T(8,128)(2,1)}, u32[]{:S(2)}, u32[]{:S(2)}) collective-permute-start(bf16[256,896]{1,0:T(8,128)(2,1)S(1)} %collective-permute-done.4.refs_3_), channel_id=1, source_target_pairs={{0,4},{1,5},{4,8},{5,9},{8,12},{9,13},{12,14},{13,15},{14,10},{15,... | collective-permute-start | bytes 1376264 | tf_op jit(solution)/shard_map/ppermute | solution.py:115
  40.7 0.8 copy-start.30
  57.7 39.2 %collective-permute-start.10 = (bf16[256,896]{1,0:T(8,128)(2,1)}, bf16[256,896]{1,0:T(8,128)(2,1)}, u32[]{:S(2)}, u32[]{:S(2)}) collective-permute-start(bf16[256,896]{1,0:T(8,128)(2,1)} %collective-permute-done.6.refs_1_), channel_id=1, source_target_pairs={{0,2},{1,3},{4,0},{5,1},{8,4},{9,5},{12,8},{13,9},{14,12},{15,13},... | collective-permute-start | bytes 1376264 | tf_op jit(solution)/shard_map/ppermute | solution.py:115
  59.4 32.7 %collective-permute-start.12 = (bf16[256,896]{1,0:T(8,128)(2,1)}, bf16[256,896]{1,0:T(8,128)(2,1)}, u32[]{:S(2)}, u32[]{:S(2)}) collective-permute-start(bf16[256,896]{1,0:T(8,128)(2,1)} %collective-permute-done.8.refs_3_), channel_id=1, source_target_pairs={{0,4},{1,5},{4,8},{5,9},{8,12},{9,13},{12,14},{13,15},{14,10},{15,... | collective-permute-start | bytes 1376264 | tf_op jit(solution)/shard_map/ppermute | solution.py:115
  59.7 29.1 %collective-permute-start.9 = (bf16[272,896]{1,0:T(8,128)(2,1)}, bf16[272,896]{1,0:T(8,128)(2,1)}, u32[]{:S(2)}, u32[]{:S(2)}) collective-permute-start(bf16[272,896]{1,0:T(8,128)(2,1)} %collective-permute-done.5.refs_0_.refs_11_), channel_id=1, source_target_pairs={{0,2},{1,3},{4,0},{5,1},{8,4},{9,5},{12,8},{13,9},{14,12},{15,13},... | collective-permute-start | bytes 1462280 | tf_op jit(solution)/shard_map/ppermute | solution.py:115
  61.4 23.6 %collective-permute-start.11 = (bf16[272,896]{1,0:T(8,128)(2,1)}, bf16[272,896]{1,0:T(8,128)(2,1)S(1)}, u32[]{:S(2)}, u32[]{:S(2)}) collective-permute-start(bf16[272,896]{1,0:T(8,128)(2,1)} %collective-permute-done.7.refs_2_.refs_15_), channel_id=1, source_target_pairs={{0,4},{1,5},{4,8},{5,9},{8,12},{9,13},{12,14},{13,15},{14,10},{15,... | collective-permute-start | bytes 1462280 | tf_op jit(solution)/shard_map/ppermute | solution.py:115
  61.8 0.8 copy-start.12
  62.5 4.9 %copy-start.5 = (bf16[272,896]{1,0:T(8,128)(2,1)S(1)}, bf16[272,896]{1,0:T(8,128)(2,1)}, u32[]{:S(2)}) copy-start(bf16[272,896]{1,0:T(8,128)(2,1)} %copy-done.4) | copy-start | bytes 1462276
  62.5 4.9 %copy-start.8 = (bf16[272,896]{1,0:T(8,128)(2,1)S(1)}, bf16[272,896]{1,0:T(8,128)(2,1)}, u32[]{:S(2)}) copy-start(bf16[272,896]{1,0:T(8,128)(2,1)} %copy-done.7) | copy-start | bytes 1462276
  62.5 4.9 %copy-start.29 = (bf16[256,896]{1,0:T(8,128)(2,1)S(1)}, bf16[256,896]{1,0:T(8,128)(2,1)}, u32[]{:S(2)}) copy-start(bf16[256,896]{1,0:T(8,128)(2,1)} %copy-done.28) | copy-start | bytes 1376260
  62.5 4.9 %copy-start.31 = (bf16[256,896]{1,0:T(8,128)(2,1)S(1)}, bf16[256,896]{1,0:T(8,128)(2,1)}, u32[]{:S(2)}) copy-start(bf16[256,896]{1,0:T(8,128)(2,1)} %copy-done.30) | copy-start | bytes 1376260
  66.8 0.6 copy-start.14
  73.3 0.6 copy-start.16
  73.9 24.3 %copy-start.13 = (f32[7168]{0:T(1024)S(1)}, f32[7168]{0:T(1024)}, u32[]{:S(2)}) copy-start(f32[7168]{0:T(1024)} %param.11) | copy-start | bytes 86020
  81.1 0.7 copy-start.10
  85.8 21.7 %collective-permute-start.13 = (bf16[144,896]{1,0:T(8,128)(2,1)}, bf16[144,896]{1,0:T(8,128)(2,1)S(1)}, u32[]{:S(2)}, u32[]{:S(2)}) collective-permute-start(bf16[144,896]{1,0:T(8,128)(2,1)} %constant_dynamic-slice_fusion.5), channel_id=1, source_target_pairs={{0,4},{1,5},{4,8},{5,9},{8,12},{9,13},{12,14},{13,15},{14,10},{15,... | collective-permute-start | bytes 774152 | tf_op jit(solution)/shard_map/ppermute | solution.py:115
  90.6 17.0 %collective-permute-start.14 = (bf16[128,896]{1,0:T(8,128)(2,1)}, bf16[128,896]{1,0:T(8,128)(2,1)}, u32[]{:S(2)}, u32[]{:S(2)}) collective-permute-start(bf16[128,896]{1,0:T(8,128)(2,1)} %constant_dynamic-slice_fusion.4), channel_id=1, source_target_pairs={{0,2},{1,3},{4,0},{5,1},{8,4},{9,5},{12,8},{13,9},{14,12},{15,13},... | collective-permute-start | bytes 688136 | tf_op jit(solution)/shard_map/ppermute | solution.py:115
  93.9 13.7 %collective-permute-start.15 = (bf16[128,896]{1,0:T(8,128)(2,1)}, bf16[128,896]{1,0:T(8,128)(2,1)}, u32[]{:S(2)}, u32[]{:S(2)}) collective-permute-start(bf16[128,896]{1,0:T(8,128)(2,1)} %constant_dynamic-slice_fusion.3), channel_id=1, source_target_pairs={{0,4},{1,5},{4,8},{5,9},{8,12},{9,13},{12,14},{13,15},{14,10},{15,... | collective-permute-start | bytes 688136 | tf_op jit(solution)/shard_map/ppermute | solution.py:115
  97.9 9.7 %collective-permute-start.16 = (bf16[128,896]{1,0:T(8,128)(2,1)S(1)}, bf16[128,896]{1,0:T(8,128)(2,1)S(1)}, u32[]{:S(2)}, u32[]{:S(2)}) collective-permute-start(bf16[128,896]{1,0:T(8,128)(2,1)S(1)} %constant_dynamic-slice_fusion.2), channel_id=1, source_target_pairs={{0,2},{1,3},{4,0},{5,1},{8,4},{9,5},{12,8},{13,9},{14,12},{15,13},... | collective-permute-start | bytes 688136 | tf_op jit(solution)/shard_map/ppermute | solution.py:115
  98.2 1.0 copy-start.11
  99.2 8.4 %copy-start.6 = (bf16[272,896]{1,0:T(8,128)(2,1)S(1)}, bf16[272,896]{1,0:T(8,128)(2,1)}, u32[]{:S(2)}) copy-start(bf16[272,896]{1,0:T(8,128)(2,1)} %copy-done.4) | copy-start | bytes 1462276
  99.2 8.4 %copy-start.9 = (bf16[272,896]{1,0:T(8,128)(2,1)S(1)}, bf16[272,896]{1,0:T(8,128)(2,1)}, u32[]{:S(2)}) copy-start(bf16[272,896]{1,0:T(8,128)(2,1)} %copy-done.7) | copy-start | bytes 1462276
  106.3 0.6 copy-start.22
  112.4 0.8 copy-start.2
  113.8 3.1 %copy-start = (bf16[512,7168]{1,0:T(8,128)(2,1)S(1)}, bf16[512,7168]{1,0:T(8,128)(2,1)}, u32[]{:S(2)}) copy-start(bf16[512,7168]{1,0:T(8,128)(2,1)} %all-gather.8.cloned.1.call-done.lower_ref.upper_ref) | copy-start | bytes 22020100
  116.9 1.0 copy-start.3
  118.0 5.1 %copy-start.1 = (bf16[512,7168]{1,0:T(8,128)(2,1)S(1)}, bf16[512,7168]{1,0:T(8,128)(2,1)}, u32[]{:S(2)}) copy-start(bf16[512,7168]{1,0:T(8,128)(2,1)} %all-gather.8.cloned.1.call-done.lower_ref.upper_ref) | copy-start | bytes 22020100
  121.3 12.8 %collective-permute-start.17 = (bf16[64,3584]{1,0:T(8,128)(2,1)S(1)}, bf16[64,3584]{1,0:T(8,128)(2,1)S(1)}, u32[]{:S(2)}, u32[]{:S(2)}) collective-permute-start(bf16[64,3584]{1,0:T(8,128)(2,1)S(1)} %get-tuple-element.51), channel_id=1, source_target_pairs={{0,4},{1,5},{4,8},{5,9},{8,12},{9,13},{12,14},{13,15},{14,10},{15,... | collective-permute-start | bytes 1376264 | tf_op jit(solution)/shard_map/ppermute | solution.py:115
  125.2 20.9 %collective-permute-start.21 = (bf16[64,3584]{1,0:T(8,128)(2,1)S(1)}, bf16[64,3584]{1,0:T(8,128)(2,1)S(1)}, u32[]{:S(2)}, u32[]{:S(2)}) collective-permute-start(bf16[64,3584]{1,0:T(8,128)(2,1)S(1)} %constant_dynamic-slice_fusion.1), channel_id=1, source_target_pairs={{0,2},{1,3},{4,0},{5,1},{8,4},{9,5},{12,8},{13,9},{14,12},{15,13},... | collective-permute-start | bytes 1376264 | tf_op jit(solution)/shard_map/ppermute | solution.py:115
  125.5 19.3 %collective-permute-start.27 = (bf16[64,3584]{1,0:T(8,128)(2,1)S(1)}, bf16[64,3584]{1,0:T(8,128)(2,1)S(1)}, u32[]{:S(2)}, u32[]{:S(2)}) collective-permute-start(bf16[64,3584]{1,0:T(8,128)(2,1)S(1)} %get-tuple-element.52), channel_id=1, source_target_pairs={{0,2},{1,3},{4,0},{5,1},{8,4},{9,5},{12,8},{13,9},{14,12},{15,13},... | collective-permute-start | bytes 1376264 | tf_op jit(solution)/shard_map/ppermute | solution.py:115
  129.3 19.3 %collective-permute-start.24 = (bf16[64,3584]{1,0:T(8,128)(2,1)S(1)}, bf16[64,3584]{1,0:T(8,128)(2,1)S(1)}, u32[]{:S(2)}, u32[]{:S(2)}) collective-permute-start(bf16[64,3584]{1,0:T(8,128)(2,1)S(1)} %constant_dynamic-slice_fusion), channel_id=1, source_target_pairs={{0,4},{1,5},{4,8},{5,9},{8,12},{9,13},{12,14},{13,15},{14,10},{15,... | collective-permute-start | bytes 1376264 | tf_op jit(solution)/shard_map/ppermute | solution.py:115
  134.9 18.8 %collective-permute-start.18 = (bf16[64,3584]{1,0:T(8,128)(2,1)S(1)}, bf16[64,3584]{1,0:T(8,128)(2,1)S(1)}, u32[]{:S(2)}, u32[]{:S(2)}) collective-permute-start(bf16[64,3584]{1,0:T(8,128)(2,1)S(1)} %shard_map.98), channel_id=1, source_target_pairs={{0,4},{1,5},{4,8},{5,9},{8,12},{9,13},{12,14},{13,15},{14,10},{15,... | collective-permute-start | bytes 1376264 | tf_op jit(solution)/shard_map/ppermute | solution.py:115
  145.7 13.5 %collective-permute-start.28 = (bf16[64,3584]{1,0:T(8,128)(2,1)S(1)}, bf16[64,3584]{1,0:T(8,128)(2,1)S(1)}, u32[]{:S(2)}, u32[]{:S(2)}) collective-permute-start(bf16[64,3584]{1,0:T(8,128)(2,1)S(1)} %shard_map.105), channel_id=1, source_target_pairs={{0,2},{1,3},{4,0},{5,1},{8,4},{9,5},{12,8},{13,9},{14,12},{15,13},... | collective-permute-start | bytes 1376264 | tf_op jit(solution)/shard_map/ppermute | solution.py:115
  146.9 22.2 %collective-permute-start.22 = (bf16[64,3584]{1,0:T(8,128)(2,1)S(1)}, bf16[64,3584]{1,0:T(8,128)(2,1)S(1)}, u32[]{:S(2)}, u32[]{:S(2)}) collective-permute-start(bf16[64,3584]{1,0:T(8,128)(2,1)S(1)} %shard_map.101), channel_id=1, source_target_pairs={{0,2},{1,3},{4,0},{5,1},{8,4},{9,5},{12,8},{13,9},{14,12},{15,13},... | collective-permute-start | bytes 1376264 | tf_op jit(solution)/shard_map/ppermute | solution.py:115
  149.4 20.8 %collective-permute-start.25 = (bf16[64,3584]{1,0:T(8,128)(2,1)S(1)}, bf16[64,3584]{1,0:T(8,128)(2,1)S(1)}, u32[]{:S(2)}, u32[]{:S(2)}) collective-permute-start(bf16[64,3584]{1,0:T(8,128)(2,1)S(1)} %shard_map.103), channel_id=1, source_target_pairs={{0,4},{1,5},{4,8},{5,9},{8,12},{9,13},{12,14},{13,15},{14,10},{15,... | collective-permute-start | bytes 1376264 | tf_op jit(solution)/shard_map/ppermute | solution.py:115
  154.6 18.8 %collective-permute-start.19 = (bf16[64,3584]{1,0:T(8,128)(2,1)S(1)}, bf16[64,3584]{1,0:T(8,128)(2,1)S(1)}, u32[]{:S(2)}, u32[]{:S(2)}) collective-permute-start(bf16[64,3584]{1,0:T(8,128)(2,1)S(1)} %shard_map.99), channel_id=1, source_target_pairs={{0,4},{1,5},{4,8},{5,9},{8,12},{9,13},{12,14},{13,15},{14,10},{15,... | collective-permute-start | bytes 1376264 | tf_op jit(solution)/shard_map/ppermute | solution.py:115
  160.0 18.8 %collective-permute-start.29 = (bf16[64,3584]{1,0:T(8,128)(2,1)S(1)}, bf16[64,3584]{1,0:T(8,128)(2,1)S(1)}, u32[]{:S(2)}, u32[]{:S(2)}) collective-permute-start(bf16[64,3584]{1,0:T(8,128)(2,1)S(1)} %shard_map.106), channel_id=1, source_target_pairs={{0,2},{1,3},{4,0},{5,1},{8,4},{9,5},{12,8},{13,9},{14,12},{15,13},... | collective-permute-start | bytes 1376264 | tf_op jit(solution)/shard_map/ppermute | solution.py:115
  169.8 18.6 %collective-permute-start.23 = (bf16[64,3584]{1,0:T(8,128)(2,1)S(1)}, bf16[64,3584]{1,0:T(8,128)(2,1)S(1)}, u32[]{:S(2)}, u32[]{:S(2)}) collective-permute-start(bf16[64,3584]{1,0:T(8,128)(2,1)S(1)} %shard_map.102), channel_id=1, source_target_pairs={{0,2},{1,3},{4,0},{5,1},{8,4},{9,5},{12,8},{13,9},{14,12},{15,13},... | collective-permute-start | bytes 1376264 | tf_op jit(solution)/shard_map/ppermute | solution.py:115
  171.0 9.0 %copy-start.15 = (bf16[64,896]{1,0:T(8,128)(2,1)S(1)}, bf16[64,896]{1,0:T(8,128)(2,1)}, u32[]{:S(2)}) copy-start(bf16[64,896]{1,0:T(8,128)(2,1)} %copy-done.14) | copy-start | bytes 344068
  171.0 9.0 %copy-start.17 = (bf16[64,896]{1,0:T(8,128)(2,1)S(1)}, bf16[64,896]{1,0:T(8,128)(2,1)}, u32[]{:S(2)}) copy-start(bf16[64,896]{1,0:T(8,128)(2,1)} %copy-done.16) | copy-start | bytes 344068
  171.1 9.0 %copy-start.19 = (bf16[64,896]{1,0:T(8,128)(2,1)S(1)}, bf16[64,896]{1,0:T(8,128)(2,1)}, u32[]{:S(2)}) copy-start(bf16[64,896]{1,0:T(8,128)(2,1)} %copy-done.18) | copy-start | bytes 344068
  171.1 9.0 %copy-start.21 = (bf16[64,896]{1,0:T(8,128)(2,1)S(1)}, bf16[64,896]{1,0:T(8,128)(2,1)}, u32[]{:S(2)}) copy-start(bf16[64,896]{1,0:T(8,128)(2,1)} %copy-done.20) | copy-start | bytes 344068
  171.1 9.0 %copy-start.23 = (bf16[64,896]{1,0:T(8,128)(2,1)S(1)}, bf16[64,896]{1,0:T(8,128)(2,1)}, u32[]{:S(2)}) copy-start(bf16[64,896]{1,0:T(8,128)(2,1)} %copy-done.22) | copy-start | bytes 344068
  171.1 9.0 %copy-start.25 = (bf16[64,896]{1,0:T(8,128)(2,1)S(1)}, bf16[64,896]{1,0:T(8,128)(2,1)}, u32[]{:S(2)}) copy-start(bf16[64,896]{1,0:T(8,128)(2,1)} %copy-done.24) | copy-start | bytes 344068
  171.1 9.0 %copy-start.27 = (bf16[64,896]{1,0:T(8,128)(2,1)S(1)}, bf16[64,896]{1,0:T(8,128)(2,1)}, u32[]{:S(2)}) copy-start(bf16[64,896]{1,0:T(8,128)(2,1)} %copy-done.26) | copy-start | bytes 344068
  171.1 17.3 %collective-permute-start.26 = (bf16[64,3584]{1,0:T(8,128)(2,1)S(1)}, bf16[64,3584]{1,0:T(8,128)(2,1)S(1)}, u32[]{:S(2)}, u32[]{:S(2)}) collective-permute-start(bf16[64,3584]{1,0:T(8,128)(2,1)S(1)} %shard_map.104), channel_id=1, source_target_pairs={{0,4},{1,5},{4,8},{5,9},{8,12},{9,13},{12,14},{13,15},{14,10},{15,... | collective-permute-start | bytes 1376264 | tf_op jit(solution)/shard_map/ppermute | solution.py:115
  174.2 15.9 %collective-permute-start.20 = (bf16[64,3584]{1,0:T(8,128)(2,1)S(1)}, bf16[64,3584]{1,0:T(8,128)(2,1)S(1)}, u32[]{:S(2)}, u32[]{:S(2)}) collective-permute-start(bf16[64,3584]{1,0:T(8,128)(2,1)S(1)} %shard_map.100), channel_id=1, source_target_pairs={{0,4},{1,5},{4,8},{5,9},{8,12},{9,13},{12,14},{13,15},{14,10},{15,... | collective-permute-start | bytes 1376264 | tf_op jit(solution)/shard_map/ppermute | solution.py:115
  179.7 13.7 %collective-permute-start.30 = (bf16[64,3584]{1,0:T(8,128)(2,1)S(1)}, bf16[64,3584]{1,0:T(8,128)(2,1)S(1)}, u32[]{:S(2)}, u32[]{:S(2)}) collective-permute-start(bf16[64,3584]{1,0:T(8,128)(2,1)S(1)} %shard_map.107), channel_id=1, source_target_pairs={{0,2},{1,3},{4,0},{5,1},{8,4},{9,5},{12,8},{13,9},{14,12},{15,13},... | collective-permute-start | bytes 1376264 | tf_op jit(solution)/shard_map/ppermute | solution.py:115
  (4 other events, 2.5 us)
Sparse Core Ops, SparseCore 0:
  11.1 20.9 all-gather.3
  33.6 19.4 all-gather.5
  54.7 19.4 all-gather.7

commit v5 on v0

--- a/solution.py
+++ b/solution.py
@@ -1,6 +1,8 @@
 import jax
 import jax.numpy as jnp
 from jax import lax
+from jax.experimental import pallas as pl
+from jax.experimental.pallas import tpu as pltpu
 from jax.sharding import PartitionSpec as P
 
 FSPLIT = 8
@@ -43,7 +45,7 @@
     return jnp.dot(hidden, w_down, preferred_element_type=jnp.float32).astype(jnp.bfloat16)
 
 
-def body(residual, attn_out, norm_gain, expert_routes, route_gain, w_gate, w_up, w_down):
+def routed_body(residual, attn_out, norm_gain, expert_routes, route_gain, w_gate, w_up, w_down):
     devices = lax.axis_size("ep")
     tok_here = expert_routes.shape[0]
     route_slots = expert_routes.shape[1]
@@ -74,6 +76,470 @@
     return (stream_rows.astype(jnp.float32) + routed_sum).astype(jnp.bfloat16)
 
 
+def ring_order(chips):
+    return list(range(0, chips, 2)) + list(reversed(range(1, chips, 2)))
+
+
+def swap_cores(value):
+    return lax.ppermute(value, "ep", [(i, i ^ 1) for i in range(lax.axis_size("ep"))])
+
+
+def pair_gather(value):
+    pairs = [[i, i + 1] for i in range(0, lax.axis_size("ep"), 2)]
+    both = lax.all_gather(value, "ep", axis_index_groups=pairs, axis=0, tiled=True)
+    return pltpu.with_memory_space_constraint(both, pltpu.HBM)
+
+
+def ring_shift(value, ring, step):
+    chips = len(ring)
+    pairs = [
+        (2 * ring[i] + core, 2 * ring[(i + step) % chips] + core)
+        for i in range(chips)
+        for core in range(2)
+    ]
+    return lax.ppermute(value, "ep", pairs)
+
+
+COST_SCALE = 3
+VMEM_BYTES = 32 * 1024 * 1024
+IN_VMEM = pl.BlockSpec(memory_space=pltpu.VMEM)
+IN_SMEM = pl.BlockSpec(memory_space=pltpu.SMEM)
+IN_HBM = pl.BlockSpec(memory_space=pltpu.HBM)
+
+
+def local_call(
+    kernel, out_shape, operands, flops, bytes_accessed, aliases=None, scratch=(), far=()
+):
+    return pl.pallas_call(
+        kernel,
+        out_shape=out_shape,
+        in_specs=[
+            IN_SMEM if k == 0 else IN_HBM if k in far else IN_VMEM for k in range(len(operands))
+        ],
+        out_specs=jax.tree.map(
+            lambda made: IN_SMEM if made.dtype == jnp.int32 else IN_VMEM, out_shape
+        ),
+        scratch_shapes=list(scratch),
+        input_output_aliases=aliases or {},
+        compiler_params=pltpu.CompilerParams(vmem_limit_bytes=VMEM_BYTES),
+        cost_estimate=pl.CostEstimate(
+            flops=flops, bytes_accessed=bytes_accessed, transcendentals=0
+        ),
+    )(*operands)
+
+
+def first_blocks(where, stream, swapped, routes, route_gain, experts):
+    chips, _, tok_here, feat_here = stream.shape
+    width = 2 * feat_here
+    rows = chips * tok_here // 2
+    head = -(-3 * experts // 16) * 16
+
+    def kernel(where_ref, stream_ref, swapped_ref, routes_ref, gain_ref, *outs):
+        core = where_ref[chips + 1]
+        for q in range(chips):
+            mine = stream_ref[q, core]
+            other = swapped_ref[q]
+            left = jnp.where(core == 0, mine, other)
+            right = jnp.where(core == 0, other, mine)
+            out_ref = outs[2 * q // chips]
+            at = q * tok_here - (2 * q // chips) * rows + (head if 2 * q < chips else 0)
+            out_ref[at : at + tok_here, :] = jnp.concatenate([left, right], axis=1)
+        square = (tok_here, tok_here)
+        diagonal = lax.broadcasted_iota(jnp.int32, square, 0) == lax.broadcasted_iota(
+            jnp.int32, square, 1
+        )
+        row_at = lax.broadcasted_iota(jnp.int32, (head, tok_here), 0)
+        top = jnp.zeros((head, tok_here), jnp.float32)
+        for expert in range(experts):
+            gains = jnp.where(routes_ref[...] == expert, gain_ref[...], 0.0)
+            gains = jnp.sum(gains, axis=1, keepdims=True)
+            left = jnp.sum(jnp.where(diagonal, gains, 0.0), axis=0, keepdims=True)
+            for part in range(3):
+                piece = left.astype(jnp.bfloat16).astype(jnp.float32)
+                top = jnp.where(row_at == 3 * expert + part, piece, top)
+                left = left - piece
+        outs[0][:head, :] = jnp.zeros((head, width), jnp.bfloat16)
+        outs[0][:head, :tok_here] = top.astype(jnp.bfloat16)
+
+    return local_call(
+        kernel,
+        [
+            jax.ShapeDtypeStruct((head + rows, width), jnp.bfloat16),
+            jax.ShapeDtypeStruct((rows, width), jnp.bfloat16),
+        ],
+        [where, stream, swapped, routes, route_gain],
+        flops=2 * rows * width,
+        bytes_accessed=8 * rows * width,
+    )
+
+
+def accumulate(where, positions, parts, norm_gain, tables, carried, headers, fetched=None):
+    count = len(positions)
+    width = parts[0][0].shape[1]
+    chips = norm_gain.shape[0]
+    model_width = chips * width
+    hidden_here = tables[0].shape[1]
+    both = 2 * hidden_here
+    rows = parts[0][1].shape[0]
+    head = parts[0][0].shape[0] - rows
+    tokens = 2 * rows
+    tok_here = tokens // chips
+    side = 128
+    last = headers is not None
+    first = carried is None
+    slots = 4 * count
+
+    def kernel(where_ref, *refs):
+        refs = list(refs)
+        xs = [[refs.pop(0) for _ in range(2)] for _ in range(count)]
+        scale_ref = refs.pop(0)
+        stored = [refs.pop(0), refs.pop(0)]
+        acc_in, sq_in = (None, None) if first else (refs.pop(0), refs.pop(0))
+        tops = [refs.pop(0) for _ in headers] if last else []
+        source_ref = refs.pop(0) if fetched is not None else None
+        owns = [refs.pop(0) for _ in range(count)]
+        if last:
+            hidden_ref = refs.pop(0)
+        else:
+            acc_out, sq_out, done_ref = refs.pop(0), refs.pop(0), refs.pop(0)
+            done_ref[0] = 0
+        brought_ref = refs.pop(0) if fetched is not None else None
+        table_ref, sems = refs.pop(0), refs.pop(0)
+        gain_ref = refs.pop(0) if last else None
+        copies = {}
+        for core in range(2):
+            for which in range(2):
+                for b in range(count):
+                    row = (core * chips + where_ref[positions[b]]) * width
+                    slot = (core * 2 + which) * count + b
+                    copies[core, which, b] = pltpu.make_async_copy(
+                        stored[which].at[pl.ds(pl.multiple_of(row, width), width), :],
+                        table_ref.at[slot],
+                        sems.at[slot],
+                    )
+                    copies[core, which, b].start()
+        if fetched is not None:
+            bringing = pltpu.make_async_copy(source_ref, brought_ref, sems.at[slots])
+            bringing.start()
+        begin = where_ref[0] * tok_here
+        for b in range(count):
+            for k in range(2):
+
+                @pl.when((begin >= k * rows) & (begin < (k + 1) * rows))
+                def _():
+                    row = begin - k * rows + (head if k == 0 else 0)
+                    owns[b][...] = xs[b][k][pl.ds(pl.multiple_of(row, 16), tok_here), :]
+
+        if last:
+            expert = where_ref[chips]
+            square = (tok_here, tok_here)
+            row_at = lax.broadcasted_iota(jnp.int32, (head, tok_here), 0)
+            diagonal = lax.broadcasted_iota(jnp.int32, square, 0) == lax.broadcasted_iota(
+                jnp.int32, square, 1
+            )
+            for d in range(chips):
+                parts_of = tops[d][:head, :tok_here].astype(jnp.float32)
+                named = (row_at >= 3 * expert) & (row_at < 3 * expert + 3)
+                along = jnp.sum(jnp.where(named, parts_of, 0.0), axis=0, keepdims=True)
+                column = jnp.sum(jnp.where(diagonal, along, 0.0), axis=1, keepdims=True)
+                at = pl.multiple_of(where_ref[d] * tok_here, tok_here)
+                gain_ref[pl.ds(at, tok_here), :] = column
+
+        scaled, squared = [], []
+        for k in range(2):
+            span = slice(k * rows, (k + 1) * rows)
+            squares = None if first else sq_in[span, :]
+            for b in range(count):
+                at = head if k == 0 else 0
+                values = xs[b][k][at : at + rows, :].astype(jnp.float32)
+                for lane in range(0, width, side):
+                    piece = values[:, lane : lane + side]
+                    squares = piece * piece if squares is None else squares + piece * piece
+                scale = scale_ref[where_ref[positions[b]]]
+                scaled.append((values * scale).astype(jnp.bfloat16))
+            squared.append(squares)
+            if not last:
+                sq_out[span, :] = squares
+        for core in range(2):
+            acts = []
+            for which in range(2):
+                for b in range(count):
+                    copies[core, which, b].wait()
+                for k in range(2):
+                    span = slice(k * rows, (k + 1) * rows)
+                    at = core * both + which * hidden_here
+                    cols = slice(at, at + hidden_here)
+                    total = None if first else acc_in[span, cols]
+                    for b in range(count):
+                        product = jnp.dot(
+                            scaled[k * count + b],
+                            table_ref[(core * 2 + which) * count + b],
+                            preferred_element_type=jnp.float32,
+                        )
+                        total = product if total is None else total + product
+                    if last:
+                        acts.append(total)
+                    else:
+                        acc_out[span, cols] = total
+            if last:
+                for k in range(2):
+                    span = slice(k * rows, (k + 1) * rows)
+                    mean = jnp.sum(squared[k], axis=1, keepdims=True) / model_width
+                    inv_rms = lax.rsqrt(mean + epsilon)
+                    gate_act, up_act = acts[k] * inv_rms, acts[2 + k] * inv_rms
+                    act = gate_act * jax.nn.sigmoid(gate_act) * up_act * gain_ref[span, :]
+                    cols = slice(core * hidden_here, (core + 1) * hidden_here)
+                    hidden_ref[span, cols] = act.astype(jnp.bfloat16)
+        if fetched is not None:
+            bringing.wait()
+
+    operands = [where] + [piece for block in parts for piece in block]
+    operands.append(norm_gain)
+    distant = [len(operands), len(operands) + 1]
+    operands.extend(tables)
+    aliases = {}
+    if not first:
+        if not last:
+            aliases = {len(operands): count, len(operands) + 1: count + 1}
+        operands.extend(carried[:2])
+    out_shape = [jax.ShapeDtypeStruct((tok_here, width), jnp.bfloat16)] * count
+    if last:
+        operands.extend(headers)
+        out_shape.append(jax.ShapeDtypeStruct((tokens, both), jnp.bfloat16))
+    else:
+        out_shape.append(jax.ShapeDtypeStruct((tokens, 2 * both), jnp.float32))
+        out_shape.append(jax.ShapeDtypeStruct((tokens, side), jnp.float32))
+        out_shape.append(jax.ShapeDtypeStruct((1,), jnp.int32))
+    if fetched is not None:
+        distant.append(len(operands))
+        operands.append(fetched)
+        out_shape.append(jax.ShapeDtypeStruct(fetched.shape, fetched.dtype))
+    scratch = [
+        pltpu.VMEM((slots, width, hidden_here), jnp.bfloat16),
+        pltpu.SemaphoreType.DMA((slots + 1,)),
+    ]
+    if last:
+        scratch.append(pltpu.VMEM((tokens, 1), jnp.float32))
+    made = local_call(
+        kernel,
+        out_shape,
+        operands,
+        flops=COST_SCALE * 4 * count * tokens * width * both,
+        bytes_accessed=count * width * (tokens + 2 * both) * 2 + tokens * both * 16,
+        aliases=aliases,
+        scratch=scratch,
+        far=distant,
+    )
+    return made[:count], made[count:]
+
+
+def leading_rows(where, wanted, hidden, down, chips):
+    tokens, units = hidden.shape
+    model_width = down.shape[1]
+    half = model_width // 2
+    rows = tokens // chips
+
+    def kernel(where_ref, hidden_ref, down_ref, kept_ref, *outs):
+        kept_ref[...] = hidden_ref[...]
+        for (position, part), out_ref in zip(wanted, outs):
+            at = pl.multiple_of(where_ref[position] * rows, rows)
+            out = jnp.dot(
+                hidden_ref[pl.ds(at, rows), :],
+                down_ref[:, part * half : (part + 1) * half],
+                preferred_element_type=jnp.float32,
+            )
+            out_ref[...] = out.astype(jnp.bfloat16)
+
+    return local_call(
+        kernel,
+        [jax.ShapeDtypeStruct(hidden.shape, hidden.dtype)]
+        + [jax.ShapeDtypeStruct((rows, half), jnp.bfloat16)] * len(wanted),
+        [where, hidden, down],
+        flops=2 * rows * units * half * len(wanted),
+        bytes_accessed=2 * units * model_width,
+    )
+
+
+def contribution(where, hidden, down, part):
+    tokens, units = hidden.shape
+    half = down.shape[1] // 2
+    tile = 512 if half % 512 == 0 else half
+
+    def kernel(where_ref, hidden_ref, down_ref, out_ref):
+        for start in range(0, half, tile):
+            out = jnp.dot(
+                hidden_ref[...],
+                down_ref[:, part * half + start : part * half + start + tile],
+                preferred_element_type=jnp.float32,
+            )
+            out_ref[:, start : start + tile] = out.astype(jnp.bfloat16)
+
+    return local_call(
+        kernel,
+        jax.ShapeDtypeStruct((tokens, half), jnp.bfloat16),
+        [where, hidden, down],
+        flops=2 * tokens * units * half,
+        bytes_accessed=2 * half * (units + tokens),
+    )
+
+
+def add_rows(where, position, table, moved):
+    rows, width = moved.shape
+
+    def kernel(where_ref, table_ref, moved_ref, out_ref):
+        at = pl.multiple_of(where_ref[position] * rows, rows)
+        total = table_ref[pl.ds(at, rows), :].astype(jnp.float32)
+        out_ref[...] = (total + moved_ref[...].astype(jnp.float32)).astype(jnp.bfloat16)
+
+    return local_call(
+        kernel,
+        jax.ShapeDtypeStruct((rows, width), jnp.bfloat16),
+        [where, table, moved],
+        flops=rows * width,
+        bytes_accessed=rows * width * 6,
+    )
+
+
+def own_rows(where, positions, pieces, tables):
+    rows, width = pieces[0].shape
+    chips = len(pieces)
+    model_width = chips * width
+    half = model_width // 2
+
+    def kernel(where_ref, *refs):
+        out_ref = refs[-1]
+        at = pl.multiple_of(where_ref[0] * rows, rows)
+        for part in range(2):
+            out_ref[:, part * half : (part + 1) * half] = refs[chips + part][
+                pl.ds(at, rows), :
+            ].astype(jnp.float32)
+        for k in range(chips):
+            start = pl.multiple_of(where_ref[positions[k]] * width, width)
+            out_ref[:, pl.ds(start, width)] += refs[k][...].astype(jnp.float32)
+
+    return local_call(
+        kernel,
+        jax.ShapeDtypeStruct((rows, model_width), jnp.float32),
+        [where, *pieces, *tables],
+        flops=rows * model_width,
+        bytes_accessed=rows * model_width * 8,
+    )
+
+
+def final_sum(where, base, arrived):
+    rows, model_width = base.shape
+    half = model_width // 2
+
+    def kernel(where_ref, base_ref, *refs):
+        out_ref = refs[-1]
+        for part in range(2):
+            cols = slice(part * half, (part + 1) * half)
+            total = base_ref[:, cols]
+            for k in range(len(arrived[part])):
+                total = total + refs[k + part * len(arrived[0])][...].astype(jnp.float32)
+            out_ref[:, cols] = total.astype(jnp.bfloat16)
+
+    return local_call(
+        kernel,
+        jax.ShapeDtypeStruct((rows, model_width), jnp.bfloat16),
+        [where, base, *arrived[0], *arrived[1]],
+        flops=rows * model_width * 3,
+        bytes_accessed=rows * model_width * 10,
+    )
+
+
+def dense_body(residual, attn_out, norm_gain, expert_routes, route_gain, w_gate, w_up, w_down):
+    devices = lax.axis_size("ep")
+    experts = devices // FSPLIT
+    chips = devices // 2
+    far = chips // 2
+    tok_here = expert_routes.shape[0]
+    feat_here = residual.shape[1]
+    model_width = w_gate.shape[0]
+    width = 2 * feat_here
+    ring = ring_order(chips)
+    me = lax.axis_index("ep")
+    core = me % 2
+    seen = [
+        [ring[(ring.index(i // 2) + d) % chips] for d in range(chips)] + [i // FSPLIT, i % 2]
+        for i in range(devices)
+    ]
+    where = lax.dynamic_index_in_dim(jnp.asarray(seen, jnp.int32), me, 0, keepdims=False)
+
+    stream_feat = (residual.astype(jnp.float32) + attn_out.astype(jnp.float32)).astype(jnp.bfloat16)
+    by_core = stream_feat.reshape(chips, 2, tok_here, feat_here)
+    swapped = swap_cores(lax.dynamic_index_in_dim(by_core, 1 - core, 1, keepdims=False))
+
+    swapped, w_gate, w_up, w_down = lax.optimization_barrier((swapped, w_gate, w_up, w_down))
+    tables = [pair_gather(w_gate), pair_gather(w_up)]
+    down = pair_gather(w_down)
+    blocks = {0: first_blocks(where, by_core, swapped, expert_routes, route_gain, experts)}
+
+    for distance in range(1, far):
+        for sign in (-1, 1):
+            blocks[sign * distance] = [
+                ring_shift(part, ring, -sign) for part in blocks[sign * (distance - 1)]
+            ]
+    groups = [[0]] + [[d, chips - d] for d in range(1, far)] + [[far]]
+    gain_rows = norm_gain.reshape(chips, 1, width)
+    carried, owns, positions, headers = None, [], [], None
+    for group in groups:
+        if group == [far]:
+            headers = [blocks[d if d <= far else d - chips][0] for d in range(chips)]
+        parts = [blocks[d if d <= far else d - chips] for d in group]
+        made, carried = accumulate(
+            where,
+            group,
+            parts,
+            gain_rows,
+            tables,
+            carried,
+            headers,
+            down if group == groups[-2] else None,
+        )
+        owns.extend(made)
+        positions.extend(group)
+        if group == groups[max(far - 3, 0)]:
+            lower, upper, *carried = lax.optimization_barrier(
+                (blocks[1 - far][0], blocks[far - 1][1], *carried)
+            )
+            blocks[far] = [ring_shift(lower, ring, 1), ring_shift(upper, ring, -1)]
+        if group == groups[-2]:
+            down = carried[-1]
+
+    leading = [(far, 0), (far, 1), (far - 1, 1), (chips - far + 1, 0)]
+    hidden, lower, upper, after, before = leading_rows(where, leading, carried[0], down, chips)
+    moving = {1: [ring_shift(lower, ring, 1), None], -1: [None, ring_shift(upper, ring, -1)]}
+    second = {1: ring_shift(after, ring, 1), -1: ring_shift(before, ring, -1)}
+    everything = [contribution(where, hidden, down, part) for part in range(2)]
+    base = own_rows(where, positions, owns, everything)
+    for distance in range(far - 1, 0, -1):
+        for sign, order in ((1, (1, 0)), (-1, (0, 1))):
+            position = (sign * distance) % chips
+            sent = [None, None]
+            for part in order:
+                if moving[sign][part] is None:
+                    sent[part] = second[sign]
+                else:
+                    value = add_rows(where, position, everything[part], moving[sign][part])
+                    sent[part] = ring_shift(value, ring, sign)
+            moving[sign] = sent
+    arrived = [
+        [moving[sign][part] for sign in (1, -1) if moving[sign][part] is not None]
+        for part in range(2)
+    ]
+    return final_sum(where, base, arrived)
+
+
+def body(residual, attn_out, norm_gain, expert_routes, route_gain, w_gate, w_up, w_down):
+    tok_here, route_slots = expert_routes.shape
+    devices = lax.axis_size("ep")
+    capacity = route_slots * tok_here // (devices // FSPLIT)
+    dense = capacity >= tok_here and devices % 8 == 0
+    chosen = dense_body if dense else routed_body
+    return chosen(residual, attn_out, norm_gain, expert_routes, route_gain, w_gate, w_up, w_down)
+
+
 def solution(mesh):
     in_specs = (
         P("groups", "ep"),

time: 733 us -> 186 us (0.25)
  the two profiles are of different devices: /device:TPU:15 before, /device:TPU:0 now
where the time goes in v5:
time: 186 us
  waiting for transfers between devices  86 us (46%)
  Pallas kernels  43.3 us (23%)
  starting transfers between devices  30.2 us (16%)
  between operations  13.5 us (7%)
  local copies, waits for them, and re-layouts  11 us (6%)
    ppermute x28, waiting for transfers between devices, ring_shift(): return lax.ppermute(value, 'ep', pairs)  83.1 us
    pallas_call x21, Pallas kernels, local_call(): pl.pallas_call(kernel, out_shape=out_shape, in_specs=[IN_SMEM if k == 0 e...  43.3 us
    ppermute x28, starting transfers between devices, ring_shift(): return lax.ppermute(value, 'ep', pairs)  29.6 us
    unnamed x54, local copies, waits for them, and re-layouts  9.76 us
  transfers between devices with their start and end apart: 32, of which 16 were waited for; matrix products, arithmetic and copies ran while one was open for 0% of the time, Pallas kernels for 18%

profile of v5, /device:TPU:0, one launch (start us, length us, event | category | flops | bytes accessed | tf_op | source)
XLA Modules:
  0.0 185.7 jit_solution(17437303103864593874)
XLA Ops:
  6.5 1.8 add_convert_fusion
  9.5 1.5 collective-permute-done.swapped_ref
  11.1 0.7 all-gather.6.cloned.1.call-update
  11.9 0.7 all-gather.8.cloned.1.call-update
  12.7 0.7 dynamic-slice_bitcast_fusion.1.where_ref
  13.4 0.8 shard_map.91
  14.2 3.0 %collective-permute-start.3 = (bf16[272,896]{1,0:T(8,128)(2,1)S(1)}, bf16[272,896]{1,0:T(8,128)(2,1)S(1)}, u32[]{:S(2)}, u32[]{:S(2)}) collective-permute-start(bf16[272,896]{1,0:T(8,128)(2,1)S(1)} %get-tuple-element.39.refs_0_.refs_7_), channel_id=1, source_target_pairs={{0,4},{1,5},{4,8},{5,9},{8,12},{9,13},{12,14},{13,15},{14,10},{15,... | collective-permute-start | bytes 1462280 | tf_op jit(solution)/shard_map/ppermute | solution.py:100
  17.2 2.0 %collective-permute-start.2 = (bf16[256,896]{1,0:T(8,128)(2,1)S(1)}, bf16[256,896]{1,0:T(8,128)(2,1)S(1)}, u32[]{:S(2)}, u32[]{:S(2)}) collective-permute-start(bf16[256,896]{1,0:T(8,128)(2,1)S(1)} %get-tuple-element.40.refs_1_), channel_id=1, source_target_pairs={{0,2},{1,3},{4,0},{5,1},{8,4},{9,5},{12,8},{13,9},{14,12},{15,13},... | collective-permute-start | bytes 1376264 | tf_op jit(solution)/shard_map/ppermute | solution.py:100
  19.3 0.8 copy-done.9
  20.1 9.0 %collective-permute-done.3.refs_2_.refs_14_ = bf16[272,896]{1,0:T(8,128)(2,1)S(1)} collective-permute-done((bf16[272,896]{1,0:T(8,128)(2,1)S(1)}, bf16[272,896]{1,0:T(8,128)(2,1)S(1)}, u32[]{:S(2)}, u32[]{:S(2)}) %collective-permute-start.3) | collective-permute-done | bytes 487456 | tf_op jit(solution)/shard_map/ppermute | solution.py:100
  29.1 2.1 %collective-permute-start.7 = (bf16[272,896]{1,0:T(8,128)(2,1)S(1)}, bf16[272,896]{1,0:T(8,128)(2,1)}, u32[]{:S(2)}, u32[]{:S(2)}) collective-permute-start(bf16[272,896]{1,0:T(8,128)(2,1)S(1)} %collective-permute-done.3.refs_2_.refs_14_), channel_id=1, source_target_pairs={{0,4},{1,5},{4,8},{5,9},{8,12},{9,13},{12,14},{13,15},{14,10},{15,... | collective-permute-start | bytes 1462280 | tf_op jit(solution)/shard_map/ppermute | solution.py:100
  31.2 0.8 copy-done.3
  32.0 0.8 copy-done.6
  32.8 8.3 %collective-permute-done.2.refs_1_ = bf16[256,896]{1,0:T(8,128)(2,1)S(1)} collective-permute-done((bf16[256,896]{1,0:T(8,128)(2,1)S(1)}, bf16[256,896]{1,0:T(8,128)(2,1)S(1)}, u32[]{:S(2)}, u32[]{:S(2)}) %collective-permute-start.2) | collective-permute-done | bytes 458784 | tf_op jit(solution)/shard_map/ppermute | solution.py:100
  41.1 0.8 copy-done.20
  41.9 2.0 %collective-permute-start.8 = (bf16[256,896]{1,0:T(8,128)(2,1)S(1)}, bf16[256,896]{1,0:T(8,128)(2,1)}, u32[]{:S(2)}, u32[]{:S(2)}) collective-permute-start(bf16[256,896]{1,0:T(8,128)(2,1)S(1)} %collective-permute-done.4.refs_3_), channel_id=1, source_target_pairs={{0,4},{1,5},{4,8},{5,9},{8,12},{9,13},{12,14},{13,15},{14,10},{15,... | collective-permute-start | bytes 1376264 | tf_op jit(solution)/shard_map/ppermute | solution.py:100
  43.9 0.8 copy-done.22
  44.7 15.7 %collective-permute-done.6.refs_1_ = bf16[256,896]{1,0:T(8,128)(2,1)} collective-permute-done((bf16[256,896]{1,0:T(8,128)(2,1)S(1)}, bf16[256,896]{1,0:T(8,128)(2,1)}, u32[]{:S(2)}, u32[]{:S(2)}) %collective-permute-start.6) | collective-permute-done | bytes 458784 | tf_op jit(solution)/shard_map/ppermute | solution.py:100
  60.6 1.7 collective-permute-start.12
  62.4 1.6 collective-permute-start.9
  64.4 1.1 copy-done.10
  65.5 3.8 %shard_map.92 = (bf16[64,896]{1,0:T(8,128)(2,1)S(1)}, f32[512,1024]{1,0:T(8,128)S(1)}, f32[512,128]{1,0:T(8,128)S(1)}, s32[1]{0:T(128)}) custom-call(s32[10]{0:T(128)S(1)} %dynamic-slice_bitcast_fusion.1.where_ref, bf16[272,896]{1,0:T(8,128)(2,1)S(1)} %get-tuple-element.39.refs_0_.refs_7_, bf16[256,896]{1,0:T(8,128)(2,1)S(1)} %copy-done.10, ...), custom_call_target="tpu_custom_call" | custom-call | flops 2818572288 | bytes 6946816 | tf_op jit(solution)/shard_map/pallas_call | solution.py:113
  69.4 4.6 %shard_map.93 = (bf16[64,896]{1,0:T(8,128)(2,1)S(1)}, bf16[64,896]{1,0:T(8,128)(2,1)S(1)}, f32[512,1024]{1,0:T(8,128)S(1)}, f32[512,128]{1,0:T(8,128)S(1)}, s32[1]{0:T(128)}) custom-call(s32[10]{0:T(128)S(1)} %dynamic-slice_bitcast_fusion.1.where_ref, bf16[272,896]{1,0:T(8,128)(2,1)S(1)} %copy-done.7, ...), custom_call_target="tpu_custom_call", output_to_operand_aliasing={{2}: (8, {}), {3}: (9, {})} | custom-call | flops 5637144576 | bytes 9699328 | tf_op jit(solution)/shard_map/pallas_call | solution.py:113
  75.4 7.4 %collective-permute-done.9.refs_2_.refs_12_ = bf16[272,896]{1,0:T(8,128)(2,1)S(1)} collective-permute-done((bf16[272,896]{1,0:T(8,128)(2,1)}, bf16[272,896]{1,0:T(8,128)(2,1)S(1)}, u32[]{:S(2)}, u32[]{:S(2)}) %collective-permute-start.9) | collective-permute-done | bytes 487456 | tf_op jit(solution)/shard_map/ppermute | solution.py:100
  82.7 0.8 copy-done
  83.6 1.4 collective-permute-start.13
  85.6 5.6 %shard_map.94 = (bf16[64,896]{1,0:T(8,128)(2,1)S(1)}, bf16[64,896]{1,0:T(8,128)(2,1)S(1)}, f32[512,1024]{1,0:T(8,128)S(1)}, f32[512,128]{1,0:T(8,128)S(1)}, s32[1]{0:T(128)}) custom-call(s32[10]{0:T(128)S(1)} %dynamic-slice_bitcast_fusion.1.where_ref, ...), custom_call_target="tpu_custom_call", output_to_operand_aliasing={{2}: (8, {}), {3}: (9, {})} | custom-call | flops 5637144576 | bytes 9699328 | tf_op jit(solution)/shard_map/pallas_call | solution.py:113
  92.5 1.0 copy-done.1
  93.5 6.2 %shard_map.95 = (bf16[64,896]{1,0:T(8,128)(2,1)S(1)}, bf16[64,896]{1,0:T(8,128)(2,1)S(1)}, f32[512,1024]{1,0:T(8,128)S(1)}, f32[512,128]{1,0:T(8,128)S(1)}, s32[1]{0:T(128)}, /*index=5*/bf16[512,7168]{1,0:T(8,128)(2,1)S(1)}) custom-call(s32[10]{0:T(128)S(1)} %dynamic-slice_bitcast_fusion.1.where_ref, ...), custom_call_target="tpu_custom_call", output_to_operand_aliasing={{2}: (8, {}), {3}: (9, {})} | custom-call | flops 5637144576 | bytes 9699328 | tf_op jit(solution)/shard_map/pallas_call | solution.py:113
  99.8 4.4 %shard_map.96 = (bf16[64,896]{1,0:T(8,128)(2,1)S(1)}, bf16[512,512]{1,0:T(8,128)(2,1)S(1)}) custom-call(s32[10]{0:T(128)S(1)} %dynamic-slice_bitcast_fusion.1.where_ref, bf16[272,896]{1,0:T(8,128)(2,1)S(1)} %collective-permute-done.13.refs_0_.refs_11_, bf16[256,896]{1,0:T(8,128)(2,1)} %collective-permute-done.14.refs_1_, f32[8,1,896]{2,1,0:T(1,128)S(1)} %bitcast.12, ...), custom_call_target="tpu_custom_call" | custom-call | flops 2818572288 | bytes 6946816 | tf_op jit(solution)/shard_map/pallas_call | solution.py:113
  104.3 3.2 %shard_map.97 = (bf16[512,512]{1,0:T(8,128)(2,1)S(1)}, bf16[64,3584]{1,0:T(8,128)(2,1)S(1)}, bf16[64,3584]{1,0:T(8,128)(2,1)S(1)}, bf16[64,3584]{1,0:T(8,128)(2,1)S(1)}, bf16[64,3584]{1,0:T(8,128)(2,1)S(1)}) custom-call(s32[10]{0:T(128)S(1)} %dynamic-slice_bitcast_fusion.1.where_ref, bf16[512,512]{1,0:T(8,128)(2,1)S(1)} %get-tuple-element.64.hidden_ref, ...), custom_call_target="tpu_custom_call" | custom-call | flops 939524096 | bytes 7340032 | tf_op jit(solution)/shard_map/pallas_call | solution.py:113
  107.5 1.5 collective-permute-start.15
  109.6 1.4 collective-permute-start.19
  110.9 2.6 %shard_map.98.refs_8_.table_ref = bf16[512,3584]{1,0:T(8,128)(2,1)S(1)} custom-call(s32[10]{0:T(128)S(1)} %dynamic-slice_bitcast_fusion.1.where_ref, bf16[512,512]{1,0:T(8,128)(2,1)S(1)} %get-tuple-element.66.hidden_ref, bf16[512,7168]{1,0:T(8,128)(2,1)S(1)} %get-tuple-element.65.down_ref), custom_call_target="tpu_custom_call" | custom-call | flops 1879048192 | bytes 7340032 | tf_op jit(solution)/shard_map/pallas_call | solution.py:113
  113.5 2.6 %shard_map.99.refs_9_.table_ref = bf16[512,3584]{1,0:T(8,128)(2,1)S(1)} custom-call(s32[10]{0:T(128)S(1)} %dynamic-slice_bitcast_fusion.1.where_ref, bf16[512,512]{1,0:T(8,128)(2,1)S(1)} %get-tuple-element.66.hidden_ref, bf16[512,7168]{1,0:T(8,128)(2,1)S(1)} %get-tuple-element.65.down_ref), custom_call_target="tpu_custom_call" | custom-call | flops 1879048192 | bytes 7340032 | tf_op jit(solution)/shard_map/pallas_call | solution.py:113
  116.2 0.7 collective-permute-start.22
  116.9 3.0 %collective-permute-done.15.moved_ref = bf16[64,3584]{1,0:T(8,128)(2,1)S(1)} collective-permute-done((bf16[64,3584]{1,0:T(8,128)(2,1)S(1)}, bf16[64,3584]{1,0:T(8,128)(2,1)S(1)}, u32[]{:S(2)}, u32[]{:S(2)}) %collective-permute-start.15) | collective-permute-done | bytes 458784 | tf_op jit(solution)/shard_map/ppermute | solution.py:100
  119.8 0.7 shard_map.101
  120.5 1.3 collective-permute-start.16
  122.4 0.7 shard_map.108
  123.1 0.7 collective-permute-start.26
  123.7 8.5 %collective-permute-done.19.moved_ref = bf16[64,3584]{1,0:T(8,128)(2,1)S(1)} collective-permute-done((bf16[64,3584]{1,0:T(8,128)(2,1)S(1)}, bf16[64,3584]{1,0:T(8,128)(2,1)S(1)}, u32[]{:S(2)}, u32[]{:S(2)}) %collective-permute-start.19) | collective-permute-done | bytes 458784 | tf_op jit(solution)/shard_map/ppermute | solution.py:100
  132.2 0.7 shard_map.104
  133.6 0.7 shard_map.106
  134.3 1.5 collective-permute-start.23
  135.7 3.8 %collective-permute-done.16.moved_ref = bf16[64,3584]{1,0:T(8,128)(2,1)S(1)} collective-permute-done((bf16[64,3584]{1,0:T(8,128)(2,1)S(1)}, bf16[64,3584]{1,0:T(8,128)(2,1)S(1)}, u32[]{:S(2)}, u32[]{:S(2)}) %collective-permute-start.16) | collective-permute-done | bytes 458784 | tf_op jit(solution)/shard_map/ppermute | solution.py:100
  139.5 0.7 shard_map.102
  140.2 1.3 collective-permute-start.17
  142.1 0.7 shard_map.109
  142.7 0.7 collective-permute-start.27
  143.4 8.5 %collective-permute-done.20.moved_ref = bf16[64,3584]{1,0:T(8,128)(2,1)S(1)} collective-permute-done((bf16[64,3584]{1,0:T(8,128)(2,1)S(1)}, bf16[64,3584]{1,0:T(8,128)(2,1)S(1)}, u32[]{:S(2)}, u32[]{:S(2)}) %collective-permute-start.20) | collective-permute-done | bytes 458784 | tf_op jit(solution)/shard_map/ppermute | solution.py:100
  151.9 0.7 shard_map.105
  152.6 0.7 collective-permute-start.21
  153.2 0.7 shard_map.107
  154.0 1.5 collective-permute-start.24
  155.4 3.7 %collective-permute-done.17.moved_ref = bf16[64,3584]{1,0:T(8,128)(2,1)S(1)} collective-permute-done((bf16[64,3584]{1,0:T(8,128)(2,1)S(1)}, bf16[64,3584]{1,0:T(8,128)(2,1)S(1)}, u32[]{:S(2)}, u32[]{:S(2)}) %collective-permute-start.17) | collective-permute-done | bytes 458784 | tf_op jit(solution)/shard_map/ppermute | solution.py:100
  159.2 0.7 shard_map.103
  159.8 1.3 collective-permute-start.18
  161.7 0.7 shard_map.110
  163.1 0.8 shard_map.100.base_ref
  163.9 7.6 %collective-permute-done.21.refs_1_ = bf16[64,3584]{1,0:T(8,128)(2,1)S(1)} collective-permute-done((bf16[64,3584]{1,0:T(8,128)(2,1)S(1)}, bf16[64,3584]{1,0:T(8,128)(2,1)S(1)}, u32[]{:S(2)}, u32[]{:S(2)}) %collective-permute-start.21) | collective-permute-done | bytes 458784 | tf_op jit(solution)/shard_map/ppermute | solution.py:100
  171.6 5.0 %collective-permute-done.18.refs_0_ = bf16[64,3584]{1,0:T(8,128)(2,1)S(1)} collective-permute-done((bf16[64,3584]{1,0:T(8,128)(2,1)S(1)}, bf16[64,3584]{1,0:T(8,128)(2,1)S(1)}, u32[]{:S(2)}, u32[]{:S(2)}) %collective-permute-start.18) | collective-permute-done | bytes 458784 | tf_op jit(solution)/shard_map/ppermute | solution.py:100
  176.6 0.8 collective-permute-done.28.refs_3_
  177.4 1.8 shard_map.111
  (82 shorter events, 9.3 us)
Async XLA Ops:
  6.5 57.9 %all-gather.4.cloned.1.call-start = ((), (), s32[]{:S(2)}) async-start(), calls=%async_computation | async-start | bytes 11010048 | tf_op jit(solution)/shard_map/all_gather | solution.py:89
  8.9 2.1 %collective-permute-start = (bf16[8,64,448]{2,1,0:T(8,128)(2,1)S(1)}, bf16[8,64,448]{2,1,0:T(8,128)(2,1)S(1)}, u32[]{:S(2)}, u32[]{:S(2)}) collective-permute-start(bf16[8,64,448]{2,1,0:T(8,128)(2,1)S(1)} %dynamic-slice_bitcast_fusion), channel_id=1, source_target_pairs={{0,1},{1,0},{2,3},{3,2},{4,5},{5,4},{6,7},{7,6},{8,9},{9,8},{10,11... | collective-permute-start | bytes 1376264 | tf_op jit(solution)/shard_map/ppermute | solution.py:84
  11.0 1.5 copy-start.24
  11.0 1.6 copy-start.25
  11.0 53.4 %copy-start.11 = (f32[7168]{0:T(1024)S(1)}, f32[7168]{0:T(1024)}, u32[]{:S(2)}) copy-start(f32[7168]{0:T(1024)} %param.11) | copy-start | bytes 86020
  11.1 53.4 %all-gather.6.cloned.1.call-start = ((), (), s32[]{:S(2)}) async-start(), calls=%async_computation.1 | async-start | bytes 11010048 | tf_op jit(solution)/shard_map/all_gather | solution.py:89
  11.8 80.7 %all-gather.8.cloned.1.call-start = ((), (), s32[]{:S(2)}) async-start(), calls=%async_computation.2 | async-start | bytes 11010048 | tf_op jit(solution)/shard_map/all_gather | solution.py:89
  14.2 14.9 %collective-permute-start.3 = (bf16[272,896]{1,0:T(8,128)(2,1)S(1)}, bf16[272,896]{1,0:T(8,128)(2,1)S(1)}, u32[]{:S(2)}, u32[]{:S(2)}) collective-permute-start(bf16[272,896]{1,0:T(8,128)(2,1)S(1)} %get-tuple-element.39.refs_0_.refs_7_), channel_id=1, source_target_pairs={{0,4},{1,5},{4,8},{5,9},{8,12},{9,13},{12,14},{13,15},{14,10},{15,... | collective-permute-start | bytes 1462280 | tf_op jit(solution)/shard_map/ppermute | solution.py:100
  17.2 14.8 %collective-permute-start.1 = (bf16[272,896]{1,0:T(8,128)(2,1)S(1)}, bf16[272,896]{1,0:T(8,128)(2,1)S(1)}, u32[]{:S(2)}, u32[]{:S(2)}) collective-permute-start(bf16[272,896]{1,0:T(8,128)(2,1)S(1)} %get-tuple-element.39.refs_0_.refs_7_), channel_id=1, source_target_pairs={{0,2},{1,3},{4,0},{5,1},{8,4},{9,5},{12,8},{13,9},{14,12},{15,13},... | collective-permute-start | bytes 1462280 | tf_op jit(solution)/shard_map/ppermute | solution.py:100
  17.2 23.8 %collective-permute-start.2 = (bf16[256,896]{1,0:T(8,128)(2,1)S(1)}, bf16[256,896]{1,0:T(8,128)(2,1)S(1)}, u32[]{:S(2)}, u32[]{:S(2)}) collective-permute-start(bf16[256,896]{1,0:T(8,128)(2,1)S(1)} %get-tuple-element.40.refs_1_), channel_id=1, source_target_pairs={{0,2},{1,3},{4,0},{5,1},{8,4},{9,5},{12,8},{13,9},{14,12},{15,13},... | collective-permute-start | bytes 1376264 | tf_op jit(solution)/shard_map/ppermute | solution.py:100
  19.2 22.7 %collective-permute-start.4 = (bf16[256,896]{1,0:T(8,128)(2,1)S(1)}, bf16[256,896]{1,0:T(8,128)(2,1)S(1)}, u32[]{:S(2)}, u32[]{:S(2)}) collective-permute-start(bf16[256,896]{1,0:T(8,128)(2,1)S(1)} %get-tuple-element.40.refs_1_), channel_id=1, source_target_pairs={{0,4},{1,5},{4,8},{5,9},{8,12},{9,13},{12,14},{13,15},{14,10},{15,... | collective-permute-start | bytes 1376264 | tf_op jit(solution)/shard_map/ppermute | solution.py:100
  19.3 0.8 copy-start.9
  29.1 33.3 %collective-permute-start.7 = (bf16[272,896]{1,0:T(8,128)(2,1)S(1)}, bf16[272,896]{1,0:T(8,128)(2,1)}, u32[]{:S(2)}, u32[]{:S(2)}) collective-permute-start(bf16[272,896]{1,0:T(8,128)(2,1)S(1)} %collective-permute-done.3.refs_2_.refs_14_), channel_id=1, source_target_pairs={{0,4},{1,5},{4,8},{5,9},{8,12},{9,13},{12,14},{13,15},{14,10},{15,... | collective-permute-start | bytes 1462280 | tf_op jit(solution)/shard_map/ppermute | solution.py:100
  31.2 0.8 copy-start.3
  32.0 32.0 %collective-permute-start.5 = (bf16[272,896]{1,0:T(8,128)(2,1)S(1)}, bf16[272,896]{1,0:T(8,128)(2,1)}, u32[]{:S(2)}, u32[]{:S(2)}) collective-permute-start(bf16[272,896]{1,0:T(8,128)(2,1)S(1)} %collective-permute-done.1.refs_0_.refs_8_), channel_id=1, source_target_pairs={{0,2},{1,3},{4,0},{5,1},{8,4},{9,5},{12,8},{13,9},{14,12},{15,13},... | collective-permute-start | bytes 1462280 | tf_op jit(solution)/shard_map/ppermute | solution.py:100
  32.0 0.8 copy-start.6
  41.1 19.3 %collective-permute-start.6 = (bf16[256,896]{1,0:T(8,128)(2,1)S(1)}, bf16[256,896]{1,0:T(8,128)(2,1)}, u32[]{:S(2)}, u32[]{:S(2)}) collective-permute-start(bf16[256,896]{1,0:T(8,128)(2,1)S(1)} %collective-permute-done.2.refs_1_), channel_id=1, source_target_pairs={{0,2},{1,3},{4,0},{5,1},{8,4},{9,5},{12,8},{13,9},{14,12},{15,13},... | collective-permute-start | bytes 1376264 | tf_op jit(solution)/shard_map/ppermute | solution.py:100
  41.1 0.8 copy-start.20
  41.9 18.7 %collective-permute-start.8 = (bf16[256,896]{1,0:T(8,128)(2,1)S(1)}, bf16[256,896]{1,0:T(8,128)(2,1)}, u32[]{:S(2)}, u32[]{:S(2)}) collective-permute-start(bf16[256,896]{1,0:T(8,128)(2,1)S(1)} %collective-permute-done.4.refs_3_), channel_id=1, source_target_pairs={{0,4},{1,5},{4,8},{5,9},{8,12},{9,13},{12,14},{13,15},{14,10},{15,... | collective-permute-start | bytes 1376264 | tf_op jit(solution)/shard_map/ppermute | solution.py:100
  43.9 0.8 copy-start.22
  60.3 15.0 %collective-permute-start.10 = (bf16[256,896]{1,0:T(8,128)(2,1)}, bf16[256,896]{1,0:T(8,128)(2,1)}, u32[]{:S(2)}, u32[]{:S(2)}) collective-permute-start(bf16[256,896]{1,0:T(8,128)(2,1)} %collective-permute-done.6.refs_1_), channel_id=1, source_target_pairs={{0,2},{1,3},{4,0},{5,1},{8,4},{9,5},{12,8},{13,9},{14,12},{15,13},... | collective-permute-start | bytes 1376264 | tf_op jit(solution)/shard_map/ppermute | solution.py:100
  60.6 31.9 %collective-permute-start.12 = (bf16[256,896]{1,0:T(8,128)(2,1)}, bf16[256,896]{1,0:T(8,128)(2,1)}, u32[]{:S(2)}, u32[]{:S(2)}) collective-permute-start(bf16[256,896]{1,0:T(8,128)(2,1)} %collective-permute-done.8.refs_3_), channel_id=1, source_target_pairs={{0,4},{1,5},{4,8},{5,9},{8,12},{9,13},{12,14},{13,15},{14,10},{15,... | collective-permute-start | bytes 1376264 | tf_op jit(solution)/shard_map/ppermute | solution.py:100
  62.4 20.4 %collective-permute-start.9 = (bf16[272,896]{1,0:T(8,128)(2,1)}, bf16[272,896]{1,0:T(8,128)(2,1)S(1)}, u32[]{:S(2)}, u32[]{:S(2)}) collective-permute-start(bf16[272,896]{1,0:T(8,128)(2,1)} %collective-permute-done.7.refs_2_.refs_13_), channel_id=1, source_target_pairs={{0,4},{1,5},{4,8},{5,9},{8,12},{9,13},{12,14},{13,15},{14,10},{15,... | collective-permute-start | bytes 1462280 | tf_op jit(solution)/shard_map/ppermute | solution.py:100
  64.0 28.5 %collective-permute-start.11 = (bf16[272,896]{1,0:T(8,128)(2,1)}, bf16[272,896]{1,0:T(8,128)(2,1)}, u32[]{:S(2)}, u32[]{:S(2)}) collective-permute-start(bf16[272,896]{1,0:T(8,128)(2,1)} %collective-permute-done.5.refs_0_.refs_9_), channel_id=1, source_target_pairs={{0,2},{1,3},{4,0},{5,1},{8,4},{9,5},{12,8},{13,9},{14,12},{15,13},... | collective-permute-start | bytes 1462280 | tf_op jit(solution)/shard_map/ppermute | solution.py:100
  64.4 1.1 copy-start.10
  65.5 3.9 %copy-start.4 = (bf16[272,896]{1,0:T(8,128)(2,1)S(1)}, bf16[272,896]{1,0:T(8,128)(2,1)}, u32[]{:S(2)}) copy-start(bf16[272,896]{1,0:T(8,128)(2,1)} %copy-done.3) | copy-start | bytes 1462276
  65.5 3.9 %copy-start.7 = (bf16[272,896]{1,0:T(8,128)(2,1)S(1)}, bf16[272,896]{1,0:T(8,128)(2,1)}, u32[]{:S(2)}) copy-start(bf16[272,896]{1,0:T(8,128)(2,1)} %copy-done.6) | copy-start | bytes 1462276
  65.5 3.9 %copy-start.21 = (bf16[256,896]{1,0:T(8,128)(2,1)S(1)}, bf16[256,896]{1,0:T(8,128)(2,1)}, u32[]{:S(2)}) copy-start(bf16[256,896]{1,0:T(8,128)(2,1)} %copy-done.20) | copy-start | bytes 1376260
  65.5 3.9 %copy-start.23 = (bf16[256,896]{1,0:T(8,128)(2,1)S(1)}, bf16[256,896]{1,0:T(8,128)(2,1)}, u32[]{:S(2)}) copy-start(bf16[256,896]{1,0:T(8,128)(2,1)} %copy-done.22) | copy-start | bytes 1376260
  74.1 0.6 copy-start.12
  74.7 0.6 copy-start.14
  82.7 0.9 copy-start
  83.6 16.2 %collective-permute-start.13 = (bf16[272,896]{1,0:T(8,128)(2,1)}, bf16[272,896]{1,0:T(8,128)(2,1)S(1)}, u32[]{:S(2)}, u32[]{:S(2)}) collective-permute-start(bf16[272,896]{1,0:T(8,128)(2,1)} %copy-done), channel_id=1, source_target_pairs={{0,4},{1,5},{4,8},{5,9},{8,12},{9,13},{12,14},{13,15},{14,10},{15,... | collective-permute-start | bytes 1462280 | tf_op jit(solution)/shard_map/ppermute | solution.py:100
  85.0 14.8 %collective-permute-start.14 = (bf16[256,896]{1,0:T(8,128)(2,1)}, bf16[256,896]{1,0:T(8,128)(2,1)}, u32[]{:S(2)}, u32[]{:S(2)}) collective-permute-start(bf16[256,896]{1,0:T(8,128)(2,1)} %collective-permute-done.10.refs_1_), channel_id=1, source_target_pairs={{0,2},{1,3},{4,0},{5,1},{8,4},{9,5},{12,8},{13,9},{14,12},{15,13},... | collective-permute-start | bytes 1376264 | tf_op jit(solution)/shard_map/ppermute | solution.py:100
  91.2 0.6 copy-start.16
  91.8 0.7 copy-start.18
  92.5 1.0 copy-start.1
  93.5 6.3 %copy-start.2 = (bf16[272,896]{1,0:T(8,128)(2,1)S(1)}, bf16[272,896]{1,0:T(8,128)(2,1)}, u32[]{:S(2)}) copy-start(bf16[272,896]{1,0:T(8,128)(2,1)} %copy-done) | copy-start | bytes 1462276
  93.5 6.3 %copy-start.5 = (bf16[272,896]{1,0:T(8,128)(2,1)S(1)}, bf16[272,896]{1,0:T(8,128)(2,1)}, u32[]{:S(2)}) copy-start(bf16[272,896]{1,0:T(8,128)(2,1)} %copy-done.3) | copy-start | bytes 1462276
  93.5 6.3 %copy-start.8 = (bf16[272,896]{1,0:T(8,128)(2,1)S(1)}, bf16[272,896]{1,0:T(8,128)(2,1)}, u32[]{:S(2)}) copy-start(bf16[272,896]{1,0:T(8,128)(2,1)} %copy-done.6) | copy-start | bytes 1462276
  107.5 12.3 %collective-permute-start.15 = (bf16[64,3584]{1,0:T(8,128)(2,1)S(1)}, bf16[64,3584]{1,0:T(8,128)(2,1)S(1)}, u32[]{:S(2)}, u32[]{:S(2)}) collective-permute-start(bf16[64,3584]{1,0:T(8,128)(2,1)S(1)} %get-tuple-element.67), channel_id=1, source_target_pairs={{0,4},{1,5},{4,8},{5,9},{8,12},{9,13},{12,14},{13,15},{14,10},{15,... | collective-permute-start | bytes 1376264 | tf_op jit(solution)/shard_map/ppermute | solution.py:100
  109.0 13.5 %collective-permute-start.25 = (bf16[64,3584]{1,0:T(8,128)(2,1)S(1)}, bf16[64,3584]{1,0:T(8,128)(2,1)S(1)}, u32[]{:S(2)}, u32[]{:S(2)}) collective-permute-start(bf16[64,3584]{1,0:T(8,128)(2,1)S(1)} %get-tuple-element.70), channel_id=1, source_target_pairs={{0,2},{1,3},{4,0},{5,1},{8,4},{9,5},{12,8},{13,9},{14,12},{15,13},... | collective-permute-start | bytes 1376264 | tf_op jit(solution)/shard_map/ppermute | solution.py:100
  109.6 22.7 %collective-permute-start.19 = (bf16[64,3584]{1,0:T(8,128)(2,1)S(1)}, bf16[64,3584]{1,0:T(8,128)(2,1)S(1)}, u32[]{:S(2)}, u32[]{:S(2)}) collective-permute-start(bf16[64,3584]{1,0:T(8,128)(2,1)S(1)} %get-tuple-element.68), channel_id=1, source_target_pairs={{0,2},{1,3},{4,0},{5,1},{8,4},{9,5},{12,8},{13,9},{14,12},{15,13},... | collective-permute-start | bytes 1376264 | tf_op jit(solution)/shard_map/ppermute | solution.py:100
  116.2 17.4 %collective-permute-start.22 = (bf16[64,3584]{1,0:T(8,128)(2,1)S(1)}, bf16[64,3584]{1,0:T(8,128)(2,1)S(1)}, u32[]{:S(2)}, u32[]{:S(2)}) collective-permute-start(bf16[64,3584]{1,0:T(8,128)(2,1)S(1)} %get-tuple-element.69), channel_id=1, source_target_pairs={{0,4},{1,5},{4,8},{5,9},{8,12},{9,13},{12,14},{13,15},{14,10},{15,... | collective-permute-start | bytes 1376264 | tf_op jit(solution)/shard_map/ppermute | solution.py:100
  120.5 19.0 %collective-permute-start.16 = (bf16[64,3584]{1,0:T(8,128)(2,1)S(1)}, bf16[64,3584]{1,0:T(8,128)(2,1)S(1)}, u32[]{:S(2)}, u32[]{:S(2)}) collective-permute-start(bf16[64,3584]{1,0:T(8,128)(2,1)S(1)} %shard_map.101), channel_id=1, source_target_pairs={{0,4},{1,5},{4,8},{5,9},{8,12},{9,13},{12,14},{13,15},{14,10},{15,... | collective-permute-start | bytes 1376264 | tf_op jit(solution)/shard_map/ppermute | solution.py:100
  123.1 19.0 %collective-permute-start.26 = (bf16[64,3584]{1,0:T(8,128)(2,1)S(1)}, bf16[64,3584]{1,0:T(8,128)(2,1)S(1)}, u32[]{:S(2)}, u32[]{:S(2)}) collective-permute-start(bf16[64,3584]{1,0:T(8,128)(2,1)S(1)} %shard_map.108), channel_id=1, source_target_pairs={{0,2},{1,3},{4,0},{5,1},{8,4},{9,5},{12,8},{13,9},{14,12},{15,13},... | collective-permute-start | bytes 1376264 | tf_op jit(solution)/shard_map/ppermute | solution.py:100
  132.9 19.0 %collective-permute-start.20 = (bf16[64,3584]{1,0:T(8,128)(2,1)S(1)}, bf16[64,3584]{1,0:T(8,128)(2,1)S(1)}, u32[]{:S(2)}, u32[]{:S(2)}) collective-permute-start(bf16[64,3584]{1,0:T(8,128)(2,1)S(1)} %shard_map.104), channel_id=1, source_target_pairs={{0,2},{1,3},{4,0},{5,1},{8,4},{9,5},{12,8},{13,9},{14,12},{15,13},... | collective-permute-start | bytes 1376264 | tf_op jit(solution)/shard_map/ppermute | solution.py:100
  134.3 19.0 %collective-permute-start.23 = (bf16[64,3584]{1,0:T(8,128)(2,1)S(1)}, bf16[64,3584]{1,0:T(8,128)(2,1)S(1)}, u32[]{:S(2)}, u32[]{:S(2)}) collective-permute-start(bf16[64,3584]{1,0:T(8,128)(2,1)S(1)} %shard_map.106), channel_id=1, source_target_pairs={{0,4},{1,5},{4,8},{5,9},{8,12},{9,13},{12,14},{13,15},{14,10},{15,... | collective-permute-start | bytes 1376264 | tf_op jit(solution)/shard_map/ppermute | solution.py:100
  140.2 19.0 %collective-permute-start.17 = (bf16[64,3584]{1,0:T(8,128)(2,1)S(1)}, bf16[64,3584]{1,0:T(8,128)(2,1)S(1)}, u32[]{:S(2)}, u32[]{:S(2)}) collective-permute-start(bf16[64,3584]{1,0:T(8,128)(2,1)S(1)} %shard_map.102), channel_id=1, source_target_pairs={{0,4},{1,5},{4,8},{5,9},{8,12},{9,13},{12,14},{13,15},{14,10},{15,... | collective-permute-start | bytes 1376264 | tf_op jit(solution)/shard_map/ppermute | solution.py:100
  142.7 19.0 %collective-permute-start.27 = (bf16[64,3584]{1,0:T(8,128)(2,1)S(1)}, bf16[64,3584]{1,0:T(8,128)(2,1)S(1)}, u32[]{:S(2)}, u32[]{:S(2)}) collective-permute-start(bf16[64,3584]{1,0:T(8,128)(2,1)S(1)} %shard_map.109), channel_id=1, source_target_pairs={{0,2},{1,3},{4,0},{5,1},{8,4},{9,5},{12,8},{13,9},{14,12},{15,13},... | collective-permute-start | bytes 1376264 | tf_op jit(solution)/shard_map/ppermute | solution.py:100
  152.6 19.0 %collective-permute-start.21 = (bf16[64,3584]{1,0:T(8,128)(2,1)S(1)}, bf16[64,3584]{1,0:T(8,128)(2,1)S(1)}, u32[]{:S(2)}, u32[]{:S(2)}) collective-permute-start(bf16[64,3584]{1,0:T(8,128)(2,1)S(1)} %shard_map.105), channel_id=1, source_target_pairs={{0,2},{1,3},{4,0},{5,1},{8,4},{9,5},{12,8},{13,9},{14,12},{15,13},... | collective-permute-start | bytes 1376264 | tf_op jit(solution)/shard_map/ppermute | solution.py:100
  153.9 9.2 %copy-start.13 = (bf16[64,896]{1,0:T(8,128)(2,1)S(1)}, bf16[64,896]{1,0:T(8,128)(2,1)}, u32[]{:S(2)}) copy-start(bf16[64,896]{1,0:T(8,128)(2,1)} %copy-done.12) | copy-start | bytes 344068
  153.9 9.1 %copy-start.15 = (bf16[64,896]{1,0:T(8,128)(2,1)S(1)}, bf16[64,896]{1,0:T(8,128)(2,1)}, u32[]{:S(2)}) copy-start(bf16[64,896]{1,0:T(8,128)(2,1)} %copy-done.14) | copy-start | bytes 344068
  153.9 9.1 %copy-start.17 = (bf16[64,896]{1,0:T(8,128)(2,1)S(1)}, bf16[64,896]{1,0:T(8,128)(2,1)}, u32[]{:S(2)}) copy-start(bf16[64,896]{1,0:T(8,128)(2,1)} %copy-done.16) | copy-start | bytes 344068
  153.9 9.1 %copy-start.19 = (bf16[64,896]{1,0:T(8,128)(2,1)S(1)}, bf16[64,896]{1,0:T(8,128)(2,1)}, u32[]{:S(2)}) copy-start(bf16[64,896]{1,0:T(8,128)(2,1)} %copy-done.18) | copy-start | bytes 344068
  154.0 17.6 %collective-permute-start.24 = (bf16[64,3584]{1,0:T(8,128)(2,1)S(1)}, bf16[64,3584]{1,0:T(8,128)(2,1)S(1)}, u32[]{:S(2)}, u32[]{:S(2)}) collective-permute-start(bf16[64,3584]{1,0:T(8,128)(2,1)S(1)} %shard_map.107), channel_id=1, source_target_pairs={{0,4},{1,5},{4,8},{5,9},{8,12},{9,13},{12,14},{13,15},{14,10},{15,... | collective-permute-start | bytes 1376264 | tf_op jit(solution)/shard_map/ppermute | solution.py:100
  159.8 16.8 %collective-permute-start.18 = (bf16[64,3584]{1,0:T(8,128)(2,1)S(1)}, bf16[64,3584]{1,0:T(8,128)(2,1)S(1)}, u32[]{:S(2)}, u32[]{:S(2)}) collective-permute-start(bf16[64,3584]{1,0:T(8,128)(2,1)S(1)} %shard_map.103), channel_id=1, source_target_pairs={{0,4},{1,5},{4,8},{5,9},{8,12},{9,13},{12,14},{13,15},{14,10},{15,... | collective-permute-start | bytes 1376264 | tf_op jit(solution)/shard_map/ppermute | solution.py:100
  162.4 15.0 %collective-permute-start.28 = (bf16[64,3584]{1,0:T(8,128)(2,1)S(1)}, bf16[64,3584]{1,0:T(8,128)(2,1)S(1)}, u32[]{:S(2)}, u32[]{:S(2)}) collective-permute-start(bf16[64,3584]{1,0:T(8,128)(2,1)S(1)} %shard_map.110), channel_id=1, source_target_pairs={{0,2},{1,3},{4,0},{5,1},{8,4},{9,5},{12,8},{13,9},{14,12},{15,13},... | collective-permute-start | bytes 1376264 | tf_op jit(solution)/shard_map/ppermute | solution.py:100
Sparse Core Ops, SparseCore 0:
  11.1 20.9 all-gather.3
  33.6 19.4 all-gather.5
  54.7 19.4 all-gather.7

commit v6 on v5

--- a/solution.py
+++ b/solution.py
@@ -84,12 +84,6 @@
     return lax.ppermute(value, "ep", [(i, i ^ 1) for i in range(lax.axis_size("ep"))])
 
 
-def pair_gather(value):
-    pairs = [[i, i + 1] for i in range(0, lax.axis_size("ep"), 2)]
-    both = lax.all_gather(value, "ep", axis_index_groups=pairs, axis=0, tiled=True)
-    return pltpu.with_memory_space_constraint(both, pltpu.HBM)
-
-
 def ring_shift(value, ring, step):
     chips = len(ring)
     pairs = [
@@ -101,7 +95,7 @@
 
 
 COST_SCALE = 3
-VMEM_BYTES = 32 * 1024 * 1024
+VMEM_BYTES = 20 * 1024 * 1024
 IN_VMEM = pl.BlockSpec(memory_space=pltpu.VMEM)
 IN_SMEM = pl.BlockSpec(memory_space=pltpu.SMEM)
 IN_HBM = pl.BlockSpec(memory_space=pltpu.HBM)
@@ -131,103 +125,123 @@
 def first_blocks(where, stream, swapped, routes, route_gain, experts):
     chips, _, tok_here, feat_here = stream.shape
     width = 2 * feat_here
-    rows = chips * tok_here // 2
-    head = -(-3 * experts // 16) * 16
-
-    def kernel(where_ref, stream_ref, swapped_ref, routes_ref, gain_ref, *outs):
+    tokens = chips * tok_here
+    head = -(-3 * (experts + 1) // 16) * 16
+
+    def kernel(where_ref, stream_ref, swapped_ref, routes_ref, gain_ref, out_ref):
         core = where_ref[chips + 1]
+        square = (tok_here, tok_here)
+        diagonal = lax.broadcasted_iota(jnp.int32, square, 0) == lax.broadcasted_iota(
+            jnp.int32, square, 1
+        )
+
+        def along(column):
+            return jnp.sum(jnp.where(diagonal, column, 0.0), axis=0, keepdims=True)
+
+        def split(left):
+            for _ in range(3):
+                piece = left.astype(jnp.bfloat16).astype(jnp.float32)
+                left = left - piece
+                yield piece
+
+        row_at = lax.broadcasted_iota(jnp.int32, (head, tok_here), 0)
         for q in range(chips):
             mine = stream_ref[q, core]
             other = swapped_ref[q]
             left = jnp.where(core == 0, mine, other)
             right = jnp.where(core == 0, other, mine)
-            out_ref = outs[2 * q // chips]
-            at = q * tok_here - (2 * q // chips) * rows + (head if 2 * q < chips else 0)
+            at = head + q * tok_here
             out_ref[at : at + tok_here, :] = jnp.concatenate([left, right], axis=1)
-        square = (tok_here, tok_here)
-        diagonal = lax.broadcasted_iota(jnp.int32, square, 0) == lax.broadcasted_iota(
-            jnp.int32, square, 1
-        )
-        row_at = lax.broadcasted_iota(jnp.int32, (head, tok_here), 0)
-        top = jnp.zeros((head, tok_here), jnp.float32)
-        for expert in range(experts):
-            gains = jnp.where(routes_ref[...] == expert, gain_ref[...], 0.0)
-            gains = jnp.sum(gains, axis=1, keepdims=True)
-            left = jnp.sum(jnp.where(diagonal, gains, 0.0), axis=0, keepdims=True)
-            for part in range(3):
-                piece = left.astype(jnp.bfloat16).astype(jnp.float32)
-                top = jnp.where(row_at == 3 * expert + part, piece, top)
-                left = left - piece
-        outs[0][:head, :] = jnp.zeros((head, width), jnp.bfloat16)
-        outs[0][:head, :tok_here] = top.astype(jnp.bfloat16)
+            left, right = left.astype(jnp.float32), right.astype(jnp.float32)
+            squares = jnp.sum(left * left + right * right, axis=1, keepdims=True)
+            top = jnp.zeros((head, tok_here), jnp.float32)
+            for row, piece in enumerate(split(along(squares))):
+                top = jnp.where(row_at == row, piece, top)
+            if q == 0:
+                for expert in range(experts):
+                    gains = jnp.where(routes_ref[...] == expert, gain_ref[...], 0.0)
+                    gains = jnp.sum(gains, axis=1, keepdims=True)
+                    for row, piece in enumerate(split(along(gains))):
+                        top = jnp.where(row_at == 3 * (expert + 1) + row, piece, top)
+            out_ref[:head, q * tok_here : (q + 1) * tok_here] = top.astype(jnp.bfloat16)
+        if width > tokens:
+            out_ref[:head, tokens:] = jnp.zeros((head, width - tokens), jnp.bfloat16)
 
     return local_call(
         kernel,
-        [
-            jax.ShapeDtypeStruct((head + rows, width), jnp.bfloat16),
-            jax.ShapeDtypeStruct((rows, width), jnp.bfloat16),
-        ],
+        jax.ShapeDtypeStruct((head + tokens, width), jnp.bfloat16),
         [where, stream, swapped, routes, route_gain],
-        flops=2 * rows * width,
-        bytes_accessed=8 * rows * width,
-    )
-
-
-def accumulate(where, positions, parts, norm_gain, tables, carried, headers, fetched=None):
+        flops=4 * tokens * width,
+        bytes_accessed=4 * tokens * width,
+    )
+
+
+def accumulate(where, positions, parts, norm_gain, tables, tok_here, carried, headers, ahead):
     count = len(positions)
     width = parts[0][0].shape[1]
     chips = norm_gain.shape[0]
     model_width = chips * width
-    hidden_here = tables[0].shape[1]
+    hidden_here = tables[0].shape[-1]
     both = 2 * hidden_here
-    rows = parts[0][1].shape[0]
-    head = parts[0][0].shape[0] - rows
-    tokens = 2 * rows
-    tok_here = tokens // chips
-    side = 128
+    tokens = chips * tok_here
+    sizes = [piece.shape[0] for piece in parts[0]]
+    head = sum(sizes) - tokens
+    offsets = [head] + [0] * (len(sizes) - 1)
+    sizes = [size - at for size, at in zip(sizes, offsets)]
+    starts = [sum(sizes[:k]) for k in range(len(sizes))]
     last = headers is not None
     first = carried is None
-    slots = 4 * count
+    slots = 0 if last else 4 * count
 
     def kernel(where_ref, *refs):
         refs = list(refs)
-        xs = [[refs.pop(0) for _ in range(2)] for _ in range(count)]
+        xs = [[refs.pop(0) for _ in sizes] for _ in range(count)]
         scale_ref = refs.pop(0)
-        stored = [refs.pop(0), refs.pop(0)]
-        acc_in, sq_in = (None, None) if first else (refs.pop(0), refs.pop(0))
+        stored = [refs.pop(0) for _ in tables]
+        acc_in = None if first else refs.pop(0)
         tops = [refs.pop(0) for _ in headers] if last else []
-        source_ref = refs.pop(0) if fetched is not None else None
+        sources = [refs.pop(0) for _ in ahead[1]] if ahead else []
         owns = [refs.pop(0) for _ in range(count)]
         if last:
             hidden_ref = refs.pop(0)
         else:
-            acc_out, sq_out, done_ref = refs.pop(0), refs.pop(0), refs.pop(0)
-            done_ref[0] = 0
-        brought_ref = refs.pop(0) if fetched is not None else None
-        table_ref, sems = refs.pop(0), refs.pop(0)
-        gain_ref = refs.pop(0) if last else None
-        copies = {}
-        for core in range(2):
-            for which in range(2):
+            acc_out = refs.pop(0)
+        if ahead:
+            next_ref, down_ref = refs.pop(0), refs.pop(0)
+        if last:
+            column_ref = refs.pop(0)
+        else:
+            table_ref, sems = refs.pop(0), refs.pop(0)
+
+        def fetch(which, position, target, sem):
+            row = pl.multiple_of(where_ref[position] * width, width)
+            copy = pltpu.make_async_copy(stored[which].at[pl.ds(row, width), :], target, sem)
+            copy.start()
+            return copy
+
+        copies, later = {}, []
+        if not last:
+            for which in range(4):
                 for b in range(count):
-                    row = (core * chips + where_ref[positions[b]]) * width
-                    slot = (core * 2 + which) * count + b
-                    copies[core, which, b] = pltpu.make_async_copy(
-                        stored[which].at[pl.ds(pl.multiple_of(row, width), width), :],
-                        table_ref.at[slot],
-                        sems.at[slot],
+                    slot = which * count + b
+                    copies[which, b] = fetch(
+                        which, positions[b], table_ref.at[slot], sems.at[slot]
                     )
-                    copies[core, which, b].start()
-        if fetched is not None:
-            bringing = pltpu.make_async_copy(source_ref, brought_ref, sems.at[slots])
-            bringing.start()
+        if ahead:
+            for which in range(4):
+                later.append(fetch(which, ahead[0], next_ref.at[which], sems.at[slots + which]))
+            for k, source in enumerate(sources):
+                target = down_ref.at[k * hidden_here : (k + 1) * hidden_here, :]
+                copy = pltpu.make_async_copy(source, target, sems.at[slots + 4 + k])
+                copy.start()
+                later.append(copy)
         begin = where_ref[0] * tok_here
         for b in range(count):
-            for k in range(2):
-
-                @pl.when((begin >= k * rows) & (begin < (k + 1) * rows))
+            for k, size in enumerate(sizes):
+
+                @pl.when((begin >= starts[k]) & (begin < starts[k] + size))
                 def _():
-                    row = begin - k * rows + (head if k == 0 else 0)
+                    row = begin - starts[k] + offsets[k]
                     owns[b][...] = xs[b][k][pl.ds(pl.multiple_of(row, 16), tok_here), :]
 
         if last:
@@ -237,89 +251,90 @@
             diagonal = lax.broadcasted_iota(jnp.int32, square, 0) == lax.broadcasted_iota(
                 jnp.int32, square, 1
             )
+
+            def column(row, values):
+                named = (row_at >= row) & (row_at < row + 3)
+                along = jnp.sum(jnp.where(named, values, 0.0), axis=0, keepdims=True)
+                return jnp.sum(jnp.where(diagonal, along, 0.0), axis=1, keepdims=True)
+
             for d in range(chips):
-                parts_of = tops[d][:head, :tok_here].astype(jnp.float32)
-                named = (row_at >= 3 * expert) & (row_at < 3 * expert + 3)
-                along = jnp.sum(jnp.where(named, parts_of, 0.0), axis=0, keepdims=True)
-                column = jnp.sum(jnp.where(diagonal, along, 0.0), axis=1, keepdims=True)
+                values = tops[d][:head, :tok_here].astype(jnp.float32)
                 at = pl.multiple_of(where_ref[d] * tok_here, tok_here)
-                gain_ref[pl.ds(at, tok_here), :] = column
-
-        scaled, squared = [], []
-        for k in range(2):
-            span = slice(k * rows, (k + 1) * rows)
-            squares = None if first else sq_in[span, :]
+                column_ref[pl.ds(at, tok_here), 0:1] = column(3 * (expert + 1), values)
+            for q in range(chips):
+                span = slice(q * tok_here, (q + 1) * tok_here)
+                total = tops[0][:head, span].astype(jnp.float32)
+                for d in range(1, chips):
+                    total = total + tops[d][:head, span].astype(jnp.float32)
+                mean = column(0, total) / model_width
+                column_ref[span, 1:2] = lax.rsqrt(mean + epsilon)
+
+        scaled = []
+        for k, size in enumerate(sizes):
             for b in range(count):
-                at = head if k == 0 else 0
-                values = xs[b][k][at : at + rows, :].astype(jnp.float32)
-                for lane in range(0, width, side):
-                    piece = values[:, lane : lane + side]
-                    squares = piece * piece if squares is None else squares + piece * piece
+                values = xs[b][k][offsets[k] : offsets[k] + size, :].astype(jnp.float32)
                 scale = scale_ref[where_ref[positions[b]]]
                 scaled.append((values * scale).astype(jnp.bfloat16))
-            squared.append(squares)
-            if not last:
-                sq_out[span, :] = squares
-        for core in range(2):
-            acts = []
-            for which in range(2):
+        acts = {}
+        for which in range(4):
+            cols = slice(which * hidden_here, (which + 1) * hidden_here)
+            for b in range(count):
+                if not last:
+                    copies[which, b].wait()
+            for k, size in enumerate(sizes):
+                span = slice(starts[k], starts[k] + size)
+                total = None if first else acc_in[span, cols]
                 for b in range(count):
-                    copies[core, which, b].wait()
-                for k in range(2):
-                    span = slice(k * rows, (k + 1) * rows)
-                    at = core * both + which * hidden_here
-                    cols = slice(at, at + hidden_here)
-                    total = None if first else acc_in[span, cols]
-                    for b in range(count):
-                        product = jnp.dot(
-                            scaled[k * count + b],
-                            table_ref[(core * 2 + which) * count + b],
-                            preferred_element_type=jnp.float32,
-                        )
-                        total = product if total is None else total + product
                     if last:
-                        acts.append(total)
+                        table = stored[0][which]
                     else:
-                        acc_out[span, cols] = total
-            if last:
-                for k in range(2):
-                    span = slice(k * rows, (k + 1) * rows)
-                    mean = jnp.sum(squared[k], axis=1, keepdims=True) / model_width
-                    inv_rms = lax.rsqrt(mean + epsilon)
-                    gate_act, up_act = acts[k] * inv_rms, acts[2 + k] * inv_rms
-                    act = gate_act * jax.nn.sigmoid(gate_act) * up_act * gain_ref[span, :]
-                    cols = slice(core * hidden_here, (core + 1) * hidden_here)
-                    hidden_ref[span, cols] = act.astype(jnp.bfloat16)
-        if fetched is not None:
-            bringing.wait()
+                        table = table_ref[which * count + b]
+                    product = jnp.dot(
+                        scaled[k * count + b], table, preferred_element_type=jnp.float32
+                    )
+                    total = product if total is None else total + product
+                if not last:
+                    acc_out[span, cols] = total
+                elif which % 2 == 0:
+                    acts[k] = total
+                else:
+                    gain, inv_rms = column_ref[span, 0:1], column_ref[span, 1:2]
+                    gate_act, up_act = acts[k] * inv_rms, total * inv_rms
+                    act = gate_act * jax.nn.sigmoid(gate_act) * up_act * gain
+                    core = which // 2
+                    out_cols = slice(core * hidden_here, (core + 1) * hidden_here)
+                    hidden_ref[span, out_cols] = act.astype(jnp.bfloat16)
+        for copy in later:
+            copy.wait()
 
     operands = [where] + [piece for block in parts for piece in block]
     operands.append(norm_gain)
-    distant = [len(operands), len(operands) + 1]
+    distant = [] if last else list(range(len(operands), len(operands) + len(tables)))
     operands.extend(tables)
     aliases = {}
     if not first:
         if not last:
-            aliases = {len(operands): count, len(operands) + 1: count + 1}
-        operands.extend(carried[:2])
+            aliases = {len(operands): count}
+        operands.append(carried)
     out_shape = [jax.ShapeDtypeStruct((tok_here, width), jnp.bfloat16)] * count
     if last:
         operands.extend(headers)
         out_shape.append(jax.ShapeDtypeStruct((tokens, both), jnp.bfloat16))
     else:
         out_shape.append(jax.ShapeDtypeStruct((tokens, 2 * both), jnp.float32))
-        out_shape.append(jax.ShapeDtypeStruct((tokens, side), jnp.float32))
-        out_shape.append(jax.ShapeDtypeStruct((1,), jnp.int32))
-    if fetched is not None:
-        distant.append(len(operands))
-        operands.append(fetched)
-        out_shape.append(jax.ShapeDtypeStruct(fetched.shape, fetched.dtype))
-    scratch = [
-        pltpu.VMEM((slots, width, hidden_here), jnp.bfloat16),
-        pltpu.SemaphoreType.DMA((slots + 1,)),
-    ]
+    if ahead:
+        for source in ahead[1]:
+            distant.append(len(operands))
+            operands.append(source)
+        out_shape.append(jax.ShapeDtypeStruct((4, width, hidden_here), jnp.bfloat16))
+        out_shape.append(jax.ShapeDtypeStruct((both, model_width), jnp.bfloat16))
     if last:
-        scratch.append(pltpu.VMEM((tokens, 1), jnp.float32))
+        scratch = [pltpu.VMEM((tokens, 2), jnp.float32)]
+    else:
+        scratch = [
+            pltpu.VMEM((slots, width, hidden_here), jnp.bfloat16),
+            pltpu.SemaphoreType.DMA((slots + 6,)),
+        ]
     made = local_call(
         kernel,
         out_shape,
@@ -341,14 +356,19 @@
 
     def kernel(where_ref, hidden_ref, down_ref, kept_ref, *outs):
         kept_ref[...] = hidden_ref[...]
-        for (position, part), out_ref in zip(wanted, outs):
-            at = pl.multiple_of(where_ref[position] * rows, rows)
+        for part in range(2):
+            chosen = [k for k, (_, at) in enumerate(wanted) if at == part]
+            taken = [
+                hidden_ref[pl.ds(pl.multiple_of(where_ref[wanted[k][0]] * rows, rows), rows), :]
+                for k in chosen
+            ]
             out = jnp.dot(
-                hidden_ref[pl.ds(at, rows), :],
+                jnp.concatenate(taken, axis=0),
                 down_ref[:, part * half : (part + 1) * half],
                 preferred_element_type=jnp.float32,
-            )
-            out_ref[...] = out.astype(jnp.bfloat16)
+            ).astype(jnp.bfloat16)
+            for at, k in enumerate(chosen):
+                outs[k][...] = out[at * rows : (at + 1) * rows, :]
 
     return local_call(
         kernel,
@@ -470,45 +490,43 @@
     by_core = stream_feat.reshape(chips, 2, tok_here, feat_here)
     swapped = swap_cores(lax.dynamic_index_in_dim(by_core, 1 - core, 1, keepdims=False))
 
-    swapped, w_gate, w_up, w_down = lax.optimization_barrier((swapped, w_gate, w_up, w_down))
-    tables = [pair_gather(w_gate), pair_gather(w_up)]
-    down = pair_gather(w_down)
+    swapped, w_gate, w_up = lax.optimization_barrier((swapped, w_gate, w_up))
+    tables = [pltpu.with_memory_space_constraint(table, pltpu.HBM) for table in (w_gate, w_up)]
+    tables += [swap_cores(w_gate), swap_cores(w_up)]
     blocks = {0: first_blocks(where, by_core, swapped, expert_routes, route_gain, experts)}
+    w_down = lax.optimization_barrier((swapped, w_down))[1]
+    down = [pltpu.with_memory_space_constraint(w_down, pltpu.HBM), swap_cores(w_down)]
 
     for distance in range(1, far):
         for sign in (-1, 1):
-            blocks[sign * distance] = [
-                ring_shift(part, ring, -sign) for part in blocks[sign * (distance - 1)]
-            ]
+            blocks[sign * distance] = ring_shift(blocks[sign * (distance - 1)], ring, -sign)
     groups = [[0]] + [[d, chips - d] for d in range(1, far)] + [[far]]
     gain_rows = norm_gain.reshape(chips, 1, width)
-    carried, owns, positions, headers = None, [], [], None
+    carried, owns, positions, headers, ahead = None, [], [], None, None
     for group in groups:
+        parts = [[blocks[d if d <= far else d - chips]] for d in group]
         if group == [far]:
-            headers = [blocks[d if d <= far else d - chips][0] for d in range(chips)]
-        parts = [blocks[d if d <= far else d - chips] for d in group]
-        made, carried = accumulate(
-            where,
-            group,
-            parts,
-            gain_rows,
-            tables,
-            carried,
-            headers,
-            down if group == groups[-2] else None,
+            parts = [blocks[far]]
+            headers = [blocks[d if d < far else d - chips] for d in range(chips) if d != far]
+            headers.insert(far, blocks[far][0])
+        if group == groups[-2]:
+            ahead = (far, down)
+        made, (carried, *rest) = accumulate(
+            where, group, parts, gain_rows, tables, tok_here, carried, headers, ahead
         )
         owns.extend(made)
         positions.extend(group)
         if group == groups[max(far - 3, 0)]:
-            lower, upper, *carried = lax.optimization_barrier(
-                (blocks[1 - far][0], blocks[far - 1][1], *carried)
+            lower, upper, carried = lax.optimization_barrier(
+                (blocks[1 - far], blocks[far - 1], carried)
             )
-            blocks[far] = [ring_shift(lower, ring, 1), ring_shift(upper, ring, -1)]
+            cut = lower.shape[0] - far * tok_here
+            blocks[far] = [ring_shift(lower[:cut], ring, 1), ring_shift(upper[cut:], ring, -1)]
         if group == groups[-2]:
-            down = carried[-1]
+            tables, down, ahead = [rest[0]], rest[1], None
 
     leading = [(far, 0), (far, 1), (far - 1, 1), (chips - far + 1, 0)]
-    hidden, lower, upper, after, before = leading_rows(where, leading, carried[0], down, chips)
+    hidden, lower, upper, after, before = leading_rows(where, leading, carried, down, chips)
     moving = {1: [ring_shift(lower, ring, 1), None], -1: [None, ring_shift(upper, ring, -1)]}
     second = {1: ring_shift(after, ring, 1), -1: ring_shift(before, ring, -1)}
     everything = [contribution(where, hidden, down, part) for part in range(2)]
@@ -536,6 +554,7 @@
     devices = lax.axis_size("ep")
     capacity = route_slots * tok_here // (devices // FSPLIT)
     dense = capacity >= tok_here and devices % 8 == 0
+    dense = dense and devices * tok_here <= 4 * residual.shape[1]
     chosen = dense_body if dense else routed_body
     return chosen(residual, attn_out, norm_gain, expert_routes, route_gain, w_gate, w_up, w_down)
 

time: 186 us -> 168 us (0.903)
  between operations: 13.5 us -> 0.23 us
  local copies, waits for them, and re-layouts: 11 us -> 1.55 us
  waiting for transfers between devices: 86 us -> 93.8 us
  starting transfers between devices: 30.2 us -> 26.6 us
    unnamed x54 -> x8, local copies, waits for them, and re-layouts: 9.76 us -> 0.2 us
    ppermute x28 -> x22, waiting for transfers between devices: 83.1 us -> 92.3 us  [ring_shift(): return lax.ppermute(value, 'ep', pairs)]
    ppermute x28 -> x22, starting transfers between devices: 29.6 us -> 25.2 us  [ring_shift(): return lax.ppermute(value, 'ep', pairs)]
  transfers between devices with their start and end apart: 32 -> 26, of which waited for: 16 -> 16; matrix products, arithmetic and copies ran while one was open for 0% -> 1% of each run, Pallas kernels for 18% -> 23%
where the time goes in v6:
time: 168 us
  waiting for transfers between devices  93.8 us (56%)
  Pallas kernels  44.2 us (26%)
  starting transfers between devices  26.6 us (16%)
  other arithmetic  1.82 us (1%)
    ppermute x22, waiting for transfers between devices, ring_shift(): return lax.ppermute(value, 'ep', pairs)  92.3 us
    pallas_call x21, Pallas kernels, local_call(): pl.pallas_call(kernel, out_shape=out_shape, in_specs=[IN_SMEM if k == 0 e...  44.2 us
    ppermute x22, starting transfers between devices, ring_shift(): return lax.ppermute(value, 'ep', pairs)  25.2 us
  transfers between devices with their start and end apart: 26, of which 16 were waited for; matrix products, arithmetic and copies ran while one was open for 1% of the time, Pallas kernels for 23%

profile of v6, /device:TPU:0, one launch (start us, length us, event | category | flops | bytes accessed | tf_op | source)
XLA Modules:
  0.0 168.3 jit_solution(10154631209701387650)
XLA Ops:
  0.0 1.8 %add_convert_fusion = bf16[1024,448]{0,1:T(8,128)(2,1)S(1)} fusion(bf16[1024,448]{0,1:T(8,128)(2,1)} %param.10, bf16[1024,448]{0,1:T(8,128)(2,1)} %param.9), kind=kLoop, calls=%fused_computation | loop fusion | flops 1835008 | bytes 2752512 | tf_op jit(solution)/shard_map/convert_element_type | solution.py:489
  1.8 0.5 copy.13
  2.4 0.5 collective-permute-start
  3.0 1.5 collective-permute-done.swapped_ref
  4.5 0.4 collective-permute-start.1
  5.0 0.4 collective-permute-start.9
  5.6 0.7 dynamic-slice_bitcast_fusion.1.where_ref
  6.3 1.3 shard_map.91.refs_0_.refs_5_
  7.5 2.8 %collective-permute-start.4 = (bf16[528,896]{1,0:T(8,128)(2,1)S(1)}, bf16[528,896]{1,0:T(8,128)(2,1)S(1)}, u32[]{:S(2)}, u32[]{:S(2)}) collective-permute-start(bf16[528,896]{1,0:T(8,128)(2,1)S(1)} %shard_map.91.refs_0_.refs_5_), channel_id=1, source_target_pairs={{0,4},{1,5},{4,8},{5,9},{8,12},{9,13},{12,14},{13,15},{14,10},{15,... | collective-permute-start | bytes 2838536 | tf_op jit(solution)/shard_map/ppermute | solution.py:94
  10.3 21.4 %collective-permute-done.4.refs_1_.refs_12_ = bf16[528,896]{1,0:T(8,128)(2,1)S(1)} collective-permute-done((bf16[528,896]{1,0:T(8,128)(2,1)S(1)}, bf16[528,896]{1,0:T(8,128)(2,1)S(1)}, u32[]{:S(2)}, u32[]{:S(2)}) %collective-permute-start.4) | collective-permute-done | bytes 946208 | tf_op jit(solution)/shard_map/ppermute | solution.py:94
  31.7 1.8 %collective-permute-start.6 = (bf16[528,896]{1,0:T(8,128)(2,1)S(1)}, bf16[528,896]{1,0:T(8,128)(2,1)S(1)}, u32[]{:S(2)}, u32[]{:S(2)}) collective-permute-start(bf16[528,896]{1,0:T(8,128)(2,1)S(1)} %collective-permute-done.4.refs_1_.refs_12_), channel_id=1, source_target_pairs={{0,4},{1,5},{4,8},{5,9},{8,12},{9,13},{12,14},{13,15},{14,10},{15,... | collective-permute-start | bytes 2838536 | tf_op jit(solution)/shard_map/ppermute | solution.py:94
  33.5 0.2 collective-permute-start.5
  33.8 20.6 %collective-permute-done.6.refs_1_.refs_11_ = bf16[528,896]{1,0:T(8,128)(2,1)S(1)} collective-permute-done((bf16[528,896]{1,0:T(8,128)(2,1)S(1)}, bf16[528,896]{1,0:T(8,128)(2,1)S(1)}, u32[]{:S(2)}, u32[]{:S(2)}) %collective-permute-start.6) | collective-permute-done | bytes 946208 | tf_op jit(solution)/shard_map/ppermute | solution.py:94
  54.4 1.6 collective-permute-start.7
  56.0 0.5 collective-permute-start.8
  56.5 4.4 %shard_map.92 = (bf16[64,896]{1,0:T(8,128)(2,1)S(1)}, f32[512,1024]{1,0:T(8,128)S(1)}) custom-call(s32[10]{0:T(128)S(1)} %dynamic-slice_bitcast_fusion.1.where_ref, bf16[528,896]{1,0:T(8,128)(2,1)S(1)} %shard_map.91.refs_0_.refs_5_, f32[8,1,896]{2,1,0:T(1,128)S(1)} %bitcast.8, bf16[7168,256]{1,0:T(8,128)(2,1)} %refs_3_.3, bf16[7168,256]{1,0:T(8,128)(2,1)} %refs_4_.2, ...), custom_call_target="tpu_custom_call" | custom-call | flops 2818572288 | bytes 6946816 | tf_op jit(solution)/shard_map/pallas_call | solution.py:107
  60.9 6.8 %shard_map.93 = (bf16[64,896]{1,0:T(8,128)(2,1)S(1)}, bf16[64,896]{1,0:T(8,128)(2,1)S(1)}, f32[512,1024]{1,0:T(8,128)S(1)}) custom-call(s32[10]{0:T(128)S(1)} %dynamic-slice_bitcast_fusion.1.where_ref, bf16[528,896]{1,0:T(8,128)(2,1)S(1)} %collective-permute-done.3.refs_0_.refs_6_, ...), custom_call_target="tpu_custom_call", output_to_operand_aliasing={{2}: (8, {})} | custom-call | flops 5637144576 | bytes 9699328 | tf_op jit(solution)/shard_map/pallas_call | solution.py:107
  67.7 8.5 %collective-permute-done.7.refs_1_.refs_10_ = bf16[528,896]{1,0:T(8,128)(2,1)S(1)} collective-permute-done((bf16[528,896]{1,0:T(8,128)(2,1)S(1)}, bf16[528,896]{1,0:T(8,128)(2,1)S(1)}, u32[]{:S(2)}, u32[]{:S(2)}) %collective-permute-start.7) | collective-permute-done | bytes 946208 | tf_op jit(solution)/shard_map/ppermute | solution.py:94
  76.2 1.0 collective-permute-done.8.refs_0_.refs_8_
  77.3 1.6 collective-permute-start.10
  78.9 0.5 collective-permute-start.11
  79.4 6.8 %shard_map.94 = (bf16[64,896]{1,0:T(8,128)(2,1)S(1)}, bf16[64,896]{1,0:T(8,128)(2,1)S(1)}, f32[512,1024]{1,0:T(8,128)S(1)}) custom-call(s32[10]{0:T(128)S(1)} %dynamic-slice_bitcast_fusion.1.where_ref, bf16[528,896]{1,0:T(8,128)(2,1)S(1)} %collective-permute-done.5.refs_0_.refs_7_, ...), custom_call_target="tpu_custom_call", output_to_operand_aliasing={{2}: (8, {})} | custom-call | flops 5637144576 | bytes 9699328 | tf_op jit(solution)/shard_map/pallas_call | solution.py:107
  86.2 6.8 %shard_map.95 = (bf16[64,896]{1,0:T(8,128)(2,1)S(1)}, bf16[64,896]{1,0:T(8,128)(2,1)S(1)}, f32[512,1024]{1,0:T(8,128)S(1)}, bf16[4,896,256]{2,1,0:T(8,128)(2,1)S(1)}, bf16[512,7168]{1,0:T(8,128)(2,1)S(1)}) custom-call(s32[10]{0:T(128)S(1)} %dynamic-slice_bitcast_fusion.1.where_ref, ...), custom_call_target="tpu_custom_call", output_to_operand_aliasing={{2}: (8, {})} | custom-call | flops 5637144576 | bytes 9699328 | tf_op jit(solution)/shard_map/pallas_call | solution.py:107
  93.0 2.1 %shard_map.96 = (bf16[64,896]{1,0:T(8,128)(2,1)S(1)}, bf16[512,512]{1,0:T(8,128)(2,1)S(1)}) custom-call(s32[10]{0:T(128)S(1)} %dynamic-slice_bitcast_fusion.1.where_ref, bf16[272,896]{1,0:T(8,128)(2,1)S(1)} %collective-permute-done.10.refs_0_.refs_9_, bf16[256,896]{1,0:T(8,128)(2,1)S(1)} %collective-permute-done.11.refs_1_, f32[8,1,896]{2,1,0:T(1,128)S(1)} %bitcast.12, ...), custom_call_target="tpu_custom_call" | custom-call | flops 2818572288 | bytes 6946816 | tf_op jit(solution)/shard_map/pallas_call | solution.py:107
  95.1 1.8 %shard_map.97 = (bf16[512,512]{1,0:T(8,128)(2,1)S(1)}, bf16[64,3584]{1,0:T(8,128)(2,1)S(1)}, bf16[64,3584]{1,0:T(8,128)(2,1)S(1)}, bf16[64,3584]{1,0:T(8,128)(2,1)S(1)}, bf16[64,3584]{1,0:T(8,128)(2,1)S(1)}) custom-call(s32[10]{0:T(128)S(1)} %dynamic-slice_bitcast_fusion.1.where_ref, bf16[512,512]{1,0:T(8,128)(2,1)S(1)} %get-tuple-element.52.hidden_ref, ...), custom_call_target="tpu_custom_call" | custom-call | flops 939524096 | bytes 7340032 | tf_op jit(solution)/shard_map/pallas_call | solution.py:107
  96.9 1.6 collective-permute-start.12
  98.6 0.4 collective-permute-start.22
  99.0 0.7 collective-permute-start.16
  99.7 2.6 %shard_map.98.refs_8_.table_ref = bf16[512,3584]{1,0:T(8,128)(2,1)S(1)} custom-call(s32[10]{0:T(128)S(1)} %dynamic-slice_bitcast_fusion.1.where_ref, bf16[512,512]{1,0:T(8,128)(2,1)S(1)} %get-tuple-element.54.hidden_ref, bf16[512,7168]{1,0:T(8,128)(2,1)S(1)} %get-tuple-element.53.down_ref), custom_call_target="tpu_custom_call" | custom-call | flops 1879048192 | bytes 7340032 | tf_op jit(solution)/shard_map/pallas_call | solution.py:107
  102.4 2.6 %shard_map.99.refs_9_.table_ref = bf16[512,3584]{1,0:T(8,128)(2,1)S(1)} custom-call(s32[10]{0:T(128)S(1)} %dynamic-slice_bitcast_fusion.1.where_ref, bf16[512,512]{1,0:T(8,128)(2,1)S(1)} %get-tuple-element.54.hidden_ref, bf16[512,7168]{1,0:T(8,128)(2,1)S(1)} %get-tuple-element.53.down_ref), custom_call_target="tpu_custom_call" | custom-call | flops 1879048192 | bytes 7340032 | tf_op jit(solution)/shard_map/pallas_call | solution.py:107
  105.0 1.3 collective-permute-start.19
  106.3 2.2 %collective-permute-done.12.moved_ref = bf16[64,3584]{1,0:T(8,128)(2,1)S(1)} collective-permute-done((bf16[64,3584]{1,0:T(8,128)(2,1)S(1)}, bf16[64,3584]{1,0:T(8,128)(2,1)S(1)}, u32[]{:S(2)}, u32[]{:S(2)}) %collective-permute-start.12) | collective-permute-done | bytes 458784 | tf_op jit(solution)/shard_map/ppermute | solution.py:94
  108.6 0.7 shard_map.101
  109.2 2.2 %collective-permute-start.13 = (bf16[64,3584]{1,0:T(8,128)(2,1)S(1)}, bf16[64,3584]{1,0:T(8,128)(2,1)S(1)}, u32[]{:S(2)}, u32[]{:S(2)}) collective-permute-start(bf16[64,3584]{1,0:T(8,128)(2,1)S(1)} %shard_map.101), channel_id=1, source_target_pairs={{0,4},{1,5},{4,8},{5,9},{8,12},{9,13},{12,14},{13,15},{14,10},{15,... | collective-permute-start | bytes 1376264 | tf_op jit(solution)/shard_map/ppermute | solution.py:94
  111.4 0.6 collective-permute-done.22.moved_ref
  112.0 0.7 shard_map.108
  112.7 0.5 collective-permute-start.23
  113.2 8.7 %collective-permute-done.16.moved_ref = bf16[64,3584]{1,0:T(8,128)(2,1)S(1)} collective-permute-done((bf16[64,3584]{1,0:T(8,128)(2,1)S(1)}, bf16[64,3584]{1,0:T(8,128)(2,1)S(1)}, u32[]{:S(2)}, u32[]{:S(2)}) %collective-permute-start.16) | collective-permute-done | bytes 458784 | tf_op jit(solution)/shard_map/ppermute | solution.py:94
  121.9 0.7 shard_map.104
  122.5 0.5 collective-permute-start.17
  123.0 0.6 shard_map.106
  123.7 1.6 collective-permute-start.20
  125.3 3.0 %collective-permute-done.13.moved_ref = bf16[64,3584]{1,0:T(8,128)(2,1)S(1)} collective-permute-done((bf16[64,3584]{1,0:T(8,128)(2,1)S(1)}, bf16[64,3584]{1,0:T(8,128)(2,1)S(1)}, u32[]{:S(2)}, u32[]{:S(2)}) %collective-permute-start.13) | collective-permute-done | bytes 458784 | tf_op jit(solution)/shard_map/ppermute | solution.py:94
  128.3 0.6 shard_map.102
  129.0 2.1 %collective-permute-start.14 = (bf16[64,3584]{1,0:T(8,128)(2,1)S(1)}, bf16[64,3584]{1,0:T(8,128)(2,1)S(1)}, u32[]{:S(2)}, u32[]{:S(2)}) collective-permute-start(bf16[64,3584]{1,0:T(8,128)(2,1)S(1)} %shard_map.102), channel_id=1, source_target_pairs={{0,4},{1,5},{4,8},{5,9},{8,12},{9,13},{12,14},{13,15},{14,10},{15,... | collective-permute-start | bytes 1376264 | tf_op jit(solution)/shard_map/ppermute | solution.py:94
  131.1 0.6 collective-permute-done.23.moved_ref
  131.7 0.6 shard_map.109
  132.3 0.5 collective-permute-start.24
  132.8 8.7 %collective-permute-done.17.moved_ref = bf16[64,3584]{1,0:T(8,128)(2,1)S(1)} collective-permute-done((bf16[64,3584]{1,0:T(8,128)(2,1)S(1)}, bf16[64,3584]{1,0:T(8,128)(2,1)S(1)}, u32[]{:S(2)}, u32[]{:S(2)}) %collective-permute-start.17) | collective-permute-done | bytes 458784 | tf_op jit(solution)/shard_map/ppermute | solution.py:94
  141.5 0.6 shard_map.105
  142.2 0.5 collective-permute-start.18
  142.7 0.6 shard_map.107
  143.3 1.6 collective-permute-start.21
  145.0 3.0 %collective-permute-done.14.moved_ref = bf16[64,3584]{1,0:T(8,128)(2,1)S(1)} collective-permute-done((bf16[64,3584]{1,0:T(8,128)(2,1)S(1)}, bf16[64,3584]{1,0:T(8,128)(2,1)S(1)}, u32[]{:S(2)}, u32[]{:S(2)}) %collective-permute-start.14) | collective-permute-done | bytes 458784 | tf_op jit(solution)/shard_map/ppermute | solution.py:94
  148.0 0.6 shard_map.103
  148.6 2.1 %collective-permute-start.15 = (bf16[64,3584]{1,0:T(8,128)(2,1)S(1)}, bf16[64,3584]{1,0:T(8,128)(2,1)S(1)}, u32[]{:S(2)}, u32[]{:S(2)}) collective-permute-start(bf16[64,3584]{1,0:T(8,128)(2,1)S(1)} %shard_map.103), channel_id=1, source_target_pairs={{0,4},{1,5},{4,8},{5,9},{8,12},{9,13},{12,14},{13,15},{14,10},{15,... | collective-permute-start | bytes 1376264 | tf_op jit(solution)/shard_map/ppermute | solution.py:94
  150.7 0.6 collective-permute-done.24.moved_ref
  151.3 0.6 shard_map.110
  152.0 0.5 collective-permute-start.25
  152.5 0.8 shard_map.100.base_ref
  153.3 7.8 %collective-permute-done.18.refs_1_ = bf16[64,3584]{1,0:T(8,128)(2,1)S(1)} collective-permute-done((bf16[64,3584]{1,0:T(8,128)(2,1)S(1)}, bf16[64,3584]{1,0:T(8,128)(2,1)S(1)}, u32[]{:S(2)}, u32[]{:S(2)}) %collective-permute-start.18) | collective-permute-done | bytes 458784 | tf_op jit(solution)/shard_map/ppermute | solution.py:94
  161.2 4.1 %collective-permute-done.15.refs_0_ = bf16[64,3584]{1,0:T(8,128)(2,1)S(1)} collective-permute-done((bf16[64,3584]{1,0:T(8,128)(2,1)S(1)}, bf16[64,3584]{1,0:T(8,128)(2,1)S(1)}, u32[]{:S(2)}, u32[]{:S(2)}) %collective-permute-start.15) | collective-permute-done | bytes 458784 | tf_op jit(solution)/shard_map/ppermute | solution.py:94
  165.3 1.3 collective-permute-done.25.refs_3_
  166.6 1.7 %shard_map.111 = bf16[64,7168]{1,0:T(8,128)(2,1)} custom-call(s32[10]{0:T(128)S(1)} %dynamic-slice_bitcast_fusion.1.where_ref, f32[64,7168]{1,0:T(8,128)S(1)} %shard_map.100.base_ref, bf16[64,3584]{1,0:T(8,128)(2,1)S(1)} %collective-permute-done.15.refs_0_, bf16[64,3584]{1,0:T(8,128)(2,1)S(1)} %collective-permute-done.18.refs_1_, ...), custom_call_target="tpu_custom_call" | custom-call | flops 1376256 | bytes 4587520 | tf_op jit(solution)/shard_map/pallas_call | solution.py:107
  (23 shorter events, 0.5 us)
Async XLA Ops:
  0.0 5.4 %copy-start.1 = (s32[64,2]{0,1:T(2,128)S(1)}, s32[64,2]{0,1:T(2,128)}, u32[]{:S(2)}) copy-start(s32[64,2]{0,1:T(2,128)} %param.12) | copy-start | bytes 1540
  0.0 5.5 %copy-start.2 = (f32[64,2]{0,1:T(2,128)S(1)}, f32[64,2]{0,1:T(2,128)}, u32[]{:S(2)}) copy-start(f32[64,2]{0,1:T(2,128)} %param.13) | copy-start | bytes 1540
  0.0 56.5 %copy-start = (f32[7168]{0:T(1024)S(1)}, f32[7168]{0:T(1024)}, u32[]{:S(2)}) copy-start(f32[7168]{0:T(1024)} %param.11) | copy-start | bytes 86020
  2.4 2.1 %collective-permute-start = (bf16[8,64,448]{2,1,0:T(8,128)(2,1)S(1)}, bf16[8,64,448]{2,1,0:T(8,128)(2,1)S(1)}, u32[]{:S(2)}, u32[]{:S(2)}) collective-permute-start(bf16[8,64,448]{2,1,0:T(8,128)(2,1)S(1)} %dynamic-slice_bitcast_fusion), channel_id=1, source_target_pairs={{0,1},{1,0},{2,3},{3,2},{4,5},{5,4},{6,7},{7,6},{8,9},{9,8},{10,11... | collective-permute-start | bytes 1376264 | tf_op jit(solution)/shard_map/ppermute | solution.py:84
  4.5 51.9 %collective-permute-start.1 = (bf16[7168,256]{1,0:T(8,128)(2,1)}, bf16[7168,256]{1,0:T(8,128)(2,1)}, u32[]{:S(2)}, u32[]{:S(2)}) collective-permute-start(bf16[7168,256]{1,0:T(8,128)(2,1)} %refs_3_.3), channel_id=1, source_target_pairs={{0,1},{1,0},{2,3},{3,2},{4,5},{5,4},{6,7},{7,6},{8,9},{9,8},{10,11... | collective-permute-start | bytes 11010056 | tf_op jit(solution)/shard_map/ppermute | solution.py:84
  4.9 51.6 %collective-permute-start.2 = (bf16[7168,256]{1,0:T(8,128)(2,1)}, bf16[7168,256]{1,0:T(8,128)(2,1)}, u32[]{:S(2)}, u32[]{:S(2)}) collective-permute-start(bf16[7168,256]{1,0:T(8,128)(2,1)} %refs_4_.2), channel_id=1, source_target_pairs={{0,1},{1,0},{2,3},{3,2},{4,5},{5,4},{6,7},{7,6},{8,9},{9,8},{10,11... | collective-permute-start | bytes 11010056 | tf_op jit(solution)/shard_map/ppermute | solution.py:84
  5.0 81.2 %collective-permute-start.9 = (bf16[256,7168]{1,0:T(8,128)(2,1)}, bf16[256,7168]{1,0:T(8,128)(2,1)}, u32[]{:S(2)}, u32[]{:S(2)}) collective-permute-start(bf16[256,7168]{1,0:T(8,128)(2,1)} %refs_8_), channel_id=1, source_target_pairs={{0,1},{1,0},{2,3},{3,2},{4,5},{5,4},{6,7},{7,6},{8,9},{9,8},{10,11... | collective-permute-start | bytes 11010056 | tf_op jit(solution)/shard_map/ppermute | solution.py:84
  7.5 24.2 %collective-permute-start.4 = (bf16[528,896]{1,0:T(8,128)(2,1)S(1)}, bf16[528,896]{1,0:T(8,128)(2,1)S(1)}, u32[]{:S(2)}, u32[]{:S(2)}) collective-permute-start(bf16[528,896]{1,0:T(8,128)(2,1)S(1)} %shard_map.91.refs_0_.refs_5_), channel_id=1, source_target_pairs={{0,4},{1,5},{4,8},{5,9},{8,12},{9,13},{12,14},{13,15},{14,10},{15,... | collective-permute-start | bytes 2838536 | tf_op jit(solution)/shard_map/ppermute | solution.py:94
  10.3 23.2 %collective-permute-start.3 = (bf16[528,896]{1,0:T(8,128)(2,1)S(1)}, bf16[528,896]{1,0:T(8,128)(2,1)S(1)}, u32[]{:S(2)}, u32[]{:S(2)}) collective-permute-start(bf16[528,896]{1,0:T(8,128)(2,1)S(1)} %shard_map.91.refs_0_.refs_5_), channel_id=1, source_target_pairs={{0,2},{1,3},{4,0},{5,1},{8,4},{9,5},{12,8},{13,9},{14,12},{15,13},... | collective-permute-start | bytes 2838536 | tf_op jit(solution)/shard_map/ppermute | solution.py:94
  31.7 22.7 %collective-permute-start.6 = (bf16[528,896]{1,0:T(8,128)(2,1)S(1)}, bf16[528,896]{1,0:T(8,128)(2,1)S(1)}, u32[]{:S(2)}, u32[]{:S(2)}) collective-permute-start(bf16[528,896]{1,0:T(8,128)(2,1)S(1)} %collective-permute-done.4.refs_1_.refs_12_), channel_id=1, source_target_pairs={{0,4},{1,5},{4,8},{5,9},{8,12},{9,13},{12,14},{13,15},{14,10},{15,... | collective-permute-start | bytes 2838536 | tf_op jit(solution)/shard_map/ppermute | solution.py:94
  33.5 22.4 %collective-permute-start.5 = (bf16[528,896]{1,0:T(8,128)(2,1)S(1)}, bf16[528,896]{1,0:T(8,128)(2,1)S(1)}, u32[]{:S(2)}, u32[]{:S(2)}) collective-permute-start(bf16[528,896]{1,0:T(8,128)(2,1)S(1)} %collective-permute-done.3.refs_0_.refs_6_), channel_id=1, source_target_pairs={{0,2},{1,3},{4,0},{5,1},{8,4},{9,5},{12,8},{13,9},{14,12},{15,13},... | collective-permute-start | bytes 2838536 | tf_op jit(solution)/shard_map/ppermute | solution.py:94
  54.4 21.8 %collective-permute-start.7 = (bf16[528,896]{1,0:T(8,128)(2,1)S(1)}, bf16[528,896]{1,0:T(8,128)(2,1)S(1)}, u32[]{:S(2)}, u32[]{:S(2)}) collective-permute-start(bf16[528,896]{1,0:T(8,128)(2,1)S(1)} %collective-permute-done.6.refs_1_.refs_11_), channel_id=1, source_target_pairs={{0,4},{1,5},{4,8},{5,9},{8,12},{9,13},{12,14},{13,15},{14,10},{15,... | collective-permute-start | bytes 2838536 | tf_op jit(solution)/shard_map/ppermute | solution.py:94
  56.0 21.2 %collective-permute-start.8 = (bf16[528,896]{1,0:T(8,128)(2,1)S(1)}, bf16[528,896]{1,0:T(8,128)(2,1)S(1)}, u32[]{:S(2)}, u32[]{:S(2)}) collective-permute-start(bf16[528,896]{1,0:T(8,128)(2,1)S(1)} %collective-permute-done.5.refs_0_.refs_7_), channel_id=1, source_target_pairs={{0,2},{1,3},{4,0},{5,1},{8,4},{9,5},{12,8},{13,9},{14,12},{15,13},... | collective-permute-start | bytes 2838536 | tf_op jit(solution)/shard_map/ppermute | solution.py:94
  77.3 15.8 %collective-permute-start.10 = (bf16[272,896]{1,0:T(8,128)(2,1)S(1)}, bf16[272,896]{1,0:T(8,128)(2,1)S(1)}, u32[]{:S(2)}, u32[]{:S(2)}) collective-permute-start(bf16[272,896]{1,0:T(8,128)(2,1)S(1)} %slice.6), channel_id=1, source_target_pairs={{0,4},{1,5},{4,8},{5,9},{8,12},{9,13},{12,14},{13,15},{14,10},{15,... | collective-permute-start | bytes 1462280 | tf_op jit(solution)/shard_map/ppermute | solution.py:94
  78.9 14.1 %collective-permute-start.11 = (bf16[256,896]{1,0:T(8,128)(2,1)S(1)}, bf16[256,896]{1,0:T(8,128)(2,1)S(1)}, u32[]{:S(2)}, u32[]{:S(2)}) collective-permute-start(bf16[256,896]{1,0:T(8,128)(2,1)S(1)} %slice.7), channel_id=1, source_target_pairs={{0,2},{1,3},{4,0},{5,1},{8,4},{9,5},{12,8},{13,9},{14,12},{15,13},... | collective-permute-start | bytes 1376264 | tf_op jit(solution)/shard_map/ppermute | solution.py:94
  96.9 11.6 %collective-permute-start.12 = (bf16[64,3584]{1,0:T(8,128)(2,1)S(1)}, bf16[64,3584]{1,0:T(8,128)(2,1)S(1)}, u32[]{:S(2)}, u32[]{:S(2)}) collective-permute-start(bf16[64,3584]{1,0:T(8,128)(2,1)S(1)} %get-tuple-element.55), channel_id=1, source_target_pairs={{0,4},{1,5},{4,8},{5,9},{8,12},{9,13},{12,14},{13,15},{14,10},{15,... | collective-permute-start | bytes 1376264 | tf_op jit(solution)/shard_map/ppermute | solution.py:94
  98.6 13.5 %collective-permute-start.22 = (bf16[64,3584]{1,0:T(8,128)(2,1)S(1)}, bf16[64,3584]{1,0:T(8,128)(2,1)S(1)}, u32[]{:S(2)}, u32[]{:S(2)}) collective-permute-start(bf16[64,3584]{1,0:T(8,128)(2,1)S(1)} %get-tuple-element.58), channel_id=1, source_target_pairs={{0,2},{1,3},{4,0},{5,1},{8,4},{9,5},{12,8},{13,9},{14,12},{15,13},... | collective-permute-start | bytes 1376264 | tf_op jit(solution)/shard_map/ppermute | solution.py:94
  99.0 22.8 %collective-permute-start.16 = (bf16[64,3584]{1,0:T(8,128)(2,1)S(1)}, bf16[64,3584]{1,0:T(8,128)(2,1)S(1)}, u32[]{:S(2)}, u32[]{:S(2)}) collective-permute-start(bf16[64,3584]{1,0:T(8,128)(2,1)S(1)} %get-tuple-element.56), channel_id=1, source_target_pairs={{0,2},{1,3},{4,0},{5,1},{8,4},{9,5},{12,8},{13,9},{14,12},{15,13},... | collective-permute-start | bytes 1376264 | tf_op jit(solution)/shard_map/ppermute | solution.py:94
  105.0 18.0 %collective-permute-start.19 = (bf16[64,3584]{1,0:T(8,128)(2,1)S(1)}, bf16[64,3584]{1,0:T(8,128)(2,1)S(1)}, u32[]{:S(2)}, u32[]{:S(2)}) collective-permute-start(bf16[64,3584]{1,0:T(8,128)(2,1)S(1)} %get-tuple-element.57), channel_id=1, source_target_pairs={{0,4},{1,5},{4,8},{5,9},{8,12},{9,13},{12,14},{13,15},{14,10},{15,... | collective-permute-start | bytes 1376264 | tf_op jit(solution)/shard_map/ppermute | solution.py:94
  109.2 19.1 %collective-permute-start.13 = (bf16[64,3584]{1,0:T(8,128)(2,1)S(1)}, bf16[64,3584]{1,0:T(8,128)(2,1)S(1)}, u32[]{:S(2)}, u32[]{:S(2)}) collective-permute-start(bf16[64,3584]{1,0:T(8,128)(2,1)S(1)} %shard_map.101), channel_id=1, source_target_pairs={{0,4},{1,5},{4,8},{5,9},{8,12},{9,13},{12,14},{13,15},{14,10},{15,... | collective-permute-start | bytes 1376264 | tf_op jit(solution)/shard_map/ppermute | solution.py:94
  112.7 19.0 %collective-permute-start.23 = (bf16[64,3584]{1,0:T(8,128)(2,1)S(1)}, bf16[64,3584]{1,0:T(8,128)(2,1)S(1)}, u32[]{:S(2)}, u32[]{:S(2)}) collective-permute-start(bf16[64,3584]{1,0:T(8,128)(2,1)S(1)} %shard_map.108), channel_id=1, source_target_pairs={{0,2},{1,3},{4,0},{5,1},{8,4},{9,5},{12,8},{13,9},{14,12},{15,13},... | collective-permute-start | bytes 1376264 | tf_op jit(solution)/shard_map/ppermute | solution.py:94
  122.5 19.0 %collective-permute-start.17 = (bf16[64,3584]{1,0:T(8,128)(2,1)S(1)}, bf16[64,3584]{1,0:T(8,128)(2,1)S(1)}, u32[]{:S(2)}, u32[]{:S(2)}) collective-permute-start(bf16[64,3584]{1,0:T(8,128)(2,1)S(1)} %shard_map.104), channel_id=1, source_target_pairs={{0,2},{1,3},{4,0},{5,1},{8,4},{9,5},{12,8},{13,9},{14,12},{15,13},... | collective-permute-start | bytes 1376264 | tf_op jit(solution)/shard_map/ppermute | solution.py:94
  123.7 19.0 %collective-permute-start.20 = (bf16[64,3584]{1,0:T(8,128)(2,1)S(1)}, bf16[64,3584]{1,0:T(8,128)(2,1)S(1)}, u32[]{:S(2)}, u32[]{:S(2)}) collective-permute-start(bf16[64,3584]{1,0:T(8,128)(2,1)S(1)} %shard_map.106), channel_id=1, source_target_pairs={{0,4},{1,5},{4,8},{5,9},{8,12},{9,13},{12,14},{13,15},{14,10},{15,... | collective-permute-start | bytes 1376264 | tf_op jit(solution)/shard_map/ppermute | solution.py:94
  129.0 19.0 %collective-permute-start.14 = (bf16[64,3584]{1,0:T(8,128)(2,1)S(1)}, bf16[64,3584]{1,0:T(8,128)(2,1)S(1)}, u32[]{:S(2)}, u32[]{:S(2)}) collective-permute-start(bf16[64,3584]{1,0:T(8,128)(2,1)S(1)} %shard_map.102), channel_id=1, source_target_pairs={{0,4},{1,5},{4,8},{5,9},{8,12},{9,13},{12,14},{13,15},{14,10},{15,... | collective-permute-start | bytes 1376264 | tf_op jit(solution)/shard_map/ppermute | solution.py:94
  132.3 19.0 %collective-permute-start.24 = (bf16[64,3584]{1,0:T(8,128)(2,1)S(1)}, bf16[64,3584]{1,0:T(8,128)(2,1)S(1)}, u32[]{:S(2)}, u32[]{:S(2)}) collective-permute-start(bf16[64,3584]{1,0:T(8,128)(2,1)S(1)} %shard_map.109), channel_id=1, source_target_pairs={{0,2},{1,3},{4,0},{5,1},{8,4},{9,5},{12,8},{13,9},{14,12},{15,13},... | collective-permute-start | bytes 1376264 | tf_op jit(solution)/shard_map/ppermute | solution.py:94
  142.2 19.0 %collective-permute-start.18 = (bf16[64,3584]{1,0:T(8,128)(2,1)S(1)}, bf16[64,3584]{1,0:T(8,128)(2,1)S(1)}, u32[]{:S(2)}, u32[]{:S(2)}) collective-permute-start(bf16[64,3584]{1,0:T(8,128)(2,1)S(1)} %shard_map.105), channel_id=1, source_target_pairs={{0,2},{1,3},{4,0},{5,1},{8,4},{9,5},{12,8},{13,9},{14,12},{15,13},... | collective-permute-start | bytes 1376264 | tf_op jit(solution)/shard_map/ppermute | solution.py:94
  143.3 17.8 %collective-permute-start.21 = (bf16[64,3584]{1,0:T(8,128)(2,1)S(1)}, bf16[64,3584]{1,0:T(8,128)(2,1)S(1)}, u32[]{:S(2)}, u32[]{:S(2)}) collective-permute-start(bf16[64,3584]{1,0:T(8,128)(2,1)S(1)} %shard_map.107), channel_id=1, source_target_pairs={{0,4},{1,5},{4,8},{5,9},{8,12},{9,13},{12,14},{13,15},{14,10},{15,... | collective-permute-start | bytes 1376264 | tf_op jit(solution)/shard_map/ppermute | solution.py:94
  148.6 16.6 %collective-permute-start.15 = (bf16[64,3584]{1,0:T(8,128)(2,1)S(1)}, bf16[64,3584]{1,0:T(8,128)(2,1)S(1)}, u32[]{:S(2)}, u32[]{:S(2)}) collective-permute-start(bf16[64,3584]{1,0:T(8,128)(2,1)S(1)} %shard_map.103), channel_id=1, source_target_pairs={{0,4},{1,5},{4,8},{5,9},{8,12},{9,13},{12,14},{13,15},{14,10},{15,... | collective-permute-start | bytes 1376264 | tf_op jit(solution)/shard_map/ppermute | solution.py:94
  152.0 14.6 %collective-permute-start.25 = (bf16[64,3584]{1,0:T(8,128)(2,1)S(1)}, bf16[64,3584]{1,0:T(8,128)(2,1)S(1)}, u32[]{:S(2)}, u32[]{:S(2)}) collective-permute-start(bf16[64,3584]{1,0:T(8,128)(2,1)S(1)} %shard_map.110), channel_id=1, source_target_pairs={{0,2},{1,3},{4,0},{5,1},{8,4},{9,5},{12,8},{13,9},{14,12},{15,13},... | collective-permute-start | bytes 1376264 | tf_op jit(solution)/shard_map/ppermute | solution.py:94

commit v7 on v6

--- a/solution.py
+++ b/solution.py
@@ -96,13 +96,14 @@
 
 COST_SCALE = 3
 VMEM_BYTES = 20 * 1024 * 1024
+WIDE_VMEM_BYTES = 60 * 1024 * 1024
 IN_VMEM = pl.BlockSpec(memory_space=pltpu.VMEM)
 IN_SMEM = pl.BlockSpec(memory_space=pltpu.SMEM)
 IN_HBM = pl.BlockSpec(memory_space=pltpu.HBM)
 
 
 def local_call(
-    kernel, out_shape, operands, flops, bytes_accessed, aliases=None, scratch=(), far=()
+    kernel, out_shape, operands, flops, bytes_accessed, aliases=None, scratch=(), far=(), vmem_bytes=None
 ):
     return pl.pallas_call(
         kernel,
@@ -115,7 +116,7 @@
         ),
         scratch_shapes=list(scratch),
         input_output_aliases=aliases or {},
-        compiler_params=pltpu.CompilerParams(vmem_limit_bytes=VMEM_BYTES),
+        compiler_params=pltpu.CompilerParams(vmem_limit_bytes=vmem_bytes or VMEM_BYTES),
         cost_estimate=pl.CostEstimate(
             flops=flops, bytes_accessed=bytes_accessed, transcendentals=0
         ),
@@ -417,6 +418,7 @@
         [where, table, moved],
         flops=rows * width,
         bytes_accessed=rows * width * 6,
+        vmem_bytes=WIDE_VMEM_BYTES,
     )
 
 
@@ -516,7 +518,7 @@
         )
         owns.extend(made)
         positions.extend(group)
-        if group == groups[max(far - 3, 0)]:
+        if group == groups[max(far - 2, 0)]:
             lower, upper, carried = lax.optimization_barrier(
                 (blocks[1 - far], blocks[far - 1], carried)
             )

time: 168 us -> 166 us (0.988)
  waiting for transfers between devices: 93.8 us -> 49.3 us
  Pallas kernels: 44.2 us -> 68.7 us
  local copies, waits for them, and re-layouts: 1.55 us -> 21.2 us
  starting transfers between devices: 26.6 us -> 24.6 us
    ppermute x22, waiting for transfers between devices: 92.3 us -> 47.7 us  [ring_shift(): return lax.ppermute(value, 'ep', pairs)]
    pallas_call x21, Pallas kernels: 44.2 us -> 68.7 us  [local_call(): pl.pallas_call(kernel, out_shape=out_shape, in_specs=[IN_SMEM if k == 0 e...]
    unnamed x8 -> x68, local copies, waits for them, and re-layouts: 0.2 us -> 19.8 us
    ppermute x22, starting transfers between devices: 25.2 us -> 23.2 us  [ring_shift(): return lax.ppermute(value, 'ep', pairs)]
  transfers between devices with their start and end apart: 26 -> 26, of which waited for: 16 -> 8; matrix products, arithmetic and copies ran while one was open for 1% -> 1% of each run, Pallas kernels for 23% -> 38%
where the time goes in v7:
time: 166 us
  Pallas kernels  68.7 us (41%)
  waiting for transfers between devices  49.3 us (30%)
  starting transfers between devices  24.6 us (15%)
  local copies, waits for them, and re-layouts  21.2 us (13%)
  other arithmetic  1.82 us (1%)
    pallas_call x21, Pallas kernels, local_call(): pl.pallas_call(kernel, out_shape=out_shape, in_specs=[IN_SMEM if k == 0 e...  68.7 us
    ppermute x22, waiting for transfers between devices, ring_shift(): return lax.ppermute(value, 'ep', pairs)  47.7 us
    ppermute x22, starting transfers between devices, ring_shift(): return lax.ppermute(value, 'ep', pairs)  23.2 us
    unnamed x68, local copies, waits for them, and re-layouts  19.8 us
  transfers between devices with their start and end apart: 26, of which 8 were waited for; matrix products, arithmetic and copies ran while one was open for 1% of the time, Pallas kernels for 38%

profile of v7, /device:TPU:0, one launch (start us, length us, event | category | flops | bytes accessed | tf_op | source)
XLA Modules:
  0.0 165.9 jit_solution(3983392514054359831)
XLA Ops:
  0.0 1.8 %add_convert_fusion = bf16[1024,448]{0,1:T(8,128)(2,1)S(1)} fusion(bf16[1024,448]{0,1:T(8,128)(2,1)} %param.10, bf16[1024,448]{0,1:T(8,128)(2,1)} %param.9), kind=kLoop, calls=%fused_computation | loop fusion | flops 1835008 | bytes 2752512 | tf_op jit(solution)/shard_map/convert_element_type | solution.py:491
  3.0 1.5 collective-permute-done.swapped_ref
  6.3 1.3 shard_map.91.refs_0_.refs_5_
  7.5 2.8 %collective-permute-start.4 = (bf16[528,896]{1,0:T(8,128)(2,1)S(1)}, bf16[528,896]{1,0:T(8,128)(2,1)S(1)}, u32[]{:S(2)}, u32[]{:S(2)}) collective-permute-start(bf16[528,896]{1,0:T(8,128)(2,1)S(1)} %shard_map.91.refs_0_.refs_5_), channel_id=1, source_target_pairs={{0,4},{1,5},{4,8},{5,9},{8,12},{9,13},{12,14},{13,15},{14,10},{15,... | collective-permute-start | bytes 2838536 | tf_op jit(solution)/shard_map/ppermute | solution.py:94
  10.3 21.4 %collective-permute-done.4.refs_1_.refs_12_ = bf16[528,896]{1,0:T(8,128)(2,1)S(1)} collective-permute-done((bf16[528,896]{1,0:T(8,128)(2,1)S(1)}, bf16[528,896]{1,0:T(8,128)(2,1)S(1)}, u32[]{:S(2)}, u32[]{:S(2)}) %collective-permute-start.4) | collective-permute-done | bytes 946208 | tf_op jit(solution)/shard_map/ppermute | solution.py:94
  31.7 1.8 %collective-permute-start.6 = (bf16[528,896]{1,0:T(8,128)(2,1)S(1)}, bf16[528,896]{1,0:T(8,128)(2,1)S(1)}, u32[]{:S(2)}, u32[]{:S(2)}) collective-permute-start(bf16[528,896]{1,0:T(8,128)(2,1)S(1)} %collective-permute-done.4.refs_1_.refs_12_), channel_id=1, source_target_pairs={{0,4},{1,5},{4,8},{5,9},{8,12},{9,13},{12,14},{13,15},{14,10},{15,... | collective-permute-start | bytes 2838536 | tf_op jit(solution)/shard_map/ppermute | solution.py:94
  33.8 20.6 %collective-permute-done.6.refs_1_.refs_11_ = bf16[528,896]{1,0:T(8,128)(2,1)S(1)} collective-permute-done((bf16[528,896]{1,0:T(8,128)(2,1)S(1)}, bf16[528,896]{1,0:T(8,128)(2,1)S(1)}, u32[]{:S(2)}, u32[]{:S(2)}) %collective-permute-start.6) | collective-permute-done | bytes 946208 | tf_op jit(solution)/shard_map/ppermute | solution.py:94
  54.4 1.6 collective-permute-start.8
  56.5 4.4 %shard_map.92 = (bf16[64,896]{1,0:T(8,128)(2,1)S(1)}, f32[512,1024]{1,0:T(8,128)S(1)}) custom-call(s32[10]{0:T(128)S(1)} %dynamic-slice_bitcast_fusion.1.where_ref, bf16[528,896]{1,0:T(8,128)(2,1)S(1)} %shard_map.91.refs_0_.refs_5_, f32[8,1,896]{2,1,0:T(1,128)S(1)} %bitcast.8, bf16[7168,256]{1,0:T(8,128)(2,1)} %refs_3_.3, bf16[7168,256]{1,0:T(8,128)(2,1)} %refs_4_.2, ...), custom_call_target="tpu_custom_call" | custom-call | flops 2818572288 | bytes 6946816 | tf_op jit(solution)/shard_map/pallas_call | solution.py:108
  60.9 6.8 %shard_map.93 = (bf16[64,896]{1,0:T(8,128)(2,1)S(1)}, bf16[64,896]{1,0:T(8,128)(2,1)S(1)}, f32[512,1024]{1,0:T(8,128)S(1)}) custom-call(s32[10]{0:T(128)S(1)} %dynamic-slice_bitcast_fusion.1.where_ref, bf16[528,896]{1,0:T(8,128)(2,1)S(1)} %collective-permute-done.3.refs_0_.refs_6_, ...), custom_call_target="tpu_custom_call", output_to_operand_aliasing={{2}: (8, {})} | custom-call | flops 5637144576 | bytes 9699328 | tf_op jit(solution)/shard_map/pallas_call | solution.py:108
  67.7 6.8 %shard_map.94 = (bf16[64,896]{1,0:T(8,128)(2,1)S(1)}, bf16[64,896]{1,0:T(8,128)(2,1)S(1)}, f32[512,1024]{1,0:T(8,128)S(1)}) custom-call(s32[10]{0:T(128)S(1)} %dynamic-slice_bitcast_fusion.1.where_ref, bf16[528,896]{1,0:T(8,128)(2,1)S(1)} %collective-permute-done.5.refs_0_.refs_7_, ...), custom_call_target="tpu_custom_call", output_to_operand_aliasing={{2}: (8, {})} | custom-call | flops 5637144576 | bytes 9699328 | tf_op jit(solution)/shard_map/pallas_call | solution.py:108
  74.5 1.7 %collective-permute-done.8.refs_1_.refs_10_ = bf16[528,896]{1,0:T(8,128)(2,1)S(1)} collective-permute-done((bf16[528,896]{1,0:T(8,128)(2,1)S(1)}, bf16[528,896]{1,0:T(8,128)(2,1)S(1)}, u32[]{:S(2)}, u32[]{:S(2)}) %collective-permute-start.8) | collective-permute-done | bytes 946208 | tf_op jit(solution)/shard_map/ppermute | solution.py:94
  76.2 1.0 collective-permute-done.7.refs_0_.refs_8_
  77.2 0.8 collective-permute-start.11
  78.1 1.3 collective-permute-start.10
  79.4 6.8 %shard_map.95 = (bf16[64,896]{1,0:T(8,128)(2,1)S(1)}, bf16[64,896]{1,0:T(8,128)(2,1)S(1)}, f32[512,1024]{1,0:T(8,128)S(1)}, bf16[4,896,256]{2,1,0:T(8,128)(2,1)S(1)}, bf16[512,7168]{1,0:T(8,128)(2,1)S(1)}) custom-call(s32[10]{0:T(128)S(1)} %dynamic-slice_bitcast_fusion.1.where_ref, ...), custom_call_target="tpu_custom_call", output_to_operand_aliasing={{2}: (8, {})} | custom-call | flops 5637144576 | bytes 9699328 | tf_op jit(solution)/shard_map/pallas_call | solution.py:108
  86.2 0.9 collective-permute-done.11.refs_1_
  87.2 1.5 collective-permute-done.10.refs_0_.refs_9_
  88.6 2.0 %shard_map.96 = (bf16[64,896]{1,0:T(8,128)(2,1)S(1)}, bf16[512,512]{1,0:T(8,128)(2,1)S(1)}) custom-call(s32[10]{0:T(128)S(1)} %dynamic-slice_bitcast_fusion.1.where_ref, bf16[272,896]{1,0:T(8,128)(2,1)S(1)} %collective-permute-done.10.refs_0_.refs_9_, bf16[256,896]{1,0:T(8,128)(2,1)S(1)} %collective-permute-done.11.refs_1_, f32[8,1,896]{2,1,0:T(1,128)S(1)} %bitcast.12, ...), custom_call_target="tpu_custom_call" | custom-call | flops 2818572288 | bytes 6946816 | tf_op jit(solution)/shard_map/pallas_call | solution.py:108
  90.7 1.8 %shard_map.97 = (bf16[512,512]{1,0:T(8,128)(2,1)S(1)}, bf16[64,3584]{1,0:T(8,128)(2,1)S(1)}, bf16[64,3584]{1,0:T(8,128)(2,1)S(1)}, bf16[64,3584]{1,0:T(8,128)(2,1)S(1)}, bf16[64,3584]{1,0:T(8,128)(2,1)S(1)}) custom-call(s32[10]{0:T(128)S(1)} %dynamic-slice_bitcast_fusion.1.where_ref, bf16[512,512]{1,0:T(8,128)(2,1)S(1)} %get-tuple-element.52.hidden_ref, ...), custom_call_target="tpu_custom_call" | custom-call | flops 939524096 | bytes 7340032 | tf_op jit(solution)/shard_map/pallas_call | solution.py:108
  92.5 1.1 collective-permute-start.22
  93.6 1.0 collective-permute-start.12
  94.6 1.0 collective-permute-start.19
  95.6 2.6 %shard_map.99.refs_9_.table_ref = bf16[512,3584]{1,0:T(8,128)(2,1)S(1)} custom-call(s32[10]{0:T(128)S(1)} %dynamic-slice_bitcast_fusion.1.where_ref, bf16[512,512]{1,0:T(8,128)(2,1)S(1)} %get-tuple-element.54.hidden_ref, bf16[512,7168]{1,0:T(8,128)(2,1)S(1)} %get-tuple-element.53.down_ref), custom_call_target="tpu_custom_call" | custom-call | flops 1879048192 | bytes 7340032 | tf_op jit(solution)/shard_map/pallas_call | solution.py:108
  98.3 1.8 %copy-done = bf16[512,3584]{1,0:T(8,128)(2,1)} copy-done((bf16[512,3584]{1,0:T(8,128)(2,1)}, bf16[512,3584]{1,0:T(8,128)(2,1)S(1)}, u32[]{:S(2)}) %copy-start) | copy-done | bytes 3670040
  100.1 2.6 %shard_map.98.refs_8_.table_ref = bf16[512,3584]{1,0:T(8,128)(2,1)S(1)} custom-call(s32[10]{0:T(128)S(1)} %dynamic-slice_bitcast_fusion.1.where_ref, bf16[512,512]{1,0:T(8,128)(2,1)S(1)} %get-tuple-element.54.hidden_ref, bf16[512,7168]{1,0:T(8,128)(2,1)S(1)} %get-tuple-element.53.down_ref), custom_call_target="tpu_custom_call" | custom-call | flops 1879048192 | bytes 7340032 | tf_op jit(solution)/shard_map/pallas_call | solution.py:108
  102.7 1.8 %copy-done.2 = bf16[512,3584]{1,0:T(8,128)(2,1)} copy-done((bf16[512,3584]{1,0:T(8,128)(2,1)}, bf16[512,3584]{1,0:T(8,128)(2,1)S(1)}, u32[]{:S(2)}) %copy-start.2) | copy-done | bytes 3670040
  104.5 1.0 collective-permute-start.16
  106.3 3.0 %shard_map.108 = bf16[64,3584]{1,0:T(8,128)(2,1)} custom-call(s32[10]{0:T(128)} %copy-done.5, bf16[512,3584]{1,0:T(8,128)(2,1)} %copy-done, bf16[64,3584]{1,0:T(8,128)(2,1)} %copy-done.30), custom_call_target="tpu_custom_call" | custom-call | flops 229376 | bytes 1376256 | tf_op jit(solution)/shard_map/pallas_call | solution.py:108
  109.3 1.0 collective-permute-start.23
  111.1 3.0 %shard_map.101 = bf16[64,3584]{1,0:T(8,128)(2,1)} custom-call(s32[10]{0:T(128)} %copy-done.5, bf16[512,3584]{1,0:T(8,128)(2,1)} %copy-done.2, bf16[64,3584]{1,0:T(8,128)(2,1)} %copy-done.29), custom_call_target="tpu_custom_call" | custom-call | flops 229376 | bytes 1376256 | tf_op jit(solution)/shard_map/pallas_call | solution.py:108
  114.2 1.0 collective-permute-start.13
  115.1 0.8 copy-done.28
  115.9 3.1 %shard_map.106 = bf16[64,3584]{1,0:T(8,128)(2,1)} custom-call(s32[10]{0:T(128)} %copy-done.5, bf16[512,3584]{1,0:T(8,128)(2,1)} %copy-done, bf16[64,3584]{1,0:T(8,128)(2,1)} %copy-done.28), custom_call_target="tpu_custom_call" | custom-call | flops 229376 | bytes 1376256 | tf_op jit(solution)/shard_map/pallas_call | solution.py:108
  119.0 1.0 collective-permute-start.20
  120.0 0.8 copy-done.23
  120.8 3.1 %shard_map.104 = bf16[64,3584]{1,0:T(8,128)(2,1)} custom-call(s32[10]{0:T(128)} %copy-done.5, bf16[512,3584]{1,0:T(8,128)(2,1)} %copy-done.2, bf16[64,3584]{1,0:T(8,128)(2,1)} %copy-done.23), custom_call_target="tpu_custom_call" | custom-call | flops 229376 | bytes 1376256 | tf_op jit(solution)/shard_map/pallas_call | solution.py:108
  123.9 1.0 collective-permute-start.17
  125.7 3.0 %shard_map.109 = bf16[64,3584]{1,0:T(8,128)(2,1)} custom-call(s32[10]{0:T(128)} %copy-done.5, bf16[512,3584]{1,0:T(8,128)(2,1)} %copy-done, bf16[64,3584]{1,0:T(8,128)(2,1)} %copy-done.24), custom_call_target="tpu_custom_call" | custom-call | flops 229376 | bytes 1376256 | tf_op jit(solution)/shard_map/pallas_call | solution.py:108
  128.7 1.0 collective-permute-start.24
  129.7 0.8 copy-done.25
  130.5 3.0 %shard_map.102 = bf16[64,3584]{1,0:T(8,128)(2,1)} custom-call(s32[10]{0:T(128)} %copy-done.5, bf16[512,3584]{1,0:T(8,128)(2,1)} %copy-done.2, bf16[64,3584]{1,0:T(8,128)(2,1)} %copy-done.25), custom_call_target="tpu_custom_call" | custom-call | flops 229376 | bytes 1376256 | tf_op jit(solution)/shard_map/pallas_call | solution.py:108
  133.5 1.0 collective-permute-start.14
  134.5 0.8 copy-done.26
  135.3 3.1 %shard_map.107 = bf16[64,3584]{1,0:T(8,128)(2,1)} custom-call(s32[10]{0:T(128)} %copy-done.5, bf16[512,3584]{1,0:T(8,128)(2,1)} %copy-done, bf16[64,3584]{1,0:T(8,128)(2,1)} %copy-done.26), custom_call_target="tpu_custom_call" | custom-call | flops 229376 | bytes 1376256 | tf_op jit(solution)/shard_map/pallas_call | solution.py:108
  138.4 1.0 collective-permute-start.21
  139.4 0.8 copy-done.27
  140.1 3.0 %shard_map.105 = bf16[64,3584]{1,0:T(8,128)(2,1)} custom-call(s32[10]{0:T(128)} %copy-done.5, bf16[512,3584]{1,0:T(8,128)(2,1)} %copy-done.2, bf16[64,3584]{1,0:T(8,128)(2,1)} %copy-done.27), custom_call_target="tpu_custom_call" | custom-call | flops 229376 | bytes 1376256 | tf_op jit(solution)/shard_map/pallas_call | solution.py:108
  143.2 1.0 collective-permute-start.18
  144.7 3.0 %shard_map.110 = bf16[64,3584]{1,0:T(8,128)(2,1)} custom-call(s32[10]{0:T(128)} %copy-done.5, bf16[512,3584]{1,0:T(8,128)(2,1)} %copy-done, bf16[64,3584]{1,0:T(8,128)(2,1)} %collective-permute-done.24.moved_ref), custom_call_target="tpu_custom_call" | custom-call | flops 229376 | bytes 1376256 | tf_op jit(solution)/shard_map/pallas_call | solution.py:108
  147.8 1.1 collective-permute-start.25
  148.8 3.0 %shard_map.103 = bf16[64,3584]{1,0:T(8,128)(2,1)} custom-call(s32[10]{0:T(128)} %copy-done.5, bf16[512,3584]{1,0:T(8,128)(2,1)} %copy-done.2, bf16[64,3584]{1,0:T(8,128)(2,1)} %collective-permute-done.14.moved_ref), custom_call_target="tpu_custom_call" | custom-call | flops 229376 | bytes 1376256 | tf_op jit(solution)/shard_map/pallas_call | solution.py:108
  151.9 1.0 collective-permute-start.15
  152.8 2.0 %copy-done.3 = bf16[512,3584]{1,0:T(8,128)(2,1)S(1)} copy-done((bf16[512,3584]{1,0:T(8,128)(2,1)S(1)}, bf16[512,3584]{1,0:T(8,128)(2,1)}, u32[]{:S(2)}) %copy-start.3) | copy-done | bytes 3670040
  155.5 0.9 copy-done.8
  156.4 0.9 copy-done.10
  157.3 0.9 copy-done.12
  158.2 0.9 copy-done.14
  159.1 0.9 copy-done.16
  160.0 0.9 copy-done.18
  160.9 0.9 copy-done.20
  161.8 0.9 copy-done.22
  162.7 0.8 shard_map.100.base_ref
  163.6 2.4 %shard_map.111 = bf16[64,7168]{1,0:T(8,128)(2,1)} custom-call(s32[10]{0:T(128)S(1)} %copy-done.6, f32[64,7168]{1,0:T(8,128)S(1)} %shard_map.100.base_ref, bf16[64,3584]{1,0:T(8,128)(2,1)S(1)} %collective-permute-done.15.refs_0_, bf16[64,3584]{1,0:T(8,128)(2,1)} %collective-permute-done.18.refs_1_, bf16[64,3584]{1,0:T(8,128)(2,1)S(1)} %collective-permute-done.21.refs_2_, ...), custom_call_target="tpu_custom_call" | custom-call | flops 1376256 | bytes 4587520 | tf_op jit(solution)/shard_map/pallas_call | solution.py:108
  (83 shorter events, 7.3 us)
Async XLA Ops:
  0.0 5.4 %copy-start.31 = (s32[64,2]{0,1:T(2,128)S(1)}, s32[64,2]{0,1:T(2,128)}, u32[]{:S(2)}) copy-start(s32[64,2]{0,1:T(2,128)} %param.12) | copy-start | bytes 1540
  0.0 5.5 %copy-start.32 = (f32[64,2]{0,1:T(2,128)S(1)}, f32[64,2]{0,1:T(2,128)}, u32[]{:S(2)}) copy-start(f32[64,2]{0,1:T(2,128)} %param.13) | copy-start | bytes 1540
  0.0 56.4 %copy-start.4 = (f32[7168]{0:T(1024)S(1)}, f32[7168]{0:T(1024)}, u32[]{:S(2)}) copy-start(f32[7168]{0:T(1024)} %param.11) | copy-start | bytes 86020
  2.4 2.1 %collective-permute-start = (bf16[8,64,448]{2,1,0:T(8,128)(2,1)S(1)}, bf16[8,64,448]{2,1,0:T(8,128)(2,1)S(1)}, u32[]{:S(2)}, u32[]{:S(2)}) collective-permute-start(bf16[8,64,448]{2,1,0:T(8,128)(2,1)S(1)} %dynamic-slice_bitcast_fusion), channel_id=1, source_target_pairs={{0,1},{1,0},{2,3},{3,2},{4,5},{5,4},{6,7},{7,6},{8,9},{9,8},{10,11... | collective-permute-start | bytes 1376264 | tf_op jit(solution)/shard_map/ppermute | solution.py:84
  4.5 51.9 %collective-permute-start.1 = (bf16[7168,256]{1,0:T(8,128)(2,1)}, bf16[7168,256]{1,0:T(8,128)(2,1)}, u32[]{:S(2)}, u32[]{:S(2)}) collective-permute-start(bf16[7168,256]{1,0:T(8,128)(2,1)} %refs_3_.3), channel_id=1, source_target_pairs={{0,1},{1,0},{2,3},{3,2},{4,5},{5,4},{6,7},{7,6},{8,9},{9,8},{10,11... | collective-permute-start | bytes 11010056 | tf_op jit(solution)/shard_map/ppermute | solution.py:84
  4.9 51.6 %collective-permute-start.2 = (bf16[7168,256]{1,0:T(8,128)(2,1)}, bf16[7168,256]{1,0:T(8,128)(2,1)}, u32[]{:S(2)}, u32[]{:S(2)}) collective-permute-start(bf16[7168,256]{1,0:T(8,128)(2,1)} %refs_4_.2), channel_id=1, source_target_pairs={{0,1},{1,0},{2,3},{3,2},{4,5},{5,4},{6,7},{7,6},{8,9},{9,8},{10,11... | collective-permute-start | bytes 11010056 | tf_op jit(solution)/shard_map/ppermute | solution.py:84
  5.0 74.4 %collective-permute-start.9 = (bf16[256,7168]{1,0:T(8,128)(2,1)}, bf16[256,7168]{1,0:T(8,128)(2,1)}, u32[]{:S(2)}, u32[]{:S(2)}) collective-permute-start(bf16[256,7168]{1,0:T(8,128)(2,1)} %refs_8_), channel_id=1, source_target_pairs={{0,1},{1,0},{2,3},{3,2},{4,5},{5,4},{6,7},{7,6},{8,9},{9,8},{10,11... | collective-permute-start | bytes 11010056 | tf_op jit(solution)/shard_map/ppermute | solution.py:84
  6.3 92.0 %copy-start.5 = (s32[10]{0:T(128)}, s32[10]{0:T(128)S(1)}, u32[]{:S(2)}) copy-start(s32[10]{0:T(128)S(1)} %dynamic-slice_bitcast_fusion.1.where_ref) | copy-start | bytes 124
  7.5 24.2 %collective-permute-start.4 = (bf16[528,896]{1,0:T(8,128)(2,1)S(1)}, bf16[528,896]{1,0:T(8,128)(2,1)S(1)}, u32[]{:S(2)}, u32[]{:S(2)}) collective-permute-start(bf16[528,896]{1,0:T(8,128)(2,1)S(1)} %shard_map.91.refs_0_.refs_5_), channel_id=1, source_target_pairs={{0,4},{1,5},{4,8},{5,9},{8,12},{9,13},{12,14},{13,15},{14,10},{15,... | collective-permute-start | bytes 2838536 | tf_op jit(solution)/shard_map/ppermute | solution.py:94
  10.3 23.2 %collective-permute-start.3 = (bf16[528,896]{1,0:T(8,128)(2,1)S(1)}, bf16[528,896]{1,0:T(8,128)(2,1)S(1)}, u32[]{:S(2)}, u32[]{:S(2)}) collective-permute-start(bf16[528,896]{1,0:T(8,128)(2,1)S(1)} %shard_map.91.refs_0_.refs_5_), channel_id=1, source_target_pairs={{0,2},{1,3},{4,0},{5,1},{8,4},{9,5},{12,8},{13,9},{14,12},{15,13},... | collective-permute-start | bytes 2838536 | tf_op jit(solution)/shard_map/ppermute | solution.py:94
  31.7 22.7 %collective-permute-start.6 = (bf16[528,896]{1,0:T(8,128)(2,1)S(1)}, bf16[528,896]{1,0:T(8,128)(2,1)S(1)}, u32[]{:S(2)}, u32[]{:S(2)}) collective-permute-start(bf16[528,896]{1,0:T(8,128)(2,1)S(1)} %collective-permute-done.4.refs_1_.refs_12_), channel_id=1, source_target_pairs={{0,4},{1,5},{4,8},{5,9},{8,12},{9,13},{12,14},{13,15},{14,10},{15,... | collective-permute-start | bytes 2838536 | tf_op jit(solution)/shard_map/ppermute | solution.py:94
  33.5 22.4 %collective-permute-start.5 = (bf16[528,896]{1,0:T(8,128)(2,1)S(1)}, bf16[528,896]{1,0:T(8,128)(2,1)S(1)}, u32[]{:S(2)}, u32[]{:S(2)}) collective-permute-start(bf16[528,896]{1,0:T(8,128)(2,1)S(1)} %collective-permute-done.3.refs_0_.refs_6_), channel_id=1, source_target_pairs={{0,2},{1,3},{4,0},{5,1},{8,4},{9,5},{12,8},{13,9},{14,12},{15,13},... | collective-permute-start | bytes 2838536 | tf_op jit(solution)/shard_map/ppermute | solution.py:94
  54.4 21.8 %collective-permute-start.8 = (bf16[528,896]{1,0:T(8,128)(2,1)S(1)}, bf16[528,896]{1,0:T(8,128)(2,1)S(1)}, u32[]{:S(2)}, u32[]{:S(2)}) collective-permute-start(bf16[528,896]{1,0:T(8,128)(2,1)S(1)} %collective-permute-done.6.refs_1_.refs_11_), channel_id=1, source_target_pairs={{0,4},{1,5},{4,8},{5,9},{8,12},{9,13},{12,14},{13,15},{14,10},{15,... | collective-permute-start | bytes 2838536 | tf_op jit(solution)/shard_map/ppermute | solution.py:94
  56.0 21.2 %collective-permute-start.7 = (bf16[528,896]{1,0:T(8,128)(2,1)S(1)}, bf16[528,896]{1,0:T(8,128)(2,1)S(1)}, u32[]{:S(2)}, u32[]{:S(2)}) collective-permute-start(bf16[528,896]{1,0:T(8,128)(2,1)S(1)} %collective-permute-done.5.refs_0_.refs_7_), channel_id=1, source_target_pairs={{0,2},{1,3},{4,0},{5,1},{8,4},{9,5},{12,8},{13,9},{14,12},{15,13},... | collective-permute-start | bytes 2838536 | tf_op jit(solution)/shard_map/ppermute | solution.py:94
  60.9 6.8 %copy-start.7 = (bf16[64,896]{1,0:T(8,128)(2,1)}, bf16[64,896]{1,0:T(8,128)(2,1)S(1)}, u32[]{:S(2)}) copy-start(bf16[64,896]{1,0:T(8,128)(2,1)S(1)} %get-tuple-element.35.refs_0_) | copy-start | bytes 344068
  67.7 6.8 %copy-start.9 = (bf16[64,896]{1,0:T(8,128)(2,1)}, bf16[64,896]{1,0:T(8,128)(2,1)S(1)}, u32[]{:S(2)}) copy-start(bf16[64,896]{1,0:T(8,128)(2,1)S(1)} %get-tuple-element.37.refs_1_) | copy-start | bytes 344068
  67.7 6.8 %copy-start.11 = (bf16[64,896]{1,0:T(8,128)(2,1)}, bf16[64,896]{1,0:T(8,128)(2,1)S(1)}, u32[]{:S(2)}) copy-start(bf16[64,896]{1,0:T(8,128)(2,1)S(1)} %get-tuple-element.38.refs_2_) | copy-start | bytes 344068
  74.5 3.5 %copy-start.13 = (bf16[64,896]{1,0:T(8,128)(2,1)}, bf16[64,896]{1,0:T(8,128)(2,1)S(1)}, u32[]{:S(2)}) copy-start(bf16[64,896]{1,0:T(8,128)(2,1)S(1)} %get-tuple-element.40.refs_3_) | copy-start | bytes 344068
  74.5 3.5 %copy-start.15 = (bf16[64,896]{1,0:T(8,128)(2,1)}, bf16[64,896]{1,0:T(8,128)(2,1)S(1)}, u32[]{:S(2)}) copy-start(bf16[64,896]{1,0:T(8,128)(2,1)S(1)} %get-tuple-element.41.refs_4_) | copy-start | bytes 344068
  77.2 9.9 %collective-permute-start.11 = (bf16[256,896]{1,0:T(8,128)(2,1)S(1)}, bf16[256,896]{1,0:T(8,128)(2,1)S(1)}, u32[]{:S(2)}, u32[]{:S(2)}) collective-permute-start(bf16[256,896]{1,0:T(8,128)(2,1)S(1)} %slice.7), channel_id=1, source_target_pairs={{0,2},{1,3},{4,0},{5,1},{8,4},{9,5},{12,8},{13,9},{14,12},{15,13},... | collective-permute-start | bytes 1376264 | tf_op jit(solution)/shard_map/ppermute | solution.py:94
  78.1 10.5 %collective-permute-start.10 = (bf16[272,896]{1,0:T(8,128)(2,1)S(1)}, bf16[272,896]{1,0:T(8,128)(2,1)S(1)}, u32[]{:S(2)}, u32[]{:S(2)}) collective-permute-start(bf16[272,896]{1,0:T(8,128)(2,1)S(1)} %slice.6), channel_id=1, source_target_pairs={{0,4},{1,5},{4,8},{5,9},{8,12},{9,13},{12,14},{13,15},{14,10},{15,... | collective-permute-start | bytes 1462280 | tf_op jit(solution)/shard_map/ppermute | solution.py:94
  86.2 4.5 %copy-start.17 = (bf16[64,896]{1,0:T(8,128)(2,1)}, bf16[64,896]{1,0:T(8,128)(2,1)S(1)}, u32[]{:S(2)}) copy-start(bf16[64,896]{1,0:T(8,128)(2,1)S(1)} %get-tuple-element.45.refs_5_) | copy-start | bytes 344068
  86.2 4.5 %copy-start.19 = (bf16[64,896]{1,0:T(8,128)(2,1)}, bf16[64,896]{1,0:T(8,128)(2,1)S(1)}, u32[]{:S(2)}) copy-start(bf16[64,896]{1,0:T(8,128)(2,1)S(1)} %get-tuple-element.46.refs_6_) | copy-start | bytes 344068
  90.7 1.8 %copy-start.21 = (bf16[64,896]{1,0:T(8,128)(2,1)}, bf16[64,896]{1,0:T(8,128)(2,1)S(1)}, u32[]{:S(2)}) copy-start(bf16[64,896]{1,0:T(8,128)(2,1)S(1)} %get-tuple-element.51.refs_7_) | copy-start | bytes 344068
  92.5 13.0 %collective-permute-start.22 = (bf16[64,3584]{1,0:T(8,128)(2,1)S(1)}, bf16[64,3584]{1,0:T(8,128)(2,1)S(1)}, u32[]{:S(2)}, u32[]{:S(2)}) collective-permute-start(bf16[64,3584]{1,0:T(8,128)(2,1)S(1)} %get-tuple-element.58), channel_id=1, source_target_pairs={{0,2},{1,3},{4,0},{5,1},{8,4},{9,5},{12,8},{13,9},{14,12},{15,13},... | collective-permute-start | bytes 1376264 | tf_op jit(solution)/shard_map/ppermute | solution.py:94
  93.6 16.7 %collective-permute-start.12 = (bf16[64,3584]{1,0:T(8,128)(2,1)S(1)}, bf16[64,3584]{1,0:T(8,128)(2,1)S(1)}, u32[]{:S(2)}, u32[]{:S(2)}) collective-permute-start(bf16[64,3584]{1,0:T(8,128)(2,1)S(1)} %get-tuple-element.55), channel_id=1, source_target_pairs={{0,4},{1,5},{4,8},{5,9},{8,12},{9,13},{12,14},{13,15},{14,10},{15,... | collective-permute-start | bytes 1376264 | tf_op jit(solution)/shard_map/ppermute | solution.py:94
  94.6 20.5 %collective-permute-start.19 = (bf16[64,3584]{1,0:T(8,128)(2,1)S(1)}, bf16[64,3584]{1,0:T(8,128)(2,1)S(1)}, u32[]{:S(2)}, u32[]{:S(2)}) collective-permute-start(bf16[64,3584]{1,0:T(8,128)(2,1)S(1)} %get-tuple-element.57), channel_id=1, source_target_pairs={{0,4},{1,5},{4,8},{5,9},{8,12},{9,13},{12,14},{13,15},{14,10},{15,... | collective-permute-start | bytes 1376264 | tf_op jit(solution)/shard_map/ppermute | solution.py:94
  98.3 1.8 %copy-start = (bf16[512,3584]{1,0:T(8,128)(2,1)}, bf16[512,3584]{1,0:T(8,128)(2,1)S(1)}, u32[]{:S(2)}) copy-start(bf16[512,3584]{1,0:T(8,128)(2,1)S(1)} %shard_map.99.refs_9_.table_ref) | copy-start | bytes 11010052
  102.7 1.8 %copy-start.2 = (bf16[512,3584]{1,0:T(8,128)(2,1)}, bf16[512,3584]{1,0:T(8,128)(2,1)S(1)}, u32[]{:S(2)}) copy-start(bf16[512,3584]{1,0:T(8,128)(2,1)S(1)} %shard_map.98.refs_8_.table_ref) | copy-start | bytes 11010052
  104.5 15.5 %collective-permute-start.16 = (bf16[64,3584]{1,0:T(8,128)(2,1)S(1)}, bf16[64,3584]{1,0:T(8,128)(2,1)S(1)}, u32[]{:S(2)}, u32[]{:S(2)}) collective-permute-start(bf16[64,3584]{1,0:T(8,128)(2,1)S(1)} %get-tuple-element.56), channel_id=1, source_target_pairs={{0,2},{1,3},{4,0},{5,1},{8,4},{9,5},{12,8},{13,9},{14,12},{15,13},... | collective-permute-start | bytes 1376264 | tf_op jit(solution)/shard_map/ppermute | solution.py:94
  105.5 0.8 copy-start.30
  109.3 15.6 %collective-permute-start.23 = (bf16[64,3584]{1,0:T(8,128)(2,1)}, bf16[64,3584]{1,0:T(8,128)(2,1)S(1)}, u32[]{:S(2)}, u32[]{:S(2)}) collective-permute-start(bf16[64,3584]{1,0:T(8,128)(2,1)} %shard_map.108), channel_id=1, source_target_pairs={{0,2},{1,3},{4,0},{5,1},{8,4},{9,5},{12,8},{13,9},{14,12},{15,13},... | collective-permute-start | bytes 1376264 | tf_op jit(solution)/shard_map/ppermute | solution.py:94
  110.4 0.8 copy-start.29
  114.2 15.6 %collective-permute-start.13 = (bf16[64,3584]{1,0:T(8,128)(2,1)}, bf16[64,3584]{1,0:T(8,128)(2,1)S(1)}, u32[]{:S(2)}, u32[]{:S(2)}) collective-permute-start(bf16[64,3584]{1,0:T(8,128)(2,1)} %shard_map.101), channel_id=1, source_target_pairs={{0,4},{1,5},{4,8},{5,9},{8,12},{9,13},{12,14},{13,15},{14,10},{15,... | collective-permute-start | bytes 1376264 | tf_op jit(solution)/shard_map/ppermute | solution.py:94
  115.1 0.8 copy-start.28
  119.0 15.5 %collective-permute-start.20 = (bf16[64,3584]{1,0:T(8,128)(2,1)}, bf16[64,3584]{1,0:T(8,128)(2,1)S(1)}, u32[]{:S(2)}, u32[]{:S(2)}) collective-permute-start(bf16[64,3584]{1,0:T(8,128)(2,1)} %shard_map.106), channel_id=1, source_target_pairs={{0,4},{1,5},{4,8},{5,9},{8,12},{9,13},{12,14},{13,15},{14,10},{15,... | collective-permute-start | bytes 1376264 | tf_op jit(solution)/shard_map/ppermute | solution.py:94
  120.0 0.8 copy-start.23
  123.9 15.5 %collective-permute-start.17 = (bf16[64,3584]{1,0:T(8,128)(2,1)}, bf16[64,3584]{1,0:T(8,128)(2,1)S(1)}, u32[]{:S(2)}, u32[]{:S(2)}) collective-permute-start(bf16[64,3584]{1,0:T(8,128)(2,1)} %shard_map.104), channel_id=1, source_target_pairs={{0,2},{1,3},{4,0},{5,1},{8,4},{9,5},{12,8},{13,9},{14,12},{15,13},... | collective-permute-start | bytes 1376264 | tf_op jit(solution)/shard_map/ppermute | solution.py:94
  124.9 0.8 copy-start.24
  128.7 16.1 %collective-permute-start.24 = (bf16[64,3584]{1,0:T(8,128)(2,1)}, bf16[64,3584]{1,0:T(8,128)(2,1)}, u32[]{:S(2)}, u32[]{:S(2)}) collective-permute-start(bf16[64,3584]{1,0:T(8,128)(2,1)} %shard_map.109), channel_id=1, source_target_pairs={{0,2},{1,3},{4,0},{5,1},{8,4},{9,5},{12,8},{13,9},{14,12},{15,13},... | collective-permute-start | bytes 1376264 | tf_op jit(solution)/shard_map/ppermute | solution.py:94
  129.7 0.8 copy-start.25
  133.5 15.3 %collective-permute-start.14 = (bf16[64,3584]{1,0:T(8,128)(2,1)}, bf16[64,3584]{1,0:T(8,128)(2,1)}, u32[]{:S(2)}, u32[]{:S(2)}) collective-permute-start(bf16[64,3584]{1,0:T(8,128)(2,1)} %shard_map.102), channel_id=1, source_target_pairs={{0,4},{1,5},{4,8},{5,9},{8,12},{9,13},{12,14},{13,15},{14,10},{15,... | collective-permute-start | bytes 1376264 | tf_op jit(solution)/shard_map/ppermute | solution.py:94
  134.5 0.8 copy-start.26
  138.4 25.2 %collective-permute-start.21 = (bf16[64,3584]{1,0:T(8,128)(2,1)}, bf16[64,3584]{1,0:T(8,128)(2,1)S(1)}, u32[]{:S(2)}, u32[]{:S(2)}) collective-permute-start(bf16[64,3584]{1,0:T(8,128)(2,1)} %shard_map.107), channel_id=1, source_target_pairs={{0,4},{1,5},{4,8},{5,9},{8,12},{9,13},{12,14},{13,15},{14,10},{15,... | collective-permute-start | bytes 1376264 | tf_op jit(solution)/shard_map/ppermute | solution.py:94
  139.4 0.8 copy-start.27
  143.2 9.7 %copy-start.1 = (bf16[512,3584]{1,0:T(8,128)(2,1)S(1)}, bf16[512,3584]{1,0:T(8,128)(2,1)}, u32[]{:S(2)}) copy-start(bf16[512,3584]{1,0:T(8,128)(2,1)} %copy-done) | copy-start | bytes 11010052
  143.2 20.4 %collective-permute-start.18 = (bf16[64,3584]{1,0:T(8,128)(2,1)}, bf16[64,3584]{1,0:T(8,128)(2,1)}, u32[]{:S(2)}, u32[]{:S(2)}) collective-permute-start(bf16[64,3584]{1,0:T(8,128)(2,1)} %shard_map.105), channel_id=1, source_target_pairs={{0,2},{1,3},{4,0},{5,1},{8,4},{9,5},{12,8},{13,9},{14,12},{15,13},... | collective-permute-start | bytes 1376264 | tf_op jit(solution)/shard_map/ppermute | solution.py:94
  147.8 15.8 %collective-permute-start.25 = (bf16[64,3584]{1,0:T(8,128)(2,1)}, bf16[64,3584]{1,0:T(8,128)(2,1)}, u32[]{:S(2)}, u32[]{:S(2)}) collective-permute-start(bf16[64,3584]{1,0:T(8,128)(2,1)} %shard_map.110), channel_id=1, source_target_pairs={{0,2},{1,3},{4,0},{5,1},{8,4},{9,5},{12,8},{13,9},{14,12},{15,13},... | collective-permute-start | bytes 1376264 | tf_op jit(solution)/shard_map/ppermute | solution.py:94
  151.9 11.7 %collective-permute-start.15 = (bf16[64,3584]{1,0:T(8,128)(2,1)}, bf16[64,3584]{1,0:T(8,128)(2,1)S(1)}, u32[]{:S(2)}, u32[]{:S(2)}) collective-permute-start(bf16[64,3584]{1,0:T(8,128)(2,1)} %shard_map.103), channel_id=1, source_target_pairs={{0,4},{1,5},{4,8},{5,9},{8,12},{9,13},{12,14},{13,15},{14,10},{15,... | collective-permute-start | bytes 1376264 | tf_op jit(solution)/shard_map/ppermute | solution.py:94
  152.8 2.0 %copy-start.3 = (bf16[512,3584]{1,0:T(8,128)(2,1)S(1)}, bf16[512,3584]{1,0:T(8,128)(2,1)}, u32[]{:S(2)}) copy-start(bf16[512,3584]{1,0:T(8,128)(2,1)} %copy-done.2) | copy-start | bytes 11010052
  154.9 0.6 copy-start.6
  155.5 0.9 copy-start.8
  156.4 0.9 copy-start.10
  157.3 0.9 copy-start.12
  158.2 0.9 copy-start.14
  159.1 0.9 copy-start.16
  160.0 0.9 copy-start.18
  160.9 0.9 copy-start.20
  161.8 0.9 copy-start.22

commit v8 on v6

--- a/solution.py
+++ b/solution.py
@@ -169,7 +169,7 @@
 
     return local_call(
         kernel,
-        jax.ShapeDtypeStruct((head + tokens, width), jnp.bfloat16),
+        pltpu.HBM((head + tokens, width), jnp.bfloat16),
         [where, stream, swapped, routes, route_gain],
         flops=4 * tokens * width,
         bytes_accessed=4 * tokens * width,
@@ -373,7 +373,7 @@
     return local_call(
         kernel,
         [jax.ShapeDtypeStruct(hidden.shape, hidden.dtype)]
-        + [jax.ShapeDtypeStruct((rows, half), jnp.bfloat16)] * len(wanted),
+        + [pltpu.HBM((rows, half), jnp.bfloat16)] * len(wanted),
         [where, hidden, down],
         flops=2 * rows * units * half * len(wanted),
         bytes_accessed=2 * units * model_width,
@@ -405,67 +405,83 @@
 
 def add_rows(where, position, table, moved):
     rows, width = moved.shape
+    steps = 2
 
     def kernel(where_ref, table_ref, moved_ref, out_ref):
-        at = pl.multiple_of(where_ref[position] * rows, rows)
-        total = table_ref[pl.ds(at, rows), :].astype(jnp.float32)
-        out_ref[...] = (total + moved_ref[...].astype(jnp.float32)).astype(jnp.bfloat16)
+        total = table_ref[...].astype(jnp.float32) + moved_ref[...].astype(jnp.float32)
+        out_ref[...] = total.astype(jnp.bfloat16)
+
+    here = pl.BlockSpec((rows, width // steps), lambda i, where: (0, i))
+    return pl.pallas_call(
+        kernel,
+        grid_spec=pltpu.PrefetchScalarGridSpec(
+            num_scalar_prefetch=1,
+            grid=(steps,),
+            in_specs=[
+                pl.BlockSpec((rows, width // steps), lambda i, where: (where[position], i)),
+                here,
+            ],
+            out_specs=here,
+        ),
+        out_shape=pltpu.HBM((rows, width), jnp.bfloat16),
+        compiler_params=pltpu.CompilerParams(vmem_limit_bytes=VMEM_BYTES),
+        cost_estimate=pl.CostEstimate(
+            flops=rows * width, bytes_accessed=rows * width * 6, transcendentals=0
+        ),
+    )(where, table, moved)
+
+
+def collect(where, positions, pieces):
+    rows, width = pieces[0].shape
+    model_width = len(pieces) * width
+
+    def kernel(where_ref, *refs):
+        for k, position in enumerate(positions):
+            start = pl.multiple_of(where_ref[position] * width, width)
+            refs[-1][:, pl.ds(start, width)] = refs[k][...]
 
     return local_call(
         kernel,
-        jax.ShapeDtypeStruct((rows, width), jnp.bfloat16),
-        [where, table, moved],
-        flops=rows * width,
-        bytes_accessed=rows * width * 6,
-    )
-
-
-def own_rows(where, positions, pieces, tables):
-    rows, width = pieces[0].shape
-    chips = len(pieces)
-    model_width = chips * width
+        jax.ShapeDtypeStruct((rows, model_width), jnp.bfloat16),
+        [where, *pieces],
+        flops=rows * model_width,
+        bytes_accessed=rows * model_width * 4,
+    )
+
+
+def final_sum(where, stream, tables, arrived):
+    rows, model_width = stream.shape
     half = model_width // 2
+    steps = 2
+    came = [value for part in arrived for value in part]
 
     def kernel(where_ref, *refs):
         out_ref = refs[-1]
-        at = pl.multiple_of(where_ref[0] * rows, rows)
         for part in range(2):
-            out_ref[:, part * half : (part + 1) * half] = refs[chips + part][
-                pl.ds(at, rows), :
-            ].astype(jnp.float32)
-        for k in range(chips):
-            start = pl.multiple_of(where_ref[positions[k]] * width, width)
-            out_ref[:, pl.ds(start, width)] += refs[k][...].astype(jnp.float32)
-
-    return local_call(
-        kernel,
-        jax.ShapeDtypeStruct((rows, model_width), jnp.float32),
-        [where, *pieces, *tables],
-        flops=rows * model_width,
-        bytes_accessed=rows * model_width * 8,
-    )
-
-
-def final_sum(where, base, arrived):
-    rows, model_width = base.shape
-    half = model_width // 2
-
-    def kernel(where_ref, base_ref, *refs):
-        out_ref = refs[-1]
-        for part in range(2):
-            cols = slice(part * half, (part + 1) * half)
-            total = base_ref[:, cols]
+            total = refs[part][...].astype(jnp.float32) + refs[2 + part][...].astype(jnp.float32)
             for k in range(len(arrived[part])):
-                total = total + refs[k + part * len(arrived[0])][...].astype(jnp.float32)
-            out_ref[:, cols] = total.astype(jnp.bfloat16)
-
-    return local_call(
-        kernel,
-        jax.ShapeDtypeStruct((rows, model_width), jnp.bfloat16),
-        [where, base, *arrived[0], *arrived[1]],
-        flops=rows * model_width * 3,
-        bytes_accessed=rows * model_width * 10,
-    )
+                total = total + refs[4 + k + part * len(arrived[0])][...].astype(jnp.float32)
+            start = pl.multiple_of(part * half + pl.program_id(0) * (half // steps), 128)
+            out_ref[:, pl.ds(start, half // steps)] = total.astype(jnp.bfloat16)
+
+    block = (rows, half // steps)
+    here = pl.BlockSpec(block, lambda i, where: (0, i))
+    return pl.pallas_call(
+        kernel,
+        grid_spec=pltpu.PrefetchScalarGridSpec(
+            num_scalar_prefetch=1,
+            grid=(steps,),
+            in_specs=[here, pl.BlockSpec(block, lambda i, where: (0, steps + i))]
+            + [pl.BlockSpec(block, lambda i, where: (where[0], i))] * 2
+            + [here] * len(came),
+            out_specs=pl.BlockSpec((rows, model_width), lambda i, where: (0, 0)),
+        ),
+        out_shape=jax.ShapeDtypeStruct((rows, model_width), jnp.bfloat16),
+        compiler_params=pltpu.CompilerParams(vmem_limit_bytes=VMEM_BYTES),
+        cost_estimate=pl.CostEstimate(
+            flops=rows * model_width * 3, bytes_accessed=rows * model_width * 10, transcendentals=0
+        ),
+    )(where, stream, stream, *tables, *came)
 
 
 def dense_body(residual, attn_out, norm_gain, expert_routes, route_gain, w_gate, w_up, w_down):
@@ -516,7 +532,7 @@
         )
         owns.extend(made)
         positions.extend(group)
-        if group == groups[max(far - 3, 0)]:
+        if group == groups[max(far - 2, 0)]:
             lower, upper, carried = lax.optimization_barrier(
                 (blocks[1 - far], blocks[far - 1], carried)
             )
@@ -529,8 +545,9 @@
     hidden, lower, upper, after, before = leading_rows(where, leading, carried, down, chips)
     moving = {1: [ring_shift(lower, ring, 1), None], -1: [None, ring_shift(upper, ring, -1)]}
     second = {1: ring_shift(after, ring, 1), -1: ring_shift(before, ring, -1)}
+    stream_rows = collect(where, positions, owns)
+    stream_rows, hidden = lax.optimization_barrier((stream_rows, hidden))
     everything = [contribution(where, hidden, down, part) for part in range(2)]
-    base = own_rows(where, positions, owns, everything)
     for distance in range(far - 1, 0, -1):
         for sign, order in ((1, (1, 0)), (-1, (0, 1))):
             position = (sign * distance) % chips
@@ -546,7 +563,7 @@
         [moving[sign][part] for sign in (1, -1) if moving[sign][part] is not None]
         for part in range(2)
     ]
-    return final_sum(where, base, arrived)
+    return final_sum(where, stream_rows, everything, arrived)
 
 
 def body(residual, attn_out, norm_gain, expert_routes, route_gain, w_gate, w_up, w_down):

time: 168 us -> 166 us (0.988)
  waiting for transfers between devices: 93.8 us -> 82 us
  Pallas kernels: 44.2 us -> 54.8 us
  starting transfers between devices: 26.6 us -> 24.3 us
    pallas_call x0 -> x11, Pallas kernels: none -> 17.1 us  [the longest x10 14.8 us: add_rows(): pl.pallas_call(kernel, grid_spec=pltpu.PrefetchScalarGridSpec(num_scalar_...]
    ppermute x22, waiting for transfers between devices: 92.3 us -> 80.4 us  [ring_shift(): return lax.ppermute(value, 'ep', pairs)]
    pallas_call x21 -> x10, Pallas kernels: 44.2 us -> 37.7 us  [local_call(): pl.pallas_call(kernel, out_shape=out_shape, in_specs=[IN_SMEM if k == 0 e...]
    ppermute x22, starting transfers between devices: 25.2 us -> 22.9 us  [ring_shift(): return lax.ppermute(value, 'ep', pairs)]
  transfers between devices with their start and end apart: 26 -> 26, of which waited for: 16 -> 16; matrix products, arithmetic and copies ran while one was open for 1% -> 1% of each run, Pallas kernels for 23% -> 29%
where the time goes in v8:
time: 166 us
  waiting for transfers between devices  82 us (49%)
  Pallas kernels  54.8 us (33%)
  starting transfers between devices  24.3 us (15%)
  local copies, waits for them, and re-layouts  2.74 us (2%)
  other arithmetic  1.82 us (1%)
    ppermute x22, waiting for transfers between devices, ring_shift(): return lax.ppermute(value, 'ep', pairs)  80.4 us
    pallas_call x10, Pallas kernels, local_call(): pl.pallas_call(kernel, out_shape=out_shape, in_specs=[IN_SMEM if k == 0 e...  37.7 us
    ppermute x22, starting transfers between devices, ring_shift(): return lax.ppermute(value, 'ep', pairs)  22.9 us
    pallas_call x10, Pallas kernels, add_rows(): pl.pallas_call(kernel, grid_spec=pltpu.PrefetchScalarGridSpec(num_scalar_...  14.8 us
  transfers between devices with their start and end apart: 26, of which 16 were waited for; matrix products, arithmetic and copies ran while one was open for 1% of the time, Pallas kernels for 29%

profile of v8, /device:TPU:0, one launch (start us, length us, event | category | flops | bytes accessed | tf_op | source)
XLA Modules:
  0.0 165.9 jit_solution(5029232371471752852)
XLA Ops:
  0.0 1.8 %add_convert_fusion = bf16[1024,448]{0,1:T(8,128)(2,1)S(1)} fusion(bf16[1024,448]{0,1:T(8,128)(2,1)} %param.10, bf16[1024,448]{0,1:T(8,128)(2,1)} %param.9), kind=kLoop, calls=%fused_computation | loop fusion | flops 1835008 | bytes 2752512 | tf_op jit(solution)/shard_map/convert_element_type | solution.py:505
  1.8 0.5 copy.13
  2.4 0.5 collective-permute-start
  3.0 1.5 collective-permute-done.swapped_ref
  4.5 0.4 collective-permute-start.1
  5.0 0.4 collective-permute-start.9
  5.6 0.7 dynamic-slice_bitcast_fusion.1.where_ref
  6.3 2.2 %shard_map.91.refs_0_.refs_5_ = bf16[528,896]{1,0:T(8,128)(2,1)} custom-call(s32[10]{0:T(128)S(1)} %dynamic-slice_bitcast_fusion.1.where_ref, bf16[8,2,64,448]{3,2,1,0:T(8,128)(2,1)S(1)} %bitcast.7, bf16[8,64,448]{2,1,0:T(8,128)(2,1)S(1)} %collective-permute-done.swapped_ref, s32[64,2]{1,0:T(8,128)S(1)} %copy.14.routes_ref, f32[64,2]{1,0:T(8,128)S(1)} %copy.15.gain_ref), custom_call_target="tpu_custom_call" | custom-call | flops 1835008 | bytes 1835008 | tf_op jit(solution)/shard_map/pallas_call | solution.py:107
  8.5 2.7 %collective-permute-start.4 = (bf16[528,896]{1,0:T(8,128)(2,1)}, bf16[528,896]{1,0:T(8,128)(2,1)S(1)}, u32[]{:S(2)}, u32[]{:S(2)}) collective-permute-start(bf16[528,896]{1,0:T(8,128)(2,1)} %shard_map.91.refs_0_.refs_5_), channel_id=1, source_target_pairs={{0,4},{1,5},{4,8},{5,9},{8,12},{9,13},{12,14},{13,15},{14,10},{15,... | collective-permute-start | bytes 2838536 | tf_op jit(solution)/shard_map/ppermute | solution.py:94
  11.2 21.6 %collective-permute-done.4.refs_1_.refs_12_ = bf16[528,896]{1,0:T(8,128)(2,1)S(1)} collective-permute-done((bf16[528,896]{1,0:T(8,128)(2,1)}, bf16[528,896]{1,0:T(8,128)(2,1)S(1)}, u32[]{:S(2)}, u32[]{:S(2)}) %collective-permute-start.4) | collective-permute-done | bytes 946208 | tf_op jit(solution)/shard_map/ppermute | solution.py:94
  32.8 1.8 %collective-permute-start.6 = (bf16[528,896]{1,0:T(8,128)(2,1)S(1)}, bf16[528,896]{1,0:T(8,128)(2,1)S(1)}, u32[]{:S(2)}, u32[]{:S(2)}) collective-permute-start(bf16[528,896]{1,0:T(8,128)(2,1)S(1)} %collective-permute-done.4.refs_1_.refs_12_), channel_id=1, source_target_pairs={{0,4},{1,5},{4,8},{5,9},{8,12},{9,13},{12,14},{13,15},{14,10},{15,... | collective-permute-start | bytes 2838536 | tf_op jit(solution)/shard_map/ppermute | solution.py:94
  34.9 20.6 %collective-permute-done.6.refs_1_.refs_11_ = bf16[528,896]{1,0:T(8,128)(2,1)S(1)} collective-permute-done((bf16[528,896]{1,0:T(8,128)(2,1)S(1)}, bf16[528,896]{1,0:T(8,128)(2,1)S(1)}, u32[]{:S(2)}, u32[]{:S(2)}) %collective-permute-start.6) | collective-permute-done | bytes 946208 | tf_op jit(solution)/shard_map/ppermute | solution.py:94
  55.5 1.6 collective-permute-start.8
  57.1 0.5 collective-permute-start.7
  57.6 1.2 copy-done
  58.7 4.4 %shard_map.92 = (bf16[64,896]{1,0:T(8,128)(2,1)S(1)}, f32[512,1024]{1,0:T(8,128)S(1)}) custom-call(s32[10]{0:T(128)S(1)} %dynamic-slice_bitcast_fusion.1.where_ref, bf16[528,896]{1,0:T(8,128)(2,1)S(1)} %copy-done, f32[8,1,896]{2,1,0:T(1,128)S(1)} %bitcast.8, bf16[7168,256]{1,0:T(8,128)(2,1)} %refs_3_.3, bf16[7168,256]{1,0:T(8,128)(2,1)} %refs_4_.2, ...), custom_call_target="tpu_custom_call" | custom-call | flops 2818572288 | bytes 6946816 | tf_op jit(solution)/shard_map/pallas_call | solution.py:107
  63.2 6.8 %shard_map.93 = (bf16[64,896]{1,0:T(8,128)(2,1)S(1)}, bf16[64,896]{1,0:T(8,128)(2,1)S(1)}, f32[512,1024]{1,0:T(8,128)S(1)}) custom-call(s32[10]{0:T(128)S(1)} %dynamic-slice_bitcast_fusion.1.where_ref, bf16[528,896]{1,0:T(8,128)(2,1)S(1)} %collective-permute-done.3.refs_0_.refs_6_, ...), custom_call_target="tpu_custom_call", output_to_operand_aliasing={{2}: (8, {})} | custom-call | flops 5637144576 | bytes 9699328 | tf_op jit(solution)/shard_map/pallas_call | solution.py:107
  69.9 6.8 %shard_map.94 = (bf16[64,896]{1,0:T(8,128)(2,1)S(1)}, bf16[64,896]{1,0:T(8,128)(2,1)S(1)}, f32[512,1024]{1,0:T(8,128)S(1)}) custom-call(s32[10]{0:T(128)S(1)} %dynamic-slice_bitcast_fusion.1.where_ref, bf16[528,896]{1,0:T(8,128)(2,1)S(1)} %collective-permute-done.5.refs_0_.refs_7_, ...), custom_call_target="tpu_custom_call", output_to_operand_aliasing={{2}: (8, {})} | custom-call | flops 5637144576 | bytes 9699328 | tf_op jit(solution)/shard_map/pallas_call | solution.py:107
  76.7 0.6 collective-permute-done.8.refs_1_.refs_10_
  77.3 1.0 collective-permute-done.7.refs_0_.refs_8_
  78.3 0.8 collective-permute-start.11
  79.2 1.3 collective-permute-start.10
  80.5 6.8 %shard_map.95 = (bf16[64,896]{1,0:T(8,128)(2,1)S(1)}, bf16[64,896]{1,0:T(8,128)(2,1)S(1)}, f32[512,1024]{1,0:T(8,128)S(1)}, bf16[4,896,256]{2,1,0:T(8,128)(2,1)S(1)}, bf16[512,7168]{1,0:T(8,128)(2,1)S(1)}) custom-call(s32[10]{0:T(128)S(1)} %dynamic-slice_bitcast_fusion.1.where_ref, ...), custom_call_target="tpu_custom_call", output_to_operand_aliasing={{2}: (8, {})} | custom-call | flops 5637144576 | bytes 9699328 | tf_op jit(solution)/shard_map/pallas_call | solution.py:107
  87.3 0.9 collective-permute-done.11.refs_1_
  88.3 1.5 collective-permute-done.10.refs_0_.refs_9_
  89.7 2.0 %shard_map.96 = (bf16[64,896]{1,0:T(8,128)(2,1)S(1)}, bf16[512,512]{1,0:T(8,128)(2,1)S(1)}) custom-call(s32[10]{0:T(128)S(1)} %dynamic-slice_bitcast_fusion.1.where_ref, bf16[272,896]{1,0:T(8,128)(2,1)S(1)} %collective-permute-done.10.refs_0_.refs_9_, bf16[256,896]{1,0:T(8,128)(2,1)S(1)} %collective-permute-done.11.refs_1_, f32[8,1,896]{2,1,0:T(1,128)S(1)} %bitcast.12, ...), custom_call_target="tpu_custom_call" | custom-call | flops 2818572288 | bytes 6946816 | tf_op jit(solution)/shard_map/pallas_call | solution.py:107
  91.8 2.9 %shard_map.98 = (bf16[512,512]{1,0:T(8,128)(2,1)S(1)}, bf16[64,3584]{1,0:T(8,128)(2,1)}, bf16[64,3584]{1,0:T(8,128)(2,1)}, bf16[64,3584]{1,0:T(8,128)(2,1)}, bf16[64,3584]{1,0:T(8,128)(2,1)}) custom-call(s32[10]{0:T(128)S(1)} %dynamic-slice_bitcast_fusion.1.where_ref, bf16[512,512]{1,0:T(8,128)(2,1)S(1)} %get-tuple-element.54.hidden_ref, ...), custom_call_target="tpu_custom_call" | custom-call | flops 939524096 | bytes 7340032 | tf_op jit(solution)/shard_map/pallas_call | solution.py:107
  94.6 1.1 collective-permute-start.22
  95.8 0.9 collective-permute-start.12
  96.7 0.6 shard_map.97.refs_0_.refs_1_
  97.3 1.0 collective-permute-start.19
  98.3 2.6 %shard_map.100.table_ref.refs_3_ = bf16[512,3584]{1,0:T(8,128)(2,1)S(1)} custom-call(s32[10]{0:T(128)S(1)} %dynamic-slice_bitcast_fusion.1.where_ref, bf16[512,512]{1,0:T(8,128)(2,1)S(1)} %get-tuple-element.58.hidden_ref, bf16[512,7168]{1,0:T(8,128)(2,1)S(1)} %get-tuple-element.55.down_ref), custom_call_target="tpu_custom_call" | custom-call | flops 1879048192 | bytes 7340032 | tf_op jit(solution)/shard_map/pallas_call | solution.py:107
  101.0 2.6 %shard_map.99.table_ref.refs_2_ = bf16[512,3584]{1,0:T(8,128)(2,1)S(1)} custom-call(s32[10]{0:T(128)S(1)} %dynamic-slice_bitcast_fusion.1.where_ref, bf16[512,512]{1,0:T(8,128)(2,1)S(1)} %get-tuple-element.58.hidden_ref, bf16[512,7168]{1,0:T(8,128)(2,1)S(1)} %get-tuple-element.55.down_ref), custom_call_target="tpu_custom_call" | custom-call | flops 1879048192 | bytes 7340032 | tf_op jit(solution)/shard_map/pallas_call | solution.py:107
  103.6 1.1 collective-permute-start.16
  104.7 1.2 collective-permute-done.22.moved_ref
  105.8 1.5 shard_map.108
  107.3 0.9 collective-permute-start.23
  108.2 1.3 collective-permute-done.12.moved_ref
  109.5 1.5 shard_map.101
  110.9 0.9 collective-permute-start.13
  111.8 7.5 %collective-permute-done.19.moved_ref = bf16[64,3584]{1,0:T(8,128)(2,1)S(1)} collective-permute-done((bf16[64,3584]{1,0:T(8,128)(2,1)}, bf16[64,3584]{1,0:T(8,128)(2,1)S(1)}, u32[]{:S(2)}, u32[]{:S(2)}) %collective-permute-start.19) | collective-permute-done | bytes 458784 | tf_op jit(solution)/shard_map/ppermute | solution.py:94
  119.3 1.5 shard_map.106
  120.8 0.9 collective-permute-start.20
  121.7 1.5 shard_map.104
  123.2 1.1 collective-permute-start.17
  124.3 2.6 %collective-permute-done.23.moved_ref = bf16[64,3584]{1,0:T(8,128)(2,1)S(1)} collective-permute-done((bf16[64,3584]{1,0:T(8,128)(2,1)}, bf16[64,3584]{1,0:T(8,128)(2,1)S(1)}, u32[]{:S(2)}, u32[]{:S(2)}) %collective-permute-start.23) | collective-permute-done | bytes 458784 | tf_op jit(solution)/shard_map/ppermute | solution.py:94
  126.9 1.5 shard_map.109
  128.4 1.0 collective-permute-start.24
  129.4 1.5 shard_map.102
  130.9 1.0 collective-permute-start.14
  131.9 7.0 %collective-permute-done.20.moved_ref = bf16[64,3584]{1,0:T(8,128)(2,1)S(1)} collective-permute-done((bf16[64,3584]{1,0:T(8,128)(2,1)}, bf16[64,3584]{1,0:T(8,128)(2,1)S(1)}, u32[]{:S(2)}, u32[]{:S(2)}) %collective-permute-start.20) | collective-permute-done | bytes 458784 | tf_op jit(solution)/shard_map/ppermute | solution.py:94
  139.0 1.5 shard_map.107
  140.5 0.9 collective-permute-start.21
  141.4 1.5 shard_map.105
  142.8 1.1 collective-permute-start.18
  144.0 2.7 %collective-permute-done.24.moved_ref = bf16[64,3584]{1,0:T(8,128)(2,1)S(1)} collective-permute-done((bf16[64,3584]{1,0:T(8,128)(2,1)}, bf16[64,3584]{1,0:T(8,128)(2,1)S(1)}, u32[]{:S(2)}, u32[]{:S(2)}) %collective-permute-start.24) | collective-permute-done | bytes 458784 | tf_op jit(solution)/shard_map/ppermute | solution.py:94
  146.7 1.5 shard_map.110
  148.2 1.1 collective-permute-start.25
  149.3 1.5 shard_map.103
  150.8 0.9 collective-permute-start.15
  151.7 7.0 %collective-permute-done.21.refs_6_ = bf16[64,3584]{1,0:T(8,128)(2,1)S(1)} collective-permute-done((bf16[64,3584]{1,0:T(8,128)(2,1)}, bf16[64,3584]{1,0:T(8,128)(2,1)S(1)}, u32[]{:S(2)}, u32[]{:S(2)}) %collective-permute-start.21) | collective-permute-done | bytes 458784 | tf_op jit(solution)/shard_map/ppermute | solution.py:94
  158.6 4.1 %collective-permute-done.25.refs_7_ = bf16[64,3584]{1,0:T(8,128)(2,1)S(1)} collective-permute-done((bf16[64,3584]{1,0:T(8,128)(2,1)}, bf16[64,3584]{1,0:T(8,128)(2,1)S(1)}, u32[]{:S(2)}, u32[]{:S(2)}) %collective-permute-start.25) | collective-permute-done | bytes 458784 | tf_op jit(solution)/shard_map/ppermute | solution.py:94
  162.8 0.8 collective-permute-done.15.refs_4_
  163.6 2.3 %shard_map.111 = bf16[64,7168]{1,0:T(8,128)(2,1)} custom-call(s32[10]{0:T(128)S(1)} %dynamic-slice_bitcast_fusion.1.where_ref, bf16[64,7168]{1,0:T(8,128)(2,1)S(1)} %shard_map.97.refs_0_.refs_1_, bf16[64,7168]{1,0:T(8,128)(2,1)S(1)} %shard_map.97.refs_0_.refs_1_, bf16[512,3584]{1,0:T(8,128)(2,1)S(1)} %shard_map.99.table_ref.refs_2_, ...), custom_call_target="tpu_custom_call" | custom-call | flops 1376256 | bytes 4587520 | tf_op jit(solution)/shard_map/pallas_call | solution.py:469
  (29 shorter events, 0.7 us)
Async XLA Ops:
  0.0 5.4 %copy-start.3 = (s32[64,2]{0,1:T(2,128)S(1)}, s32[64,2]{0,1:T(2,128)}, u32[]{:S(2)}) copy-start(s32[64,2]{0,1:T(2,128)} %param.12) | copy-start | bytes 1540
  0.0 5.5 %copy-start.4 = (f32[64,2]{0,1:T(2,128)S(1)}, f32[64,2]{0,1:T(2,128)}, u32[]{:S(2)}) copy-start(f32[64,2]{0,1:T(2,128)} %param.13) | copy-start | bytes 1540
  0.0 57.5 %copy-start.2 = (f32[7168]{0:T(1024)S(1)}, f32[7168]{0:T(1024)}, u32[]{:S(2)}) copy-start(f32[7168]{0:T(1024)} %param.11) | copy-start | bytes 86020
  2.4 2.1 %collective-permute-start = (bf16[8,64,448]{2,1,0:T(8,128)(2,1)S(1)}, bf16[8,64,448]{2,1,0:T(8,128)(2,1)S(1)}, u32[]{:S(2)}, u32[]{:S(2)}) collective-permute-start(bf16[8,64,448]{2,1,0:T(8,128)(2,1)S(1)} %dynamic-slice_bitcast_fusion), channel_id=1, source_target_pairs={{0,1},{1,0},{2,3},{3,2},{4,5},{5,4},{6,7},{7,6},{8,9},{9,8},{10,11... | collective-permute-start | bytes 1376264 | tf_op jit(solution)/shard_map/ppermute | solution.py:84
  4.5 53.0 %collective-permute-start.1 = (bf16[7168,256]{1,0:T(8,128)(2,1)}, bf16[7168,256]{1,0:T(8,128)(2,1)}, u32[]{:S(2)}, u32[]{:S(2)}) collective-permute-start(bf16[7168,256]{1,0:T(8,128)(2,1)} %refs_3_.3), channel_id=1, source_target_pairs={{0,1},{1,0},{2,3},{3,2},{4,5},{5,4},{6,7},{7,6},{8,9},{9,8},{10,11... | collective-permute-start | bytes 11010056 | tf_op jit(solution)/shard_map/ppermute | solution.py:84
  4.9 52.7 %collective-permute-start.2 = (bf16[7168,256]{1,0:T(8,128)(2,1)}, bf16[7168,256]{1,0:T(8,128)(2,1)}, u32[]{:S(2)}, u32[]{:S(2)}) collective-permute-start(bf16[7168,256]{1,0:T(8,128)(2,1)} %refs_4_.2), channel_id=1, source_target_pairs={{0,1},{1,0},{2,3},{3,2},{4,5},{5,4},{6,7},{7,6},{8,9},{9,8},{10,11... | collective-permute-start | bytes 11010056 | tf_op jit(solution)/shard_map/ppermute | solution.py:84
  5.0 75.5 %collective-permute-start.9 = (bf16[256,7168]{1,0:T(8,128)(2,1)}, bf16[256,7168]{1,0:T(8,128)(2,1)}, u32[]{:S(2)}, u32[]{:S(2)}) collective-permute-start(bf16[256,7168]{1,0:T(8,128)(2,1)} %refs_8_), channel_id=1, source_target_pairs={{0,1},{1,0},{2,3},{3,2},{4,5},{5,4},{6,7},{7,6},{8,9},{9,8},{10,11... | collective-permute-start | bytes 11010056 | tf_op jit(solution)/shard_map/ppermute | solution.py:84
  8.5 24.4 %collective-permute-start.4 = (bf16[528,896]{1,0:T(8,128)(2,1)}, bf16[528,896]{1,0:T(8,128)(2,1)S(1)}, u32[]{:S(2)}, u32[]{:S(2)}) collective-permute-start(bf16[528,896]{1,0:T(8,128)(2,1)} %shard_map.91.refs_0_.refs_5_), channel_id=1, source_target_pairs={{0,4},{1,5},{4,8},{5,9},{8,12},{9,13},{12,14},{13,15},{14,10},{15,... | collective-permute-start | bytes 2838536 | tf_op jit(solution)/shard_map/ppermute | solution.py:94
  11.2 23.4 %collective-permute-start.3 = (bf16[528,896]{1,0:T(8,128)(2,1)}, bf16[528,896]{1,0:T(8,128)(2,1)S(1)}, u32[]{:S(2)}, u32[]{:S(2)}) collective-permute-start(bf16[528,896]{1,0:T(8,128)(2,1)} %shard_map.91.refs_0_.refs_5_), channel_id=1, source_target_pairs={{0,2},{1,3},{4,0},{5,1},{8,4},{9,5},{12,8},{13,9},{14,12},{15,13},... | collective-permute-start | bytes 2838536 | tf_op jit(solution)/shard_map/ppermute | solution.py:94
  32.8 22.7 %collective-permute-start.6 = (bf16[528,896]{1,0:T(8,128)(2,1)S(1)}, bf16[528,896]{1,0:T(8,128)(2,1)S(1)}, u32[]{:S(2)}, u32[]{:S(2)}) collective-permute-start(bf16[528,896]{1,0:T(8,128)(2,1)S(1)} %collective-permute-done.4.refs_1_.refs_12_), channel_id=1, source_target_pairs={{0,4},{1,5},{4,8},{5,9},{8,12},{9,13},{12,14},{13,15},{14,10},{15,... | collective-permute-start | bytes 2838536 | tf_op jit(solution)/shard_map/ppermute | solution.py:94
  34.6 22.4 %collective-permute-start.5 = (bf16[528,896]{1,0:T(8,128)(2,1)S(1)}, bf16[528,896]{1,0:T(8,128)(2,1)S(1)}, u32[]{:S(2)}, u32[]{:S(2)}) collective-permute-start(bf16[528,896]{1,0:T(8,128)(2,1)S(1)} %collective-permute-done.3.refs_0_.refs_6_), channel_id=1, source_target_pairs={{0,2},{1,3},{4,0},{5,1},{8,4},{9,5},{12,8},{13,9},{14,12},{15,13},... | collective-permute-start | bytes 2838536 | tf_op jit(solution)/shard_map/ppermute | solution.py:94
  55.5 21.8 %collective-permute-start.8 = (bf16[528,896]{1,0:T(8,128)(2,1)S(1)}, bf16[528,896]{1,0:T(8,128)(2,1)S(1)}, u32[]{:S(2)}, u32[]{:S(2)}) collective-permute-start(bf16[528,896]{1,0:T(8,128)(2,1)S(1)} %collective-permute-done.6.refs_1_.refs_11_), channel_id=1, source_target_pairs={{0,4},{1,5},{4,8},{5,9},{8,12},{9,13},{12,14},{13,15},{14,10},{15,... | collective-permute-start | bytes 2838536 | tf_op jit(solution)/shard_map/ppermute | solution.py:94
  57.1 21.2 %collective-permute-start.7 = (bf16[528,896]{1,0:T(8,128)(2,1)S(1)}, bf16[528,896]{1,0:T(8,128)(2,1)S(1)}, u32[]{:S(2)}, u32[]{:S(2)}) collective-permute-start(bf16[528,896]{1,0:T(8,128)(2,1)S(1)} %collective-permute-done.5.refs_0_.refs_7_), channel_id=1, source_target_pairs={{0,2},{1,3},{4,0},{5,1},{8,4},{9,5},{12,8},{13,9},{14,12},{15,13},... | collective-permute-start | bytes 2838536 | tf_op jit(solution)/shard_map/ppermute | solution.py:94
  57.5 1.2 copy-start
  78.3 9.9 %collective-permute-start.11 = (bf16[256,896]{1,0:T(8,128)(2,1)S(1)}, bf16[256,896]{1,0:T(8,128)(2,1)S(1)}, u32[]{:S(2)}, u32[]{:S(2)}) collective-permute-start(bf16[256,896]{1,0:T(8,128)(2,1)S(1)} %slice.7), channel_id=1, source_target_pairs={{0,2},{1,3},{4,0},{5,1},{8,4},{9,5},{12,8},{13,9},{14,12},{15,13},... | collective-permute-start | bytes 1376264 | tf_op jit(solution)/shard_map/ppermute | solution.py:94
  79.2 10.5 %copy-start.1 = (bf16[528,896]{1,0:T(8,128)(2,1)S(1)}, bf16[528,896]{1,0:T(8,128)(2,1)}, u32[]{:S(2)}) copy-start(bf16[528,896]{1,0:T(8,128)(2,1)} %shard_map.91.refs_0_.refs_5_) | copy-start | bytes 2838532
  79.2 10.5 %collective-permute-start.10 = (bf16[272,896]{1,0:T(8,128)(2,1)S(1)}, bf16[272,896]{1,0:T(8,128)(2,1)S(1)}, u32[]{:S(2)}, u32[]{:S(2)}) collective-permute-start(bf16[272,896]{1,0:T(8,128)(2,1)S(1)} %slice.6), channel_id=1, source_target_pairs={{0,4},{1,5},{4,8},{5,9},{8,12},{9,13},{12,14},{13,15},{14,10},{15,... | collective-permute-start | bytes 1462280 | tf_op jit(solution)/shard_map/ppermute | solution.py:94
  94.6 11.2 %collective-permute-start.22 = (bf16[64,3584]{1,0:T(8,128)(2,1)}, bf16[64,3584]{1,0:T(8,128)(2,1)S(1)}, u32[]{:S(2)}, u32[]{:S(2)}) collective-permute-start(bf16[64,3584]{1,0:T(8,128)(2,1)} %get-tuple-element.62), channel_id=1, source_target_pairs={{0,2},{1,3},{4,0},{5,1},{8,4},{9,5},{12,8},{13,9},{14,12},{15,13},... | collective-permute-start | bytes 1376264 | tf_op jit(solution)/shard_map/ppermute | solution.py:94
  95.8 13.7 %collective-permute-start.12 = (bf16[64,3584]{1,0:T(8,128)(2,1)}, bf16[64,3584]{1,0:T(8,128)(2,1)S(1)}, u32[]{:S(2)}, u32[]{:S(2)}) collective-permute-start(bf16[64,3584]{1,0:T(8,128)(2,1)} %get-tuple-element.59), channel_id=1, source_target_pairs={{0,4},{1,5},{4,8},{5,9},{8,12},{9,13},{12,14},{13,15},{14,10},{15,... | collective-permute-start | bytes 1376264 | tf_op jit(solution)/shard_map/ppermute | solution.py:94
  97.3 22.0 %collective-permute-start.19 = (bf16[64,3584]{1,0:T(8,128)(2,1)}, bf16[64,3584]{1,0:T(8,128)(2,1)S(1)}, u32[]{:S(2)}, u32[]{:S(2)}) collective-permute-start(bf16[64,3584]{1,0:T(8,128)(2,1)} %get-tuple-element.61), channel_id=1, source_target_pairs={{0,4},{1,5},{4,8},{5,9},{8,12},{9,13},{12,14},{13,15},{14,10},{15,... | collective-permute-start | bytes 1376264 | tf_op jit(solution)/shard_map/ppermute | solution.py:94
  101.0 2.6 %copy-start.5 = (bf16[64,3584]{1,0:T(8,128)(2,1)S(1)}, bf16[64,3584]{1,0:T(8,128)(2,1)}, u32[]{:S(2)}) copy-start(bf16[64,3584]{1,0:T(8,128)(2,1)} %get-tuple-element.60) | copy-start | bytes 1376260
  103.6 18.1 %collective-permute-start.16 = (bf16[64,3584]{1,0:T(8,128)(2,1)S(1)}, bf16[64,3584]{1,0:T(8,128)(2,1)S(1)}, u32[]{:S(2)}, u32[]{:S(2)}) collective-permute-start(bf16[64,3584]{1,0:T(8,128)(2,1)S(1)} %copy-done.5), channel_id=1, source_target_pairs={{0,2},{1,3},{4,0},{5,1},{8,4},{9,5},{12,8},{13,9},{14,12},{15,13},... | collective-permute-start | bytes 1376264 | tf_op jit(solution)/shard_map/ppermute | solution.py:94
  107.3 19.6 %collective-permute-start.23 = (bf16[64,3584]{1,0:T(8,128)(2,1)}, bf16[64,3584]{1,0:T(8,128)(2,1)S(1)}, u32[]{:S(2)}, u32[]{:S(2)}) collective-permute-start(bf16[64,3584]{1,0:T(8,128)(2,1)} %shard_map.108), channel_id=1, source_target_pairs={{0,2},{1,3},{4,0},{5,1},{8,4},{9,5},{12,8},{13,9},{14,12},{15,13},... | collective-permute-start | bytes 1376264 | tf_op jit(solution)/shard_map/ppermute | solution.py:94
  110.9 18.5 %collective-permute-start.13 = (bf16[64,3584]{1,0:T(8,128)(2,1)}, bf16[64,3584]{1,0:T(8,128)(2,1)S(1)}, u32[]{:S(2)}, u32[]{:S(2)}) collective-permute-start(bf16[64,3584]{1,0:T(8,128)(2,1)} %shard_map.101), channel_id=1, source_target_pairs={{0,4},{1,5},{4,8},{5,9},{8,12},{9,13},{12,14},{13,15},{14,10},{15,... | collective-permute-start | bytes 1376264 | tf_op jit(solution)/shard_map/ppermute | solution.py:94
  120.8 18.1 %collective-permute-start.20 = (bf16[64,3584]{1,0:T(8,128)(2,1)}, bf16[64,3584]{1,0:T(8,128)(2,1)S(1)}, u32[]{:S(2)}, u32[]{:S(2)}) collective-permute-start(bf16[64,3584]{1,0:T(8,128)(2,1)} %shard_map.106), channel_id=1, source_target_pairs={{0,4},{1,5},{4,8},{5,9},{8,12},{9,13},{12,14},{13,15},{14,10},{15,... | collective-permute-start | bytes 1376264 | tf_op jit(solution)/shard_map/ppermute | solution.py:94
  123.2 18.2 %collective-permute-start.17 = (bf16[64,3584]{1,0:T(8,128)(2,1)}, bf16[64,3584]{1,0:T(8,128)(2,1)S(1)}, u32[]{:S(2)}, u32[]{:S(2)}) collective-permute-start(bf16[64,3584]{1,0:T(8,128)(2,1)} %shard_map.104), channel_id=1, source_target_pairs={{0,2},{1,3},{4,0},{5,1},{8,4},{9,5},{12,8},{13,9},{14,12},{15,13},... | collective-permute-start | bytes 1376264 | tf_op jit(solution)/shard_map/ppermute | solution.py:94
  128.4 18.3 %collective-permute-start.24 = (bf16[64,3584]{1,0:T(8,128)(2,1)}, bf16[64,3584]{1,0:T(8,128)(2,1)S(1)}, u32[]{:S(2)}, u32[]{:S(2)}) collective-permute-start(bf16[64,3584]{1,0:T(8,128)(2,1)} %shard_map.109), channel_id=1, source_target_pairs={{0,2},{1,3},{4,0},{5,1},{8,4},{9,5},{12,8},{13,9},{14,12},{15,13},... | collective-permute-start | bytes 1376264 | tf_op jit(solution)/shard_map/ppermute | solution.py:94
  130.9 18.4 %collective-permute-start.14 = (bf16[64,3584]{1,0:T(8,128)(2,1)}, bf16[64,3584]{1,0:T(8,128)(2,1)S(1)}, u32[]{:S(2)}, u32[]{:S(2)}) collective-permute-start(bf16[64,3584]{1,0:T(8,128)(2,1)} %shard_map.102), channel_id=1, source_target_pairs={{0,4},{1,5},{4,8},{5,9},{8,12},{9,13},{12,14},{13,15},{14,10},{15,... | collective-permute-start | bytes 1376264 | tf_op jit(solution)/shard_map/ppermute | solution.py:94
  140.5 18.1 %collective-permute-start.21 = (bf16[64,3584]{1,0:T(8,128)(2,1)}, bf16[64,3584]{1,0:T(8,128)(2,1)S(1)}, u32[]{:S(2)}, u32[]{:S(2)}) collective-permute-start(bf16[64,3584]{1,0:T(8,128)(2,1)} %shard_map.107), channel_id=1, source_target_pairs={{0,4},{1,5},{4,8},{5,9},{8,12},{9,13},{12,14},{13,15},{14,10},{15,... | collective-permute-start | bytes 1376264 | tf_op jit(solution)/shard_map/ppermute | solution.py:94
  142.8 15.8 %collective-permute-start.18 = (bf16[64,3584]{1,0:T(8,128)(2,1)}, bf16[64,3584]{1,0:T(8,128)(2,1)S(1)}, u32[]{:S(2)}, u32[]{:S(2)}) collective-permute-start(bf16[64,3584]{1,0:T(8,128)(2,1)} %shard_map.105), channel_id=1, source_target_pairs={{0,2},{1,3},{4,0},{5,1},{8,4},{9,5},{12,8},{13,9},{14,12},{15,13},... | collective-permute-start | bytes 1376264 | tf_op jit(solution)/shard_map/ppermute | solution.py:94
  148.2 14.6 %collective-permute-start.25 = (bf16[64,3584]{1,0:T(8,128)(2,1)}, bf16[64,3584]{1,0:T(8,128)(2,1)S(1)}, u32[]{:S(2)}, u32[]{:S(2)}) collective-permute-start(bf16[64,3584]{1,0:T(8,128)(2,1)} %shard_map.110), channel_id=1, source_target_pairs={{0,2},{1,3},{4,0},{5,1},{8,4},{9,5},{12,8},{13,9},{14,12},{15,13},... | collective-permute-start | bytes 1376264 | tf_op jit(solution)/shard_map/ppermute | solution.py:94
  150.8 12.8 %collective-permute-start.15 = (bf16[64,3584]{1,0:T(8,128)(2,1)}, bf16[64,3584]{1,0:T(8,128)(2,1)S(1)}, u32[]{:S(2)}, u32[]{:S(2)}) collective-permute-start(bf16[64,3584]{1,0:T(8,128)(2,1)} %shard_map.103), channel_id=1, source_target_pairs={{0,4},{1,5},{4,8},{5,9},{8,12},{9,13},{12,14},{13,15},{14,10},{15,... | collective-permute-start | bytes 1376264 | tf_op jit(solution)/shard_map/ppermute | solution.py:94

commit v9 on v8

--- a/solution.py
+++ b/solution.py
@@ -96,6 +96,7 @@
 
 COST_SCALE = 3
 VMEM_BYTES = 20 * 1024 * 1024
+WIDE_VMEM_BYTES = 121 * 512 * 1024
 IN_VMEM = pl.BlockSpec(memory_space=pltpu.VMEM)
 IN_SMEM = pl.BlockSpec(memory_space=pltpu.SMEM)
 IN_HBM = pl.BlockSpec(memory_space=pltpu.HBM)
@@ -380,27 +381,32 @@
     )
 
 
-def contribution(where, hidden, down, part):
+def contribution(hidden, down, part):
     tokens, units = hidden.shape
     half = down.shape[1] // 2
-    tile = 512 if half % 512 == 0 else half
-
-    def kernel(where_ref, hidden_ref, down_ref, out_ref):
-        for start in range(0, half, tile):
-            out = jnp.dot(
-                hidden_ref[...],
-                down_ref[:, part * half + start : part * half + start + tile],
-                preferred_element_type=jnp.float32,
-            )
-            out_ref[:, start : start + tile] = out.astype(jnp.bfloat16)
-
-    return local_call(
-        kernel,
-        jax.ShapeDtypeStruct((tokens, half), jnp.bfloat16),
-        [where, hidden, down],
-        flops=2 * tokens * units * half,
-        bytes_accessed=2 * half * (units + tokens),
-    )
+    steps = 7 if half % (7 * 128) == 0 else 1
+    tile = half // steps
+
+    def kernel(hidden_ref, down_ref, out_ref):
+        out = jnp.dot(hidden_ref[...], down_ref[...], preferred_element_type=jnp.float32)
+        out_ref[...] = out.astype(jnp.bfloat16)
+
+    return pl.pallas_call(
+        kernel,
+        grid=(steps,),
+        in_specs=[
+            pl.BlockSpec((tokens, units), lambda i: (0, 0)),
+            pl.BlockSpec((units, tile), lambda i: (0, part * steps + i)),
+        ],
+        out_specs=pl.BlockSpec((tokens, tile), lambda i: (0, i)),
+        out_shape=pltpu.HBM((tokens, half), jnp.bfloat16),
+        compiler_params=pltpu.CompilerParams(vmem_limit_bytes=VMEM_BYTES),
+        cost_estimate=pl.CostEstimate(
+            flops=2 * tokens * units * half,
+            bytes_accessed=2 * half * (units + tokens),
+            transcendentals=0,
+        ),
+    )(hidden, down)
 
 
 def add_rows(where, position, table, moved):
@@ -424,7 +430,7 @@
             out_specs=here,
         ),
         out_shape=pltpu.HBM((rows, width), jnp.bfloat16),
-        compiler_params=pltpu.CompilerParams(vmem_limit_bytes=VMEM_BYTES),
+        compiler_params=pltpu.CompilerParams(vmem_limit_bytes=WIDE_VMEM_BYTES),
         cost_estimate=pl.CostEstimate(
             flops=rows * width, bytes_accessed=rows * width * 6, transcendentals=0
         ),
@@ -442,7 +448,7 @@
 
     return local_call(
         kernel,
-        jax.ShapeDtypeStruct((rows, model_width), jnp.bfloat16),
+        pltpu.HBM((rows, model_width), jnp.bfloat16),
         [where, *pieces],
         flops=rows * model_width,
         bytes_accessed=rows * model_width * 4,
@@ -547,7 +553,7 @@
     second = {1: ring_shift(after, ring, 1), -1: ring_shift(before, ring, -1)}
     stream_rows = collect(where, positions, owns)
     stream_rows, hidden = lax.optimization_barrier((stream_rows, hidden))
-    everything = [contribution(where, hidden, down, part) for part in range(2)]
+    everything = [contribution(hidden, down, part) for part in range(2)]
     for distance in range(far - 1, 0, -1):
         for sign, order in ((1, (1, 0)), (-1, (0, 1))):
             position = (sign * distance) % chips

time: 166 us -> 175 us (1.054)
  waiting for transfers between devices: 82 us -> 59.9 us
  Pallas kernels: 54.8 us -> 73.6 us
  local copies, waits for them, and re-layouts: 2.74 us -> 14.6 us
    ppermute x22, waiting for transfers between devices: 80.4 us -> 58.4 us  [ring_shift(): return lax.ppermute(value, 'ep', pairs)]
    pallas_call x10, Pallas kernels: 14.8 us -> 27.4 us  [add_rows(): pl.pallas_call(kernel, grid_spec=pltpu.PrefetchScalarGridSpec(num_scalar_...]
    unnamed x14 -> x44, local copies, waits for them, and re-layouts: 1.39 us -> 13.2 us
    pallas_call x0 -> x2, Pallas kernels: none -> 10.4 us  [contribution(): pl.pallas_call(kernel, grid=(steps,), in_specs=[pl.BlockSpec((tokens, uni...]
    pallas_call x10 -> x8, Pallas kernels: 37.7 us -> 33.5 us  [local_call(): pl.pallas_call(kernel, out_shape=out_shape, in_specs=[IN_SMEM if k == 0 e...]
  transfers between devices with their start and end apart: 26 -> 26, of which waited for: 16 -> 13; matrix products, arithmetic and copies ran while one was open for 1% -> 1% of each run, Pallas kernels for 29% -> 38%
where the time goes in v9:
time: 175 us
  Pallas kernels  73.6 us (42%)
  waiting for transfers between devices  59.9 us (34%)
  starting transfers between devices  24.5 us (14%)
  local copies, waits for them, and re-layouts  14.6 us (8%)
  other arithmetic  1.82 us (1%)
    ppermute x22, waiting for transfers between devices, ring_shift(): return lax.ppermute(value, 'ep', pairs)  58.4 us
    pallas_call x8, Pallas kernels, local_call(): pl.pallas_call(kernel, out_shape=out_shape, in_specs=[IN_SMEM if k == 0 e...  33.5 us
    pallas_call x10, Pallas kernels, add_rows(): pl.pallas_call(kernel, grid_spec=pltpu.PrefetchScalarGridSpec(num_scalar_...  27.4 us
    ppermute x22, starting transfers between devices, ring_shift(): return lax.ppermute(value, 'ep', pairs)  23.1 us
    unnamed x44, local copies, waits for them, and re-layouts  13.2 us
    pallas_call x2, Pallas kernels, contribution(): pl.pallas_call(kernel, grid=(steps,), in_specs=[pl.BlockSpec((tokens, uni...  10.4 us
  transfers between devices with their start and end apart: 26, of which 13 were waited for; matrix products, arithmetic and copies ran while one was open for 1% of the time, Pallas kernels for 38%

profile of v9, /device:TPU:0, one launch (start us, length us, event | category | flops | bytes accessed | tf_op | source)
XLA Modules:
  0.0 174.6 jit_solution(11409253519407520231)
XLA Ops:
  0.0 1.8 %add_convert_fusion = bf16[1024,448]{0,1:T(8,128)(2,1)S(1)} fusion(bf16[1024,448]{0,1:T(8,128)(2,1)} %param.10, bf16[1024,448]{0,1:T(8,128)(2,1)} %param.9), kind=kLoop, calls=%fused_computation | loop fusion | flops 1835008 | bytes 2752512 | tf_op jit(solution)/shard_map/convert_element_type | solution.py:511
  3.0 1.5 collective-permute-done.swapped_ref
  6.3 2.2 %shard_map.91.refs_0_.refs_5_ = bf16[528,896]{1,0:T(8,128)(2,1)} custom-call(s32[10]{0:T(128)S(1)} %dynamic-slice_bitcast_fusion.1.where_ref, bf16[8,2,64,448]{3,2,1,0:T(8,128)(2,1)S(1)} %bitcast.7, bf16[8,64,448]{2,1,0:T(8,128)(2,1)S(1)} %collective-permute-done.swapped_ref, s32[64,2]{1,0:T(8,128)S(1)} %copy.14.routes_ref, f32[64,2]{1,0:T(8,128)S(1)} %copy.15.gain_ref), custom_call_target="tpu_custom_call" | custom-call | flops 1835008 | bytes 1835008 | tf_op jit(solution)/shard_map/pallas_call | solution.py:108
  8.5 2.7 %collective-permute-start.4 = (bf16[528,896]{1,0:T(8,128)(2,1)}, bf16[528,896]{1,0:T(8,128)(2,1)S(1)}, u32[]{:S(2)}, u32[]{:S(2)}) collective-permute-start(bf16[528,896]{1,0:T(8,128)(2,1)} %shard_map.91.refs_0_.refs_5_), channel_id=1, source_target_pairs={{0,4},{1,5},{4,8},{5,9},{8,12},{9,13},{12,14},{13,15},{14,10},{15,... | collective-permute-start | bytes 2838536 | tf_op jit(solution)/shard_map/ppermute | solution.py:94
  11.2 21.6 %collective-permute-done.4.refs_1_.refs_12_ = bf16[528,896]{1,0:T(8,128)(2,1)S(1)} collective-permute-done((bf16[528,896]{1,0:T(8,128)(2,1)}, bf16[528,896]{1,0:T(8,128)(2,1)S(1)}, u32[]{:S(2)}, u32[]{:S(2)}) %collective-permute-start.4) | collective-permute-done | bytes 946208 | tf_op jit(solution)/shard_map/ppermute | solution.py:94
  32.9 1.8 %collective-permute-start.6 = (bf16[528,896]{1,0:T(8,128)(2,1)S(1)}, bf16[528,896]{1,0:T(8,128)(2,1)S(1)}, u32[]{:S(2)}, u32[]{:S(2)}) collective-permute-start(bf16[528,896]{1,0:T(8,128)(2,1)S(1)} %collective-permute-done.4.refs_1_.refs_12_), channel_id=1, source_target_pairs={{0,4},{1,5},{4,8},{5,9},{8,12},{9,13},{12,14},{13,15},{14,10},{15,... | collective-permute-start | bytes 2838536 | tf_op jit(solution)/shard_map/ppermute | solution.py:94
  34.9 20.6 %collective-permute-done.6.refs_1_.refs_11_ = bf16[528,896]{1,0:T(8,128)(2,1)S(1)} collective-permute-done((bf16[528,896]{1,0:T(8,128)(2,1)S(1)}, bf16[528,896]{1,0:T(8,128)(2,1)S(1)}, u32[]{:S(2)}, u32[]{:S(2)}) %collective-permute-start.6) | collective-permute-done | bytes 946208 | tf_op jit(solution)/shard_map/ppermute | solution.py:94
  55.5 1.6 collective-permute-start.8
  57.6 1.2 copy-done.2
  58.8 4.4 %shard_map.92 = (bf16[64,896]{1,0:T(8,128)(2,1)S(1)}, f32[512,1024]{1,0:T(8,128)S(1)}) custom-call(s32[10]{0:T(128)S(1)} %dynamic-slice_bitcast_fusion.1.where_ref, bf16[528,896]{1,0:T(8,128)(2,1)S(1)} %copy-done.2, f32[8,1,896]{2,1,0:T(1,128)S(1)} %bitcast.8, bf16[7168,256]{1,0:T(8,128)(2,1)} %refs_3_.3, bf16[7168,256]{1,0:T(8,128)(2,1)} %refs_4_.2, ...), custom_call_target="tpu_custom_call" | custom-call | flops 2818572288 | bytes 6946816 | tf_op jit(solution)/shard_map/pallas_call | solution.py:108
  63.2 6.8 %shard_map.93 = (bf16[64,896]{1,0:T(8,128)(2,1)S(1)}, bf16[64,896]{1,0:T(8,128)(2,1)S(1)}, f32[512,1024]{1,0:T(8,128)S(1)}) custom-call(s32[10]{0:T(128)S(1)} %dynamic-slice_bitcast_fusion.1.where_ref, bf16[528,896]{1,0:T(8,128)(2,1)S(1)} %collective-permute-done.3.refs_0_.refs_6_, ...), custom_call_target="tpu_custom_call", output_to_operand_aliasing={{2}: (8, {})} | custom-call | flops 5637144576 | bytes 9699328 | tf_op jit(solution)/shard_map/pallas_call | solution.py:108
  70.0 6.8 %shard_map.94 = (bf16[64,896]{1,0:T(8,128)(2,1)S(1)}, bf16[64,896]{1,0:T(8,128)(2,1)S(1)}, f32[512,1024]{1,0:T(8,128)S(1)}) custom-call(s32[10]{0:T(128)S(1)} %dynamic-slice_bitcast_fusion.1.where_ref, bf16[528,896]{1,0:T(8,128)(2,1)S(1)} %collective-permute-done.5.refs_0_.refs_7_, ...), custom_call_target="tpu_custom_call", output_to_operand_aliasing={{2}: (8, {})} | custom-call | flops 5637144576 | bytes 9699328 | tf_op jit(solution)/shard_map/pallas_call | solution.py:108
  77.3 1.0 collective-permute-done.7.refs_0_.refs_8_
  78.4 0.8 collective-permute-start.11
  79.2 1.3 collective-permute-start.10
  80.6 6.8 %shard_map.95 = (bf16[64,896]{1,0:T(8,128)(2,1)S(1)}, bf16[64,896]{1,0:T(8,128)(2,1)S(1)}, f32[512,1024]{1,0:T(8,128)S(1)}, bf16[4,896,256]{2,1,0:T(8,128)(2,1)S(1)}, bf16[512,7168]{1,0:T(8,128)(2,1)S(1)}) custom-call(s32[10]{0:T(128)S(1)} %dynamic-slice_bitcast_fusion.1.where_ref, ...), custom_call_target="tpu_custom_call", output_to_operand_aliasing={{2}: (8, {})} | custom-call | flops 5637144576 | bytes 9699328 | tf_op jit(solution)/shard_map/pallas_call | solution.py:108
  87.3 0.9 collective-permute-done.11.refs_1_
  88.3 1.5 collective-permute-done.10.refs_0_.refs_9_
  89.7 2.1 %shard_map.96 = (bf16[64,896]{1,0:T(8,128)(2,1)S(1)}, bf16[512,512]{1,0:T(8,128)(2,1)S(1)}) custom-call(s32[10]{0:T(128)S(1)} %dynamic-slice_bitcast_fusion.1.where_ref, bf16[272,896]{1,0:T(8,128)(2,1)S(1)} %collective-permute-done.10.refs_0_.refs_9_, bf16[256,896]{1,0:T(8,128)(2,1)S(1)} %collective-permute-done.11.refs_1_, f32[8,1,896]{2,1,0:T(1,128)S(1)} %bitcast.12, ...), custom_call_target="tpu_custom_call" | custom-call | flops 2818572288 | bytes 6946816 | tf_op jit(solution)/shard_map/pallas_call | solution.py:108
  91.8 3.0 %shard_map.98 = (bf16[512,512]{1,0:T(8,128)(2,1)S(1)}, bf16[64,3584]{1,0:T(8,128)(2,1)}, bf16[64,3584]{1,0:T(8,128)(2,1)}, bf16[64,3584]{1,0:T(8,128)(2,1)}, bf16[64,3584]{1,0:T(8,128)(2,1)}) custom-call(s32[10]{0:T(128)S(1)} %dynamic-slice_bitcast_fusion.1.where_ref, bf16[512,512]{1,0:T(8,128)(2,1)S(1)} %get-tuple-element.54.hidden_ref, ...), custom_call_target="tpu_custom_call" | custom-call | flops 939524096 | bytes 7340032 | tf_op jit(solution)/shard_map/pallas_call | solution.py:108
  94.8 1.2 collective-permute-start.22
  96.0 0.9 collective-permute-start.12
  96.8 1.5 shard_map.97.refs_0_.refs_1_
  98.4 1.0 collective-permute-start.19
  99.4 5.2 %shard_map.100.table_ref.refs_3_ = bf16[512,3584]{1,0:T(8,128)(2,1)} custom-call(bf16[512,512]{1,0:T(8,128)(2,1)S(1)} %get-tuple-element.58.hidden_ref, bf16[512,7168]{1,0:T(8,128)(2,1)S(1)} %get-tuple-element.55.down_ref), custom_call_target="tpu_custom_call" | custom-call | flops 1879048192 | bytes 7340032 | tf_op jit(solution)/shard_map/pallas_call | solution.py:394
  104.6 5.2 %shard_map.99.table_ref.refs_2_ = bf16[512,3584]{1,0:T(8,128)(2,1)} custom-call(bf16[512,512]{1,0:T(8,128)(2,1)S(1)} %get-tuple-element.58.hidden_ref, bf16[512,7168]{1,0:T(8,128)(2,1)S(1)} %get-tuple-element.55.down_ref), custom_call_target="tpu_custom_call" | custom-call | flops 1879048192 | bytes 7340032 | tf_op jit(solution)/shard_map/pallas_call | solution.py:394
  109.8 1.0 collective-permute-start.16
  110.8 0.8 copy-done.9
  111.6 2.7 %shard_map.108 = bf16[64,3584]{1,0:T(8,128)(2,1)} custom-call(s32[10]{0:T(128)} %copy-done.6, bf16[512,3584]{1,0:T(8,128)(2,1)} %shard_map.100.table_ref.refs_3_, bf16[64,3584]{1,0:T(8,128)(2,1)} %copy-done.9), custom_call_target="tpu_custom_call" | custom-call | flops 229376 | bytes 1376256 | tf_op jit(solution)/shard_map/pallas_call | solution.py:421
  114.4 1.2 collective-permute-start.23
  115.5 0.8 copy-done.8
  116.3 2.8 %shard_map.101 = bf16[64,3584]{1,0:T(8,128)(2,1)} custom-call(s32[10]{0:T(128)} %copy-done.6, bf16[512,3584]{1,0:T(8,128)(2,1)} %shard_map.99.table_ref.refs_2_, bf16[64,3584]{1,0:T(8,128)(2,1)} %copy-done.8), custom_call_target="tpu_custom_call" | custom-call | flops 229376 | bytes 1376256 | tf_op jit(solution)/shard_map/pallas_call | solution.py:421
  119.1 0.9 collective-permute-start.13
  120.0 0.8 copy-done.17
  120.8 2.7 %shard_map.106 = bf16[64,3584]{1,0:T(8,128)(2,1)} custom-call(s32[10]{0:T(128)} %copy-done.6, bf16[512,3584]{1,0:T(8,128)(2,1)} %shard_map.100.table_ref.refs_3_, bf16[64,3584]{1,0:T(8,128)(2,1)} %copy-done.17), custom_call_target="tpu_custom_call" | custom-call | flops 229376 | bytes 1376256 | tf_op jit(solution)/shard_map/pallas_call | solution.py:421
  123.5 1.0 collective-permute-start.20
  124.5 0.8 copy-done.10
  125.3 2.7 %shard_map.104 = bf16[64,3584]{1,0:T(8,128)(2,1)} custom-call(s32[10]{0:T(128)} %copy-done.6, bf16[512,3584]{1,0:T(8,128)(2,1)} %shard_map.99.table_ref.refs_2_, bf16[64,3584]{1,0:T(8,128)(2,1)} %copy-done.10), custom_call_target="tpu_custom_call" | custom-call | flops 229376 | bytes 1376256 | tf_op jit(solution)/shard_map/pallas_call | solution.py:421
  128.0 1.0 collective-permute-start.17
  129.0 0.8 collective-permute-done.23.moved_ref
  129.8 0.8 copy-done.11
  130.6 2.7 %shard_map.109 = bf16[64,3584]{1,0:T(8,128)(2,1)} custom-call(s32[10]{0:T(128)} %copy-done.6, bf16[512,3584]{1,0:T(8,128)(2,1)} %shard_map.100.table_ref.refs_3_, bf16[64,3584]{1,0:T(8,128)(2,1)} %copy-done.11), custom_call_target="tpu_custom_call" | custom-call | flops 229376 | bytes 1376256 | tf_op jit(solution)/shard_map/pallas_call | solution.py:421
  133.3 1.3 collective-permute-start.24
  134.6 0.8 copy-done.12
  135.3 2.8 %shard_map.102 = bf16[64,3584]{1,0:T(8,128)(2,1)} custom-call(s32[10]{0:T(128)} %copy-done.6, bf16[512,3584]{1,0:T(8,128)(2,1)} %shard_map.99.table_ref.refs_2_, bf16[64,3584]{1,0:T(8,128)(2,1)} %copy-done.12), custom_call_target="tpu_custom_call" | custom-call | flops 229376 | bytes 1376256 | tf_op jit(solution)/shard_map/pallas_call | solution.py:421
  139.2 0.8 copy-done.13
  139.9 2.7 %shard_map.107 = bf16[64,3584]{1,0:T(8,128)(2,1)} custom-call(s32[10]{0:T(128)} %copy-done.6, bf16[512,3584]{1,0:T(8,128)(2,1)} %shard_map.100.table_ref.refs_3_, bf16[64,3584]{1,0:T(8,128)(2,1)} %copy-done.13), custom_call_target="tpu_custom_call" | custom-call | flops 229376 | bytes 1376256 | tf_op jit(solution)/shard_map/pallas_call | solution.py:421
  142.7 1.2 collective-permute-start.21
  143.9 0.8 copy-done.14
  144.7 2.7 %shard_map.105 = bf16[64,3584]{1,0:T(8,128)(2,1)} custom-call(s32[10]{0:T(128)} %copy-done.6, bf16[512,3584]{1,0:T(8,128)(2,1)} %shard_map.99.table_ref.refs_2_, bf16[64,3584]{1,0:T(8,128)(2,1)} %copy-done.14), custom_call_target="tpu_custom_call" | custom-call | flops 229376 | bytes 1376256 | tf_op jit(solution)/shard_map/pallas_call | solution.py:421
  147.4 0.8 collective-permute-start.18
  148.2 3.3 %collective-permute-done.24.moved_ref = bf16[64,3584]{1,0:T(8,128)(2,1)S(1)} collective-permute-done((bf16[64,3584]{1,0:T(8,128)(2,1)}, bf16[64,3584]{1,0:T(8,128)(2,1)S(1)}, u32[]{:S(2)}, u32[]{:S(2)}) %collective-permute-start.24) | collective-permute-done | bytes 458784 | tf_op jit(solution)/shard_map/ppermute | solution.py:94
  151.5 0.8 copy-done.15
  152.3 2.7 %shard_map.110 = bf16[64,3584]{1,0:T(8,128)(2,1)} custom-call(s32[10]{0:T(128)} %copy-done.6, bf16[512,3584]{1,0:T(8,128)(2,1)} %shard_map.100.table_ref.refs_3_, bf16[64,3584]{1,0:T(8,128)(2,1)} %copy-done.15), custom_call_target="tpu_custom_call" | custom-call | flops 229376 | bytes 1376256 | tf_op jit(solution)/shard_map/pallas_call | solution.py:421
  155.0 1.0 collective-permute-start.25
  156.0 0.8 copy-done.16
  156.8 2.8 %shard_map.103 = bf16[64,3584]{1,0:T(8,128)(2,1)} custom-call(s32[10]{0:T(128)} %copy-done.6, bf16[512,3584]{1,0:T(8,128)(2,1)} %shard_map.99.table_ref.refs_2_, bf16[64,3584]{1,0:T(8,128)(2,1)} %copy-done.16), custom_call_target="tpu_custom_call" | custom-call | flops 229376 | bytes 1376256 | tf_op jit(solution)/shard_map/pallas_call | solution.py:421
  159.5 1.0 collective-permute-start.15
  160.6 0.8 collective-permute-done.18.refs_5_
  161.3 5.5 %collective-permute-done.25.refs_7_ = bf16[64,3584]{1,0:T(8,128)(2,1)S(1)} collective-permute-done((bf16[64,3584]{1,0:T(8,128)(2,1)}, bf16[64,3584]{1,0:T(8,128)(2,1)S(1)}, u32[]{:S(2)}, u32[]{:S(2)}) %collective-permute-start.25) | collective-permute-done | bytes 458784 | tf_op jit(solution)/shard_map/ppermute | solution.py:94
  166.8 1.4 collective-permute-done.15.refs_4_
  168.2 2.0 %copy-done = bf16[512,3584]{1,0:T(8,128)(2,1)S(1)} copy-done((bf16[512,3584]{1,0:T(8,128)(2,1)S(1)}, bf16[512,3584]{1,0:T(8,128)(2,1)}, u32[]{:S(2)}) %copy-start) | copy-done | bytes 3670040
  170.3 2.0 %copy-done.1 = bf16[512,3584]{1,0:T(8,128)(2,1)S(1)} copy-done((bf16[512,3584]{1,0:T(8,128)(2,1)S(1)}, bf16[512,3584]{1,0:T(8,128)(2,1)}, u32[]{:S(2)}) %copy-start.1) | copy-done | bytes 3670040
  172.3 2.3 %shard_map.111 = bf16[64,7168]{1,0:T(8,128)(2,1)} custom-call(s32[10]{0:T(128)S(1)} %copy-done.7, bf16[64,7168]{1,0:T(8,128)(2,1)S(1)} %copy-done.4, bf16[64,7168]{1,0:T(8,128)(2,1)S(1)} %copy-done.4, bf16[512,3584]{1,0:T(8,128)(2,1)S(1)} %copy-done.1, bf16[512,3584]{1,0:T(8,128)(2,1)S(1)} %copy-done, bf16[64,3584]{1,0:T(8,128)(2,1)S(1)} %collective-permute-done.15.refs_4_, ...), custom_call_target="tpu_custom_call" | custom-call | flops 1376256 | bytes 4587520 | tf_op jit(solution)/shard_map/pallas_call | solution.py:475
  (59 shorter events, 5.4 us)
Async XLA Ops:
  0.0 5.4 %copy-start.18 = (s32[64,2]{0,1:T(2,128)S(1)}, s32[64,2]{0,1:T(2,128)}, u32[]{:S(2)}) copy-start(s32[64,2]{0,1:T(2,128)} %param.12) | copy-start | bytes 1540
  0.0 5.5 %copy-start.19 = (f32[64,2]{0,1:T(2,128)S(1)}, f32[64,2]{0,1:T(2,128)}, u32[]{:S(2)}) copy-start(f32[64,2]{0,1:T(2,128)} %param.13) | copy-start | bytes 1540
  0.0 57.6 %copy-start.5 = (f32[7168]{0:T(1024)S(1)}, f32[7168]{0:T(1024)}, u32[]{:S(2)}) copy-start(f32[7168]{0:T(1024)} %param.11) | copy-start | bytes 86020
  2.4 2.1 %collective-permute-start = (bf16[8,64,448]{2,1,0:T(8,128)(2,1)S(1)}, bf16[8,64,448]{2,1,0:T(8,128)(2,1)S(1)}, u32[]{:S(2)}, u32[]{:S(2)}) collective-permute-start(bf16[8,64,448]{2,1,0:T(8,128)(2,1)S(1)} %dynamic-slice_bitcast_fusion), channel_id=1, source_target_pairs={{0,1},{1,0},{2,3},{3,2},{4,5},{5,4},{6,7},{7,6},{8,9},{9,8},{10,11... | collective-permute-start | bytes 1376264 | tf_op jit(solution)/shard_map/ppermute | solution.py:84
  4.5 53.1 %collective-permute-start.1 = (bf16[7168,256]{1,0:T(8,128)(2,1)}, bf16[7168,256]{1,0:T(8,128)(2,1)}, u32[]{:S(2)}, u32[]{:S(2)}) collective-permute-start(bf16[7168,256]{1,0:T(8,128)(2,1)} %refs_3_.3), channel_id=1, source_target_pairs={{0,1},{1,0},{2,3},{3,2},{4,5},{5,4},{6,7},{7,6},{8,9},{9,8},{10,11... | collective-permute-start | bytes 11010056 | tf_op jit(solution)/shard_map/ppermute | solution.py:84
  4.9 52.7 %collective-permute-start.2 = (bf16[7168,256]{1,0:T(8,128)(2,1)}, bf16[7168,256]{1,0:T(8,128)(2,1)}, u32[]{:S(2)}, u32[]{:S(2)}) collective-permute-start(bf16[7168,256]{1,0:T(8,128)(2,1)} %refs_4_.2), channel_id=1, source_target_pairs={{0,1},{1,0},{2,3},{3,2},{4,5},{5,4},{6,7},{7,6},{8,9},{9,8},{10,11... | collective-permute-start | bytes 11010056 | tf_op jit(solution)/shard_map/ppermute | solution.py:84
  5.0 75.5 %collective-permute-start.9 = (bf16[256,7168]{1,0:T(8,128)(2,1)}, bf16[256,7168]{1,0:T(8,128)(2,1)}, u32[]{:S(2)}, u32[]{:S(2)}) collective-permute-start(bf16[256,7168]{1,0:T(8,128)(2,1)} %refs_8_), channel_id=1, source_target_pairs={{0,1},{1,0},{2,3},{3,2},{4,5},{5,4},{6,7},{7,6},{8,9},{9,8},{10,11... | collective-permute-start | bytes 11010056 | tf_op jit(solution)/shard_map/ppermute | solution.py:84
  6.3 90.6 %copy-start.6 = (s32[10]{0:T(128)}, s32[10]{0:T(128)S(1)}, u32[]{:S(2)}) copy-start(s32[10]{0:T(128)S(1)} %dynamic-slice_bitcast_fusion.1.where_ref) | copy-start | bytes 124
  8.5 24.4 %collective-permute-start.4 = (bf16[528,896]{1,0:T(8,128)(2,1)}, bf16[528,896]{1,0:T(8,128)(2,1)S(1)}, u32[]{:S(2)}, u32[]{:S(2)}) collective-permute-start(bf16[528,896]{1,0:T(8,128)(2,1)} %shard_map.91.refs_0_.refs_5_), channel_id=1, source_target_pairs={{0,4},{1,5},{4,8},{5,9},{8,12},{9,13},{12,14},{13,15},{14,10},{15,... | collective-permute-start | bytes 2838536 | tf_op jit(solution)/shard_map/ppermute | solution.py:94
  11.2 23.4 %collective-permute-start.3 = (bf16[528,896]{1,0:T(8,128)(2,1)}, bf16[528,896]{1,0:T(8,128)(2,1)S(1)}, u32[]{:S(2)}, u32[]{:S(2)}) collective-permute-start(bf16[528,896]{1,0:T(8,128)(2,1)} %shard_map.91.refs_0_.refs_5_), channel_id=1, source_target_pairs={{0,2},{1,3},{4,0},{5,1},{8,4},{9,5},{12,8},{13,9},{14,12},{15,13},... | collective-permute-start | bytes 2838536 | tf_op jit(solution)/shard_map/ppermute | solution.py:94
  32.9 22.7 %collective-permute-start.6 = (bf16[528,896]{1,0:T(8,128)(2,1)S(1)}, bf16[528,896]{1,0:T(8,128)(2,1)S(1)}, u32[]{:S(2)}, u32[]{:S(2)}) collective-permute-start(bf16[528,896]{1,0:T(8,128)(2,1)S(1)} %collective-permute-done.4.refs_1_.refs_12_), channel_id=1, source_target_pairs={{0,4},{1,5},{4,8},{5,9},{8,12},{9,13},{12,14},{13,15},{14,10},{15,... | collective-permute-start | bytes 2838536 | tf_op jit(solution)/shard_map/ppermute | solution.py:94
  34.7 22.4 %collective-permute-start.5 = (bf16[528,896]{1,0:T(8,128)(2,1)S(1)}, bf16[528,896]{1,0:T(8,128)(2,1)S(1)}, u32[]{:S(2)}, u32[]{:S(2)}) collective-permute-start(bf16[528,896]{1,0:T(8,128)(2,1)S(1)} %collective-permute-done.3.refs_0_.refs_6_), channel_id=1, source_target_pairs={{0,2},{1,3},{4,0},{5,1},{8,4},{9,5},{12,8},{13,9},{14,12},{15,13},... | collective-permute-start | bytes 2838536 | tf_op jit(solution)/shard_map/ppermute | solution.py:94
  55.5 21.8 %collective-permute-start.8 = (bf16[528,896]{1,0:T(8,128)(2,1)S(1)}, bf16[528,896]{1,0:T(8,128)(2,1)S(1)}, u32[]{:S(2)}, u32[]{:S(2)}) collective-permute-start(bf16[528,896]{1,0:T(8,128)(2,1)S(1)} %collective-permute-done.6.refs_1_.refs_11_), channel_id=1, source_target_pairs={{0,4},{1,5},{4,8},{5,9},{8,12},{9,13},{12,14},{13,15},{14,10},{15,... | collective-permute-start | bytes 2838536 | tf_op jit(solution)/shard_map/ppermute | solution.py:94
  57.1 21.2 %collective-permute-start.7 = (bf16[528,896]{1,0:T(8,128)(2,1)S(1)}, bf16[528,896]{1,0:T(8,128)(2,1)S(1)}, u32[]{:S(2)}, u32[]{:S(2)}) collective-permute-start(bf16[528,896]{1,0:T(8,128)(2,1)S(1)} %collective-permute-done.5.refs_0_.refs_7_), channel_id=1, source_target_pairs={{0,2},{1,3},{4,0},{5,1},{8,4},{9,5},{12,8},{13,9},{14,12},{15,13},... | collective-permute-start | bytes 2838536 | tf_op jit(solution)/shard_map/ppermute | solution.py:94
  57.6 1.2 copy-start.2
  78.4 9.9 %collective-permute-start.11 = (bf16[256,896]{1,0:T(8,128)(2,1)S(1)}, bf16[256,896]{1,0:T(8,128)(2,1)S(1)}, u32[]{:S(2)}, u32[]{:S(2)}) collective-permute-start(bf16[256,896]{1,0:T(8,128)(2,1)S(1)} %slice.7), channel_id=1, source_target_pairs={{0,2},{1,3},{4,0},{5,1},{8,4},{9,5},{12,8},{13,9},{14,12},{15,13},... | collective-permute-start | bytes 1376264 | tf_op jit(solution)/shard_map/ppermute | solution.py:94
  79.2 10.5 %copy-start.3 = (bf16[528,896]{1,0:T(8,128)(2,1)S(1)}, bf16[528,896]{1,0:T(8,128)(2,1)}, u32[]{:S(2)}) copy-start(bf16[528,896]{1,0:T(8,128)(2,1)} %shard_map.91.refs_0_.refs_5_) | copy-start | bytes 2838532
  79.2 10.5 %collective-permute-start.10 = (bf16[272,896]{1,0:T(8,128)(2,1)S(1)}, bf16[272,896]{1,0:T(8,128)(2,1)S(1)}, u32[]{:S(2)}, u32[]{:S(2)}) collective-permute-start(bf16[272,896]{1,0:T(8,128)(2,1)S(1)} %slice.6), channel_id=1, source_target_pairs={{0,4},{1,5},{4,8},{5,9},{8,12},{9,13},{12,14},{13,15},{14,10},{15,... | collective-permute-start | bytes 1462280 | tf_op jit(solution)/shard_map/ppermute | solution.py:94
  94.8 16.0 %collective-permute-start.22 = (bf16[64,3584]{1,0:T(8,128)(2,1)}, bf16[64,3584]{1,0:T(8,128)(2,1)S(1)}, u32[]{:S(2)}, u32[]{:S(2)}) collective-permute-start(bf16[64,3584]{1,0:T(8,128)(2,1)} %get-tuple-element.62), channel_id=1, source_target_pairs={{0,2},{1,3},{4,0},{5,1},{8,4},{9,5},{12,8},{13,9},{14,12},{15,13},... | collective-permute-start | bytes 1376264 | tf_op jit(solution)/shard_map/ppermute | solution.py:94
  96.0 19.6 %collective-permute-start.12 = (bf16[64,3584]{1,0:T(8,128)(2,1)}, bf16[64,3584]{1,0:T(8,128)(2,1)S(1)}, u32[]{:S(2)}, u32[]{:S(2)}) collective-permute-start(bf16[64,3584]{1,0:T(8,128)(2,1)} %get-tuple-element.59), channel_id=1, source_target_pairs={{0,4},{1,5},{4,8},{5,9},{8,12},{9,13},{12,14},{13,15},{14,10},{15,... | collective-permute-start | bytes 1376264 | tf_op jit(solution)/shard_map/ppermute | solution.py:94
  98.4 21.6 %collective-permute-start.19 = (bf16[64,3584]{1,0:T(8,128)(2,1)}, bf16[64,3584]{1,0:T(8,128)(2,1)S(1)}, u32[]{:S(2)}, u32[]{:S(2)}) collective-permute-start(bf16[64,3584]{1,0:T(8,128)(2,1)} %get-tuple-element.61), channel_id=1, source_target_pairs={{0,4},{1,5},{4,8},{5,9},{8,12},{9,13},{12,14},{13,15},{14,10},{15,... | collective-permute-start | bytes 1376264 | tf_op jit(solution)/shard_map/ppermute | solution.py:94
  104.6 5.2 %copy-start.20 = (bf16[64,3584]{1,0:T(8,128)(2,1)S(1)}, bf16[64,3584]{1,0:T(8,128)(2,1)}, u32[]{:S(2)}) copy-start(bf16[64,3584]{1,0:T(8,128)(2,1)} %get-tuple-element.60) | copy-start | bytes 1376260
  109.8 14.7 %collective-permute-start.16 = (bf16[64,3584]{1,0:T(8,128)(2,1)S(1)}, bf16[64,3584]{1,0:T(8,128)(2,1)S(1)}, u32[]{:S(2)}, u32[]{:S(2)}) collective-permute-start(bf16[64,3584]{1,0:T(8,128)(2,1)S(1)} %copy-done.20), channel_id=1, source_target_pairs={{0,2},{1,3},{4,0},{5,1},{8,4},{9,5},{12,8},{13,9},{14,12},{15,13},... | collective-permute-start | bytes 1376264 | tf_op jit(solution)/shard_map/ppermute | solution.py:94
  110.8 0.8 copy-start.9
  114.4 15.4 %collective-permute-start.23 = (bf16[64,3584]{1,0:T(8,128)(2,1)}, bf16[64,3584]{1,0:T(8,128)(2,1)S(1)}, u32[]{:S(2)}, u32[]{:S(2)}) collective-permute-start(bf16[64,3584]{1,0:T(8,128)(2,1)} %shard_map.108), channel_id=1, source_target_pairs={{0,2},{1,3},{4,0},{5,1},{8,4},{9,5},{12,8},{13,9},{14,12},{15,13},... | collective-permute-start | bytes 1376264 | tf_op jit(solution)/shard_map/ppermute | solution.py:94
  115.5 0.8 copy-start.8
  119.1 15.5 %collective-permute-start.13 = (bf16[64,3584]{1,0:T(8,128)(2,1)}, bf16[64,3584]{1,0:T(8,128)(2,1)S(1)}, u32[]{:S(2)}, u32[]{:S(2)}) collective-permute-start(bf16[64,3584]{1,0:T(8,128)(2,1)} %shard_map.101), channel_id=1, source_target_pairs={{0,4},{1,5},{4,8},{5,9},{8,12},{9,13},{12,14},{13,15},{14,10},{15,... | collective-permute-start | bytes 1376264 | tf_op jit(solution)/shard_map/ppermute | solution.py:94
  120.0 0.8 copy-start.17
  123.5 15.7 %collective-permute-start.20 = (bf16[64,3584]{1,0:T(8,128)(2,1)}, bf16[64,3584]{1,0:T(8,128)(2,1)S(1)}, u32[]{:S(2)}, u32[]{:S(2)}) collective-permute-start(bf16[64,3584]{1,0:T(8,128)(2,1)} %shard_map.106), channel_id=1, source_target_pairs={{0,4},{1,5},{4,8},{5,9},{8,12},{9,13},{12,14},{13,15},{14,10},{15,... | collective-permute-start | bytes 1376264 | tf_op jit(solution)/shard_map/ppermute | solution.py:94
  124.5 0.8 copy-start.10
  128.0 15.9 %collective-permute-start.17 = (bf16[64,3584]{1,0:T(8,128)(2,1)}, bf16[64,3584]{1,0:T(8,128)(2,1)S(1)}, u32[]{:S(2)}, u32[]{:S(2)}) collective-permute-start(bf16[64,3584]{1,0:T(8,128)(2,1)} %shard_map.104), channel_id=1, source_target_pairs={{0,2},{1,3},{4,0},{5,1},{8,4},{9,5},{12,8},{13,9},{14,12},{15,13},... | collective-permute-start | bytes 1376264 | tf_op jit(solution)/shard_map/ppermute | solution.py:94
  129.8 0.8 copy-start.11
  133.3 18.2 %collective-permute-start.24 = (bf16[64,3584]{1,0:T(8,128)(2,1)}, bf16[64,3584]{1,0:T(8,128)(2,1)S(1)}, u32[]{:S(2)}, u32[]{:S(2)}) collective-permute-start(bf16[64,3584]{1,0:T(8,128)(2,1)} %shard_map.109), channel_id=1, source_target_pairs={{0,2},{1,3},{4,0},{5,1},{8,4},{9,5},{12,8},{13,9},{14,12},{15,13},... | collective-permute-start | bytes 1376264 | tf_op jit(solution)/shard_map/ppermute | solution.py:94
  134.6 0.8 copy-start.12
  138.1 17.9 %collective-permute-start.14 = (bf16[64,3584]{1,0:T(8,128)(2,1)}, bf16[64,3584]{1,0:T(8,128)(2,1)S(1)}, u32[]{:S(2)}, u32[]{:S(2)}) collective-permute-start(bf16[64,3584]{1,0:T(8,128)(2,1)} %shard_map.102), channel_id=1, source_target_pairs={{0,4},{1,5},{4,8},{5,9},{8,12},{9,13},{12,14},{13,15},{14,10},{15,... | collective-permute-start | bytes 1376264 | tf_op jit(solution)/shard_map/ppermute | solution.py:94
  139.2 0.8 copy-start.13
  142.7 17.9 %collective-permute-start.21 = (bf16[64,3584]{1,0:T(8,128)(2,1)}, bf16[64,3584]{1,0:T(8,128)(2,1)S(1)}, u32[]{:S(2)}, u32[]{:S(2)}) collective-permute-start(bf16[64,3584]{1,0:T(8,128)(2,1)} %shard_map.107), channel_id=1, source_target_pairs={{0,4},{1,5},{4,8},{5,9},{8,12},{9,13},{12,14},{13,15},{14,10},{15,... | collective-permute-start | bytes 1376264 | tf_op jit(solution)/shard_map/ppermute | solution.py:94
  143.9 0.8 copy-start.14
  147.4 20.8 %copy-start.4 = (bf16[64,7168]{1,0:T(8,128)(2,1)S(1)}, bf16[64,7168]{1,0:T(8,128)(2,1)}, u32[]{:S(2)}) copy-start(bf16[64,7168]{1,0:T(8,128)(2,1)} %shard_map.97.refs_0_.refs_1_) | copy-start | bytes 2752516
  147.4 20.8 %copy-start.7 = (s32[10]{0:T(128)S(1)}, s32[10]{0:T(128)}, u32[]{:S(2)}) copy-start(s32[10]{0:T(128)} %copy-done.6) | copy-start | bytes 124
  147.4 13.9 %collective-permute-start.18 = (bf16[64,3584]{1,0:T(8,128)(2,1)}, bf16[64,3584]{1,0:T(8,128)(2,1)S(1)}, u32[]{:S(2)}, u32[]{:S(2)}) collective-permute-start(bf16[64,3584]{1,0:T(8,128)(2,1)} %shard_map.105), channel_id=1, source_target_pairs={{0,2},{1,3},{4,0},{5,1},{8,4},{9,5},{12,8},{13,9},{14,12},{15,13},... | collective-permute-start | bytes 1376264 | tf_op jit(solution)/shard_map/ppermute | solution.py:94
  151.5 0.8 copy-start.15
  155.0 11.8 %collective-permute-start.25 = (bf16[64,3584]{1,0:T(8,128)(2,1)}, bf16[64,3584]{1,0:T(8,128)(2,1)S(1)}, u32[]{:S(2)}, u32[]{:S(2)}) collective-permute-start(bf16[64,3584]{1,0:T(8,128)(2,1)} %shard_map.110), channel_id=1, source_target_pairs={{0,2},{1,3},{4,0},{5,1},{8,4},{9,5},{12,8},{13,9},{14,12},{15,13},... | collective-permute-start | bytes 1376264 | tf_op jit(solution)/shard_map/ppermute | solution.py:94
  156.0 0.8 copy-start.16
  159.5 8.7 %collective-permute-start.15 = (bf16[64,3584]{1,0:T(8,128)(2,1)}, bf16[64,3584]{1,0:T(8,128)(2,1)S(1)}, u32[]{:S(2)}, u32[]{:S(2)}) collective-permute-start(bf16[64,3584]{1,0:T(8,128)(2,1)} %shard_map.103), channel_id=1, source_target_pairs={{0,4},{1,5},{4,8},{5,9},{8,12},{9,13},{12,14},{13,15},{14,10},{15,... | collective-permute-start | bytes 1376264 | tf_op jit(solution)/shard_map/ppermute | solution.py:94
  168.2 2.0 %copy-start = (bf16[512,3584]{1,0:T(8,128)(2,1)S(1)}, bf16[512,3584]{1,0:T(8,128)(2,1)}, u32[]{:S(2)}) copy-start(bf16[512,3584]{1,0:T(8,128)(2,1)} %shard_map.100.table_ref.refs_3_) | copy-start | bytes 11010052
  170.3 2.0 %copy-start.1 = (bf16[512,3584]{1,0:T(8,128)(2,1)S(1)}, bf16[512,3584]{1,0:T(8,128)(2,1)}, u32[]{:S(2)}) copy-start(bf16[512,3584]{1,0:T(8,128)(2,1)} %shard_map.99.table_ref.refs_2_) | copy-start | bytes 11010052

commit v10 on v8

--- a/solution.py
+++ b/solution.py
@@ -396,7 +396,7 @@
 
     return local_call(
         kernel,
-        jax.ShapeDtypeStruct((tokens, half), jnp.bfloat16),
+        pltpu.VMEM((tokens, half), jnp.bfloat16),
         [where, hidden, down],
         flops=2 * tokens * units * half,
         bytes_accessed=2 * half * (units + tokens),
@@ -406,24 +406,39 @@
 def add_rows(where, position, table, moved):
     rows, width = moved.shape
     steps = 2
-
-    def kernel(where_ref, table_ref, moved_ref, out_ref):
-        total = table_ref[...].astype(jnp.float32) + moved_ref[...].astype(jnp.float32)
-        out_ref[...] = total.astype(jnp.bfloat16)
-
-    here = pl.BlockSpec((rows, width // steps), lambda i, where: (0, i))
+    tile = width // steps
+
+    def kernel(where_ref, table_ref, moved_ref, out_ref, came_ref, sems):
+        cols = [slice(k * tile, (k + 1) * tile) for k in range(steps)]
+        reads = [
+            pltpu.make_async_copy(moved_ref.at[:, cols[k]], came_ref.at[:, cols[k]], sems.at[0, k])
+            for k in range(steps)
+        ]
+        writes = [
+            pltpu.make_async_copy(came_ref.at[:, cols[k]], out_ref.at[:, cols[k]], sems.at[1, k])
+            for k in range(steps)
+        ]
+        for read in reads:
+            read.start()
+        at = pl.multiple_of(where_ref[position] * rows, rows)
+        for k in range(steps):
+            total = table_ref[pl.ds(at, rows), cols[k]].astype(jnp.float32)
+            reads[k].wait()
+            total = total + came_ref[:, cols[k]].astype(jnp.float32)
+            came_ref[:, cols[k]] = total.astype(jnp.bfloat16)
+            writes[k].start()
+        for write in writes:
+            write.wait()
+
     return pl.pallas_call(
         kernel,
-        grid_spec=pltpu.PrefetchScalarGridSpec(
-            num_scalar_prefetch=1,
-            grid=(steps,),
-            in_specs=[
-                pl.BlockSpec((rows, width // steps), lambda i, where: (where[position], i)),
-                here,
-            ],
-            out_specs=here,
-        ),
+        in_specs=[IN_SMEM, IN_VMEM, IN_HBM],
+        out_specs=IN_HBM,
         out_shape=pltpu.HBM((rows, width), jnp.bfloat16),
+        scratch_shapes=[
+            pltpu.VMEM((rows, width), jnp.bfloat16),
+            pltpu.SemaphoreType.DMA((2, steps)),
+        ],
         compiler_params=pltpu.CompilerParams(vmem_limit_bytes=VMEM_BYTES),
         cost_estimate=pl.CostEstimate(
             flops=rows * width, bytes_accessed=rows * width * 6, transcendentals=0
@@ -442,7 +457,7 @@
 
     return local_call(
         kernel,
-        jax.ShapeDtypeStruct((rows, model_width), jnp.bfloat16),
+        pltpu.VMEM((rows, model_width), jnp.bfloat16),
         [where, *pieces],
         flops=rows * model_width,
         bytes_accessed=rows * model_width * 4,

time: 166 us -> 166 us (level)
  no operation moved by 1% of the time
where the time goes in v10:
time: 166 us
  waiting for transfers between devices  81.1 us (49%)
  Pallas kernels  55.1 us (33%)
  starting transfers between devices  24.9 us (15%)
  local copies, waits for them, and re-layouts  2.74 us (2%)
  other arithmetic  1.82 us (1%)
    ppermute x22, waiting for transfers between devices, ring_shift(): return lax.ppermute(value, 'ep', pairs)  79.5 us
    pallas_call x10, Pallas kernels, local_call(): pl.pallas_call(kernel, out_shape=out_shape, in_specs=[IN_SMEM if k == 0 e...  37.7 us
    ppermute x22, starting transfers between devices, ring_shift(): return lax.ppermute(value, 'ep', pairs)  23.5 us
    pallas_call x10, Pallas kernels, add_rows(): pl.pallas_call(kernel, in_specs=[IN_SMEM, IN_VMEM, IN_HBM], out_specs=IN_...  15.1 us
  transfers between devices with their start and end apart: 26, of which 16 were waited for; matrix products, arithmetic and copies ran while one was open for 1% of the time, Pallas kernels for 29%

profile of v10, /device:TPU:0, one launch (start us, length us, event | category | flops | bytes accessed | tf_op | source)
XLA Modules:
  0.0 165.9 jit_solution(13266548419930662665)
XLA Ops:
  0.0 1.8 %add_convert_fusion = bf16[1024,448]{0,1:T(8,128)(2,1)S(1)} fusion(bf16[1024,448]{0,1:T(8,128)(2,1)} %param.10, bf16[1024,448]{0,1:T(8,128)(2,1)} %param.9), kind=kLoop, calls=%fused_computation | loop fusion | flops 1835008 | bytes 2752512 | tf_op jit(solution)/shard_map/convert_element_type | solution.py:520
  1.8 0.5 copy.13
  2.4 0.5 collective-permute-start
  3.0 1.5 collective-permute-done.swapped_ref
  4.5 0.4 collective-permute-start.1
  5.0 0.4 collective-permute-start.9
  5.6 0.7 dynamic-slice_bitcast_fusion.1.where_ref
  6.3 2.2 %shard_map.91.refs_0_.refs_5_ = bf16[528,896]{1,0:T(8,128)(2,1)} custom-call(s32[10]{0:T(128)S(1)} %dynamic-slice_bitcast_fusion.1.where_ref, bf16[8,2,64,448]{3,2,1,0:T(8,128)(2,1)S(1)} %bitcast.7, bf16[8,64,448]{2,1,0:T(8,128)(2,1)S(1)} %collective-permute-done.swapped_ref, s32[64,2]{1,0:T(8,128)S(1)} %copy.14.routes_ref, f32[64,2]{1,0:T(8,128)S(1)} %copy.15.gain_ref), custom_call_target="tpu_custom_call" | custom-call | flops 1835008 | bytes 1835008 | tf_op jit(solution)/shard_map/pallas_call | solution.py:107
  8.5 2.7 %collective-permute-start.4 = (bf16[528,896]{1,0:T(8,128)(2,1)}, bf16[528,896]{1,0:T(8,128)(2,1)S(1)}, u32[]{:S(2)}, u32[]{:S(2)}) collective-permute-start(bf16[528,896]{1,0:T(8,128)(2,1)} %shard_map.91.refs_0_.refs_5_), channel_id=1, source_target_pairs={{0,4},{1,5},{4,8},{5,9},{8,12},{9,13},{12,14},{13,15},{14,10},{15,... | collective-permute-start | bytes 2838536 | tf_op jit(solution)/shard_map/ppermute | solution.py:94
  11.2 21.6 %collective-permute-done.4.refs_1_.refs_12_ = bf16[528,896]{1,0:T(8,128)(2,1)S(1)} collective-permute-done((bf16[528,896]{1,0:T(8,128)(2,1)}, bf16[528,896]{1,0:T(8,128)(2,1)S(1)}, u32[]{:S(2)}, u32[]{:S(2)}) %collective-permute-start.4) | collective-permute-done | bytes 946208 | tf_op jit(solution)/shard_map/ppermute | solution.py:94
  32.8 1.8 %collective-permute-start.6 = (bf16[528,896]{1,0:T(8,128)(2,1)S(1)}, bf16[528,896]{1,0:T(8,128)(2,1)S(1)}, u32[]{:S(2)}, u32[]{:S(2)}) collective-permute-start(bf16[528,896]{1,0:T(8,128)(2,1)S(1)} %collective-permute-done.4.refs_1_.refs_12_), channel_id=1, source_target_pairs={{0,4},{1,5},{4,8},{5,9},{8,12},{9,13},{12,14},{13,15},{14,10},{15,... | collective-permute-start | bytes 2838536 | tf_op jit(solution)/shard_map/ppermute | solution.py:94
  34.9 20.6 %collective-permute-done.6.refs_1_.refs_11_ = bf16[528,896]{1,0:T(8,128)(2,1)S(1)} collective-permute-done((bf16[528,896]{1,0:T(8,128)(2,1)S(1)}, bf16[528,896]{1,0:T(8,128)(2,1)S(1)}, u32[]{:S(2)}, u32[]{:S(2)}) %collective-permute-start.6) | collective-permute-done | bytes 946208 | tf_op jit(solution)/shard_map/ppermute | solution.py:94
  55.5 1.6 collective-permute-start.8
  57.1 0.5 collective-permute-start.7
  57.6 1.2 copy-done
  58.7 4.4 %shard_map.92 = (bf16[64,896]{1,0:T(8,128)(2,1)S(1)}, f32[512,1024]{1,0:T(8,128)S(1)}) custom-call(s32[10]{0:T(128)S(1)} %dynamic-slice_bitcast_fusion.1.where_ref, bf16[528,896]{1,0:T(8,128)(2,1)S(1)} %copy-done, f32[8,1,896]{2,1,0:T(1,128)S(1)} %bitcast.8, bf16[7168,256]{1,0:T(8,128)(2,1)} %refs_3_.3, bf16[7168,256]{1,0:T(8,128)(2,1)} %refs_4_.2, ...), custom_call_target="tpu_custom_call" | custom-call | flops 2818572288 | bytes 6946816 | tf_op jit(solution)/shard_map/pallas_call | solution.py:107
  63.2 6.8 %shard_map.93 = (bf16[64,896]{1,0:T(8,128)(2,1)S(1)}, bf16[64,896]{1,0:T(8,128)(2,1)S(1)}, f32[512,1024]{1,0:T(8,128)S(1)}) custom-call(s32[10]{0:T(128)S(1)} %dynamic-slice_bitcast_fusion.1.where_ref, bf16[528,896]{1,0:T(8,128)(2,1)S(1)} %collective-permute-done.3.refs_0_.refs_6_, ...), custom_call_target="tpu_custom_call", output_to_operand_aliasing={{2}: (8, {})} | custom-call | flops 5637144576 | bytes 9699328 | tf_op jit(solution)/shard_map/pallas_call | solution.py:107
  69.9 6.8 %shard_map.94 = (bf16[64,896]{1,0:T(8,128)(2,1)S(1)}, bf16[64,896]{1,0:T(8,128)(2,1)S(1)}, f32[512,1024]{1,0:T(8,128)S(1)}) custom-call(s32[10]{0:T(128)S(1)} %dynamic-slice_bitcast_fusion.1.where_ref, bf16[528,896]{1,0:T(8,128)(2,1)S(1)} %collective-permute-done.5.refs_0_.refs_7_, ...), custom_call_target="tpu_custom_call", output_to_operand_aliasing={{2}: (8, {})} | custom-call | flops 5637144576 | bytes 9699328 | tf_op jit(solution)/shard_map/pallas_call | solution.py:107
  76.7 0.6 collective-permute-done.8.refs_1_.refs_10_
  77.3 1.0 collective-permute-done.7.refs_0_.refs_8_
  78.3 0.8 collective-permute-start.11
  79.2 1.3 collective-permute-start.10
  80.5 6.8 %shard_map.95 = (bf16[64,896]{1,0:T(8,128)(2,1)S(1)}, bf16[64,896]{1,0:T(8,128)(2,1)S(1)}, f32[512,1024]{1,0:T(8,128)S(1)}, bf16[4,896,256]{2,1,0:T(8,128)(2,1)S(1)}, bf16[512,7168]{1,0:T(8,128)(2,1)S(1)}) custom-call(s32[10]{0:T(128)S(1)} %dynamic-slice_bitcast_fusion.1.where_ref, ...), custom_call_target="tpu_custom_call", output_to_operand_aliasing={{2}: (8, {})} | custom-call | flops 5637144576 | bytes 9699328 | tf_op jit(solution)/shard_map/pallas_call | solution.py:107
  87.3 0.9 collective-permute-done.11.refs_1_
  88.3 1.5 collective-permute-done.10.refs_0_.refs_9_
  89.7 2.0 %shard_map.96 = (bf16[64,896]{1,0:T(8,128)(2,1)S(1)}, bf16[512,512]{1,0:T(8,128)(2,1)S(1)}) custom-call(s32[10]{0:T(128)S(1)} %dynamic-slice_bitcast_fusion.1.where_ref, bf16[272,896]{1,0:T(8,128)(2,1)S(1)} %collective-permute-done.10.refs_0_.refs_9_, bf16[256,896]{1,0:T(8,128)(2,1)S(1)} %collective-permute-done.11.refs_1_, f32[8,1,896]{2,1,0:T(1,128)S(1)} %bitcast.12, ...), custom_call_target="tpu_custom_call" | custom-call | flops 2818572288 | bytes 6946816 | tf_op jit(solution)/shard_map/pallas_call | solution.py:107
  91.8 2.9 %shard_map.98 = (bf16[512,512]{1,0:T(8,128)(2,1)S(1)}, bf16[64,3584]{1,0:T(8,128)(2,1)}, bf16[64,3584]{1,0:T(8,128)(2,1)}, bf16[64,3584]{1,0:T(8,128)(2,1)}, bf16[64,3584]{1,0:T(8,128)(2,1)}) custom-call(s32[10]{0:T(128)S(1)} %dynamic-slice_bitcast_fusion.1.where_ref, bf16[512,512]{1,0:T(8,128)(2,1)S(1)} %get-tuple-element.54.hidden_ref, ...), custom_call_target="tpu_custom_call" | custom-call | flops 939524096 | bytes 7340032 | tf_op jit(solution)/shard_map/pallas_call | solution.py:107
  94.6 1.1 collective-permute-start.22
  95.8 0.9 collective-permute-start.12
  96.7 0.6 shard_map.97.refs_0_.refs_1_
  97.3 1.0 collective-permute-start.19
  98.3 2.6 %shard_map.100.table_ref.refs_3_ = bf16[512,3584]{1,0:T(8,128)(2,1)S(1)} custom-call(s32[10]{0:T(128)S(1)} %dynamic-slice_bitcast_fusion.1.where_ref, bf16[512,512]{1,0:T(8,128)(2,1)S(1)} %get-tuple-element.58.hidden_ref, bf16[512,7168]{1,0:T(8,128)(2,1)S(1)} %get-tuple-element.55.down_ref), custom_call_target="tpu_custom_call" | custom-call | flops 1879048192 | bytes 7340032 | tf_op jit(solution)/shard_map/pallas_call | solution.py:107
  101.0 2.6 %shard_map.99.table_ref.refs_2_ = bf16[512,3584]{1,0:T(8,128)(2,1)S(1)} custom-call(s32[10]{0:T(128)S(1)} %dynamic-slice_bitcast_fusion.1.where_ref, bf16[512,512]{1,0:T(8,128)(2,1)S(1)} %get-tuple-element.58.hidden_ref, bf16[512,7168]{1,0:T(8,128)(2,1)S(1)} %get-tuple-element.55.down_ref), custom_call_target="tpu_custom_call" | custom-call | flops 1879048192 | bytes 7340032 | tf_op jit(solution)/shard_map/pallas_call | solution.py:107
  103.6 1.1 collective-permute-start.16
  104.7 1.2 collective-permute-done.22.moved_ref
  105.8 1.5 shard_map.108
  107.4 0.9 collective-permute-start.23
  108.3 1.2 collective-permute-done.12.moved_ref
  109.5 1.5 shard_map.101
  111.0 0.9 collective-permute-start.13
  111.9 7.4 %collective-permute-done.19.moved_ref = bf16[64,3584]{1,0:T(8,128)(2,1)S(1)} collective-permute-done((bf16[64,3584]{1,0:T(8,128)(2,1)}, bf16[64,3584]{1,0:T(8,128)(2,1)S(1)}, u32[]{:S(2)}, u32[]{:S(2)}) %collective-permute-start.19) | collective-permute-done | bytes 458784 | tf_op jit(solution)/shard_map/ppermute | solution.py:94
  119.3 1.5 shard_map.106
  120.8 0.9 collective-permute-start.20
  121.8 1.5 shard_map.104
  123.3 1.2 collective-permute-start.17
  124.5 2.4 %collective-permute-done.23.moved_ref = bf16[64,3584]{1,0:T(8,128)(2,1)S(1)} collective-permute-done((bf16[64,3584]{1,0:T(8,128)(2,1)}, bf16[64,3584]{1,0:T(8,128)(2,1)S(1)}, u32[]{:S(2)}, u32[]{:S(2)}) %collective-permute-start.23) | collective-permute-done | bytes 458784 | tf_op jit(solution)/shard_map/ppermute | solution.py:94
  126.9 1.5 shard_map.109
  128.4 1.1 collective-permute-start.24
  129.5 1.5 shard_map.102
  131.0 1.0 collective-permute-start.14
  132.1 6.9 %collective-permute-done.20.moved_ref = bf16[64,3584]{1,0:T(8,128)(2,1)S(1)} collective-permute-done((bf16[64,3584]{1,0:T(8,128)(2,1)}, bf16[64,3584]{1,0:T(8,128)(2,1)S(1)}, u32[]{:S(2)}, u32[]{:S(2)}) %collective-permute-start.20) | collective-permute-done | bytes 458784 | tf_op jit(solution)/shard_map/ppermute | solution.py:94
  139.0 1.5 shard_map.107
  140.5 0.9 collective-permute-start.21
  141.4 1.5 shard_map.105
  143.0 1.2 collective-permute-start.18
  144.2 2.7 %collective-permute-done.24.moved_ref = bf16[64,3584]{1,0:T(8,128)(2,1)S(1)} collective-permute-done((bf16[64,3584]{1,0:T(8,128)(2,1)}, bf16[64,3584]{1,0:T(8,128)(2,1)S(1)}, u32[]{:S(2)}, u32[]{:S(2)}) %collective-permute-start.24) | collective-permute-done | bytes 458784 | tf_op jit(solution)/shard_map/ppermute | solution.py:94
  146.9 1.5 shard_map.110
  148.4 1.2 collective-permute-start.25
  149.6 1.5 shard_map.103
  151.1 0.9 collective-permute-start.15
  152.0 6.6 %collective-permute-done.21.refs_6_ = bf16[64,3584]{1,0:T(8,128)(2,1)S(1)} collective-permute-done((bf16[64,3584]{1,0:T(8,128)(2,1)}, bf16[64,3584]{1,0:T(8,128)(2,1)S(1)}, u32[]{:S(2)}, u32[]{:S(2)}) %collective-permute-start.21) | collective-permute-done | bytes 458784 | tf_op jit(solution)/shard_map/ppermute | solution.py:94
  158.6 4.1 %collective-permute-done.25.refs_7_ = bf16[64,3584]{1,0:T(8,128)(2,1)S(1)} collective-permute-done((bf16[64,3584]{1,0:T(8,128)(2,1)}, bf16[64,3584]{1,0:T(8,128)(2,1)S(1)}, u32[]{:S(2)}, u32[]{:S(2)}) %collective-permute-start.25) | collective-permute-done | bytes 458784 | tf_op jit(solution)/shard_map/ppermute | solution.py:94
  162.8 0.8 collective-permute-done.15.refs_4_
  163.6 2.3 %shard_map.111 = bf16[64,7168]{1,0:T(8,128)(2,1)} custom-call(s32[10]{0:T(128)S(1)} %dynamic-slice_bitcast_fusion.1.where_ref, bf16[64,7168]{1,0:T(8,128)(2,1)S(1)} %shard_map.97.refs_0_.refs_1_, bf16[64,7168]{1,0:T(8,128)(2,1)S(1)} %shard_map.97.refs_0_.refs_1_, bf16[512,3584]{1,0:T(8,128)(2,1)S(1)} %shard_map.99.table_ref.refs_2_, ...), custom_call_target="tpu_custom_call" | custom-call | flops 1376256 | bytes 4587520 | tf_op jit(solution)/shard_map/pallas_call | solution.py:484
  (29 shorter events, 0.7 us)
Async XLA Ops:
  0.0 5.4 %copy-start.3 = (s32[64,2]{0,1:T(2,128)S(1)}, s32[64,2]{0,1:T(2,128)}, u32[]{:S(2)}) copy-start(s32[64,2]{0,1:T(2,128)} %param.12) | copy-start | bytes 1540
  0.0 5.5 %copy-start.4 = (f32[64,2]{0,1:T(2,128)S(1)}, f32[64,2]{0,1:T(2,128)}, u32[]{:S(2)}) copy-start(f32[64,2]{0,1:T(2,128)} %param.13) | copy-start | bytes 1540
  0.0 57.5 %copy-start.2 = (f32[7168]{0:T(1024)S(1)}, f32[7168]{0:T(1024)}, u32[]{:S(2)}) copy-start(f32[7168]{0:T(1024)} %param.11) | copy-start | bytes 86020
  2.4 2.1 %collective-permute-start = (bf16[8,64,448]{2,1,0:T(8,128)(2,1)S(1)}, bf16[8,64,448]{2,1,0:T(8,128)(2,1)S(1)}, u32[]{:S(2)}, u32[]{:S(2)}) collective-permute-start(bf16[8,64,448]{2,1,0:T(8,128)(2,1)S(1)} %dynamic-slice_bitcast_fusion), channel_id=1, source_target_pairs={{0,1},{1,0},{2,3},{3,2},{4,5},{5,4},{6,7},{7,6},{8,9},{9,8},{10,11... | collective-permute-start | bytes 1376264 | tf_op jit(solution)/shard_map/ppermute | solution.py:84
  4.5 53.0 %collective-permute-start.1 = (bf16[7168,256]{1,0:T(8,128)(2,1)}, bf16[7168,256]{1,0:T(8,128)(2,1)}, u32[]{:S(2)}, u32[]{:S(2)}) collective-permute-start(bf16[7168,256]{1,0:T(8,128)(2,1)} %refs_3_.3), channel_id=1, source_target_pairs={{0,1},{1,0},{2,3},{3,2},{4,5},{5,4},{6,7},{7,6},{8,9},{9,8},{10,11... | collective-permute-start | bytes 11010056 | tf_op jit(solution)/shard_map/ppermute | solution.py:84
  4.9 52.7 %collective-permute-start.2 = (bf16[7168,256]{1,0:T(8,128)(2,1)}, bf16[7168,256]{1,0:T(8,128)(2,1)}, u32[]{:S(2)}, u32[]{:S(2)}) collective-permute-start(bf16[7168,256]{1,0:T(8,128)(2,1)} %refs_4_.2), channel_id=1, source_target_pairs={{0,1},{1,0},{2,3},{3,2},{4,5},{5,4},{6,7},{7,6},{8,9},{9,8},{10,11... | collective-permute-start | bytes 11010056 | tf_op jit(solution)/shard_map/ppermute | solution.py:84
  5.0 75.5 %collective-permute-start.9 = (bf16[256,7168]{1,0:T(8,128)(2,1)}, bf16[256,7168]{1,0:T(8,128)(2,1)}, u32[]{:S(2)}, u32[]{:S(2)}) collective-permute-start(bf16[256,7168]{1,0:T(8,128)(2,1)} %refs_8_), channel_id=1, source_target_pairs={{0,1},{1,0},{2,3},{3,2},{4,5},{5,4},{6,7},{7,6},{8,9},{9,8},{10,11... | collective-permute-start | bytes 11010056 | tf_op jit(solution)/shard_map/ppermute | solution.py:84
  8.5 24.4 %collective-permute-start.4 = (bf16[528,896]{1,0:T(8,128)(2,1)}, bf16[528,896]{1,0:T(8,128)(2,1)S(1)}, u32[]{:S(2)}, u32[]{:S(2)}) collective-permute-start(bf16[528,896]{1,0:T(8,128)(2,1)} %shard_map.91.refs_0_.refs_5_), channel_id=1, source_target_pairs={{0,4},{1,5},{4,8},{5,9},{8,12},{9,13},{12,14},{13,15},{14,10},{15,... | collective-permute-start | bytes 2838536 | tf_op jit(solution)/shard_map/ppermute | solution.py:94
  11.2 23.4 %collective-permute-start.3 = (bf16[528,896]{1,0:T(8,128)(2,1)}, bf16[528,896]{1,0:T(8,128)(2,1)S(1)}, u32[]{:S(2)}, u32[]{:S(2)}) collective-permute-start(bf16[528,896]{1,0:T(8,128)(2,1)} %shard_map.91.refs_0_.refs_5_), channel_id=1, source_target_pairs={{0,2},{1,3},{4,0},{5,1},{8,4},{9,5},{12,8},{13,9},{14,12},{15,13},... | collective-permute-start | bytes 2838536 | tf_op jit(solution)/shard_map/ppermute | solution.py:94
  32.8 22.7 %collective-permute-start.6 = (bf16[528,896]{1,0:T(8,128)(2,1)S(1)}, bf16[528,896]{1,0:T(8,128)(2,1)S(1)}, u32[]{:S(2)}, u32[]{:S(2)}) collective-permute-start(bf16[528,896]{1,0:T(8,128)(2,1)S(1)} %collective-permute-done.4.refs_1_.refs_12_), channel_id=1, source_target_pairs={{0,4},{1,5},{4,8},{5,9},{8,12},{9,13},{12,14},{13,15},{14,10},{15,... | collective-permute-start | bytes 2838536 | tf_op jit(solution)/shard_map/ppermute | solution.py:94
  34.6 22.4 %collective-permute-start.5 = (bf16[528,896]{1,0:T(8,128)(2,1)S(1)}, bf16[528,896]{1,0:T(8,128)(2,1)S(1)}, u32[]{:S(2)}, u32[]{:S(2)}) collective-permute-start(bf16[528,896]{1,0:T(8,128)(2,1)S(1)} %collective-permute-done.3.refs_0_.refs_6_), channel_id=1, source_target_pairs={{0,2},{1,3},{4,0},{5,1},{8,4},{9,5},{12,8},{13,9},{14,12},{15,13},... | collective-permute-start | bytes 2838536 | tf_op jit(solution)/shard_map/ppermute | solution.py:94
  55.5 21.8 %collective-permute-start.8 = (bf16[528,896]{1,0:T(8,128)(2,1)S(1)}, bf16[528,896]{1,0:T(8,128)(2,1)S(1)}, u32[]{:S(2)}, u32[]{:S(2)}) collective-permute-start(bf16[528,896]{1,0:T(8,128)(2,1)S(1)} %collective-permute-done.6.refs_1_.refs_11_), channel_id=1, source_target_pairs={{0,4},{1,5},{4,8},{5,9},{8,12},{9,13},{12,14},{13,15},{14,10},{15,... | collective-permute-start | bytes 2838536 | tf_op jit(solution)/shard_map/ppermute | solution.py:94
  57.1 21.2 %collective-permute-start.7 = (bf16[528,896]{1,0:T(8,128)(2,1)S(1)}, bf16[528,896]{1,0:T(8,128)(2,1)S(1)}, u32[]{:S(2)}, u32[]{:S(2)}) collective-permute-start(bf16[528,896]{1,0:T(8,128)(2,1)S(1)} %collective-permute-done.5.refs_0_.refs_7_), channel_id=1, source_target_pairs={{0,2},{1,3},{4,0},{5,1},{8,4},{9,5},{12,8},{13,9},{14,12},{15,13},... | collective-permute-start | bytes 2838536 | tf_op jit(solution)/shard_map/ppermute | solution.py:94
  57.5 1.2 copy-start
  78.3 9.9 %collective-permute-start.11 = (bf16[256,896]{1,0:T(8,128)(2,1)S(1)}, bf16[256,896]{1,0:T(8,128)(2,1)S(1)}, u32[]{:S(2)}, u32[]{:S(2)}) collective-permute-start(bf16[256,896]{1,0:T(8,128)(2,1)S(1)} %slice.7), channel_id=1, source_target_pairs={{0,2},{1,3},{4,0},{5,1},{8,4},{9,5},{12,8},{13,9},{14,12},{15,13},... | collective-permute-start | bytes 1376264 | tf_op jit(solution)/shard_map/ppermute | solution.py:94
  79.2 10.5 %copy-start.1 = (bf16[528,896]{1,0:T(8,128)(2,1)S(1)}, bf16[528,896]{1,0:T(8,128)(2,1)}, u32[]{:S(2)}) copy-start(bf16[528,896]{1,0:T(8,128)(2,1)} %shard_map.91.refs_0_.refs_5_) | copy-start | bytes 2838532
  79.2 10.5 %collective-permute-start.10 = (bf16[272,896]{1,0:T(8,128)(2,1)S(1)}, bf16[272,896]{1,0:T(8,128)(2,1)S(1)}, u32[]{:S(2)}, u32[]{:S(2)}) collective-permute-start(bf16[272,896]{1,0:T(8,128)(2,1)S(1)} %slice.6), channel_id=1, source_target_pairs={{0,4},{1,5},{4,8},{5,9},{8,12},{9,13},{12,14},{13,15},{14,10},{15,... | collective-permute-start | bytes 1462280 | tf_op jit(solution)/shard_map/ppermute | solution.py:94
  94.6 11.2 %collective-permute-start.22 = (bf16[64,3584]{1,0:T(8,128)(2,1)}, bf16[64,3584]{1,0:T(8,128)(2,1)S(1)}, u32[]{:S(2)}, u32[]{:S(2)}) collective-permute-start(bf16[64,3584]{1,0:T(8,128)(2,1)} %get-tuple-element.62), channel_id=1, source_target_pairs={{0,2},{1,3},{4,0},{5,1},{8,4},{9,5},{12,8},{13,9},{14,12},{15,13},... | collective-permute-start | bytes 1376264 | tf_op jit(solution)/shard_map/ppermute | solution.py:94
  95.8 13.7 %collective-permute-start.12 = (bf16[64,3584]{1,0:T(8,128)(2,1)}, bf16[64,3584]{1,0:T(8,128)(2,1)S(1)}, u32[]{:S(2)}, u32[]{:S(2)}) collective-permute-start(bf16[64,3584]{1,0:T(8,128)(2,1)} %get-tuple-element.59), channel_id=1, source_target_pairs={{0,4},{1,5},{4,8},{5,9},{8,12},{9,13},{12,14},{13,15},{14,10},{15,... | collective-permute-start | bytes 1376264 | tf_op jit(solution)/shard_map/ppermute | solution.py:94
  97.3 22.0 %collective-permute-start.19 = (bf16[64,3584]{1,0:T(8,128)(2,1)}, bf16[64,3584]{1,0:T(8,128)(2,1)S(1)}, u32[]{:S(2)}, u32[]{:S(2)}) collective-permute-start(bf16[64,3584]{1,0:T(8,128)(2,1)} %get-tuple-element.61), channel_id=1, source_target_pairs={{0,4},{1,5},{4,8},{5,9},{8,12},{9,13},{12,14},{13,15},{14,10},{15,... | collective-permute-start | bytes 1376264 | tf_op jit(solution)/shard_map/ppermute | solution.py:94
  101.0 2.6 %copy-start.5 = (bf16[64,3584]{1,0:T(8,128)(2,1)S(1)}, bf16[64,3584]{1,0:T(8,128)(2,1)}, u32[]{:S(2)}) copy-start(bf16[64,3584]{1,0:T(8,128)(2,1)} %get-tuple-element.60) | copy-start | bytes 1376260
  103.6 18.2 %collective-permute-start.16 = (bf16[64,3584]{1,0:T(8,128)(2,1)S(1)}, bf16[64,3584]{1,0:T(8,128)(2,1)S(1)}, u32[]{:S(2)}, u32[]{:S(2)}) collective-permute-start(bf16[64,3584]{1,0:T(8,128)(2,1)S(1)} %copy-done.5), channel_id=1, source_target_pairs={{0,2},{1,3},{4,0},{5,1},{8,4},{9,5},{12,8},{13,9},{14,12},{15,13},... | collective-permute-start | bytes 1376264 | tf_op jit(solution)/shard_map/ppermute | solution.py:94
  107.4 19.6 %collective-permute-start.23 = (bf16[64,3584]{1,0:T(8,128)(2,1)}, bf16[64,3584]{1,0:T(8,128)(2,1)S(1)}, u32[]{:S(2)}, u32[]{:S(2)}) collective-permute-start(bf16[64,3584]{1,0:T(8,128)(2,1)} %shard_map.108), channel_id=1, source_target_pairs={{0,2},{1,3},{4,0},{5,1},{8,4},{9,5},{12,8},{13,9},{14,12},{15,13},... | collective-permute-start | bytes 1376264 | tf_op jit(solution)/shard_map/ppermute | solution.py:94
  111.0 18.6 %collective-permute-start.13 = (bf16[64,3584]{1,0:T(8,128)(2,1)}, bf16[64,3584]{1,0:T(8,128)(2,1)S(1)}, u32[]{:S(2)}, u32[]{:S(2)}) collective-permute-start(bf16[64,3584]{1,0:T(8,128)(2,1)} %shard_map.101), channel_id=1, source_target_pairs={{0,4},{1,5},{4,8},{5,9},{8,12},{9,13},{12,14},{13,15},{14,10},{15,... | collective-permute-start | bytes 1376264 | tf_op jit(solution)/shard_map/ppermute | solution.py:94
  120.8 18.1 %collective-permute-start.20 = (bf16[64,3584]{1,0:T(8,128)(2,1)}, bf16[64,3584]{1,0:T(8,128)(2,1)S(1)}, u32[]{:S(2)}, u32[]{:S(2)}) collective-permute-start(bf16[64,3584]{1,0:T(8,128)(2,1)} %shard_map.106), channel_id=1, source_target_pairs={{0,4},{1,5},{4,8},{5,9},{8,12},{9,13},{12,14},{13,15},{14,10},{15,... | collective-permute-start | bytes 1376264 | tf_op jit(solution)/shard_map/ppermute | solution.py:94
  123.3 18.1 %collective-permute-start.17 = (bf16[64,3584]{1,0:T(8,128)(2,1)}, bf16[64,3584]{1,0:T(8,128)(2,1)S(1)}, u32[]{:S(2)}, u32[]{:S(2)}) collective-permute-start(bf16[64,3584]{1,0:T(8,128)(2,1)} %shard_map.104), channel_id=1, source_target_pairs={{0,2},{1,3},{4,0},{5,1},{8,4},{9,5},{12,8},{13,9},{14,12},{15,13},... | collective-permute-start | bytes 1376264 | tf_op jit(solution)/shard_map/ppermute | solution.py:94
  128.4 18.4 %collective-permute-start.24 = (bf16[64,3584]{1,0:T(8,128)(2,1)}, bf16[64,3584]{1,0:T(8,128)(2,1)S(1)}, u32[]{:S(2)}, u32[]{:S(2)}) collective-permute-start(bf16[64,3584]{1,0:T(8,128)(2,1)} %shard_map.109), channel_id=1, source_target_pairs={{0,2},{1,3},{4,0},{5,1},{8,4},{9,5},{12,8},{13,9},{14,12},{15,13},... | collective-permute-start | bytes 1376264 | tf_op jit(solution)/shard_map/ppermute | solution.py:94
  131.0 18.5 %collective-permute-start.14 = (bf16[64,3584]{1,0:T(8,128)(2,1)}, bf16[64,3584]{1,0:T(8,128)(2,1)S(1)}, u32[]{:S(2)}, u32[]{:S(2)}) collective-permute-start(bf16[64,3584]{1,0:T(8,128)(2,1)} %shard_map.102), channel_id=1, source_target_pairs={{0,4},{1,5},{4,8},{5,9},{8,12},{9,13},{12,14},{13,15},{14,10},{15,... | collective-permute-start | bytes 1376264 | tf_op jit(solution)/shard_map/ppermute | solution.py:94
  140.5 18.1 %collective-permute-start.21 = (bf16[64,3584]{1,0:T(8,128)(2,1)}, bf16[64,3584]{1,0:T(8,128)(2,1)S(1)}, u32[]{:S(2)}, u32[]{:S(2)}) collective-permute-start(bf16[64,3584]{1,0:T(8,128)(2,1)} %shard_map.107), channel_id=1, source_target_pairs={{0,4},{1,5},{4,8},{5,9},{8,12},{9,13},{12,14},{13,15},{14,10},{15,... | collective-permute-start | bytes 1376264 | tf_op jit(solution)/shard_map/ppermute | solution.py:94
  143.0 15.7 %collective-permute-start.18 = (bf16[64,3584]{1,0:T(8,128)(2,1)}, bf16[64,3584]{1,0:T(8,128)(2,1)S(1)}, u32[]{:S(2)}, u32[]{:S(2)}) collective-permute-start(bf16[64,3584]{1,0:T(8,128)(2,1)} %shard_map.105), channel_id=1, source_target_pairs={{0,2},{1,3},{4,0},{5,1},{8,4},{9,5},{12,8},{13,9},{14,12},{15,13},... | collective-permute-start | bytes 1376264 | tf_op jit(solution)/shard_map/ppermute | solution.py:94
  148.4 14.4 %collective-permute-start.25 = (bf16[64,3584]{1,0:T(8,128)(2,1)}, bf16[64,3584]{1,0:T(8,128)(2,1)S(1)}, u32[]{:S(2)}, u32[]{:S(2)}) collective-permute-start(bf16[64,3584]{1,0:T(8,128)(2,1)} %shard_map.110), channel_id=1, source_target_pairs={{0,2},{1,3},{4,0},{5,1},{8,4},{9,5},{12,8},{13,9},{14,12},{15,13},... | collective-permute-start | bytes 1376264 | tf_op jit(solution)/shard_map/ppermute | solution.py:94
  151.1 12.5 %collective-permute-start.15 = (bf16[64,3584]{1,0:T(8,128)(2,1)}, bf16[64,3584]{1,0:T(8,128)(2,1)S(1)}, u32[]{:S(2)}, u32[]{:S(2)}) collective-permute-start(bf16[64,3584]{1,0:T(8,128)(2,1)} %shard_map.103), channel_id=1, source_target_pairs={{0,4},{1,5},{4,8},{5,9},{8,12},{9,13},{12,14},{13,15},{14,10},{15,... | collective-permute-start | bytes 1376264 | tf_op jit(solution)/shard_map/ppermute | solution.py:94

commit v11 on v10

--- a/solution.py
+++ b/solution.py
@@ -96,6 +96,7 @@
 
 COST_SCALE = 3
 VMEM_BYTES = 20 * 1024 * 1024
+WIDE_VMEM_BYTES = 636 * 1024 * 1024 // 10
 IN_VMEM = pl.BlockSpec(memory_space=pltpu.VMEM)
 IN_SMEM = pl.BlockSpec(memory_space=pltpu.SMEM)
 IN_HBM = pl.BlockSpec(memory_space=pltpu.HBM)
@@ -396,7 +397,7 @@
 
     return local_call(
         kernel,
-        pltpu.VMEM((tokens, half), jnp.bfloat16),
+        pltpu.HBM((tokens, half), jnp.bfloat16),
         [where, hidden, down],
         flops=2 * tokens * units * half,
         bytes_accessed=2 * half * (units + tokens),
@@ -408,38 +409,48 @@
     steps = 2
     tile = width // steps
 
-    def kernel(where_ref, table_ref, moved_ref, out_ref, came_ref, sems):
-        cols = [slice(k * tile, (k + 1) * tile) for k in range(steps)]
-        reads = [
-            pltpu.make_async_copy(moved_ref.at[:, cols[k]], came_ref.at[:, cols[k]], sems.at[0, k])
-            for k in range(steps)
-        ]
-        writes = [
-            pltpu.make_async_copy(came_ref.at[:, cols[k]], out_ref.at[:, cols[k]], sems.at[1, k])
-            for k in range(steps)
-        ]
-        for read in reads:
-            read.start()
+    def kernel(where_ref, table_ref, moved_ref, out_ref, came_ref, here_ref, sems):
         at = pl.multiple_of(where_ref[position] * rows, rows)
+        reads, writes = [], []
         for k in range(steps):
-            total = table_ref[pl.ds(at, rows), cols[k]].astype(jnp.float32)
-            reads[k].wait()
-            total = total + came_ref[:, cols[k]].astype(jnp.float32)
-            came_ref[:, cols[k]] = total.astype(jnp.bfloat16)
+            cols = slice(k * tile, (k + 1) * tile)
+            reads.append(
+                [
+                    pltpu.make_async_copy(
+                        moved_ref.at[:, cols], came_ref.at[:, cols], sems.at[0, k]
+                    ),
+                    pltpu.make_async_copy(
+                        table_ref.at[pl.ds(at, rows), cols], here_ref.at[:, cols], sems.at[1, k]
+                    ),
+                ]
+            )
+            writes.append(
+                pltpu.make_async_copy(came_ref.at[:, cols], out_ref.at[:, cols], sems.at[2, k])
+            )
+        for pair in reads:
+            for read in pair:
+                read.start()
+        for k in range(steps):
+            cols = slice(k * tile, (k + 1) * tile)
+            for read in reads[k]:
+                read.wait()
+            total = here_ref[:, cols].astype(jnp.float32) + came_ref[:, cols].astype(jnp.float32)
+            came_ref[:, cols] = total.astype(jnp.bfloat16)
             writes[k].start()
         for write in writes:
             write.wait()
 
     return pl.pallas_call(
         kernel,
-        in_specs=[IN_SMEM, IN_VMEM, IN_HBM],
+        in_specs=[IN_SMEM, IN_HBM, IN_HBM],
         out_specs=IN_HBM,
         out_shape=pltpu.HBM((rows, width), jnp.bfloat16),
         scratch_shapes=[
             pltpu.VMEM((rows, width), jnp.bfloat16),
-            pltpu.SemaphoreType.DMA((2, steps)),
+            pltpu.VMEM((rows, width), jnp.bfloat16),
+            pltpu.SemaphoreType.DMA((3, steps)),
         ],
-        compiler_params=pltpu.CompilerParams(vmem_limit_bytes=VMEM_BYTES),
+        compiler_params=pltpu.CompilerParams(vmem_limit_bytes=WIDE_VMEM_BYTES),
         cost_estimate=pl.CostEstimate(
             flops=rows * width, bytes_accessed=rows * width * 6, transcendentals=0
         ),
@@ -457,7 +468,7 @@
 
     return local_call(
         kernel,
-        pltpu.VMEM((rows, model_width), jnp.bfloat16),
+        pltpu.HBM((rows, model_width), jnp.bfloat16),
         [where, *pieces],
         flops=rows * model_width,
         bytes_accessed=rows * model_width * 4,
@@ -467,36 +478,55 @@
 def final_sum(where, stream, tables, arrived):
     rows, model_width = stream.shape
     half = model_width // 2
-    steps = 2
+    counts = [len(part) for part in arrived]
     came = [value for part in arrived for value in part]
 
-    def kernel(where_ref, *refs):
-        out_ref = refs[-1]
+    def kernel(where_ref, stream_ref, *refs):
+        sources, (out_ref, held_ref, sum_ref, sems) = refs[: 2 + len(came)], refs[2 + len(came) :]
+        at = pl.multiple_of(where_ref[0] * rows, rows)
+        reads, writes, slot = [], [], 0
         for part in range(2):
-            total = refs[part][...].astype(jnp.float32) + refs[2 + part][...].astype(jnp.float32)
-            for k in range(len(arrived[part])):
-                total = total + refs[4 + k + part * len(arrived[0])][...].astype(jnp.float32)
-            start = pl.multiple_of(part * half + pl.program_id(0) * (half // steps), 128)
-            out_ref[:, pl.ds(start, half // steps)] = total.astype(jnp.bfloat16)
-
-    block = (rows, half // steps)
-    here = pl.BlockSpec(block, lambda i, where: (0, i))
+            cols = slice(part * half, (part + 1) * half)
+            first = 2 + sum(counts[:part])
+            taken = [stream_ref.at[:, cols], sources[part].at[pl.ds(at, rows), :]]
+            taken += [ref.at[...] for ref in sources[first : first + counts[part]]]
+            reads.append([])
+            for ref in taken:
+                copy = pltpu.make_async_copy(ref, held_ref.at[slot], sems.at[slot])
+                copy.start()
+                reads[part].append((copy, slot))
+                slot += 1
+        for part in range(2):
+            cols = slice(part * half, (part + 1) * half)
+            total = jnp.zeros((rows, half), jnp.float32)
+            for copy, k in reads[part]:
+                copy.wait()
+                total = total + held_ref[k].astype(jnp.float32)
+            sum_ref[:, cols] = total.astype(jnp.bfloat16)
+            write = pltpu.make_async_copy(
+                sum_ref.at[:, cols], out_ref.at[:, cols], sems.at[slot + part]
+            )
+            write.start()
+            writes.append(write)
+        for write in writes:
+            write.wait()
+
+    slots = 4 + len(came)
     return pl.pallas_call(
         kernel,
-        grid_spec=pltpu.PrefetchScalarGridSpec(
-            num_scalar_prefetch=1,
-            grid=(steps,),
-            in_specs=[here, pl.BlockSpec(block, lambda i, where: (0, steps + i))]
-            + [pl.BlockSpec(block, lambda i, where: (where[0], i))] * 2
-            + [here] * len(came),
-            out_specs=pl.BlockSpec((rows, model_width), lambda i, where: (0, 0)),
-        ),
+        in_specs=[IN_SMEM] + [IN_HBM] * (3 + len(came)),
+        out_specs=IN_HBM,
         out_shape=jax.ShapeDtypeStruct((rows, model_width), jnp.bfloat16),
-        compiler_params=pltpu.CompilerParams(vmem_limit_bytes=VMEM_BYTES),
+        scratch_shapes=[
+            pltpu.VMEM((slots, rows, half), jnp.bfloat16),
+            pltpu.VMEM((rows, model_width), jnp.bfloat16),
+            pltpu.SemaphoreType.DMA((slots + 2,)),
+        ],
+        compiler_params=pltpu.CompilerParams(vmem_limit_bytes=WIDE_VMEM_BYTES),
         cost_estimate=pl.CostEstimate(
             flops=rows * model_width * 3, bytes_accessed=rows * model_width * 10, transcendentals=0
         ),
-    )(where, stream, stream, *tables, *came)
+    )(where, stream, *tables, *came)
 
 
 def dense_body(residual, attn_out, norm_gain, expert_routes, route_gain, w_gate, w_up, w_down):

time: 166 us -> 171 us (1.030)
  Pallas kernels: 55.1 us -> 73.4 us
  waiting for transfers between devices: 81.1 us -> 67.1 us
    ppermute x22, waiting for transfers between devices: 79.5 us -> 65.5 us  [ring_shift(): return lax.ppermute(value, 'ep', pairs)]
    pallas_call x11, Pallas kernels: 17.4 us -> 31 us  [the longest x10 27.5 us: add_rows(): pl.pallas_call(kernel, in_specs=[IN_SMEM, IN_HBM, IN_HBM], out_specs=IN_H...]
    pallas_call x10, Pallas kernels: 37.7 us -> 42.4 us  [local_call(): pl.pallas_call(kernel, out_shape=out_shape, in_specs=[IN_SMEM if k == 0 e...]
  transfers between devices with their start and end apart: 26 -> 26, of which waited for: 16 -> 13; matrix products, arithmetic and copies ran while one was open for 1% -> 1% of each run, Pallas kernels for 29% -> 38%
where the time goes in v11:
time: 171 us
  Pallas kernels  73.4 us (43%)
  waiting for transfers between devices  67.1 us (39%)
  starting transfers between devices  25.2 us (15%)
  local copies, waits for them, and re-layouts  2.74 us (2%)
  other arithmetic  1.82 us (1%)
    ppermute x22, waiting for transfers between devices, ring_shift(): return lax.ppermute(value, 'ep', pairs)  65.5 us
    pallas_call x10, Pallas kernels, local_call(): pl.pallas_call(kernel, out_shape=out_shape, in_specs=[IN_SMEM if k == 0 e...  42.4 us
    pallas_call x10, Pallas kernels, add_rows(): pl.pallas_call(kernel, in_specs=[IN_SMEM, IN_HBM, IN_HBM], out_specs=IN_H...  27.5 us
    ppermute x22, starting transfers between devices, ring_shift(): return lax.ppermute(value, 'ep', pairs)  23.8 us
    pallas_call x1, Pallas kernels, final_sum(): pl.pallas_call(kernel, in_specs=[IN_SMEM] + [IN_HBM] * (3 + len(came)), o...  3.58 us
  transfers between devices with their start and end apart: 26, of which 13 were waited for; matrix products, arithmetic and copies ran while one was open for 1% of the time, Pallas kernels for 38%

profile of v11, /device:TPU:0, one launch (start us, length us, event | category | flops | bytes accessed | tf_op | source)
XLA Modules:
  0.0 170.6 jit_solution(11373559879774669160)
XLA Ops:
  0.0 1.8 %add_convert_fusion = bf16[1024,448]{0,1:T(8,128)(2,1)S(1)} fusion(bf16[1024,448]{0,1:T(8,128)(2,1)} %param.10, bf16[1024,448]{0,1:T(8,128)(2,1)} %param.9), kind=kLoop, calls=%fused_computation | loop fusion | flops 1835008 | bytes 2752512 | tf_op jit(solution)/shard_map/convert_element_type | solution.py:550
  1.8 0.5 copy.13
  2.4 0.5 collective-permute-start
  3.0 1.5 collective-permute-done.swapped_ref
  4.5 0.4 collective-permute-start.1
  4.9 0.1 collective-permute-start.2
  5.0 0.4 collective-permute-start.9
  5.4 0.1 copy.14.routes_ref
  5.6 0.7 dynamic-slice_bitcast_fusion.1.where_ref
  6.3 2.2 %shard_map.91.refs_0_.refs_5_ = bf16[528,896]{1,0:T(8,128)(2,1)} custom-call(s32[10]{0:T(128)S(1)} %dynamic-slice_bitcast_fusion.1.where_ref, bf16[8,2,64,448]{3,2,1,0:T(8,128)(2,1)S(1)} %bitcast.7, bf16[8,64,448]{2,1,0:T(8,128)(2,1)S(1)} %collective-permute-done.swapped_ref, s32[64,2]{1,0:T(8,128)S(1)} %copy.14.routes_ref, f32[64,2]{1,0:T(8,128)S(1)} %copy.15.gain_ref), custom_call_target="tpu_custom_call" | custom-call | flops 1835008 | bytes 1835008 | tf_op jit(solution)/shard_map/pallas_call | solution.py:108
  8.5 2.7 %collective-permute-start.4 = (bf16[528,896]{1,0:T(8,128)(2,1)}, bf16[528,896]{1,0:T(8,128)(2,1)S(1)}, u32[]{:S(2)}, u32[]{:S(2)}) collective-permute-start(bf16[528,896]{1,0:T(8,128)(2,1)} %shard_map.91.refs_0_.refs_5_), channel_id=1, source_target_pairs={{0,4},{1,5},{4,8},{5,9},{8,12},{9,13},{12,14},{13,15},{14,10},{15,... | collective-permute-start | bytes 2838536 | tf_op jit(solution)/shard_map/ppermute | solution.py:94
  11.2 21.6 %collective-permute-done.4.refs_1_.refs_12_ = bf16[528,896]{1,0:T(8,128)(2,1)S(1)} collective-permute-done((bf16[528,896]{1,0:T(8,128)(2,1)}, bf16[528,896]{1,0:T(8,128)(2,1)S(1)}, u32[]{:S(2)}, u32[]{:S(2)}) %collective-permute-start.4) | collective-permute-done | bytes 946208 | tf_op jit(solution)/shard_map/ppermute | solution.py:94
  32.8 1.8 %collective-permute-start.6 = (bf16[528,896]{1,0:T(8,128)(2,1)S(1)}, bf16[528,896]{1,0:T(8,128)(2,1)S(1)}, u32[]{:S(2)}, u32[]{:S(2)}) collective-permute-start(bf16[528,896]{1,0:T(8,128)(2,1)S(1)} %collective-permute-done.4.refs_1_.refs_12_), channel_id=1, source_target_pairs={{0,4},{1,5},{4,8},{5,9},{8,12},{9,13},{12,14},{13,15},{14,10},{15,... | collective-permute-start | bytes 2838536 | tf_op jit(solution)/shard_map/ppermute | solution.py:94
  34.6 0.2 collective-permute-start.5
  34.9 20.6 %collective-permute-done.6.refs_1_.refs_11_ = bf16[528,896]{1,0:T(8,128)(2,1)S(1)} collective-permute-done((bf16[528,896]{1,0:T(8,128)(2,1)S(1)}, bf16[528,896]{1,0:T(8,128)(2,1)S(1)}, u32[]{:S(2)}, u32[]{:S(2)}) %collective-permute-start.6) | collective-permute-done | bytes 946208 | tf_op jit(solution)/shard_map/ppermute | solution.py:94
  55.5 1.6 collective-permute-start.8
  57.1 0.5 collective-permute-start.7
  57.6 1.2 copy-done
  58.7 4.4 %shard_map.92 = (bf16[64,896]{1,0:T(8,128)(2,1)S(1)}, f32[512,1024]{1,0:T(8,128)S(1)}) custom-call(s32[10]{0:T(128)S(1)} %dynamic-slice_bitcast_fusion.1.where_ref, bf16[528,896]{1,0:T(8,128)(2,1)S(1)} %copy-done, f32[8,1,896]{2,1,0:T(1,128)S(1)} %bitcast.8, bf16[7168,256]{1,0:T(8,128)(2,1)} %refs_3_.3, bf16[7168,256]{1,0:T(8,128)(2,1)} %refs_4_.2, ...), custom_call_target="tpu_custom_call" | custom-call | flops 2818572288 | bytes 6946816 | tf_op jit(solution)/shard_map/pallas_call | solution.py:108
  63.2 6.8 %shard_map.93 = (bf16[64,896]{1,0:T(8,128)(2,1)S(1)}, bf16[64,896]{1,0:T(8,128)(2,1)S(1)}, f32[512,1024]{1,0:T(8,128)S(1)}) custom-call(s32[10]{0:T(128)S(1)} %dynamic-slice_bitcast_fusion.1.where_ref, bf16[528,896]{1,0:T(8,128)(2,1)S(1)} %collective-permute-done.3.refs_0_.refs_6_, ...), custom_call_target="tpu_custom_call", output_to_operand_aliasing={{2}: (8, {})} | custom-call | flops 5637144576 | bytes 9699328 | tf_op jit(solution)/shard_map/pallas_call | solution.py:108
  69.9 6.8 %shard_map.94 = (bf16[64,896]{1,0:T(8,128)(2,1)S(1)}, bf16[64,896]{1,0:T(8,128)(2,1)S(1)}, f32[512,1024]{1,0:T(8,128)S(1)}) custom-call(s32[10]{0:T(128)S(1)} %dynamic-slice_bitcast_fusion.1.where_ref, bf16[528,896]{1,0:T(8,128)(2,1)S(1)} %collective-permute-done.5.refs_0_.refs_7_, ...), custom_call_target="tpu_custom_call", output_to_operand_aliasing={{2}: (8, {})} | custom-call | flops 5637144576 | bytes 9699328 | tf_op jit(solution)/shard_map/pallas_call | solution.py:108
  76.7 0.6 collective-permute-done.8.refs_1_.refs_10_
  77.3 1.0 collective-permute-done.7.refs_0_.refs_8_
  78.3 0.8 collective-permute-start.11
  79.2 1.3 collective-permute-start.10
  80.5 6.8 %shard_map.95 = (bf16[64,896]{1,0:T(8,128)(2,1)S(1)}, bf16[64,896]{1,0:T(8,128)(2,1)S(1)}, f32[512,1024]{1,0:T(8,128)S(1)}, bf16[4,896,256]{2,1,0:T(8,128)(2,1)S(1)}, bf16[512,7168]{1,0:T(8,128)(2,1)S(1)}) custom-call(s32[10]{0:T(128)S(1)} %dynamic-slice_bitcast_fusion.1.where_ref, ...), custom_call_target="tpu_custom_call", output_to_operand_aliasing={{2}: (8, {})} | custom-call | flops 5637144576 | bytes 9699328 | tf_op jit(solution)/shard_map/pallas_call | solution.py:108
  87.3 0.9 collective-permute-done.11.refs_1_
  88.3 1.5 collective-permute-done.10.refs_0_.refs_9_
  89.7 2.1 %shard_map.96 = (bf16[64,896]{1,0:T(8,128)(2,1)S(1)}, bf16[512,512]{1,0:T(8,128)(2,1)S(1)}) custom-call(s32[10]{0:T(128)S(1)} %dynamic-slice_bitcast_fusion.1.where_ref, bf16[272,896]{1,0:T(8,128)(2,1)S(1)} %collective-permute-done.10.refs_0_.refs_9_, bf16[256,896]{1,0:T(8,128)(2,1)S(1)} %collective-permute-done.11.refs_1_, f32[8,1,896]{2,1,0:T(1,128)S(1)} %bitcast.12, ...), custom_call_target="tpu_custom_call" | custom-call | flops 2818572288 | bytes 6946816 | tf_op jit(solution)/shard_map/pallas_call | solution.py:108
  91.8 2.9 %shard_map.98 = (bf16[512,512]{1,0:T(8,128)(2,1)S(1)}, bf16[64,3584]{1,0:T(8,128)(2,1)}, bf16[64,3584]{1,0:T(8,128)(2,1)}, bf16[64,3584]{1,0:T(8,128)(2,1)}, bf16[64,3584]{1,0:T(8,128)(2,1)}) custom-call(s32[10]{0:T(128)S(1)} %dynamic-slice_bitcast_fusion.1.where_ref, bf16[512,512]{1,0:T(8,128)(2,1)S(1)} %get-tuple-element.54.hidden_ref, ...), custom_call_target="tpu_custom_call" | custom-call | flops 939524096 | bytes 7340032 | tf_op jit(solution)/shard_map/pallas_call | solution.py:108
  94.7 1.1 collective-permute-start.22
  95.8 0.9 collective-permute-start.12
  96.7 1.7 shard_map.97.stream_ref
  98.4 1.0 collective-permute-start.19
  99.4 4.4 %shard_map.100.table_ref.refs_1_ = bf16[512,3584]{1,0:T(8,128)(2,1)} custom-call(s32[10]{0:T(128)S(1)} %dynamic-slice_bitcast_fusion.1.where_ref, bf16[512,512]{1,0:T(8,128)(2,1)S(1)} %get-tuple-element.58.hidden_ref, bf16[512,7168]{1,0:T(8,128)(2,1)S(1)} %get-tuple-element.55.down_ref), custom_call_target="tpu_custom_call" | custom-call | flops 1879048192 | bytes 7340032 | tf_op jit(solution)/shard_map/pallas_call | solution.py:108
  103.8 4.4 %shard_map.99.table_ref.refs_0_ = bf16[512,3584]{1,0:T(8,128)(2,1)} custom-call(s32[10]{0:T(128)S(1)} %dynamic-slice_bitcast_fusion.1.where_ref, bf16[512,512]{1,0:T(8,128)(2,1)S(1)} %get-tuple-element.58.hidden_ref, bf16[512,7168]{1,0:T(8,128)(2,1)S(1)} %get-tuple-element.55.down_ref), custom_call_target="tpu_custom_call" | custom-call | flops 1879048192 | bytes 7340032 | tf_op jit(solution)/shard_map/pallas_call | solution.py:108
  108.2 1.0 collective-permute-start.16
  109.2 2.7 %shard_map.108 = bf16[64,3584]{1,0:T(8,128)(2,1)} custom-call(s32[10]{0:T(128)} %copy-done.3, bf16[512,3584]{1,0:T(8,128)(2,1)} %shard_map.100.table_ref.refs_1_, bf16[64,3584]{1,0:T(8,128)(2,1)} %collective-permute-done.22.moved_ref), custom_call_target="tpu_custom_call" | custom-call | flops 229376 | bytes 1376256 | tf_op jit(solution)/shard_map/pallas_call | solution.py:443
  112.0 1.2 collective-permute-start.23
  113.2 2.7 %shard_map.101 = bf16[64,3584]{1,0:T(8,128)(2,1)} custom-call(s32[10]{0:T(128)} %copy-done.3, bf16[512,3584]{1,0:T(8,128)(2,1)} %shard_map.99.table_ref.refs_0_, bf16[64,3584]{1,0:T(8,128)(2,1)} %collective-permute-done.12.moved_ref), custom_call_target="tpu_custom_call" | custom-call | flops 229376 | bytes 1376256 | tf_op jit(solution)/shard_map/pallas_call | solution.py:443
  115.9 0.9 collective-permute-start.13
  116.9 2.7 %shard_map.106 = bf16[64,3584]{1,0:T(8,128)(2,1)} custom-call(s32[10]{0:T(128)} %copy-done.3, bf16[512,3584]{1,0:T(8,128)(2,1)} %shard_map.100.table_ref.refs_1_, bf16[64,3584]{1,0:T(8,128)(2,1)} %collective-permute-done.19.moved_ref), custom_call_target="tpu_custom_call" | custom-call | flops 229376 | bytes 1376256 | tf_op jit(solution)/shard_map/pallas_call | solution.py:443
  119.6 1.0 collective-permute-start.20
  120.7 1.1 collective-permute-done.16.moved_ref
  121.8 2.8 %shard_map.104 = bf16[64,3584]{1,0:T(8,128)(2,1)} custom-call(s32[10]{0:T(128)} %copy-done.3, bf16[512,3584]{1,0:T(8,128)(2,1)} %shard_map.99.table_ref.refs_0_, bf16[64,3584]{1,0:T(8,128)(2,1)} %collective-permute-done.16.moved_ref), custom_call_target="tpu_custom_call" | custom-call | flops 229376 | bytes 1376256 | tf_op jit(solution)/shard_map/pallas_call | solution.py:443
  124.6 1.3 collective-permute-start.17
  125.8 5.8 %collective-permute-done.23.moved_ref = bf16[64,3584]{1,0:T(8,128)(2,1)} collective-permute-done((bf16[64,3584]{1,0:T(8,128)(2,1)}, bf16[64,3584]{1,0:T(8,128)(2,1)}, u32[]{:S(2)}, u32[]{:S(2)}) %collective-permute-start.23) | collective-permute-done | bytes 458784 | tf_op jit(solution)/shard_map/ppermute | solution.py:94
  131.6 2.7 %shard_map.109 = bf16[64,3584]{1,0:T(8,128)(2,1)} custom-call(s32[10]{0:T(128)} %copy-done.3, bf16[512,3584]{1,0:T(8,128)(2,1)} %shard_map.100.table_ref.refs_1_, bf16[64,3584]{1,0:T(8,128)(2,1)} %collective-permute-done.23.moved_ref), custom_call_target="tpu_custom_call" | custom-call | flops 229376 | bytes 1376256 | tf_op jit(solution)/shard_map/pallas_call | solution.py:443
  134.4 1.3 collective-permute-start.24
  135.7 2.7 %shard_map.102 = bf16[64,3584]{1,0:T(8,128)(2,1)} custom-call(s32[10]{0:T(128)} %copy-done.3, bf16[512,3584]{1,0:T(8,128)(2,1)} %shard_map.99.table_ref.refs_0_, bf16[64,3584]{1,0:T(8,128)(2,1)} %collective-permute-done.13.moved_ref), custom_call_target="tpu_custom_call" | custom-call | flops 229376 | bytes 1376256 | tf_op jit(solution)/shard_map/pallas_call | solution.py:443
  138.4 0.9 collective-permute-start.14
  139.2 2.7 %shard_map.107 = bf16[64,3584]{1,0:T(8,128)(2,1)} custom-call(s32[10]{0:T(128)} %copy-done.3, bf16[512,3584]{1,0:T(8,128)(2,1)} %shard_map.100.table_ref.refs_1_, bf16[64,3584]{1,0:T(8,128)(2,1)} %collective-permute-done.20.moved_ref), custom_call_target="tpu_custom_call" | custom-call | flops 229376 | bytes 1376256 | tf_op jit(solution)/shard_map/pallas_call | solution.py:443
  142.0 1.6 collective-permute-start.21
  143.6 2.8 %shard_map.105 = bf16[64,3584]{1,0:T(8,128)(2,1)} custom-call(s32[10]{0:T(128)} %copy-done.3, bf16[512,3584]{1,0:T(8,128)(2,1)} %shard_map.99.table_ref.refs_0_, bf16[64,3584]{1,0:T(8,128)(2,1)} %collective-permute-done.17.moved_ref), custom_call_target="tpu_custom_call" | custom-call | flops 229376 | bytes 1376256 | tf_op jit(solution)/shard_map/pallas_call | solution.py:443
  146.4 0.5 collective-permute-start.18
  146.9 4.4 %collective-permute-done.24.moved_ref = bf16[64,3584]{1,0:T(8,128)(2,1)} collective-permute-done((bf16[64,3584]{1,0:T(8,128)(2,1)}, bf16[64,3584]{1,0:T(8,128)(2,1)}, u32[]{:S(2)}, u32[]{:S(2)}) %collective-permute-start.24) | collective-permute-done | bytes 458784 | tf_op jit(solution)/shard_map/ppermute | solution.py:94
  151.3 2.7 %shard_map.110 = bf16[64,3584]{1,0:T(8,128)(2,1)} custom-call(s32[10]{0:T(128)} %copy-done.3, bf16[512,3584]{1,0:T(8,128)(2,1)} %shard_map.100.table_ref.refs_1_, bf16[64,3584]{1,0:T(8,128)(2,1)} %collective-permute-done.24.moved_ref), custom_call_target="tpu_custom_call" | custom-call | flops 229376 | bytes 1376256 | tf_op jit(solution)/shard_map/pallas_call | solution.py:443
  154.0 1.3 collective-permute-start.25
  155.3 2.7 %shard_map.103 = bf16[64,3584]{1,0:T(8,128)(2,1)} custom-call(s32[10]{0:T(128)} %copy-done.3, bf16[512,3584]{1,0:T(8,128)(2,1)} %shard_map.99.table_ref.refs_0_, bf16[64,3584]{1,0:T(8,128)(2,1)} %collective-permute-done.14.moved_ref), custom_call_target="tpu_custom_call" | custom-call | flops 229376 | bytes 1376256 | tf_op jit(solution)/shard_map/pallas_call | solution.py:443
  158.1 0.9 collective-permute-start.15
  158.9 1.7 collective-permute-done.18.refs_3_
  160.6 4.9 %collective-permute-done.25.refs_5_ = bf16[64,3584]{1,0:T(8,128)(2,1)} collective-permute-done((bf16[64,3584]{1,0:T(8,128)(2,1)}, bf16[64,3584]{1,0:T(8,128)(2,1)}, u32[]{:S(2)}, u32[]{:S(2)}) %collective-permute-start.25) | collective-permute-done | bytes 458784 | tf_op jit(solution)/shard_map/ppermute | solution.py:94
  165.5 1.4 collective-permute-done.15.refs_2_
  166.9 3.6 %shard_map.111 = bf16[64,7168]{1,0:T(8,128)(2,1)} custom-call(s32[10]{0:T(128)} %copy-done.3, bf16[64,7168]{1,0:T(8,128)(2,1)} %shard_map.97.stream_ref, bf16[512,3584]{1,0:T(8,128)(2,1)} %shard_map.99.table_ref.refs_0_, bf16[512,3584]{1,0:T(8,128)(2,1)} %shard_map.100.table_ref.refs_1_, bf16[64,3584]{1,0:T(8,128)(2,1)} %collective-permute-done.15.refs_2_, ...), custom_call_target="tpu_custom_call" | custom-call | flops 1376256 | bytes 4587520 | tf_op jit(solution)/shard_map/pallas_call | solution.py:515
  (29 shorter events, 0.3 us)
Async XLA Ops:
  0.0 5.4 %copy-start.4 = (s32[64,2]{0,1:T(2,128)S(1)}, s32[64,2]{0,1:T(2,128)}, u32[]{:S(2)}) copy-start(s32[64,2]{0,1:T(2,128)} %param.12) | copy-start | bytes 1540
  0.0 5.5 %copy-start.5 = (f32[64,2]{0,1:T(2,128)S(1)}, f32[64,2]{0,1:T(2,128)}, u32[]{:S(2)}) copy-start(f32[64,2]{0,1:T(2,128)} %param.13) | copy-start | bytes 1540
  0.0 57.5 %copy-start.2 = (f32[7168]{0:T(1024)S(1)}, f32[7168]{0:T(1024)}, u32[]{:S(2)}) copy-start(f32[7168]{0:T(1024)} %param.11) | copy-start | bytes 86020
  2.4 2.1 %collective-permute-start = (bf16[8,64,448]{2,1,0:T(8,128)(2,1)S(1)}, bf16[8,64,448]{2,1,0:T(8,128)(2,1)S(1)}, u32[]{:S(2)}, u32[]{:S(2)}) collective-permute-start(bf16[8,64,448]{2,1,0:T(8,128)(2,1)S(1)} %dynamic-slice_bitcast_fusion), channel_id=1, source_target_pairs={{0,1},{1,0},{2,3},{3,2},{4,5},{5,4},{6,7},{7,6},{8,9},{9,8},{10,11... | collective-permute-start | bytes 1376264 | tf_op jit(solution)/shard_map/ppermute | solution.py:84
  4.5 53.0 %collective-permute-start.1 = (bf16[7168,256]{1,0:T(8,128)(2,1)}, bf16[7168,256]{1,0:T(8,128)(2,1)}, u32[]{:S(2)}, u32[]{:S(2)}) collective-permute-start(bf16[7168,256]{1,0:T(8,128)(2,1)} %refs_3_.3), channel_id=1, source_target_pairs={{0,1},{1,0},{2,3},{3,2},{4,5},{5,4},{6,7},{7,6},{8,9},{9,8},{10,11... | collective-permute-start | bytes 11010056 | tf_op jit(solution)/shard_map/ppermute | solution.py:84
  4.9 52.7 %collective-permute-start.2 = (bf16[7168,256]{1,0:T(8,128)(2,1)}, bf16[7168,256]{1,0:T(8,128)(2,1)}, u32[]{:S(2)}, u32[]{:S(2)}) collective-permute-start(bf16[7168,256]{1,0:T(8,128)(2,1)} %refs_4_.2), channel_id=1, source_target_pairs={{0,1},{1,0},{2,3},{3,2},{4,5},{5,4},{6,7},{7,6},{8,9},{9,8},{10,11... | collective-permute-start | bytes 11010056 | tf_op jit(solution)/shard_map/ppermute | solution.py:84
  5.0 75.5 %collective-permute-start.9 = (bf16[256,7168]{1,0:T(8,128)(2,1)}, bf16[256,7168]{1,0:T(8,128)(2,1)}, u32[]{:S(2)}, u32[]{:S(2)}) collective-permute-start(bf16[256,7168]{1,0:T(8,128)(2,1)} %refs_8_), channel_id=1, source_target_pairs={{0,1},{1,0},{2,3},{3,2},{4,5},{5,4},{6,7},{7,6},{8,9},{9,8},{10,11... | collective-permute-start | bytes 11010056 | tf_op jit(solution)/shard_map/ppermute | solution.py:84
  6.3 97.5 %copy-start.3 = (s32[10]{0:T(128)}, s32[10]{0:T(128)S(1)}, u32[]{:S(2)}) copy-start(s32[10]{0:T(128)S(1)} %dynamic-slice_bitcast_fusion.1.where_ref) | copy-start | bytes 124
  8.5 24.4 %collective-permute-start.4 = (bf16[528,896]{1,0:T(8,128)(2,1)}, bf16[528,896]{1,0:T(8,128)(2,1)S(1)}, u32[]{:S(2)}, u32[]{:S(2)}) collective-permute-start(bf16[528,896]{1,0:T(8,128)(2,1)} %shard_map.91.refs_0_.refs_5_), channel_id=1, source_target_pairs={{0,4},{1,5},{4,8},{5,9},{8,12},{9,13},{12,14},{13,15},{14,10},{15,... | collective-permute-start | bytes 2838536 | tf_op jit(solution)/shard_map/ppermute | solution.py:94
  11.2 23.4 %collective-permute-start.3 = (bf16[528,896]{1,0:T(8,128)(2,1)}, bf16[528,896]{1,0:T(8,128)(2,1)S(1)}, u32[]{:S(2)}, u32[]{:S(2)}) collective-permute-start(bf16[528,896]{1,0:T(8,128)(2,1)} %shard_map.91.refs_0_.refs_5_), channel_id=1, source_target_pairs={{0,2},{1,3},{4,0},{5,1},{8,4},{9,5},{12,8},{13,9},{14,12},{15,13},... | collective-permute-start | bytes 2838536 | tf_op jit(solution)/shard_map/ppermute | solution.py:94
  32.8 22.7 %collective-permute-start.6 = (bf16[528,896]{1,0:T(8,128)(2,1)S(1)}, bf16[528,896]{1,0:T(8,128)(2,1)S(1)}, u32[]{:S(2)}, u32[]{:S(2)}) collective-permute-start(bf16[528,896]{1,0:T(8,128)(2,1)S(1)} %collective-permute-done.4.refs_1_.refs_12_), channel_id=1, source_target_pairs={{0,4},{1,5},{4,8},{5,9},{8,12},{9,13},{12,14},{13,15},{14,10},{15,... | collective-permute-start | bytes 2838536 | tf_op jit(solution)/shard_map/ppermute | solution.py:94
  34.6 22.4 %collective-permute-start.5 = (bf16[528,896]{1,0:T(8,128)(2,1)S(1)}, bf16[528,896]{1,0:T(8,128)(2,1)S(1)}, u32[]{:S(2)}, u32[]{:S(2)}) collective-permute-start(bf16[528,896]{1,0:T(8,128)(2,1)S(1)} %collective-permute-done.3.refs_0_.refs_6_), channel_id=1, source_target_pairs={{0,2},{1,3},{4,0},{5,1},{8,4},{9,5},{12,8},{13,9},{14,12},{15,13},... | collective-permute-start | bytes 2838536 | tf_op jit(solution)/shard_map/ppermute | solution.py:94
  55.5 21.8 %collective-permute-start.8 = (bf16[528,896]{1,0:T(8,128)(2,1)S(1)}, bf16[528,896]{1,0:T(8,128)(2,1)S(1)}, u32[]{:S(2)}, u32[]{:S(2)}) collective-permute-start(bf16[528,896]{1,0:T(8,128)(2,1)S(1)} %collective-permute-done.6.refs_1_.refs_11_), channel_id=1, source_target_pairs={{0,4},{1,5},{4,8},{5,9},{8,12},{9,13},{12,14},{13,15},{14,10},{15,... | collective-permute-start | bytes 2838536 | tf_op jit(solution)/shard_map/ppermute | solution.py:94
  57.1 21.2 %collective-permute-start.7 = (bf16[528,896]{1,0:T(8,128)(2,1)S(1)}, bf16[528,896]{1,0:T(8,128)(2,1)S(1)}, u32[]{:S(2)}, u32[]{:S(2)}) collective-permute-start(bf16[528,896]{1,0:T(8,128)(2,1)S(1)} %collective-permute-done.5.refs_0_.refs_7_), channel_id=1, source_target_pairs={{0,2},{1,3},{4,0},{5,1},{8,4},{9,5},{12,8},{13,9},{14,12},{15,13},... | collective-permute-start | bytes 2838536 | tf_op jit(solution)/shard_map/ppermute | solution.py:94
  57.5 1.2 copy-start
  78.3 9.9 %collective-permute-start.11 = (bf16[256,896]{1,0:T(8,128)(2,1)S(1)}, bf16[256,896]{1,0:T(8,128)(2,1)S(1)}, u32[]{:S(2)}, u32[]{:S(2)}) collective-permute-start(bf16[256,896]{1,0:T(8,128)(2,1)S(1)} %slice.7), channel_id=1, source_target_pairs={{0,2},{1,3},{4,0},{5,1},{8,4},{9,5},{12,8},{13,9},{14,12},{15,13},... | collective-permute-start | bytes 1376264 | tf_op jit(solution)/shard_map/ppermute | solution.py:94
  79.2 10.5 %copy-start.1 = (bf16[528,896]{1,0:T(8,128)(2,1)S(1)}, bf16[528,896]{1,0:T(8,128)(2,1)}, u32[]{:S(2)}) copy-start(bf16[528,896]{1,0:T(8,128)(2,1)} %shard_map.91.refs_0_.refs_5_) | copy-start | bytes 2838532
  79.2 10.5 %collective-permute-start.10 = (bf16[272,896]{1,0:T(8,128)(2,1)S(1)}, bf16[272,896]{1,0:T(8,128)(2,1)S(1)}, u32[]{:S(2)}, u32[]{:S(2)}) collective-permute-start(bf16[272,896]{1,0:T(8,128)(2,1)S(1)} %slice.6), channel_id=1, source_target_pairs={{0,4},{1,5},{4,8},{5,9},{8,12},{9,13},{12,14},{13,15},{14,10},{15,... | collective-permute-start | bytes 1462280 | tf_op jit(solution)/shard_map/ppermute | solution.py:94
  94.7 14.6 %collective-permute-start.22 = (bf16[64,3584]{1,0:T(8,128)(2,1)}, bf16[64,3584]{1,0:T(8,128)(2,1)}, u32[]{:S(2)}, u32[]{:S(2)}) collective-permute-start(bf16[64,3584]{1,0:T(8,128)(2,1)} %get-tuple-element.62), channel_id=1, source_target_pairs={{0,2},{1,3},{4,0},{5,1},{8,4},{9,5},{12,8},{13,9},{14,12},{15,13},... | collective-permute-start | bytes 1376264 | tf_op jit(solution)/shard_map/ppermute | solution.py:94
  95.8 17.4 %collective-permute-start.12 = (bf16[64,3584]{1,0:T(8,128)(2,1)}, bf16[64,3584]{1,0:T(8,128)(2,1)}, u32[]{:S(2)}, u32[]{:S(2)}) collective-permute-start(bf16[64,3584]{1,0:T(8,128)(2,1)} %get-tuple-element.59), channel_id=1, source_target_pairs={{0,4},{1,5},{4,8},{5,9},{8,12},{9,13},{12,14},{13,15},{14,10},{15,... | collective-permute-start | bytes 1376264 | tf_op jit(solution)/shard_map/ppermute | solution.py:94
  98.4 18.5 %collective-permute-start.19 = (bf16[64,3584]{1,0:T(8,128)(2,1)}, bf16[64,3584]{1,0:T(8,128)(2,1)}, u32[]{:S(2)}, u32[]{:S(2)}) collective-permute-start(bf16[64,3584]{1,0:T(8,128)(2,1)} %get-tuple-element.61), channel_id=1, source_target_pairs={{0,4},{1,5},{4,8},{5,9},{8,12},{9,13},{12,14},{13,15},{14,10},{15,... | collective-permute-start | bytes 1376264 | tf_op jit(solution)/shard_map/ppermute | solution.py:94
  108.2 13.6 %collective-permute-start.16 = (bf16[64,3584]{1,0:T(8,128)(2,1)}, bf16[64,3584]{1,0:T(8,128)(2,1)}, u32[]{:S(2)}, u32[]{:S(2)}) collective-permute-start(bf16[64,3584]{1,0:T(8,128)(2,1)} %get-tuple-element.60), channel_id=1, source_target_pairs={{0,2},{1,3},{4,0},{5,1},{8,4},{9,5},{12,8},{13,9},{14,12},{15,13},... | collective-permute-start | bytes 1376264 | tf_op jit(solution)/shard_map/ppermute | solution.py:94
  112.0 19.6 %collective-permute-start.23 = (bf16[64,3584]{1,0:T(8,128)(2,1)}, bf16[64,3584]{1,0:T(8,128)(2,1)}, u32[]{:S(2)}, u32[]{:S(2)}) collective-permute-start(bf16[64,3584]{1,0:T(8,128)(2,1)} %shard_map.108), channel_id=1, source_target_pairs={{0,2},{1,3},{4,0},{5,1},{8,4},{9,5},{12,8},{13,9},{14,12},{15,13},... | collective-permute-start | bytes 1376264 | tf_op jit(solution)/shard_map/ppermute | solution.py:94
  115.9 19.7 %collective-permute-start.13 = (bf16[64,3584]{1,0:T(8,128)(2,1)}, bf16[64,3584]{1,0:T(8,128)(2,1)}, u32[]{:S(2)}, u32[]{:S(2)}) collective-permute-start(bf16[64,3584]{1,0:T(8,128)(2,1)} %shard_map.101), channel_id=1, source_target_pairs={{0,4},{1,5},{4,8},{5,9},{8,12},{9,13},{12,14},{13,15},{14,10},{15,... | collective-permute-start | bytes 1376264 | tf_op jit(solution)/shard_map/ppermute | solution.py:94
  119.6 19.6 %collective-permute-start.20 = (bf16[64,3584]{1,0:T(8,128)(2,1)}, bf16[64,3584]{1,0:T(8,128)(2,1)}, u32[]{:S(2)}, u32[]{:S(2)}) collective-permute-start(bf16[64,3584]{1,0:T(8,128)(2,1)} %shard_map.106), channel_id=1, source_target_pairs={{0,4},{1,5},{4,8},{5,9},{8,12},{9,13},{12,14},{13,15},{14,10},{15,... | collective-permute-start | bytes 1376264 | tf_op jit(solution)/shard_map/ppermute | solution.py:94
  124.6 19.1 %collective-permute-start.17 = (bf16[64,3584]{1,0:T(8,128)(2,1)}, bf16[64,3584]{1,0:T(8,128)(2,1)}, u32[]{:S(2)}, u32[]{:S(2)}) collective-permute-start(bf16[64,3584]{1,0:T(8,128)(2,1)} %shard_map.104), channel_id=1, source_target_pairs={{0,2},{1,3},{4,0},{5,1},{8,4},{9,5},{12,8},{13,9},{14,12},{15,13},... | collective-permute-start | bytes 1376264 | tf_op jit(solution)/shard_map/ppermute | solution.py:94
  134.4 16.9 %collective-permute-start.24 = (bf16[64,3584]{1,0:T(8,128)(2,1)}, bf16[64,3584]{1,0:T(8,128)(2,1)}, u32[]{:S(2)}, u32[]{:S(2)}) collective-permute-start(bf16[64,3584]{1,0:T(8,128)(2,1)} %shard_map.109), channel_id=1, source_target_pairs={{0,2},{1,3},{4,0},{5,1},{8,4},{9,5},{12,8},{13,9},{14,12},{15,13},... | collective-permute-start | bytes 1376264 | tf_op jit(solution)/shard_map/ppermute | solution.py:94
  138.4 16.9 %collective-permute-start.14 = (bf16[64,3584]{1,0:T(8,128)(2,1)}, bf16[64,3584]{1,0:T(8,128)(2,1)}, u32[]{:S(2)}, u32[]{:S(2)}) collective-permute-start(bf16[64,3584]{1,0:T(8,128)(2,1)} %shard_map.102), channel_id=1, source_target_pairs={{0,4},{1,5},{4,8},{5,9},{8,12},{9,13},{12,14},{13,15},{14,10},{15,... | collective-permute-start | bytes 1376264 | tf_op jit(solution)/shard_map/ppermute | solution.py:94
  142.0 16.9 %collective-permute-start.21 = (bf16[64,3584]{1,0:T(8,128)(2,1)}, bf16[64,3584]{1,0:T(8,128)(2,1)}, u32[]{:S(2)}, u32[]{:S(2)}) collective-permute-start(bf16[64,3584]{1,0:T(8,128)(2,1)} %shard_map.107), channel_id=1, source_target_pairs={{0,4},{1,5},{4,8},{5,9},{8,12},{9,13},{12,14},{13,15},{14,10},{15,... | collective-permute-start | bytes 1376264 | tf_op jit(solution)/shard_map/ppermute | solution.py:94
  146.4 14.2 %collective-permute-start.18 = (bf16[64,3584]{1,0:T(8,128)(2,1)}, bf16[64,3584]{1,0:T(8,128)(2,1)}, u32[]{:S(2)}, u32[]{:S(2)}) collective-permute-start(bf16[64,3584]{1,0:T(8,128)(2,1)} %shard_map.105), channel_id=1, source_target_pairs={{0,2},{1,3},{4,0},{5,1},{8,4},{9,5},{12,8},{13,9},{14,12},{15,13},... | collective-permute-start | bytes 1376264 | tf_op jit(solution)/shard_map/ppermute | solution.py:94
  154.0 11.5 %collective-permute-start.25 = (bf16[64,3584]{1,0:T(8,128)(2,1)}, bf16[64,3584]{1,0:T(8,128)(2,1)}, u32[]{:S(2)}, u32[]{:S(2)}) collective-permute-start(bf16[64,3584]{1,0:T(8,128)(2,1)} %shard_map.110), channel_id=1, source_target_pairs={{0,2},{1,3},{4,0},{5,1},{8,4},{9,5},{12,8},{13,9},{14,12},{15,13},... | collective-permute-start | bytes 1376264 | tf_op jit(solution)/shard_map/ppermute | solution.py:94
  158.1 8.8 %collective-permute-start.15 = (bf16[64,3584]{1,0:T(8,128)(2,1)}, bf16[64,3584]{1,0:T(8,128)(2,1)}, u32[]{:S(2)}, u32[]{:S(2)}) collective-permute-start(bf16[64,3584]{1,0:T(8,128)(2,1)} %shard_map.103), channel_id=1, source_target_pairs={{0,4},{1,5},{4,8},{5,9},{8,12},{9,13},{12,14},{13,15},{14,10},{15,... | collective-permute-start | bytes 1376264 | tf_op jit(solution)/shard_map/ppermute | solution.py:94

commit v12 on v6

--- a/solution.py
+++ b/solution.py
@@ -108,7 +108,8 @@
         kernel,
         out_shape=out_shape,
         in_specs=[
-            IN_SMEM if k == 0 else IN_HBM if k in far else IN_VMEM for k in range(len(operands))
+            IN_SMEM if value.ndim == 1 else IN_HBM if k in far else IN_VMEM
+            for k, value in enumerate(operands)
         ],
         out_specs=jax.tree.map(
             lambda made: IN_SMEM if made.dtype == jnp.int32 else IN_VMEM, out_shape
@@ -122,14 +123,14 @@
     )(*operands)
 
 
-def first_blocks(where, stream, swapped, routes, route_gain, experts):
+def first_blocks(stream, swapped, routes, route_gain, experts):
     chips, _, tok_here, feat_here = stream.shape
     width = 2 * feat_here
     tokens = chips * tok_here
     head = -(-3 * (experts + 1) // 16) * 16
 
-    def kernel(where_ref, stream_ref, swapped_ref, routes_ref, gain_ref, out_ref):
-        core = where_ref[chips + 1]
+    def kernel(stream_ref, swapped_ref, routes_ref, gain_ref, out_ref):
+        core = lax.rem(lax.axis_index("ep"), 2)
         square = (tok_here, tok_here)
         diagonal = lax.broadcasted_iota(jnp.int32, square, 0) == lax.broadcasted_iota(
             jnp.int32, square, 1
@@ -170,19 +171,22 @@
     return local_call(
         kernel,
         jax.ShapeDtypeStruct((head + tokens, width), jnp.bfloat16),
-        [where, stream, swapped, routes, route_gain],
+        [stream, swapped, routes, route_gain],
         flops=4 * tokens * width,
         bytes_accessed=4 * tokens * width,
     )
 
 
-def accumulate(where, positions, parts, norm_gain, tables, tok_here, carried, headers, ahead):
+def accumulate(
+    where, positions, parts, norm_gain, tables, tok_here, carried, headers, ahead, leading
+):
     count = len(positions)
     width = parts[0][0].shape[1]
     chips = norm_gain.shape[0]
     model_width = chips * width
     hidden_here = tables[0].shape[-1]
     both = 2 * hidden_here
+    half = model_width // 2
     tokens = chips * tok_here
     sizes = [piece.shape[0] for piece in parts[0]]
     head = sum(sizes) - tokens
@@ -201,9 +205,11 @@
         acc_in = None if first else refs.pop(0)
         tops = [refs.pop(0) for _ in headers] if last else []
         sources = [refs.pop(0) for _ in ahead[1]] if ahead else []
+        product_ref = refs.pop(0) if leading else None
         owns = [refs.pop(0) for _ in range(count)]
         if last:
             hidden_ref = refs.pop(0)
+            leads = [refs.pop(0) for _ in leading[1]]
         else:
             acc_out = refs.pop(0)
         if ahead:
@@ -306,6 +312,17 @@
                     hidden_ref[span, out_cols] = act.astype(jnp.bfloat16)
         for copy in later:
             copy.wait()
+        for part in range(2) if last else ():
+            chosen = [k for k, (_, at) in enumerate(leading[1]) if at == part]
+            rows = [where_ref[leading[1][k][0]] * tok_here for k in chosen]
+            rows = [hidden_ref[pl.ds(pl.multiple_of(at, tok_here), tok_here), :] for at in rows]
+            out = jnp.dot(
+                jnp.concatenate(rows, axis=0),
+                product_ref[:, part * half : (part + 1) * half],
+                preferred_element_type=jnp.float32,
+            ).astype(jnp.bfloat16)
+            for at, k in enumerate(chosen):
+                leads[k][...] = out[at * tok_here : (at + 1) * tok_here, :]
 
     operands = [where] + [piece for block in parts for piece in block]
     operands.append(norm_gain)
@@ -319,7 +336,11 @@
     out_shape = [jax.ShapeDtypeStruct((tok_here, width), jnp.bfloat16)] * count
     if last:
         operands.extend(headers)
+        operands.append(leading[0])
         out_shape.append(jax.ShapeDtypeStruct((tokens, both), jnp.bfloat16))
+        out_shape.extend(
+            [jax.ShapeDtypeStruct((tok_here, half), jnp.bfloat16)] * len(leading[1])
+        )
     else:
         out_shape.append(jax.ShapeDtypeStruct((tokens, 2 * both), jnp.float32))
     if ahead:
@@ -348,38 +369,6 @@
     return made[:count], made[count:]
 
 
-def leading_rows(where, wanted, hidden, down, chips):
-    tokens, units = hidden.shape
-    model_width = down.shape[1]
-    half = model_width // 2
-    rows = tokens // chips
-
-    def kernel(where_ref, hidden_ref, down_ref, kept_ref, *outs):
-        kept_ref[...] = hidden_ref[...]
-        for part in range(2):
-            chosen = [k for k, (_, at) in enumerate(wanted) if at == part]
-            taken = [
-                hidden_ref[pl.ds(pl.multiple_of(where_ref[wanted[k][0]] * rows, rows), rows), :]
-                for k in chosen
-            ]
-            out = jnp.dot(
-                jnp.concatenate(taken, axis=0),
-                down_ref[:, part * half : (part + 1) * half],
-                preferred_element_type=jnp.float32,
-            ).astype(jnp.bfloat16)
-            for at, k in enumerate(chosen):
-                outs[k][...] = out[at * rows : (at + 1) * rows, :]
-
-    return local_call(
-        kernel,
-        [jax.ShapeDtypeStruct(hidden.shape, hidden.dtype)]
-        + [jax.ShapeDtypeStruct((rows, half), jnp.bfloat16)] * len(wanted),
-        [where, hidden, down],
-        flops=2 * rows * units * half * len(wanted),
-        bytes_accessed=2 * units * model_width,
-    )
-
-
 def contribution(where, hidden, down, part):
     tokens, units = hidden.shape
     half = down.shape[1] // 2
@@ -420,49 +409,44 @@
     )
 
 
-def own_rows(where, positions, pieces, tables):
+def collect(where, positions, pieces):
     rows, width = pieces[0].shape
-    chips = len(pieces)
-    model_width = chips * width
+    model_width = len(pieces) * width
+
+    def kernel(where_ref, *refs):
+        for k, position in enumerate(positions):
+            start = pl.multiple_of(where_ref[position] * width, width)
+            refs[-1][:, pl.ds(start, width)] = refs[k][...]
+
+    return local_call(
+        kernel,
+        jax.ShapeDtypeStruct((rows, model_width), jnp.bfloat16),
+        [where, *pieces],
+        flops=rows * model_width,
+        bytes_accessed=rows * model_width * 4,
+    )
+
+
+def final_sum(where, stream, tables, arrived):
+    rows, model_width = stream.shape
     half = model_width // 2
-
-    def kernel(where_ref, *refs):
+    came = [value for part in arrived for value in part]
+
+    def kernel(where_ref, stream_ref, *refs):
         out_ref = refs[-1]
         at = pl.multiple_of(where_ref[0] * rows, rows)
         for part in range(2):
-            out_ref[:, part * half : (part + 1) * half] = refs[chips + part][
-                pl.ds(at, rows), :
-            ].astype(jnp.float32)
-        for k in range(chips):
-            start = pl.multiple_of(where_ref[positions[k]] * width, width)
-            out_ref[:, pl.ds(start, width)] += refs[k][...].astype(jnp.float32)
+            cols = slice(part * half, (part + 1) * half)
+            total = stream_ref[:, cols].astype(jnp.float32)
+            total = total + refs[part][pl.ds(at, rows), :].astype(jnp.float32)
+            for k in range(len(arrived[part])):
+                total = total + refs[2 + k + part * len(arrived[0])][...].astype(jnp.float32)
+            out_ref[:, cols] = total.astype(jnp.bfloat16)
 
     return local_call(
         kernel,
-        jax.ShapeDtypeStruct((rows, model_width), jnp.float32),
-        [where, *pieces, *tables],
-        flops=rows * model_width,
-        bytes_accessed=rows * model_width * 8,
-    )
-
-
-def final_sum(where, base, arrived):
-    rows, model_width = base.shape
-    half = model_width // 2
-
-    def kernel(where_ref, base_ref, *refs):
-        out_ref = refs[-1]
-        for part in range(2):
-            cols = slice(part * half, (part + 1) * half)
-            total = base_ref[:, cols]
-            for k in range(len(arrived[part])):
-                total = total + refs[k + part * len(arrived[0])][...].astype(jnp.float32)
-            out_ref[:, cols] = total.astype(jnp.bfloat16)
-
-    return local_call(
-        kernel,
         jax.ShapeDtypeStruct((rows, model_width), jnp.bfloat16),
-        [where, base, *arrived[0], *arrived[1]],
+        [where, stream, *tables, *came],
         flops=rows * model_width * 3,
         bytes_accessed=rows * model_width * 10,
     )
@@ -481,7 +465,7 @@
     me = lax.axis_index("ep")
     core = me % 2
     seen = [
-        [ring[(ring.index(i // 2) + d) % chips] for d in range(chips)] + [i // FSPLIT, i % 2]
+        [ring[(ring.index(i // 2) + d) % chips] for d in range(chips)] + [i // FSPLIT]
         for i in range(devices)
     ]
     where = lax.dynamic_index_in_dim(jnp.asarray(seen, jnp.int32), me, 0, keepdims=False)
@@ -493,7 +477,7 @@
     swapped, w_gate, w_up = lax.optimization_barrier((swapped, w_gate, w_up))
     tables = [pltpu.with_memory_space_constraint(table, pltpu.HBM) for table in (w_gate, w_up)]
     tables += [swap_cores(w_gate), swap_cores(w_up)]
-    blocks = {0: first_blocks(where, by_core, swapped, expert_routes, route_gain, experts)}
+    blocks = {0: first_blocks(by_core, swapped, expert_routes, route_gain, experts)}
     w_down = lax.optimization_barrier((swapped, w_down))[1]
     down = [pltpu.with_memory_space_constraint(w_down, pltpu.HBM), swap_cores(w_down)]
 
@@ -502,21 +486,22 @@
             blocks[sign * distance] = ring_shift(blocks[sign * (distance - 1)], ring, -sign)
     groups = [[0]] + [[d, chips - d] for d in range(1, far)] + [[far]]
     gain_rows = norm_gain.reshape(chips, 1, width)
-    carried, owns, positions, headers, ahead = None, [], [], None, None
+    carried, owns, positions, headers, ahead, leading = None, [], [], None, None, None
     for group in groups:
         parts = [[blocks[d if d <= far else d - chips]] for d in group]
         if group == [far]:
             parts = [blocks[far]]
             headers = [blocks[d if d < far else d - chips] for d in range(chips) if d != far]
             headers.insert(far, blocks[far][0])
+            leading = (down, [(far, 0), (far, 1), (far - 1, 1), (chips - far + 1, 0)])
         if group == groups[-2]:
             ahead = (far, down)
         made, (carried, *rest) = accumulate(
-            where, group, parts, gain_rows, tables, tok_here, carried, headers, ahead
+            where, group, parts, gain_rows, tables, tok_here, carried, headers, ahead, leading
         )
         owns.extend(made)
         positions.extend(group)
-        if group == groups[max(far - 3, 0)]:
+        if group == groups[max(far - 2, 0)]:
             lower, upper, carried = lax.optimization_barrier(
                 (blocks[1 - far], blocks[far - 1], carried)
             )
@@ -525,12 +510,12 @@
         if group == groups[-2]:
             tables, down, ahead = [rest[0]], rest[1], None
 
-    leading = [(far, 0), (far, 1), (far - 1, 1), (chips - far + 1, 0)]
-    hidden, lower, upper, after, before = leading_rows(where, leading, carried, down, chips)
+    hidden, (lower, upper, after, before) = carried, rest
     moving = {1: [ring_shift(lower, ring, 1), None], -1: [None, ring_shift(upper, ring, -1)]}
     second = {1: ring_shift(after, ring, 1), -1: ring_shift(before, ring, -1)}
+    stream_rows = collect(where, positions, owns)
+    stream_rows, hidden = lax.optimization_barrier((stream_rows, hidden))
     everything = [contribution(where, hidden, down, part) for part in range(2)]
-    base = own_rows(where, positions, owns, everything)
     for distance in range(far - 1, 0, -1):
         for sign, order in ((1, (1, 0)), (-1, (0, 1))):
             position = (sign * distance) % chips
@@ -546,7 +531,7 @@
         [moving[sign][part] for sign in (1, -1) if moving[sign][part] is not None]
         for part in range(2)
     ]
-    return final_sum(where, base, arrived)
+    return final_sum(where, stream_rows, everything, arrived)
 
 
 def body(residual, attn_out, norm_gain, expert_routes, route_gain, w_gate, w_up, w_down):

time: 168 us -> 163 us (0.970)
  waiting for transfers between devices: 93.8 us -> 89.3 us
  starting transfers between devices: 26.6 us -> 24.7 us
    ppermute x22, waiting for transfers between devices: 92.3 us -> 87.8 us  [ring_shift(): return lax.ppermute(value, 'ep', pairs)]
    ppermute x22, starting transfers between devices: 25.2 us -> 23.3 us  [ring_shift(): return lax.ppermute(value, 'ep', pairs)]
    pallas_call x21 -> x20, Pallas kernels: 44.2 us -> 44.7 us  [local_call(): pl.pallas_call(kernel, out_shape=out_shape, in_specs=[IN_SMEM if value.nd...]
  transfers between devices with their start and end apart: 26 -> 26, of which waited for: 16 -> 18; matrix products, arithmetic and copies ran while one was open for 1% -> 1% of each run, Pallas kernels for 23% -> 24%
where the time goes in v12:
time: 163 us; the launch traced here: 162 us
  waiting for transfers between devices  89.3 us (55%)
  Pallas kernels  44.7 us (27%)
  starting transfers between devices  24.7 us (15%)
  other arithmetic  1.82 us (1%)
    ppermute x22, waiting for transfers between devices, ring_shift(): return lax.ppermute(value, 'ep', pairs)  87.8 us
    pallas_call x20, Pallas kernels, local_call(): pl.pallas_call(kernel, out_shape=out_shape, in_specs=[IN_SMEM if value.nd...  44.7 us
    ppermute x22, starting transfers between devices, ring_shift(): return lax.ppermute(value, 'ep', pairs)  23.3 us
  transfers between devices with their start and end apart: 26, of which 18 were waited for; matrix products, arithmetic and copies ran while one was open for 1% of the time, Pallas kernels for 24%

profile of v12, /device:TPU:0, one launch (start us, length us, event | category | flops | bytes accessed | tf_op | source)
XLA Modules:
  0.0 162.3 jit_solution(11883159701791899338)
XLA Ops:
  0.0 1.8 %add_convert_fusion = bf16[1024,448]{0,1:T(8,128)(2,1)S(1)} fusion(bf16[1024,448]{0,1:T(8,128)(2,1)} %param.10, bf16[1024,448]{0,1:T(8,128)(2,1)} %param.9), kind=kLoop, calls=%fused_computation | loop fusion | flops 1835008 | bytes 2752512 | tf_op jit(solution)/shard_map/convert_element_type | solution.py:473
  1.8 0.5 copy.13
  2.4 0.5 collective-permute-start
  3.0 1.5 collective-permute-done.swapped_ref
  4.5 0.4 collective-permute-start.1
  5.0 0.4 collective-permute-start.9
  5.6 0.7 shard_map.91.refs_0_.refs_5_
  6.3 2.8 %collective-permute-start.4 = (bf16[528,896]{1,0:T(8,128)(2,1)S(1)}, bf16[528,896]{1,0:T(8,128)(2,1)S(1)}, u32[]{:S(2)}, u32[]{:S(2)}) collective-permute-start(bf16[528,896]{1,0:T(8,128)(2,1)S(1)} %shard_map.91.refs_0_.refs_5_), channel_id=1, source_target_pairs={{0,4},{1,5},{4,8},{5,9},{8,12},{9,13},{12,14},{13,15},{14,10},{15,... | collective-permute-start | bytes 2838536 | tf_op jit(solution)/shard_map/ppermute | solution.py:94
  9.1 21.4 %collective-permute-done.4.refs_1_.refs_12_ = bf16[528,896]{1,0:T(8,128)(2,1)S(1)} collective-permute-done((bf16[528,896]{1,0:T(8,128)(2,1)S(1)}, bf16[528,896]{1,0:T(8,128)(2,1)S(1)}, u32[]{:S(2)}, u32[]{:S(2)}) %collective-permute-start.4) | collective-permute-done | bytes 946208 | tf_op jit(solution)/shard_map/ppermute | solution.py:94
  30.5 1.8 %collective-permute-start.6 = (bf16[528,896]{1,0:T(8,128)(2,1)S(1)}, bf16[528,896]{1,0:T(8,128)(2,1)}, u32[]{:S(2)}, u32[]{:S(2)}) collective-permute-start(bf16[528,896]{1,0:T(8,128)(2,1)S(1)} %collective-permute-done.4.refs_1_.refs_12_), channel_id=1, source_target_pairs={{0,4},{1,5},{4,8},{5,9},{8,12},{9,13},{12,14},{13,15},{14,10},{15,... | collective-permute-start | bytes 2838536 | tf_op jit(solution)/shard_map/ppermute | solution.py:94
  32.3 0.2 collective-permute-start.5
  32.5 0.7 dynamic-slice_bitcast_fusion.1.where_ref
  33.2 20.1 %collective-permute-done.6.refs_1_.refs_11_ = bf16[528,896]{1,0:T(8,128)(2,1)} collective-permute-done((bf16[528,896]{1,0:T(8,128)(2,1)S(1)}, bf16[528,896]{1,0:T(8,128)(2,1)}, u32[]{:S(2)}, u32[]{:S(2)}) %collective-permute-start.6) | collective-permute-done | bytes 946208 | tf_op jit(solution)/shard_map/ppermute | solution.py:94
  53.3 1.6 collective-permute-start.8
  54.8 0.5 collective-permute-start.7
  55.3 4.4 %shard_map.92 = (bf16[64,896]{1,0:T(8,128)(2,1)S(1)}, f32[512,1024]{1,0:T(8,128)S(1)}) custom-call(s32[9]{0:T(128)S(1)} %dynamic-slice_bitcast_fusion.1.where_ref, bf16[528,896]{1,0:T(8,128)(2,1)S(1)} %shard_map.91.refs_0_.refs_5_, f32[8,1,896]{2,1,0:T(1,128)S(1)} %bitcast.8, bf16[7168,256]{1,0:T(8,128)(2,1)} %refs_3_.3, bf16[7168,256]{1,0:T(8,128)(2,1)} %refs_4_.2, ...), custom_call_target="tpu_custom_call" | custom-call | flops 2818572288 | bytes 6946816 | tf_op jit(solution)/shard_map/pallas_call | solution.py:107
  59.7 6.8 %shard_map.93 = (bf16[64,896]{1,0:T(8,128)(2,1)S(1)}, bf16[64,896]{1,0:T(8,128)(2,1)S(1)}, f32[512,1024]{1,0:T(8,128)S(1)}) custom-call(s32[9]{0:T(128)S(1)} %dynamic-slice_bitcast_fusion.1.where_ref, bf16[528,896]{1,0:T(8,128)(2,1)S(1)} %collective-permute-done.3.refs_0_.refs_6_, ...), custom_call_target="tpu_custom_call", output_to_operand_aliasing={{2}: (8, {})} | custom-call | flops 5637144576 | bytes 9699328 | tf_op jit(solution)/shard_map/pallas_call | solution.py:107
  66.5 7.7 %shard_map.94 = (bf16[64,896]{1,0:T(8,128)(2,1)S(1)}, bf16[64,896]{1,0:T(8,128)(2,1)S(1)}, f32[512,1024]{1,0:T(8,128)S(1)}) custom-call(s32[9]{0:T(128)S(1)} %dynamic-slice_bitcast_fusion.1.where_ref, bf16[528,896]{1,0:T(8,128)(2,1)} %collective-permute-done.5.refs_0_.refs_7_, ...), custom_call_target="tpu_custom_call", output_to_operand_aliasing={{2}: (8, {})} | custom-call | flops 5637144576 | bytes 9699328 | tf_op jit(solution)/shard_map/pallas_call | solution.py:107
  74.2 1.0 collective-permute-done.8.refs_1_.refs_10_
  75.3 1.0 collective-permute-done.7.refs_0_.refs_8_
  76.3 0.8 collective-permute-start.11
  77.2 1.3 collective-permute-start.10
  78.5 6.8 %shard_map.95 = (bf16[64,896]{1,0:T(8,128)(2,1)S(1)}, bf16[64,896]{1,0:T(8,128)(2,1)S(1)}, f32[512,1024]{1,0:T(8,128)S(1)}, bf16[4,896,256]{2,1,0:T(8,128)(2,1)S(1)}, bf16[512,7168]{1,0:T(8,128)(2,1)S(1)}) custom-call(s32[9]{0:T(128)S(1)} %dynamic-slice_bitcast_fusion.1.where_ref, ...), custom_call_target="tpu_custom_call", output_to_operand_aliasing={{2}: (8, {})} | custom-call | flops 5637144576 | bytes 9699328 | tf_op jit(solution)/shard_map/pallas_call | solution.py:107
  85.3 1.0 collective-permute-done.11.refs_1_
  86.2 1.4 collective-permute-done.10.refs_0_.refs_9_
  87.7 4.1 %shard_map.96 = (bf16[64,896]{1,0:T(8,128)(2,1)S(1)}, bf16[512,512]{1,0:T(8,128)(2,1)S(1)}, bf16[64,3584]{1,0:T(8,128)(2,1)S(1)}, bf16[64,3584]{1,0:T(8,128)(2,1...) custom-call(s32[9]{0:T(128)S(1)} %dynamic-slice_bitcast_fusion.1.where_ref, ...), custom_call_target="tpu_custom_call" | custom-call | flops 2818572288 | bytes 6946816 | tf_op jit(solution)/shard_map/pallas_call | solution.py:107
  91.8 1.1 collective-permute-start.22
  92.9 1.0 collective-permute-start.12
  93.9 0.6 shard_map.97.stream_ref
  94.5 1.1 collective-permute-start.19
  95.6 2.6 %shard_map.99.table_ref.refs_1_ = bf16[512,3584]{1,0:T(8,128)(2,1)S(1)} custom-call(s32[9]{0:T(128)S(1)} %dynamic-slice_bitcast_fusion.1.where_ref, bf16[512,512]{1,0:T(8,128)(2,1)S(1)} %get-tuple-element.56.hidden_ref, bf16[512,7168]{1,0:T(8,128)(2,1)S(1)} %get-tuple-element.52.refs_13_.down_ref), custom_call_target="tpu_custom_call" | custom-call | flops 1879048192 | bytes 7340032 | tf_op jit(solution)/shard_map/pallas_call | solution.py:107
  98.2 2.6 %shard_map.98.table_ref.refs_0_ = bf16[512,3584]{1,0:T(8,128)(2,1)S(1)} custom-call(s32[9]{0:T(128)S(1)} %dynamic-slice_bitcast_fusion.1.where_ref, bf16[512,512]{1,0:T(8,128)(2,1)S(1)} %get-tuple-element.56.hidden_ref, bf16[512,7168]{1,0:T(8,128)(2,1)S(1)} %get-tuple-element.52.refs_13_.down_ref), custom_call_target="tpu_custom_call" | custom-call | flops 1879048192 | bytes 7340032 | tf_op jit(solution)/shard_map/pallas_call | solution.py:107
  100.8 1.1 collective-permute-start.16
  101.9 0.8 collective-permute-done.22.moved_ref
  102.6 0.6 shard_map.107
  103.3 0.6 collective-permute-start.23
  103.9 2.5 %collective-permute-done.12.moved_ref = bf16[64,3584]{1,0:T(8,128)(2,1)S(1)} collective-permute-done((bf16[64,3584]{1,0:T(8,128)(2,1)S(1)}, bf16[64,3584]{1,0:T(8,128)(2,1)S(1)}, u32[]{:S(2)}, u32[]{:S(2)}) %collective-permute-start.12) | collective-permute-done | bytes 458784 | tf_op jit(solution)/shard_map/ppermute | solution.py:94
  106.3 0.6 shard_map.100
  107.0 1.0 collective-permute-start.13
  108.0 8.1 %collective-permute-done.19.moved_ref = bf16[64,3584]{1,0:T(8,128)(2,1)S(1)} collective-permute-done((bf16[64,3584]{1,0:T(8,128)(2,1)S(1)}, bf16[64,3584]{1,0:T(8,128)(2,1)S(1)}, u32[]{:S(2)}, u32[]{:S(2)}) %collective-permute-start.19) | collective-permute-done | bytes 458784 | tf_op jit(solution)/shard_map/ppermute | solution.py:94
  116.2 0.6 shard_map.105
  116.8 1.0 collective-permute-start.20
  117.9 0.6 shard_map.103
  118.5 1.1 collective-permute-start.17
  119.6 4.5 %collective-permute-done.23.moved_ref = bf16[64,3584]{1,0:T(8,128)(2,1)S(1)} collective-permute-done((bf16[64,3584]{1,0:T(8,128)(2,1)S(1)}, bf16[64,3584]{1,0:T(8,128)(2,1)S(1)}, u32[]{:S(2)}, u32[]{:S(2)}) %collective-permute-start.23) | collective-permute-done | bytes 458784 | tf_op jit(solution)/shard_map/ppermute | solution.py:94
  124.1 0.6 shard_map.108
  124.8 1.1 collective-permute-start.24
  125.9 0.1 collective-permute-done.13.moved_ref
  126.0 0.6 shard_map.101
  126.7 1.0 collective-permute-start.14
  127.7 8.1 %collective-permute-done.20.moved_ref = bf16[64,3584]{1,0:T(8,128)(2,1)S(1)} collective-permute-done((bf16[64,3584]{1,0:T(8,128)(2,1)S(1)}, bf16[64,3584]{1,0:T(8,128)(2,1)S(1)}, u32[]{:S(2)}, u32[]{:S(2)}) %collective-permute-start.20) | collective-permute-done | bytes 458784 | tf_op jit(solution)/shard_map/ppermute | solution.py:94
  135.8 0.6 shard_map.106
  136.5 1.0 collective-permute-start.21
  137.5 0.6 shard_map.104
  138.2 1.1 collective-permute-start.18
  139.3 4.5 %collective-permute-done.24.moved_ref = bf16[64,3584]{1,0:T(8,128)(2,1)S(1)} collective-permute-done((bf16[64,3584]{1,0:T(8,128)(2,1)S(1)}, bf16[64,3584]{1,0:T(8,128)(2,1)S(1)}, u32[]{:S(2)}, u32[]{:S(2)}) %collective-permute-start.24) | collective-permute-done | bytes 458784 | tf_op jit(solution)/shard_map/ppermute | solution.py:94
  143.8 0.6 shard_map.109
  144.5 1.1 collective-permute-start.25
  145.7 0.6 shard_map.102
  146.3 1.0 collective-permute-start.15
  147.4 8.1 %collective-permute-done.21.refs_4_ = bf16[64,3584]{1,0:T(8,128)(2,1)S(1)} collective-permute-done((bf16[64,3584]{1,0:T(8,128)(2,1)S(1)}, bf16[64,3584]{1,0:T(8,128)(2,1)S(1)}, u32[]{:S(2)}, u32[]{:S(2)}) %collective-permute-start.21) | collective-permute-done | bytes 458784 | tf_op jit(solution)/shard_map/ppermute | solution.py:94
  155.5 4.3 %collective-permute-done.25.refs_5_ = bf16[64,3584]{1,0:T(8,128)(2,1)S(1)} collective-permute-done((bf16[64,3584]{1,0:T(8,128)(2,1)S(1)}, bf16[64,3584]{1,0:T(8,128)(2,1)S(1)}, u32[]{:S(2)}, u32[]{:S(2)}) %collective-permute-start.25) | collective-permute-done | bytes 458784 | tf_op jit(solution)/shard_map/ppermute | solution.py:94
  159.8 0.6 collective-permute-done.15.refs_2_
  160.4 1.9 %shard_map.110 = bf16[64,7168]{1,0:T(8,128)(2,1)} custom-call(s32[9]{0:T(128)S(1)} %dynamic-slice_bitcast_fusion.1.where_ref, bf16[64,7168]{1,0:T(8,128)(2,1)S(1)} %shard_map.97.stream_ref, bf16[512,3584]{1,0:T(8,128)(2,1)S(1)} %shard_map.98.table_ref.refs_0_, bf16[512,3584]{1,0:T(8,128)(2,1)S(1)} %shard_map.99.table_ref.refs_1_, ...), custom_call_target="tpu_custom_call" | custom-call | flops 1376256 | bytes 4587520 | tf_op jit(solution)/shard_map/pallas_call | solution.py:107
  (22 shorter events, 0.6 us)
Async XLA Ops:
  0.0 5.4 %copy-start.1 = (s32[64,2]{0,1:T(2,128)S(1)}, s32[64,2]{0,1:T(2,128)}, u32[]{:S(2)}) copy-start(s32[64,2]{0,1:T(2,128)} %param.12) | copy-start | bytes 1540
  0.0 5.5 %copy-start.2 = (f32[64,2]{0,1:T(2,128)S(1)}, f32[64,2]{0,1:T(2,128)}, u32[]{:S(2)}) copy-start(f32[64,2]{0,1:T(2,128)} %param.13) | copy-start | bytes 1540
  0.0 55.3 %copy-start = (f32[7168]{0:T(1024)S(1)}, f32[7168]{0:T(1024)}, u32[]{:S(2)}) copy-start(f32[7168]{0:T(1024)} %param.11) | copy-start | bytes 86020
  2.4 2.1 %collective-permute-start = (bf16[8,64,448]{2,1,0:T(8,128)(2,1)S(1)}, bf16[8,64,448]{2,1,0:T(8,128)(2,1)S(1)}, u32[]{:S(2)}, u32[]{:S(2)}) collective-permute-start(bf16[8,64,448]{2,1,0:T(8,128)(2,1)S(1)} %dynamic-slice_bitcast_fusion), channel_id=1, source_target_pairs={{0,1},{1,0},{2,3},{3,2},{4,5},{5,4},{6,7},{7,6},{8,9},{9,8},{10,11... | collective-permute-start | bytes 1376264 | tf_op jit(solution)/shard_map/ppermute | solution.py:84
  4.5 50.8 %collective-permute-start.1 = (bf16[7168,256]{1,0:T(8,128)(2,1)}, bf16[7168,256]{1,0:T(8,128)(2,1)}, u32[]{:S(2)}, u32[]{:S(2)}) collective-permute-start(bf16[7168,256]{1,0:T(8,128)(2,1)} %refs_3_.3), channel_id=1, source_target_pairs={{0,1},{1,0},{2,3},{3,2},{4,5},{5,4},{6,7},{7,6},{8,9},{9,8},{10,11... | collective-permute-start | bytes 11010056 | tf_op jit(solution)/shard_map/ppermute | solution.py:84
  4.9 50.4 %collective-permute-start.2 = (bf16[7168,256]{1,0:T(8,128)(2,1)}, bf16[7168,256]{1,0:T(8,128)(2,1)}, u32[]{:S(2)}, u32[]{:S(2)}) collective-permute-start(bf16[7168,256]{1,0:T(8,128)(2,1)} %refs_4_.2), channel_id=1, source_target_pairs={{0,1},{1,0},{2,3},{3,2},{4,5},{5,4},{6,7},{7,6},{8,9},{9,8},{10,11... | collective-permute-start | bytes 11010056 | tf_op jit(solution)/shard_map/ppermute | solution.py:84
  5.0 73.5 %collective-permute-start.9 = (bf16[256,7168]{1,0:T(8,128)(2,1)}, bf16[256,7168]{1,0:T(8,128)(2,1)}, u32[]{:S(2)}, u32[]{:S(2)}) collective-permute-start(bf16[256,7168]{1,0:T(8,128)(2,1)} %refs_8_), channel_id=1, source_target_pairs={{0,1},{1,0},{2,3},{3,2},{4,5},{5,4},{6,7},{7,6},{8,9},{9,8},{10,11... | collective-permute-start | bytes 11010056 | tf_op jit(solution)/shard_map/ppermute | solution.py:84
  6.3 24.2 %collective-permute-start.4 = (bf16[528,896]{1,0:T(8,128)(2,1)S(1)}, bf16[528,896]{1,0:T(8,128)(2,1)S(1)}, u32[]{:S(2)}, u32[]{:S(2)}) collective-permute-start(bf16[528,896]{1,0:T(8,128)(2,1)S(1)} %shard_map.91.refs_0_.refs_5_), channel_id=1, source_target_pairs={{0,4},{1,5},{4,8},{5,9},{8,12},{9,13},{12,14},{13,15},{14,10},{15,... | collective-permute-start | bytes 2838536 | tf_op jit(solution)/shard_map/ppermute | solution.py:94
  9.1 23.2 %collective-permute-start.3 = (bf16[528,896]{1,0:T(8,128)(2,1)S(1)}, bf16[528,896]{1,0:T(8,128)(2,1)S(1)}, u32[]{:S(2)}, u32[]{:S(2)}) collective-permute-start(bf16[528,896]{1,0:T(8,128)(2,1)S(1)} %shard_map.91.refs_0_.refs_5_), channel_id=1, source_target_pairs={{0,2},{1,3},{4,0},{5,1},{8,4},{9,5},{12,8},{13,9},{14,12},{15,13},... | collective-permute-start | bytes 2838536 | tf_op jit(solution)/shard_map/ppermute | solution.py:94
  30.5 22.8 %collective-permute-start.6 = (bf16[528,896]{1,0:T(8,128)(2,1)S(1)}, bf16[528,896]{1,0:T(8,128)(2,1)}, u32[]{:S(2)}, u32[]{:S(2)}) collective-permute-start(bf16[528,896]{1,0:T(8,128)(2,1)S(1)} %collective-permute-done.4.refs_1_.refs_12_), channel_id=1, source_target_pairs={{0,4},{1,5},{4,8},{5,9},{8,12},{9,13},{12,14},{13,15},{14,10},{15,... | collective-permute-start | bytes 2838536 | tf_op jit(solution)/shard_map/ppermute | solution.py:94
  32.3 22.5 %collective-permute-start.5 = (bf16[528,896]{1,0:T(8,128)(2,1)S(1)}, bf16[528,896]{1,0:T(8,128)(2,1)}, u32[]{:S(2)}, u32[]{:S(2)}) collective-permute-start(bf16[528,896]{1,0:T(8,128)(2,1)S(1)} %collective-permute-done.3.refs_0_.refs_6_), channel_id=1, source_target_pairs={{0,2},{1,3},{4,0},{5,1},{8,4},{9,5},{12,8},{13,9},{14,12},{15,13},... | collective-permute-start | bytes 2838536 | tf_op jit(solution)/shard_map/ppermute | solution.py:94
  53.3 22.0 %collective-permute-start.8 = (bf16[528,896]{1,0:T(8,128)(2,1)}, bf16[528,896]{1,0:T(8,128)(2,1)S(1)}, u32[]{:S(2)}, u32[]{:S(2)}) collective-permute-start(bf16[528,896]{1,0:T(8,128)(2,1)} %collective-permute-done.6.refs_1_.refs_11_), channel_id=1, source_target_pairs={{0,4},{1,5},{4,8},{5,9},{8,12},{9,13},{12,14},{13,15},{14,10},{15,... | collective-permute-start | bytes 2838536 | tf_op jit(solution)/shard_map/ppermute | solution.py:94
  54.8 21.4 %collective-permute-start.7 = (bf16[528,896]{1,0:T(8,128)(2,1)}, bf16[528,896]{1,0:T(8,128)(2,1)S(1)}, u32[]{:S(2)}, u32[]{:S(2)}) collective-permute-start(bf16[528,896]{1,0:T(8,128)(2,1)} %collective-permute-done.5.refs_0_.refs_7_), channel_id=1, source_target_pairs={{0,2},{1,3},{4,0},{5,1},{8,4},{9,5},{12,8},{13,9},{14,12},{15,13},... | collective-permute-start | bytes 2838536 | tf_op jit(solution)/shard_map/ppermute | solution.py:94
  76.3 9.9 %collective-permute-start.11 = (bf16[256,896]{1,0:T(8,128)(2,1)S(1)}, bf16[256,896]{1,0:T(8,128)(2,1)S(1)}, u32[]{:S(2)}, u32[]{:S(2)}) collective-permute-start(bf16[256,896]{1,0:T(8,128)(2,1)S(1)} %slice.7), channel_id=1, source_target_pairs={{0,2},{1,3},{4,0},{5,1},{8,4},{9,5},{12,8},{13,9},{14,12},{15,13},... | collective-permute-start | bytes 1376264 | tf_op jit(solution)/shard_map/ppermute | solution.py:94
  77.2 10.5 %collective-permute-start.10 = (bf16[272,896]{1,0:T(8,128)(2,1)S(1)}, bf16[272,896]{1,0:T(8,128)(2,1)S(1)}, u32[]{:S(2)}, u32[]{:S(2)}) collective-permute-start(bf16[272,896]{1,0:T(8,128)(2,1)S(1)} %slice.6), channel_id=1, source_target_pairs={{0,4},{1,5},{4,8},{5,9},{8,12},{9,13},{12,14},{13,15},{14,10},{15,... | collective-permute-start | bytes 1462280 | tf_op jit(solution)/shard_map/ppermute | solution.py:94
  91.8 10.8 %collective-permute-start.22 = (bf16[64,3584]{1,0:T(8,128)(2,1)S(1)}, bf16[64,3584]{1,0:T(8,128)(2,1)S(1)}, u32[]{:S(2)}, u32[]{:S(2)}) collective-permute-start(bf16[64,3584]{1,0:T(8,128)(2,1)S(1)} %get-tuple-element.60), channel_id=1, source_target_pairs={{0,2},{1,3},{4,0},{5,1},{8,4},{9,5},{12,8},{13,9},{14,12},{15,13},... | collective-permute-start | bytes 1376264 | tf_op jit(solution)/shard_map/ppermute | solution.py:94
  92.9 13.5 %collective-permute-start.12 = (bf16[64,3584]{1,0:T(8,128)(2,1)S(1)}, bf16[64,3584]{1,0:T(8,128)(2,1)S(1)}, u32[]{:S(2)}, u32[]{:S(2)}) collective-permute-start(bf16[64,3584]{1,0:T(8,128)(2,1)S(1)} %get-tuple-element.57), channel_id=1, source_target_pairs={{0,4},{1,5},{4,8},{5,9},{8,12},{9,13},{12,14},{13,15},{14,10},{15,... | collective-permute-start | bytes 1376264 | tf_op jit(solution)/shard_map/ppermute | solution.py:94
  94.5 21.7 %collective-permute-start.19 = (bf16[64,3584]{1,0:T(8,128)(2,1)S(1)}, bf16[64,3584]{1,0:T(8,128)(2,1)S(1)}, u32[]{:S(2)}, u32[]{:S(2)}) collective-permute-start(bf16[64,3584]{1,0:T(8,128)(2,1)S(1)} %get-tuple-element.59), channel_id=1, source_target_pairs={{0,4},{1,5},{4,8},{5,9},{8,12},{9,13},{12,14},{13,15},{14,10},{15,... | collective-permute-start | bytes 1376264 | tf_op jit(solution)/shard_map/ppermute | solution.py:94
  100.8 17.1 %collective-permute-start.16 = (bf16[64,3584]{1,0:T(8,128)(2,1)S(1)}, bf16[64,3584]{1,0:T(8,128)(2,1)S(1)}, u32[]{:S(2)}, u32[]{:S(2)}) collective-permute-start(bf16[64,3584]{1,0:T(8,128)(2,1)S(1)} %get-tuple-element.58), channel_id=1, source_target_pairs={{0,2},{1,3},{4,0},{5,1},{8,4},{9,5},{12,8},{13,9},{14,12},{15,13},... | collective-permute-start | bytes 1376264 | tf_op jit(solution)/shard_map/ppermute | solution.py:94
  103.3 20.8 %collective-permute-start.23 = (bf16[64,3584]{1,0:T(8,128)(2,1)S(1)}, bf16[64,3584]{1,0:T(8,128)(2,1)S(1)}, u32[]{:S(2)}, u32[]{:S(2)}) collective-permute-start(bf16[64,3584]{1,0:T(8,128)(2,1)S(1)} %shard_map.107), channel_id=1, source_target_pairs={{0,2},{1,3},{4,0},{5,1},{8,4},{9,5},{12,8},{13,9},{14,12},{15,13},... | collective-permute-start | bytes 1376264 | tf_op jit(solution)/shard_map/ppermute | solution.py:94
  107.0 19.0 %collective-permute-start.13 = (bf16[64,3584]{1,0:T(8,128)(2,1)S(1)}, bf16[64,3584]{1,0:T(8,128)(2,1)S(1)}, u32[]{:S(2)}, u32[]{:S(2)}) collective-permute-start(bf16[64,3584]{1,0:T(8,128)(2,1)S(1)} %shard_map.100), channel_id=1, source_target_pairs={{0,4},{1,5},{4,8},{5,9},{8,12},{9,13},{12,14},{13,15},{14,10},{15,... | collective-permute-start | bytes 1376264 | tf_op jit(solution)/shard_map/ppermute | solution.py:94
  116.8 19.0 %collective-permute-start.20 = (bf16[64,3584]{1,0:T(8,128)(2,1)S(1)}, bf16[64,3584]{1,0:T(8,128)(2,1)S(1)}, u32[]{:S(2)}, u32[]{:S(2)}) collective-permute-start(bf16[64,3584]{1,0:T(8,128)(2,1)S(1)} %shard_map.105), channel_id=1, source_target_pairs={{0,4},{1,5},{4,8},{5,9},{8,12},{9,13},{12,14},{13,15},{14,10},{15,... | collective-permute-start | bytes 1376264 | tf_op jit(solution)/shard_map/ppermute | solution.py:94
  118.5 19.0 %collective-permute-start.17 = (bf16[64,3584]{1,0:T(8,128)(2,1)S(1)}, bf16[64,3584]{1,0:T(8,128)(2,1)S(1)}, u32[]{:S(2)}, u32[]{:S(2)}) collective-permute-start(bf16[64,3584]{1,0:T(8,128)(2,1)S(1)} %shard_map.103), channel_id=1, source_target_pairs={{0,2},{1,3},{4,0},{5,1},{8,4},{9,5},{12,8},{13,9},{14,12},{15,13},... | collective-permute-start | bytes 1376264 | tf_op jit(solution)/shard_map/ppermute | solution.py:94
  124.8 19.0 %collective-permute-start.24 = (bf16[64,3584]{1,0:T(8,128)(2,1)S(1)}, bf16[64,3584]{1,0:T(8,128)(2,1)S(1)}, u32[]{:S(2)}, u32[]{:S(2)}) collective-permute-start(bf16[64,3584]{1,0:T(8,128)(2,1)S(1)} %shard_map.108), channel_id=1, source_target_pairs={{0,2},{1,3},{4,0},{5,1},{8,4},{9,5},{12,8},{13,9},{14,12},{15,13},... | collective-permute-start | bytes 1376264 | tf_op jit(solution)/shard_map/ppermute | solution.py:94
  126.7 19.0 %collective-permute-start.14 = (bf16[64,3584]{1,0:T(8,128)(2,1)S(1)}, bf16[64,3584]{1,0:T(8,128)(2,1)S(1)}, u32[]{:S(2)}, u32[]{:S(2)}) collective-permute-start(bf16[64,3584]{1,0:T(8,128)(2,1)S(1)} %shard_map.101), channel_id=1, source_target_pairs={{0,4},{1,5},{4,8},{5,9},{8,12},{9,13},{12,14},{13,15},{14,10},{15,... | collective-permute-start | bytes 1376264 | tf_op jit(solution)/shard_map/ppermute | solution.py:94
  136.5 19.0 %collective-permute-start.21 = (bf16[64,3584]{1,0:T(8,128)(2,1)S(1)}, bf16[64,3584]{1,0:T(8,128)(2,1)S(1)}, u32[]{:S(2)}, u32[]{:S(2)}) collective-permute-start(bf16[64,3584]{1,0:T(8,128)(2,1)S(1)} %shard_map.106), channel_id=1, source_target_pairs={{0,4},{1,5},{4,8},{5,9},{8,12},{9,13},{12,14},{13,15},{14,10},{15,... | collective-permute-start | bytes 1376264 | tf_op jit(solution)/shard_map/ppermute | solution.py:94
  138.2 17.3 %collective-permute-start.18 = (bf16[64,3584]{1,0:T(8,128)(2,1)S(1)}, bf16[64,3584]{1,0:T(8,128)(2,1)S(1)}, u32[]{:S(2)}, u32[]{:S(2)}) collective-permute-start(bf16[64,3584]{1,0:T(8,128)(2,1)S(1)} %shard_map.104), channel_id=1, source_target_pairs={{0,2},{1,3},{4,0},{5,1},{8,4},{9,5},{12,8},{13,9},{14,12},{15,13},... | collective-permute-start | bytes 1376264 | tf_op jit(solution)/shard_map/ppermute | solution.py:94
  144.5 15.3 %collective-permute-start.25 = (bf16[64,3584]{1,0:T(8,128)(2,1)S(1)}, bf16[64,3584]{1,0:T(8,128)(2,1)S(1)}, u32[]{:S(2)}, u32[]{:S(2)}) collective-permute-start(bf16[64,3584]{1,0:T(8,128)(2,1)S(1)} %shard_map.109), channel_id=1, source_target_pairs={{0,2},{1,3},{4,0},{5,1},{8,4},{9,5},{12,8},{13,9},{14,12},{15,13},... | collective-permute-start | bytes 1376264 | tf_op jit(solution)/shard_map/ppermute | solution.py:94
  146.3 14.0 %collective-permute-start.15 = (bf16[64,3584]{1,0:T(8,128)(2,1)S(1)}, bf16[64,3584]{1,0:T(8,128)(2,1)S(1)}, u32[]{:S(2)}, u32[]{:S(2)}) collective-permute-start(bf16[64,3584]{1,0:T(8,128)(2,1)S(1)} %shard_map.102), channel_id=1, source_target_pairs={{0,4},{1,5},{4,8},{5,9},{8,12},{9,13},{12,14},{13,15},{14,10},{15,... | collective-permute-start | bytes 1376264 | tf_op jit(solution)/shard_map/ppermute | solution.py:94

commit v13 on v12

--- a/solution.py
+++ b/solution.py
@@ -196,6 +196,7 @@
     last = headers is not None
     first = carried is None
     slots = 0 if last else 4 * count
+    side = 128
 
     def kernel(where_ref, *refs):
         refs = list(refs)
@@ -251,29 +252,28 @@
                     owns[b][...] = xs[b][k][pl.ds(pl.multiple_of(row, 16), tok_here), :]
 
         if last:
-            expert = where_ref[chips]
-            square = (tok_here, tok_here)
-            row_at = lax.broadcasted_iota(jnp.int32, (head, tok_here), 0)
-            diagonal = lax.broadcasted_iota(jnp.int32, square, 0) == lax.broadcasted_iota(
-                jnp.int32, square, 1
+            over_rows = (((0,), (0,)), ((), ()))
+            gain_row = 3 * (where_ref[chips] + 1)
+            row_at = lax.broadcasted_iota(jnp.int32, (head, side), 0)
+            named = ((row_at >= gain_row) & (row_at < gain_row + 3)).astype(jnp.bfloat16)
+            row_at = lax.rem(lax.broadcasted_iota(jnp.int32, (chips * head, side), 0), head)
+            ones = (row_at < 3).astype(jnp.bfloat16)
+            for d in range(chips):
+                gains = lax.dot_general(
+                    tops[d][:head, :tok_here],
+                    named,
+                    over_rows,
+                    preferred_element_type=jnp.float32,
+                )
+                at = pl.multiple_of(where_ref[d] * tok_here, tok_here)
+                column_ref[pl.ds(at, tok_here), 0:1] = gains[:, 0:1]
+            squares = lax.dot_general(
+                jnp.concatenate([top[:head, :tokens] for top in tops], axis=0),
+                ones,
+                over_rows,
+                preferred_element_type=jnp.float32,
             )
-
-            def column(row, values):
-                named = (row_at >= row) & (row_at < row + 3)
-                along = jnp.sum(jnp.where(named, values, 0.0), axis=0, keepdims=True)
-                return jnp.sum(jnp.where(diagonal, along, 0.0), axis=1, keepdims=True)
-
-            for d in range(chips):
-                values = tops[d][:head, :tok_here].astype(jnp.float32)
-                at = pl.multiple_of(where_ref[d] * tok_here, tok_here)
-                column_ref[pl.ds(at, tok_here), 0:1] = column(3 * (expert + 1), values)
-            for q in range(chips):
-                span = slice(q * tok_here, (q + 1) * tok_here)
-                total = tops[0][:head, span].astype(jnp.float32)
-                for d in range(1, chips):
-                    total = total + tops[d][:head, span].astype(jnp.float32)
-                mean = column(0, total) / model_width
-                column_ref[span, 1:2] = lax.rsqrt(mean + epsilon)
+            column_ref[:, 1:2] = lax.rsqrt(squares[:, 0:1] / model_width + epsilon)
 
         scaled = []
         for k, size in enumerate(sizes):
@@ -432,24 +432,47 @@
     half = model_width // 2
     came = [value for part in arrived for value in part]
 
+    steps = 2 if half % 256 == 0 else 1
+    tile = half // steps
+
     def kernel(where_ref, stream_ref, *refs):
-        out_ref = refs[-1]
+        out_ref, sum_ref, sems = refs[-3:]
         at = pl.multiple_of(where_ref[0] * rows, rows)
+        writes = []
         for part in range(2):
-            cols = slice(part * half, (part + 1) * half)
-            total = stream_ref[:, cols].astype(jnp.float32)
-            total = total + refs[part][pl.ds(at, rows), :].astype(jnp.float32)
-            for k in range(len(arrived[part])):
-                total = total + refs[2 + k + part * len(arrived[0])][...].astype(jnp.float32)
-            out_ref[:, cols] = total.astype(jnp.bfloat16)
-
-    return local_call(
-        kernel,
-        jax.ShapeDtypeStruct((rows, model_width), jnp.bfloat16),
-        [where, stream, *tables, *came],
-        flops=rows * model_width * 3,
-        bytes_accessed=rows * model_width * 10,
-    )
+            for step in range(steps):
+                here = slice(step * tile, (step + 1) * tile)
+                cols = slice(part * half + step * tile, part * half + (step + 1) * tile)
+                total = stream_ref[:, cols].astype(jnp.float32)
+                total = total + refs[part][pl.ds(at, rows), here].astype(jnp.float32)
+                for k in range(len(arrived[part])):
+                    value = refs[2 + k + part * len(arrived[0])][:, here]
+                    total = total + value.astype(jnp.float32)
+                sum_ref[:, cols] = total.astype(jnp.bfloat16)
+                writes.append(
+                    pltpu.make_async_copy(
+                        sum_ref.at[:, cols], out_ref.at[:, cols], sems.at[len(writes)]
+                    )
+                )
+                writes[-1].start()
+        for write in writes:
+            write.wait()
+
+    operands = [where, stream, *tables, *came]
+    return pl.pallas_call(
+        kernel,
+        in_specs=[IN_SMEM] + [IN_VMEM] * (len(operands) - 1),
+        out_specs=IN_HBM,
+        out_shape=jax.ShapeDtypeStruct((rows, model_width), jnp.bfloat16),
+        scratch_shapes=[
+            pltpu.VMEM((rows, model_width), jnp.bfloat16),
+            pltpu.SemaphoreType.DMA((2 * steps,)),
+        ],
+        compiler_params=pltpu.CompilerParams(vmem_limit_bytes=VMEM_BYTES),
+        cost_estimate=pl.CostEstimate(
+            flops=rows * model_width * 3, bytes_accessed=rows * model_width * 10, transcendentals=0
+        ),
+    )(*operands)
 
 
 def dense_body(residual, attn_out, norm_gain, expert_routes, route_gain, w_gate, w_up, w_down):

time: 163 us -> 163 us (level)
    pallas_call x20 -> x19, Pallas kernels: 44.7 us -> 42.9 us  [local_call(): pl.pallas_call(kernel, out_shape=out_shape, in_specs=[IN_SMEM if value.nd...]
    pallas_call x0 -> x1, Pallas kernels: none -> 1.71 us  [final_sum(): pl.pallas_call(kernel, in_specs=[IN_SMEM] + [IN_VMEM] * (len(operands) -...]
where the time goes in v13:
time: 163 us; the launch traced here: 162 us
  waiting for transfers between devices  89.4 us (55%)
  Pallas kernels  44.6 us (27%)
  starting transfers between devices  24.6 us (15%)
  other arithmetic  1.82 us (1%)
    ppermute x22, waiting for transfers between devices, ring_shift(): return lax.ppermute(value, 'ep', pairs)  87.9 us
    pallas_call x19, Pallas kernels, local_call(): pl.pallas_call(kernel, out_shape=out_shape, in_specs=[IN_SMEM if value.nd...  42.9 us
    ppermute x22, starting transfers between devices, ring_shift(): return lax.ppermute(value, 'ep', pairs)  23.2 us
  transfers between devices with their start and end apart: 26, of which 18 were waited for; matrix products, arithmetic and copies ran while one was open for 1% of the time, Pallas kernels for 24%

profile of v13, /device:TPU:0, one launch (start us, length us, event | category | flops | bytes accessed | tf_op | source)
XLA Modules:
  0.0 162.3 jit_solution(9344538560316902679)
XLA Ops:
  0.0 1.8 %add_convert_fusion = bf16[1024,448]{0,1:T(8,128)(2,1)S(1)} fusion(bf16[1024,448]{0,1:T(8,128)(2,1)} %param.10, bf16[1024,448]{0,1:T(8,128)(2,1)} %param.9), kind=kLoop, calls=%fused_computation | loop fusion | flops 1835008 | bytes 2752512 | tf_op jit(solution)/shard_map/convert_element_type | solution.py:496
  1.8 0.5 copy.13
  2.4 0.5 collective-permute-start
  3.0 1.5 collective-permute-done.swapped_ref
  4.5 0.4 collective-permute-start.1
  5.0 0.4 collective-permute-start.9
  5.6 0.7 shard_map.91.refs_0_.refs_5_
  6.3 2.8 %collective-permute-start.4 = (bf16[528,896]{1,0:T(8,128)(2,1)S(1)}, bf16[528,896]{1,0:T(8,128)(2,1)S(1)}, u32[]{:S(2)}, u32[]{:S(2)}) collective-permute-start(bf16[528,896]{1,0:T(8,128)(2,1)S(1)} %shard_map.91.refs_0_.refs_5_), channel_id=1, source_target_pairs={{0,4},{1,5},{4,8},{5,9},{8,12},{9,13},{12,14},{13,15},{14,10},{15,... | collective-permute-start | bytes 2838536 | tf_op jit(solution)/shard_map/ppermute | solution.py:94
  9.1 21.4 %collective-permute-done.4.refs_1_.refs_12_ = bf16[528,896]{1,0:T(8,128)(2,1)S(1)} collective-permute-done((bf16[528,896]{1,0:T(8,128)(2,1)S(1)}, bf16[528,896]{1,0:T(8,128)(2,1)S(1)}, u32[]{:S(2)}, u32[]{:S(2)}) %collective-permute-start.4) | collective-permute-done | bytes 946208 | tf_op jit(solution)/shard_map/ppermute | solution.py:94
  30.5 1.8 %collective-permute-start.6 = (bf16[528,896]{1,0:T(8,128)(2,1)S(1)}, bf16[528,896]{1,0:T(8,128)(2,1)}, u32[]{:S(2)}, u32[]{:S(2)}) collective-permute-start(bf16[528,896]{1,0:T(8,128)(2,1)S(1)} %collective-permute-done.4.refs_1_.refs_12_), channel_id=1, source_target_pairs={{0,4},{1,5},{4,8},{5,9},{8,12},{9,13},{12,14},{13,15},{14,10},{15,... | collective-permute-start | bytes 2838536 | tf_op jit(solution)/shard_map/ppermute | solution.py:94
  32.3 0.2 collective-permute-start.5
  32.5 0.7 dynamic-slice_bitcast_fusion.1.where_ref
  33.2 20.1 %collective-permute-done.6.refs_1_.refs_11_ = bf16[528,896]{1,0:T(8,128)(2,1)} collective-permute-done((bf16[528,896]{1,0:T(8,128)(2,1)S(1)}, bf16[528,896]{1,0:T(8,128)(2,1)}, u32[]{:S(2)}, u32[]{:S(2)}) %collective-permute-start.6) | collective-permute-done | bytes 946208 | tf_op jit(solution)/shard_map/ppermute | solution.py:94
  53.3 1.6 collective-permute-start.8
  54.8 0.5 collective-permute-start.7
  55.3 4.4 %shard_map.92 = (bf16[64,896]{1,0:T(8,128)(2,1)S(1)}, f32[512,1024]{1,0:T(8,128)S(1)}) custom-call(s32[9]{0:T(128)S(1)} %dynamic-slice_bitcast_fusion.1.where_ref, bf16[528,896]{1,0:T(8,128)(2,1)S(1)} %shard_map.91.refs_0_.refs_5_, f32[8,1,896]{2,1,0:T(1,128)S(1)} %bitcast.8, bf16[7168,256]{1,0:T(8,128)(2,1)} %refs_3_.3, bf16[7168,256]{1,0:T(8,128)(2,1)} %refs_4_.2, ...), custom_call_target="tpu_custom_call" | custom-call | flops 2818572288 | bytes 6946816 | tf_op jit(solution)/shard_map/pallas_call | solution.py:107
  59.7 6.8 %shard_map.93 = (bf16[64,896]{1,0:T(8,128)(2,1)S(1)}, bf16[64,896]{1,0:T(8,128)(2,1)S(1)}, f32[512,1024]{1,0:T(8,128)S(1)}) custom-call(s32[9]{0:T(128)S(1)} %dynamic-slice_bitcast_fusion.1.where_ref, bf16[528,896]{1,0:T(8,128)(2,1)S(1)} %collective-permute-done.3.refs_0_.refs_6_, ...), custom_call_target="tpu_custom_call", output_to_operand_aliasing={{2}: (8, {})} | custom-call | flops 5637144576 | bytes 9699328 | tf_op jit(solution)/shard_map/pallas_call | solution.py:107
  66.5 7.7 %shard_map.94 = (bf16[64,896]{1,0:T(8,128)(2,1)S(1)}, bf16[64,896]{1,0:T(8,128)(2,1)S(1)}, f32[512,1024]{1,0:T(8,128)S(1)}) custom-call(s32[9]{0:T(128)S(1)} %dynamic-slice_bitcast_fusion.1.where_ref, bf16[528,896]{1,0:T(8,128)(2,1)} %collective-permute-done.5.refs_0_.refs_7_, ...), custom_call_target="tpu_custom_call", output_to_operand_aliasing={{2}: (8, {})} | custom-call | flops 5637144576 | bytes 9699328 | tf_op jit(solution)/shard_map/pallas_call | solution.py:107
  74.2 1.0 collective-permute-done.8.refs_1_.refs_10_
  75.3 1.0 collective-permute-done.7.refs_0_.refs_8_
  76.3 0.8 collective-permute-start.11
  77.2 1.3 collective-permute-start.10
  78.5 6.8 %shard_map.95 = (bf16[64,896]{1,0:T(8,128)(2,1)S(1)}, bf16[64,896]{1,0:T(8,128)(2,1)S(1)}, f32[512,1024]{1,0:T(8,128)S(1)}, bf16[4,896,256]{2,1,0:T(8,128)(2,1)S(1)}, bf16[512,7168]{1,0:T(8,128)(2,1)S(1)}) custom-call(s32[9]{0:T(128)S(1)} %dynamic-slice_bitcast_fusion.1.where_ref, ...), custom_call_target="tpu_custom_call", output_to_operand_aliasing={{2}: (8, {})} | custom-call | flops 5637144576 | bytes 9699328 | tf_op jit(solution)/shard_map/pallas_call | solution.py:107
  85.3 1.0 collective-permute-done.11.refs_1_
  86.2 1.4 collective-permute-done.10.refs_0_.refs_9_
  87.7 4.2 %shard_map.96 = (bf16[64,896]{1,0:T(8,128)(2,1)S(1)}, bf16[512,512]{1,0:T(8,128)(2,1)S(1)}, bf16[64,3584]{1,0:T(8,128)(2,1)S(1)}, bf16[64,3584]{1,0:T(8,128)(2,1...) custom-call(s32[9]{0:T(128)S(1)} %dynamic-slice_bitcast_fusion.1.where_ref, ...), custom_call_target="tpu_custom_call" | custom-call | flops 2818572288 | bytes 6946816 | tf_op jit(solution)/shard_map/pallas_call | solution.py:107
  91.9 1.1 collective-permute-start.22
  93.0 1.0 collective-permute-start.12
  93.9 0.6 shard_map.97.stream_ref
  94.6 1.1 collective-permute-start.19
  95.6 2.6 %shard_map.99.table_ref.refs_1_ = bf16[512,3584]{1,0:T(8,128)(2,1)S(1)} custom-call(s32[9]{0:T(128)S(1)} %dynamic-slice_bitcast_fusion.1.where_ref, bf16[512,512]{1,0:T(8,128)(2,1)S(1)} %get-tuple-element.56.hidden_ref, bf16[512,7168]{1,0:T(8,128)(2,1)S(1)} %get-tuple-element.52.refs_13_.down_ref), custom_call_target="tpu_custom_call" | custom-call | flops 1879048192 | bytes 7340032 | tf_op jit(solution)/shard_map/pallas_call | solution.py:107
  98.2 2.6 %shard_map.98.table_ref.refs_0_ = bf16[512,3584]{1,0:T(8,128)(2,1)S(1)} custom-call(s32[9]{0:T(128)S(1)} %dynamic-slice_bitcast_fusion.1.where_ref, bf16[512,512]{1,0:T(8,128)(2,1)S(1)} %get-tuple-element.56.hidden_ref, bf16[512,7168]{1,0:T(8,128)(2,1)S(1)} %get-tuple-element.52.refs_13_.down_ref), custom_call_target="tpu_custom_call" | custom-call | flops 1879048192 | bytes 7340032 | tf_op jit(solution)/shard_map/pallas_call | solution.py:107
  100.9 1.1 collective-permute-start.16
  101.9 0.8 collective-permute-done.22.moved_ref
  102.7 0.6 shard_map.107
  103.4 0.5 collective-permute-start.23
  104.0 2.5 %collective-permute-done.12.moved_ref = bf16[64,3584]{1,0:T(8,128)(2,1)S(1)} collective-permute-done((bf16[64,3584]{1,0:T(8,128)(2,1)S(1)}, bf16[64,3584]{1,0:T(8,128)(2,1)S(1)}, u32[]{:S(2)}, u32[]{:S(2)}) %collective-permute-start.12) | collective-permute-done | bytes 458784 | tf_op jit(solution)/shard_map/ppermute | solution.py:94
  106.4 0.6 shard_map.100
  107.1 1.0 collective-permute-start.13
  108.1 8.2 %collective-permute-done.19.moved_ref = bf16[64,3584]{1,0:T(8,128)(2,1)S(1)} collective-permute-done((bf16[64,3584]{1,0:T(8,128)(2,1)S(1)}, bf16[64,3584]{1,0:T(8,128)(2,1)S(1)}, u32[]{:S(2)}, u32[]{:S(2)}) %collective-permute-start.19) | collective-permute-done | bytes 458784 | tf_op jit(solution)/shard_map/ppermute | solution.py:94
  116.3 0.6 shard_map.105
  116.9 1.0 collective-permute-start.20
  117.9 0.6 shard_map.103
  118.6 1.1 collective-permute-start.17
  119.7 4.5 %collective-permute-done.23.moved_ref = bf16[64,3584]{1,0:T(8,128)(2,1)S(1)} collective-permute-done((bf16[64,3584]{1,0:T(8,128)(2,1)S(1)}, bf16[64,3584]{1,0:T(8,128)(2,1)S(1)}, u32[]{:S(2)}, u32[]{:S(2)}) %collective-permute-start.23) | collective-permute-done | bytes 458784 | tf_op jit(solution)/shard_map/ppermute | solution.py:94
  124.2 0.6 shard_map.108
  124.9 1.1 collective-permute-start.24
  126.1 0.6 shard_map.101
  126.8 1.0 collective-permute-start.14
  127.8 8.2 %collective-permute-done.20.moved_ref = bf16[64,3584]{1,0:T(8,128)(2,1)S(1)} collective-permute-done((bf16[64,3584]{1,0:T(8,128)(2,1)S(1)}, bf16[64,3584]{1,0:T(8,128)(2,1)S(1)}, u32[]{:S(2)}, u32[]{:S(2)}) %collective-permute-start.20) | collective-permute-done | bytes 458784 | tf_op jit(solution)/shard_map/ppermute | solution.py:94
  135.9 0.6 shard_map.106
  136.6 1.0 collective-permute-start.21
  137.6 0.6 shard_map.104
  138.3 1.1 collective-permute-start.18
  139.4 4.5 %collective-permute-done.24.moved_ref = bf16[64,3584]{1,0:T(8,128)(2,1)S(1)} collective-permute-done((bf16[64,3584]{1,0:T(8,128)(2,1)S(1)}, bf16[64,3584]{1,0:T(8,128)(2,1)S(1)}, u32[]{:S(2)}, u32[]{:S(2)}) %collective-permute-start.24) | collective-permute-done | bytes 458784 | tf_op jit(solution)/shard_map/ppermute | solution.py:94
  143.9 0.6 shard_map.109
  144.5 1.1 collective-permute-start.25
  145.6 0.2 collective-permute-done.14.moved_ref
  145.8 0.6 shard_map.102
  146.4 1.0 collective-permute-start.15
  147.4 8.1 %collective-permute-done.21.refs_4_ = bf16[64,3584]{1,0:T(8,128)(2,1)S(1)} collective-permute-done((bf16[64,3584]{1,0:T(8,128)(2,1)S(1)}, bf16[64,3584]{1,0:T(8,128)(2,1)S(1)}, u32[]{:S(2)}, u32[]{:S(2)}) %collective-permute-start.21) | collective-permute-done | bytes 458784 | tf_op jit(solution)/shard_map/ppermute | solution.py:94
  155.6 4.3 %collective-permute-done.25.refs_5_ = bf16[64,3584]{1,0:T(8,128)(2,1)S(1)} collective-permute-done((bf16[64,3584]{1,0:T(8,128)(2,1)S(1)}, bf16[64,3584]{1,0:T(8,128)(2,1)S(1)}, u32[]{:S(2)}, u32[]{:S(2)}) %collective-permute-start.25) | collective-permute-done | bytes 458784 | tf_op jit(solution)/shard_map/ppermute | solution.py:94
  159.9 0.6 collective-permute-done.15.refs_2_
  160.5 1.7 %shard_map.110 = bf16[64,7168]{1,0:T(8,128)(2,1)} custom-call(s32[9]{0:T(128)S(1)} %dynamic-slice_bitcast_fusion.1.where_ref, bf16[64,7168]{1,0:T(8,128)(2,1)S(1)} %shard_map.97.stream_ref, bf16[512,3584]{1,0:T(8,128)(2,1)S(1)} %shard_map.98.table_ref.refs_0_, bf16[512,3584]{1,0:T(8,128)(2,1)S(1)} %shard_map.99.table_ref.refs_1_, ...), custom_call_target="tpu_custom_call" | custom-call | flops 1376256 | bytes 4587520 | tf_op jit(solution)/shard_map/pallas_call | solution.py:462
  (22 shorter events, 0.7 us)
Async XLA Ops:
  0.0 5.4 %copy-start.1 = (s32[64,2]{0,1:T(2,128)S(1)}, s32[64,2]{0,1:T(2,128)}, u32[]{:S(2)}) copy-start(s32[64,2]{0,1:T(2,128)} %param.12) | copy-start | bytes 1540
  0.0 5.5 %copy-start.2 = (f32[64,2]{0,1:T(2,128)S(1)}, f32[64,2]{0,1:T(2,128)}, u32[]{:S(2)}) copy-start(f32[64,2]{0,1:T(2,128)} %param.13) | copy-start | bytes 1540
  0.0 55.3 %copy-start = (f32[7168]{0:T(1024)S(1)}, f32[7168]{0:T(1024)}, u32[]{:S(2)}) copy-start(f32[7168]{0:T(1024)} %param.11) | copy-start | bytes 86020
  2.4 2.1 %collective-permute-start = (bf16[8,64,448]{2,1,0:T(8,128)(2,1)S(1)}, bf16[8,64,448]{2,1,0:T(8,128)(2,1)S(1)}, u32[]{:S(2)}, u32[]{:S(2)}) collective-permute-start(bf16[8,64,448]{2,1,0:T(8,128)(2,1)S(1)} %dynamic-slice_bitcast_fusion), channel_id=1, source_target_pairs={{0,1},{1,0},{2,3},{3,2},{4,5},{5,4},{6,7},{7,6},{8,9},{9,8},{10,11... | collective-permute-start | bytes 1376264 | tf_op jit(solution)/shard_map/ppermute | solution.py:84
  4.5 50.8 %collective-permute-start.1 = (bf16[7168,256]{1,0:T(8,128)(2,1)}, bf16[7168,256]{1,0:T(8,128)(2,1)}, u32[]{:S(2)}, u32[]{:S(2)}) collective-permute-start(bf16[7168,256]{1,0:T(8,128)(2,1)} %refs_3_.3), channel_id=1, source_target_pairs={{0,1},{1,0},{2,3},{3,2},{4,5},{5,4},{6,7},{7,6},{8,9},{9,8},{10,11... | collective-permute-start | bytes 11010056 | tf_op jit(solution)/shard_map/ppermute | solution.py:84
  4.9 50.4 %collective-permute-start.2 = (bf16[7168,256]{1,0:T(8,128)(2,1)}, bf16[7168,256]{1,0:T(8,128)(2,1)}, u32[]{:S(2)}, u32[]{:S(2)}) collective-permute-start(bf16[7168,256]{1,0:T(8,128)(2,1)} %refs_4_.2), channel_id=1, source_target_pairs={{0,1},{1,0},{2,3},{3,2},{4,5},{5,4},{6,7},{7,6},{8,9},{9,8},{10,11... | collective-permute-start | bytes 11010056 | tf_op jit(solution)/shard_map/ppermute | solution.py:84
  5.0 73.5 %collective-permute-start.9 = (bf16[256,7168]{1,0:T(8,128)(2,1)}, bf16[256,7168]{1,0:T(8,128)(2,1)}, u32[]{:S(2)}, u32[]{:S(2)}) collective-permute-start(bf16[256,7168]{1,0:T(8,128)(2,1)} %refs_8_), channel_id=1, source_target_pairs={{0,1},{1,0},{2,3},{3,2},{4,5},{5,4},{6,7},{7,6},{8,9},{9,8},{10,11... | collective-permute-start | bytes 11010056 | tf_op jit(solution)/shard_map/ppermute | solution.py:84
  6.3 24.2 %collective-permute-start.4 = (bf16[528,896]{1,0:T(8,128)(2,1)S(1)}, bf16[528,896]{1,0:T(8,128)(2,1)S(1)}, u32[]{:S(2)}, u32[]{:S(2)}) collective-permute-start(bf16[528,896]{1,0:T(8,128)(2,1)S(1)} %shard_map.91.refs_0_.refs_5_), channel_id=1, source_target_pairs={{0,4},{1,5},{4,8},{5,9},{8,12},{9,13},{12,14},{13,15},{14,10},{15,... | collective-permute-start | bytes 2838536 | tf_op jit(solution)/shard_map/ppermute | solution.py:94
  9.1 23.2 %collective-permute-start.3 = (bf16[528,896]{1,0:T(8,128)(2,1)S(1)}, bf16[528,896]{1,0:T(8,128)(2,1)S(1)}, u32[]{:S(2)}, u32[]{:S(2)}) collective-permute-start(bf16[528,896]{1,0:T(8,128)(2,1)S(1)} %shard_map.91.refs_0_.refs_5_), channel_id=1, source_target_pairs={{0,2},{1,3},{4,0},{5,1},{8,4},{9,5},{12,8},{13,9},{14,12},{15,13},... | collective-permute-start | bytes 2838536 | tf_op jit(solution)/shard_map/ppermute | solution.py:94
  30.5 22.8 %collective-permute-start.6 = (bf16[528,896]{1,0:T(8,128)(2,1)S(1)}, bf16[528,896]{1,0:T(8,128)(2,1)}, u32[]{:S(2)}, u32[]{:S(2)}) collective-permute-start(bf16[528,896]{1,0:T(8,128)(2,1)S(1)} %collective-permute-done.4.refs_1_.refs_12_), channel_id=1, source_target_pairs={{0,4},{1,5},{4,8},{5,9},{8,12},{9,13},{12,14},{13,15},{14,10},{15,... | collective-permute-start | bytes 2838536 | tf_op jit(solution)/shard_map/ppermute | solution.py:94
  32.3 22.5 %collective-permute-start.5 = (bf16[528,896]{1,0:T(8,128)(2,1)S(1)}, bf16[528,896]{1,0:T(8,128)(2,1)}, u32[]{:S(2)}, u32[]{:S(2)}) collective-permute-start(bf16[528,896]{1,0:T(8,128)(2,1)S(1)} %collective-permute-done.3.refs_0_.refs_6_), channel_id=1, source_target_pairs={{0,2},{1,3},{4,0},{5,1},{8,4},{9,5},{12,8},{13,9},{14,12},{15,13},... | collective-permute-start | bytes 2838536 | tf_op jit(solution)/shard_map/ppermute | solution.py:94
  53.3 22.0 %collective-permute-start.8 = (bf16[528,896]{1,0:T(8,128)(2,1)}, bf16[528,896]{1,0:T(8,128)(2,1)S(1)}, u32[]{:S(2)}, u32[]{:S(2)}) collective-permute-start(bf16[528,896]{1,0:T(8,128)(2,1)} %collective-permute-done.6.refs_1_.refs_11_), channel_id=1, source_target_pairs={{0,4},{1,5},{4,8},{5,9},{8,12},{9,13},{12,14},{13,15},{14,10},{15,... | collective-permute-start | bytes 2838536 | tf_op jit(solution)/shard_map/ppermute | solution.py:94
  54.8 21.4 %collective-permute-start.7 = (bf16[528,896]{1,0:T(8,128)(2,1)}, bf16[528,896]{1,0:T(8,128)(2,1)S(1)}, u32[]{:S(2)}, u32[]{:S(2)}) collective-permute-start(bf16[528,896]{1,0:T(8,128)(2,1)} %collective-permute-done.5.refs_0_.refs_7_), channel_id=1, source_target_pairs={{0,2},{1,3},{4,0},{5,1},{8,4},{9,5},{12,8},{13,9},{14,12},{15,13},... | collective-permute-start | bytes 2838536 | tf_op jit(solution)/shard_map/ppermute | solution.py:94
  76.3 9.9 %collective-permute-start.11 = (bf16[256,896]{1,0:T(8,128)(2,1)S(1)}, bf16[256,896]{1,0:T(8,128)(2,1)S(1)}, u32[]{:S(2)}, u32[]{:S(2)}) collective-permute-start(bf16[256,896]{1,0:T(8,128)(2,1)S(1)} %slice.7), channel_id=1, source_target_pairs={{0,2},{1,3},{4,0},{5,1},{8,4},{9,5},{12,8},{13,9},{14,12},{15,13},... | collective-permute-start | bytes 1376264 | tf_op jit(solution)/shard_map/ppermute | solution.py:94
  77.2 10.5 %collective-permute-start.10 = (bf16[272,896]{1,0:T(8,128)(2,1)S(1)}, bf16[272,896]{1,0:T(8,128)(2,1)S(1)}, u32[]{:S(2)}, u32[]{:S(2)}) collective-permute-start(bf16[272,896]{1,0:T(8,128)(2,1)S(1)} %slice.6), channel_id=1, source_target_pairs={{0,4},{1,5},{4,8},{5,9},{8,12},{9,13},{12,14},{13,15},{14,10},{15,... | collective-permute-start | bytes 1462280 | tf_op jit(solution)/shard_map/ppermute | solution.py:94
  91.9 10.9 %collective-permute-start.22 = (bf16[64,3584]{1,0:T(8,128)(2,1)S(1)}, bf16[64,3584]{1,0:T(8,128)(2,1)S(1)}, u32[]{:S(2)}, u32[]{:S(2)}) collective-permute-start(bf16[64,3584]{1,0:T(8,128)(2,1)S(1)} %get-tuple-element.60), channel_id=1, source_target_pairs={{0,2},{1,3},{4,0},{5,1},{8,4},{9,5},{12,8},{13,9},{14,12},{15,13},... | collective-permute-start | bytes 1376264 | tf_op jit(solution)/shard_map/ppermute | solution.py:94
  93.0 13.5 %collective-permute-start.12 = (bf16[64,3584]{1,0:T(8,128)(2,1)S(1)}, bf16[64,3584]{1,0:T(8,128)(2,1)S(1)}, u32[]{:S(2)}, u32[]{:S(2)}) collective-permute-start(bf16[64,3584]{1,0:T(8,128)(2,1)S(1)} %get-tuple-element.57), channel_id=1, source_target_pairs={{0,4},{1,5},{4,8},{5,9},{8,12},{9,13},{12,14},{13,15},{14,10},{15,... | collective-permute-start | bytes 1376264 | tf_op jit(solution)/shard_map/ppermute | solution.py:94
  94.6 21.7 %collective-permute-start.19 = (bf16[64,3584]{1,0:T(8,128)(2,1)S(1)}, bf16[64,3584]{1,0:T(8,128)(2,1)S(1)}, u32[]{:S(2)}, u32[]{:S(2)}) collective-permute-start(bf16[64,3584]{1,0:T(8,128)(2,1)S(1)} %get-tuple-element.59), channel_id=1, source_target_pairs={{0,4},{1,5},{4,8},{5,9},{8,12},{9,13},{12,14},{13,15},{14,10},{15,... | collective-permute-start | bytes 1376264 | tf_op jit(solution)/shard_map/ppermute | solution.py:94
  100.9 17.1 %collective-permute-start.16 = (bf16[64,3584]{1,0:T(8,128)(2,1)S(1)}, bf16[64,3584]{1,0:T(8,128)(2,1)S(1)}, u32[]{:S(2)}, u32[]{:S(2)}) collective-permute-start(bf16[64,3584]{1,0:T(8,128)(2,1)S(1)} %get-tuple-element.58), channel_id=1, source_target_pairs={{0,2},{1,3},{4,0},{5,1},{8,4},{9,5},{12,8},{13,9},{14,12},{15,13},... | collective-permute-start | bytes 1376264 | tf_op jit(solution)/shard_map/ppermute | solution.py:94
  103.4 20.8 %collective-permute-start.23 = (bf16[64,3584]{1,0:T(8,128)(2,1)S(1)}, bf16[64,3584]{1,0:T(8,128)(2,1)S(1)}, u32[]{:S(2)}, u32[]{:S(2)}) collective-permute-start(bf16[64,3584]{1,0:T(8,128)(2,1)S(1)} %shard_map.107), channel_id=1, source_target_pairs={{0,2},{1,3},{4,0},{5,1},{8,4},{9,5},{12,8},{13,9},{14,12},{15,13},... | collective-permute-start | bytes 1376264 | tf_op jit(solution)/shard_map/ppermute | solution.py:94
  107.1 19.0 %collective-permute-start.13 = (bf16[64,3584]{1,0:T(8,128)(2,1)S(1)}, bf16[64,3584]{1,0:T(8,128)(2,1)S(1)}, u32[]{:S(2)}, u32[]{:S(2)}) collective-permute-start(bf16[64,3584]{1,0:T(8,128)(2,1)S(1)} %shard_map.100), channel_id=1, source_target_pairs={{0,4},{1,5},{4,8},{5,9},{8,12},{9,13},{12,14},{13,15},{14,10},{15,... | collective-permute-start | bytes 1376264 | tf_op jit(solution)/shard_map/ppermute | solution.py:94
  116.9 19.0 %collective-permute-start.20 = (bf16[64,3584]{1,0:T(8,128)(2,1)S(1)}, bf16[64,3584]{1,0:T(8,128)(2,1)S(1)}, u32[]{:S(2)}, u32[]{:S(2)}) collective-permute-start(bf16[64,3584]{1,0:T(8,128)(2,1)S(1)} %shard_map.105), channel_id=1, source_target_pairs={{0,4},{1,5},{4,8},{5,9},{8,12},{9,13},{12,14},{13,15},{14,10},{15,... | collective-permute-start | bytes 1376264 | tf_op jit(solution)/shard_map/ppermute | solution.py:94
  118.6 19.0 %collective-permute-start.17 = (bf16[64,3584]{1,0:T(8,128)(2,1)S(1)}, bf16[64,3584]{1,0:T(8,128)(2,1)S(1)}, u32[]{:S(2)}, u32[]{:S(2)}) collective-permute-start(bf16[64,3584]{1,0:T(8,128)(2,1)S(1)} %shard_map.103), channel_id=1, source_target_pairs={{0,2},{1,3},{4,0},{5,1},{8,4},{9,5},{12,8},{13,9},{14,12},{15,13},... | collective-permute-start | bytes 1376264 | tf_op jit(solution)/shard_map/ppermute | solution.py:94
  124.9 19.0 %collective-permute-start.24 = (bf16[64,3584]{1,0:T(8,128)(2,1)S(1)}, bf16[64,3584]{1,0:T(8,128)(2,1)S(1)}, u32[]{:S(2)}, u32[]{:S(2)}) collective-permute-start(bf16[64,3584]{1,0:T(8,128)(2,1)S(1)} %shard_map.108), channel_id=1, source_target_pairs={{0,2},{1,3},{4,0},{5,1},{8,4},{9,5},{12,8},{13,9},{14,12},{15,13},... | collective-permute-start | bytes 1376264 | tf_op jit(solution)/shard_map/ppermute | solution.py:94
  126.8 19.0 %collective-permute-start.14 = (bf16[64,3584]{1,0:T(8,128)(2,1)S(1)}, bf16[64,3584]{1,0:T(8,128)(2,1)S(1)}, u32[]{:S(2)}, u32[]{:S(2)}) collective-permute-start(bf16[64,3584]{1,0:T(8,128)(2,1)S(1)} %shard_map.101), channel_id=1, source_target_pairs={{0,4},{1,5},{4,8},{5,9},{8,12},{9,13},{12,14},{13,15},{14,10},{15,... | collective-permute-start | bytes 1376264 | tf_op jit(solution)/shard_map/ppermute | solution.py:94
  136.6 19.0 %collective-permute-start.21 = (bf16[64,3584]{1,0:T(8,128)(2,1)S(1)}, bf16[64,3584]{1,0:T(8,128)(2,1)S(1)}, u32[]{:S(2)}, u32[]{:S(2)}) collective-permute-start(bf16[64,3584]{1,0:T(8,128)(2,1)S(1)} %shard_map.106), channel_id=1, source_target_pairs={{0,4},{1,5},{4,8},{5,9},{8,12},{9,13},{12,14},{13,15},{14,10},{15,... | collective-permute-start | bytes 1376264 | tf_op jit(solution)/shard_map/ppermute | solution.py:94
  138.3 17.3 %collective-permute-start.18 = (bf16[64,3584]{1,0:T(8,128)(2,1)S(1)}, bf16[64,3584]{1,0:T(8,128)(2,1)S(1)}, u32[]{:S(2)}, u32[]{:S(2)}) collective-permute-start(bf16[64,3584]{1,0:T(8,128)(2,1)S(1)} %shard_map.104), channel_id=1, source_target_pairs={{0,2},{1,3},{4,0},{5,1},{8,4},{9,5},{12,8},{13,9},{14,12},{15,13},... | collective-permute-start | bytes 1376264 | tf_op jit(solution)/shard_map/ppermute | solution.py:94
  144.5 15.3 %collective-permute-start.25 = (bf16[64,3584]{1,0:T(8,128)(2,1)S(1)}, bf16[64,3584]{1,0:T(8,128)(2,1)S(1)}, u32[]{:S(2)}, u32[]{:S(2)}) collective-permute-start(bf16[64,3584]{1,0:T(8,128)(2,1)S(1)} %shard_map.109), channel_id=1, source_target_pairs={{0,2},{1,3},{4,0},{5,1},{8,4},{9,5},{12,8},{13,9},{14,12},{15,13},... | collective-permute-start | bytes 1376264 | tf_op jit(solution)/shard_map/ppermute | solution.py:94
  146.4 14.0 %collective-permute-start.15 = (bf16[64,3584]{1,0:T(8,128)(2,1)S(1)}, bf16[64,3584]{1,0:T(8,128)(2,1)S(1)}, u32[]{:S(2)}, u32[]{:S(2)}) collective-permute-start(bf16[64,3584]{1,0:T(8,128)(2,1)S(1)} %shard_map.102), channel_id=1, source_target_pairs={{0,4},{1,5},{4,8},{5,9},{8,12},{9,13},{12,14},{13,15},{14,10},{15,... | collective-permute-start | bytes 1376264 | tf_op jit(solution)/shard_map/ppermute | solution.py:94

commit v14 on v12

--- a/solution.py
+++ b/solution.py
@@ -474,11 +474,11 @@
     by_core = stream_feat.reshape(chips, 2, tok_here, feat_here)
     swapped = swap_cores(lax.dynamic_index_in_dim(by_core, 1 - core, 1, keepdims=False))
 
-    swapped, w_gate, w_up = lax.optimization_barrier((swapped, w_gate, w_up))
+    blocks = {0: first_blocks(by_core, swapped, expert_routes, route_gain, experts)}
+
+    blocks[0], w_gate, w_up, w_down = lax.optimization_barrier((blocks[0], w_gate, w_up, w_down))
     tables = [pltpu.with_memory_space_constraint(table, pltpu.HBM) for table in (w_gate, w_up)]
     tables += [swap_cores(w_gate), swap_cores(w_up)]
-    blocks = {0: first_blocks(by_core, swapped, expert_routes, route_gain, experts)}
-    w_down = lax.optimization_barrier((swapped, w_down))[1]
     down = [pltpu.with_memory_space_constraint(w_down, pltpu.HBM), swap_cores(w_down)]
 
     for distance in range(1, far):
@@ -502,11 +502,11 @@
         owns.extend(made)
         positions.extend(group)
         if group == groups[max(far - 2, 0)]:
-            lower, upper, carried = lax.optimization_barrier(
-                (blocks[1 - far], blocks[far - 1], carried)
-            )
+            lower, carried = lax.optimization_barrier((blocks[1 - far], carried))
             cut = lower.shape[0] - far * tok_here
-            blocks[far] = [ring_shift(lower[:cut], ring, 1), ring_shift(upper[cut:], ring, -1)]
+            blocks[far] = [ring_shift(lower[:cut], ring, 1)]
+            upper, carried = lax.optimization_barrier((blocks[far - 1], carried))
+            blocks[far].append(ring_shift(upper[cut:], ring, -1))
         if group == groups[-2]:
             tables, down, ahead = [rest[0]], rest[1], None
 
@@ -514,7 +514,6 @@
     moving = {1: [ring_shift(lower, ring, 1), None], -1: [None, ring_shift(upper, ring, -1)]}
     second = {1: ring_shift(after, ring, 1), -1: ring_shift(before, ring, -1)}
     stream_rows = collect(where, positions, owns)
-    stream_rows, hidden = lax.optimization_barrier((stream_rows, hidden))
     everything = [contribution(where, hidden, down, part) for part in range(2)]
     for distance in range(far - 1, 0, -1):
         for sign, order in ((1, (1, 0)), (-1, (0, 1))):

time: 163 us -> 162 us (level)
  transfers between devices with their start and end apart: 26 -> 26, of which waited for: 18 -> 18; matrix products, arithmetic and copies ran while one was open for 1% -> 1% of each run, Pallas kernels for 24% -> 23%
where the time goes in v14:
time: 162 us
  waiting for transfers between devices  89.3 us (55%)
  Pallas kernels  44.8 us (28%)
  starting transfers between devices  24.5 us (15%)
  other arithmetic  1.82 us (1%)
    ppermute x22, waiting for transfers between devices, ring_shift(): return lax.ppermute(value, 'ep', pairs)  88 us
    pallas_call x20, Pallas kernels, local_call(): pl.pallas_call(kernel, out_shape=out_shape, in_specs=[IN_SMEM if value.nd...  44.8 us
    ppermute x22, starting transfers between devices, ring_shift(): return lax.ppermute(value, 'ep', pairs)  23 us
  transfers between devices with their start and end apart: 26, of which 18 were waited for; matrix products, arithmetic and copies ran while one was open for 1% of the time, Pallas kernels for 23%

profile of v14, /device:TPU:0, one launch (start us, length us, event | category | flops | bytes accessed | tf_op | source)
XLA Modules:
  0.0 162.1 jit_solution(14723960257687626776)
XLA Ops:
  0.0 1.8 %add_convert_fusion = bf16[1024,448]{0,1:T(8,128)(2,1)S(1)} fusion(bf16[1024,448]{0,1:T(8,128)(2,1)} %param.10, bf16[1024,448]{0,1:T(8,128)(2,1)} %param.9), kind=kLoop, calls=%fused_computation | loop fusion | flops 1835008 | bytes 2752512 | tf_op jit(solution)/shard_map/convert_element_type | solution.py:473
  1.8 0.5 copy.13
  2.4 0.5 collective-permute-start
  3.1 1.3 collective-permute-done.swapped_ref
  4.5 0.7 shard_map.91.refs_0_.refs_5_
  5.2 0.4 collective-permute-start.1
  5.8 0.4 collective-permute-start.9
  6.2 2.7 %collective-permute-start.4 = (bf16[528,896]{1,0:T(8,128)(2,1)S(1)}, bf16[528,896]{1,0:T(8,128)(2,1)S(1)}, u32[]{:S(2)}, u32[]{:S(2)}) collective-permute-start(bf16[528,896]{1,0:T(8,128)(2,1)S(1)} %shard_map.91.refs_0_.refs_5_), channel_id=1, source_target_pairs={{0,4},{1,5},{4,8},{5,9},{8,12},{9,13},{12,14},{13,15},{14,10},{15,... | collective-permute-start | bytes 2838536 | tf_op jit(solution)/shard_map/ppermute | solution.py:94
  8.9 21.4 %collective-permute-done.4.refs_1_.refs_12_ = bf16[528,896]{1,0:T(8,128)(2,1)S(1)} collective-permute-done((bf16[528,896]{1,0:T(8,128)(2,1)S(1)}, bf16[528,896]{1,0:T(8,128)(2,1)S(1)}, u32[]{:S(2)}, u32[]{:S(2)}) %collective-permute-start.4) | collective-permute-done | bytes 946208 | tf_op jit(solution)/shard_map/ppermute | solution.py:94
  30.3 1.8 %collective-permute-start.6 = (bf16[528,896]{1,0:T(8,128)(2,1)S(1)}, bf16[528,896]{1,0:T(8,128)(2,1)}, u32[]{:S(2)}, u32[]{:S(2)}) collective-permute-start(bf16[528,896]{1,0:T(8,128)(2,1)S(1)} %collective-permute-done.4.refs_1_.refs_12_), channel_id=1, source_target_pairs={{0,4},{1,5},{4,8},{5,9},{8,12},{9,13},{12,14},{13,15},{14,10},{15,... | collective-permute-start | bytes 2838536 | tf_op jit(solution)/shard_map/ppermute | solution.py:94
  32.3 0.7 dynamic-slice_bitcast_fusion.1.where_ref
  33.0 20.1 %collective-permute-done.6.refs_1_.refs_11_ = bf16[528,896]{1,0:T(8,128)(2,1)} collective-permute-done((bf16[528,896]{1,0:T(8,128)(2,1)S(1)}, bf16[528,896]{1,0:T(8,128)(2,1)}, u32[]{:S(2)}, u32[]{:S(2)}) %collective-permute-start.6) | collective-permute-done | bytes 946208 | tf_op jit(solution)/shard_map/ppermute | solution.py:94
  53.1 1.6 collective-permute-start.8
  54.6 0.5 collective-permute-start.7
  55.1 4.4 %shard_map.92 = (bf16[64,896]{1,0:T(8,128)(2,1)S(1)}, f32[512,1024]{1,0:T(8,128)S(1)}) custom-call(s32[9]{0:T(128)S(1)} %dynamic-slice_bitcast_fusion.1.where_ref, bf16[528,896]{1,0:T(8,128)(2,1)S(1)} %shard_map.91.refs_0_.refs_5_, f32[8,1,896]{2,1,0:T(1,128)S(1)} %bitcast.8, bf16[7168,256]{1,0:T(8,128)(2,1)} %refs_3_.3, bf16[7168,256]{1,0:T(8,128)(2,1)} %refs_4_.2, ...), custom_call_target="tpu_custom_call" | custom-call | flops 2818572288 | bytes 6946816 | tf_op jit(solution)/shard_map/pallas_call | solution.py:107
  59.5 6.8 %shard_map.93 = (bf16[64,896]{1,0:T(8,128)(2,1)S(1)}, bf16[64,896]{1,0:T(8,128)(2,1)S(1)}, f32[512,1024]{1,0:T(8,128)S(1)}) custom-call(s32[9]{0:T(128)S(1)} %dynamic-slice_bitcast_fusion.1.where_ref, bf16[528,896]{1,0:T(8,128)(2,1)S(1)} %collective-permute-done.3.refs_0_.refs_6_, ...), custom_call_target="tpu_custom_call", output_to_operand_aliasing={{2}: (8, {})} | custom-call | flops 5637144576 | bytes 9699328 | tf_op jit(solution)/shard_map/pallas_call | solution.py:107
  66.3 7.7 %shard_map.94 = (bf16[64,896]{1,0:T(8,128)(2,1)S(1)}, bf16[64,896]{1,0:T(8,128)(2,1)S(1)}, f32[512,1024]{1,0:T(8,128)S(1)}) custom-call(s32[9]{0:T(128)S(1)} %dynamic-slice_bitcast_fusion.1.where_ref, bf16[528,896]{1,0:T(8,128)(2,1)} %collective-permute-done.5.refs_0_.refs_7_, ...), custom_call_target="tpu_custom_call", output_to_operand_aliasing={{2}: (8, {})} | custom-call | flops 5637144576 | bytes 9699328 | tf_op jit(solution)/shard_map/pallas_call | solution.py:107
  74.1 1.0 collective-permute-done.8.refs_1_.refs_10_
  75.1 1.0 collective-permute-done.7.refs_0_.refs_8_
  76.1 0.8 collective-permute-start.11
  77.0 1.3 collective-permute-start.10
  78.3 6.8 %shard_map.95 = (bf16[64,896]{1,0:T(8,128)(2,1)S(1)}, bf16[64,896]{1,0:T(8,128)(2,1)S(1)}, f32[512,1024]{1,0:T(8,128)S(1)}, bf16[4,896,256]{2,1,0:T(8,128)(2,1)S(1)}, bf16[512,7168]{1,0:T(8,128)(2,1)S(1)}) custom-call(s32[9]{0:T(128)S(1)} %dynamic-slice_bitcast_fusion.1.where_ref, ...), custom_call_target="tpu_custom_call", output_to_operand_aliasing={{2}: (8, {})} | custom-call | flops 5637144576 | bytes 9699328 | tf_op jit(solution)/shard_map/pallas_call | solution.py:107
  85.1 1.0 collective-permute-done.11.refs_1_
  86.0 1.4 collective-permute-done.10.refs_0_.refs_9_
  87.5 4.1 %shard_map.96 = (bf16[64,896]{1,0:T(8,128)(2,1)S(1)}, bf16[512,512]{1,0:T(8,128)(2,1)S(1)}, bf16[64,3584]{1,0:T(8,128)(2,1)S(1)}, bf16[64,3584]{1,0:T(8,128)(2,1...) custom-call(s32[9]{0:T(128)S(1)} %dynamic-slice_bitcast_fusion.1.where_ref, ...), custom_call_target="tpu_custom_call" | custom-call | flops 2818572288 | bytes 6946816 | tf_op jit(solution)/shard_map/pallas_call | solution.py:107
  91.6 1.1 collective-permute-start.22
  92.7 1.0 collective-permute-start.12
  93.7 1.0 collective-permute-start.19
  94.7 2.6 %shard_map.99.table_ref.refs_1_ = bf16[512,3584]{1,0:T(8,128)(2,1)S(1)} custom-call(s32[9]{0:T(128)S(1)} %dynamic-slice_bitcast_fusion.1.where_ref, bf16[512,512]{1,0:T(8,128)(2,1)S(1)} %get-tuple-element.54.hidden_ref, bf16[512,7168]{1,0:T(8,128)(2,1)S(1)} %get-tuple-element.52.refs_13_.down_ref), custom_call_target="tpu_custom_call" | custom-call | flops 1879048192 | bytes 7340032 | tf_op jit(solution)/shard_map/pallas_call | solution.py:107
  97.3 2.6 %shard_map.98.table_ref.refs_0_ = bf16[512,3584]{1,0:T(8,128)(2,1)S(1)} custom-call(s32[9]{0:T(128)S(1)} %dynamic-slice_bitcast_fusion.1.where_ref, bf16[512,512]{1,0:T(8,128)(2,1)S(1)} %get-tuple-element.54.hidden_ref, bf16[512,7168]{1,0:T(8,128)(2,1)S(1)} %get-tuple-element.52.refs_13_.down_ref), custom_call_target="tpu_custom_call" | custom-call | flops 1879048192 | bytes 7340032 | tf_op jit(solution)/shard_map/pallas_call | solution.py:107
  100.0 1.1 collective-permute-start.16
  101.0 2.2 %collective-permute-done.22.moved_ref = bf16[64,3584]{1,0:T(8,128)(2,1)S(1)} collective-permute-done((bf16[64,3584]{1,0:T(8,128)(2,1)S(1)}, bf16[64,3584]{1,0:T(8,128)(2,1)S(1)}, u32[]{:S(2)}, u32[]{:S(2)}) %collective-permute-start.22) | collective-permute-done | bytes 458784 | tf_op jit(solution)/shard_map/ppermute | solution.py:94
  103.2 0.6 shard_map.107
  103.8 0.6 collective-permute-start.23
  104.4 1.8 %collective-permute-done.12.moved_ref = bf16[64,3584]{1,0:T(8,128)(2,1)S(1)} collective-permute-done((bf16[64,3584]{1,0:T(8,128)(2,1)S(1)}, bf16[64,3584]{1,0:T(8,128)(2,1)S(1)}, u32[]{:S(2)}, u32[]{:S(2)}) %collective-permute-start.12) | collective-permute-done | bytes 458784 | tf_op jit(solution)/shard_map/ppermute | solution.py:94
  106.2 0.6 shard_map.100
  106.9 1.0 collective-permute-start.13
  107.9 8.2 %collective-permute-done.19.moved_ref = bf16[64,3584]{1,0:T(8,128)(2,1)S(1)} collective-permute-done((bf16[64,3584]{1,0:T(8,128)(2,1)S(1)}, bf16[64,3584]{1,0:T(8,128)(2,1)S(1)}, u32[]{:S(2)}, u32[]{:S(2)}) %collective-permute-start.19) | collective-permute-done | bytes 458784 | tf_op jit(solution)/shard_map/ppermute | solution.py:94
  116.0 0.6 shard_map.105
  116.7 1.0 collective-permute-start.20
  117.7 0.6 shard_map.103
  118.4 1.1 collective-permute-start.17
  119.5 3.8 %collective-permute-done.23.moved_ref = bf16[64,3584]{1,0:T(8,128)(2,1)S(1)} collective-permute-done((bf16[64,3584]{1,0:T(8,128)(2,1)S(1)}, bf16[64,3584]{1,0:T(8,128)(2,1)S(1)}, u32[]{:S(2)}, u32[]{:S(2)}) %collective-permute-start.23) | collective-permute-done | bytes 458784 | tf_op jit(solution)/shard_map/ppermute | solution.py:94
  123.3 0.6 shard_map.108
  124.0 1.1 collective-permute-start.24
  125.0 0.8 collective-permute-done.13.moved_ref
  125.9 0.6 shard_map.101
  126.5 1.0 collective-permute-start.14
  127.5 8.2 %collective-permute-done.20.moved_ref = bf16[64,3584]{1,0:T(8,128)(2,1)S(1)} collective-permute-done((bf16[64,3584]{1,0:T(8,128)(2,1)S(1)}, bf16[64,3584]{1,0:T(8,128)(2,1)S(1)}, u32[]{:S(2)}, u32[]{:S(2)}) %collective-permute-start.20) | collective-permute-done | bytes 458784 | tf_op jit(solution)/shard_map/ppermute | solution.py:94
  135.7 0.6 shard_map.106
  136.4 1.0 collective-permute-start.21
  137.4 0.6 shard_map.104
  138.0 1.1 collective-permute-start.18
  139.1 3.8 %collective-permute-done.24.moved_ref = bf16[64,3584]{1,0:T(8,128)(2,1)S(1)} collective-permute-done((bf16[64,3584]{1,0:T(8,128)(2,1)S(1)}, bf16[64,3584]{1,0:T(8,128)(2,1)S(1)}, u32[]{:S(2)}, u32[]{:S(2)}) %collective-permute-start.24) | collective-permute-done | bytes 458784 | tf_op jit(solution)/shard_map/ppermute | solution.py:94
  143.0 0.6 shard_map.109
  143.6 1.1 collective-permute-start.25
  144.7 0.8 collective-permute-done.14.moved_ref
  145.5 0.6 shard_map.102
  146.2 1.0 collective-permute-start.15
  147.2 0.6 shard_map.97.stream_ref
  147.8 7.5 %collective-permute-done.21.refs_4_ = bf16[64,3584]{1,0:T(8,128)(2,1)S(1)} collective-permute-done((bf16[64,3584]{1,0:T(8,128)(2,1)S(1)}, bf16[64,3584]{1,0:T(8,128)(2,1)S(1)}, u32[]{:S(2)}, u32[]{:S(2)}) %collective-permute-start.21) | collective-permute-done | bytes 458784 | tf_op jit(solution)/shard_map/ppermute | solution.py:94
  155.3 4.3 %collective-permute-done.25.refs_5_ = bf16[64,3584]{1,0:T(8,128)(2,1)S(1)} collective-permute-done((bf16[64,3584]{1,0:T(8,128)(2,1)S(1)}, bf16[64,3584]{1,0:T(8,128)(2,1)S(1)}, u32[]{:S(2)}, u32[]{:S(2)}) %collective-permute-start.25) | collective-permute-done | bytes 458784 | tf_op jit(solution)/shard_map/ppermute | solution.py:94
  159.6 0.6 collective-permute-done.15.refs_2_
  160.2 1.9 %shard_map.110 = bf16[64,7168]{1,0:T(8,128)(2,1)} custom-call(s32[9]{0:T(128)S(1)} %dynamic-slice_bitcast_fusion.1.where_ref, bf16[64,7168]{1,0:T(8,128)(2,1)S(1)} %shard_map.97.stream_ref, bf16[512,3584]{1,0:T(8,128)(2,1)S(1)} %shard_map.98.table_ref.refs_0_, bf16[512,3584]{1,0:T(8,128)(2,1)S(1)} %shard_map.99.table_ref.refs_1_, ...), custom_call_target="tpu_custom_call" | custom-call | flops 1376256 | bytes 4587520 | tf_op jit(solution)/shard_map/pallas_call | solution.py:107
  (22 shorter events, 0.7 us)
Async XLA Ops:
  0.0 3.0 %copy-start.1 = (s32[64,2]{0,1:T(2,128)S(1)}, s32[64,2]{0,1:T(2,128)}, u32[]{:S(2)}) copy-start(s32[64,2]{0,1:T(2,128)} %param.12) | copy-start | bytes 1540
  0.0 3.0 %copy-start.2 = (f32[64,2]{0,1:T(2,128)S(1)}, f32[64,2]{0,1:T(2,128)}, u32[]{:S(2)}) copy-start(f32[64,2]{0,1:T(2,128)} %param.13) | copy-start | bytes 1540
  0.0 55.1 %copy-start = (f32[7168]{0:T(1024)S(1)}, f32[7168]{0:T(1024)}, u32[]{:S(2)}) copy-start(f32[7168]{0:T(1024)} %param.11) | copy-start | bytes 86020
  2.4 2.1 %collective-permute-start = (bf16[8,64,448]{2,1,0:T(8,128)(2,1)S(1)}, bf16[8,64,448]{2,1,0:T(8,128)(2,1)S(1)}, u32[]{:S(2)}, u32[]{:S(2)}) collective-permute-start(bf16[8,64,448]{2,1,0:T(8,128)(2,1)S(1)} %dynamic-slice_bitcast_fusion), channel_id=1, source_target_pairs={{0,1},{1,0},{2,3},{3,2},{4,5},{5,4},{6,7},{7,6},{8,9},{9,8},{10,11... | collective-permute-start | bytes 1376264 | tf_op jit(solution)/shard_map/ppermute | solution.py:84
  5.2 49.9 %collective-permute-start.1 = (bf16[7168,256]{1,0:T(8,128)(2,1)}, bf16[7168,256]{1,0:T(8,128)(2,1)}, u32[]{:S(2)}, u32[]{:S(2)}) collective-permute-start(bf16[7168,256]{1,0:T(8,128)(2,1)} %refs_3_.3), channel_id=1, source_target_pairs={{0,1},{1,0},{2,3},{3,2},{4,5},{5,4},{6,7},{7,6},{8,9},{9,8},{10,11... | collective-permute-start | bytes 11010056 | tf_op jit(solution)/shard_map/ppermute | solution.py:84
  5.6 49.5 %collective-permute-start.2 = (bf16[7168,256]{1,0:T(8,128)(2,1)}, bf16[7168,256]{1,0:T(8,128)(2,1)}, u32[]{:S(2)}, u32[]{:S(2)}) collective-permute-start(bf16[7168,256]{1,0:T(8,128)(2,1)} %refs_4_.2), channel_id=1, source_target_pairs={{0,1},{1,0},{2,3},{3,2},{4,5},{5,4},{6,7},{7,6},{8,9},{9,8},{10,11... | collective-permute-start | bytes 11010056 | tf_op jit(solution)/shard_map/ppermute | solution.py:84
  5.8 72.5 %collective-permute-start.9 = (bf16[256,7168]{1,0:T(8,128)(2,1)}, bf16[256,7168]{1,0:T(8,128)(2,1)}, u32[]{:S(2)}, u32[]{:S(2)}) collective-permute-start(bf16[256,7168]{1,0:T(8,128)(2,1)} %refs_8_), channel_id=1, source_target_pairs={{0,1},{1,0},{2,3},{3,2},{4,5},{5,4},{6,7},{7,6},{8,9},{9,8},{10,11... | collective-permute-start | bytes 11010056 | tf_op jit(solution)/shard_map/ppermute | solution.py:84
  6.2 24.2 %collective-permute-start.4 = (bf16[528,896]{1,0:T(8,128)(2,1)S(1)}, bf16[528,896]{1,0:T(8,128)(2,1)S(1)}, u32[]{:S(2)}, u32[]{:S(2)}) collective-permute-start(bf16[528,896]{1,0:T(8,128)(2,1)S(1)} %shard_map.91.refs_0_.refs_5_), channel_id=1, source_target_pairs={{0,4},{1,5},{4,8},{5,9},{8,12},{9,13},{12,14},{13,15},{14,10},{15,... | collective-permute-start | bytes 2838536 | tf_op jit(solution)/shard_map/ppermute | solution.py:94
  8.9 23.2 %collective-permute-start.3 = (bf16[528,896]{1,0:T(8,128)(2,1)S(1)}, bf16[528,896]{1,0:T(8,128)(2,1)S(1)}, u32[]{:S(2)}, u32[]{:S(2)}) collective-permute-start(bf16[528,896]{1,0:T(8,128)(2,1)S(1)} %shard_map.91.refs_0_.refs_5_), channel_id=1, source_target_pairs={{0,2},{1,3},{4,0},{5,1},{8,4},{9,5},{12,8},{13,9},{14,12},{15,13},... | collective-permute-start | bytes 2838536 | tf_op jit(solution)/shard_map/ppermute | solution.py:94
  30.3 22.8 %collective-permute-start.6 = (bf16[528,896]{1,0:T(8,128)(2,1)S(1)}, bf16[528,896]{1,0:T(8,128)(2,1)}, u32[]{:S(2)}, u32[]{:S(2)}) collective-permute-start(bf16[528,896]{1,0:T(8,128)(2,1)S(1)} %collective-permute-done.4.refs_1_.refs_12_), channel_id=1, source_target_pairs={{0,4},{1,5},{4,8},{5,9},{8,12},{9,13},{12,14},{13,15},{14,10},{15,... | collective-permute-start | bytes 2838536 | tf_op jit(solution)/shard_map/ppermute | solution.py:94
  32.1 22.5 %collective-permute-start.5 = (bf16[528,896]{1,0:T(8,128)(2,1)S(1)}, bf16[528,896]{1,0:T(8,128)(2,1)}, u32[]{:S(2)}, u32[]{:S(2)}) collective-permute-start(bf16[528,896]{1,0:T(8,128)(2,1)S(1)} %collective-permute-done.3.refs_0_.refs_6_), channel_id=1, source_target_pairs={{0,2},{1,3},{4,0},{5,1},{8,4},{9,5},{12,8},{13,9},{14,12},{15,13},... | collective-permute-start | bytes 2838536 | tf_op jit(solution)/shard_map/ppermute | solution.py:94
  53.1 22.0 %collective-permute-start.8 = (bf16[528,896]{1,0:T(8,128)(2,1)}, bf16[528,896]{1,0:T(8,128)(2,1)S(1)}, u32[]{:S(2)}, u32[]{:S(2)}) collective-permute-start(bf16[528,896]{1,0:T(8,128)(2,1)} %collective-permute-done.6.refs_1_.refs_11_), channel_id=1, source_target_pairs={{0,4},{1,5},{4,8},{5,9},{8,12},{9,13},{12,14},{13,15},{14,10},{15,... | collective-permute-start | bytes 2838536 | tf_op jit(solution)/shard_map/ppermute | solution.py:94
  54.6 21.4 %collective-permute-start.7 = (bf16[528,896]{1,0:T(8,128)(2,1)}, bf16[528,896]{1,0:T(8,128)(2,1)S(1)}, u32[]{:S(2)}, u32[]{:S(2)}) collective-permute-start(bf16[528,896]{1,0:T(8,128)(2,1)} %collective-permute-done.5.refs_0_.refs_7_), channel_id=1, source_target_pairs={{0,2},{1,3},{4,0},{5,1},{8,4},{9,5},{12,8},{13,9},{14,12},{15,13},... | collective-permute-start | bytes 2838536 | tf_op jit(solution)/shard_map/ppermute | solution.py:94
  76.1 9.9 %collective-permute-start.11 = (bf16[256,896]{1,0:T(8,128)(2,1)S(1)}, bf16[256,896]{1,0:T(8,128)(2,1)S(1)}, u32[]{:S(2)}, u32[]{:S(2)}) collective-permute-start(bf16[256,896]{1,0:T(8,128)(2,1)S(1)} %slice.7), channel_id=1, source_target_pairs={{0,2},{1,3},{4,0},{5,1},{8,4},{9,5},{12,8},{13,9},{14,12},{15,13},... | collective-permute-start | bytes 1376264 | tf_op jit(solution)/shard_map/ppermute | solution.py:94
  77.0 10.5 %collective-permute-start.10 = (bf16[272,896]{1,0:T(8,128)(2,1)S(1)}, bf16[272,896]{1,0:T(8,128)(2,1)S(1)}, u32[]{:S(2)}, u32[]{:S(2)}) collective-permute-start(bf16[272,896]{1,0:T(8,128)(2,1)S(1)} %slice.6), channel_id=1, source_target_pairs={{0,4},{1,5},{4,8},{5,9},{8,12},{9,13},{12,14},{13,15},{14,10},{15,... | collective-permute-start | bytes 1462280 | tf_op jit(solution)/shard_map/ppermute | solution.py:94
  91.6 11.5 %collective-permute-start.22 = (bf16[64,3584]{1,0:T(8,128)(2,1)S(1)}, bf16[64,3584]{1,0:T(8,128)(2,1)S(1)}, u32[]{:S(2)}, u32[]{:S(2)}) collective-permute-start(bf16[64,3584]{1,0:T(8,128)(2,1)S(1)} %get-tuple-element.58), channel_id=1, source_target_pairs={{0,2},{1,3},{4,0},{5,1},{8,4},{9,5},{12,8},{13,9},{14,12},{15,13},... | collective-permute-start | bytes 1376264 | tf_op jit(solution)/shard_map/ppermute | solution.py:94
  92.7 13.5 %collective-permute-start.12 = (bf16[64,3584]{1,0:T(8,128)(2,1)S(1)}, bf16[64,3584]{1,0:T(8,128)(2,1)S(1)}, u32[]{:S(2)}, u32[]{:S(2)}) collective-permute-start(bf16[64,3584]{1,0:T(8,128)(2,1)S(1)} %get-tuple-element.55), channel_id=1, source_target_pairs={{0,4},{1,5},{4,8},{5,9},{8,12},{9,13},{12,14},{13,15},{14,10},{15,... | collective-permute-start | bytes 1376264 | tf_op jit(solution)/shard_map/ppermute | solution.py:94
  93.7 22.3 %collective-permute-start.19 = (bf16[64,3584]{1,0:T(8,128)(2,1)S(1)}, bf16[64,3584]{1,0:T(8,128)(2,1)S(1)}, u32[]{:S(2)}, u32[]{:S(2)}) collective-permute-start(bf16[64,3584]{1,0:T(8,128)(2,1)S(1)} %get-tuple-element.57), channel_id=1, source_target_pairs={{0,4},{1,5},{4,8},{5,9},{8,12},{9,13},{12,14},{13,15},{14,10},{15,... | collective-permute-start | bytes 1376264 | tf_op jit(solution)/shard_map/ppermute | solution.py:94
  100.0 17.7 %collective-permute-start.16 = (bf16[64,3584]{1,0:T(8,128)(2,1)S(1)}, bf16[64,3584]{1,0:T(8,128)(2,1)S(1)}, u32[]{:S(2)}, u32[]{:S(2)}) collective-permute-start(bf16[64,3584]{1,0:T(8,128)(2,1)S(1)} %get-tuple-element.56), channel_id=1, source_target_pairs={{0,2},{1,3},{4,0},{5,1},{8,4},{9,5},{12,8},{13,9},{14,12},{15,13},... | collective-permute-start | bytes 1376264 | tf_op jit(solution)/shard_map/ppermute | solution.py:94
  103.8 19.5 %collective-permute-start.23 = (bf16[64,3584]{1,0:T(8,128)(2,1)S(1)}, bf16[64,3584]{1,0:T(8,128)(2,1)S(1)}, u32[]{:S(2)}, u32[]{:S(2)}) collective-permute-start(bf16[64,3584]{1,0:T(8,128)(2,1)S(1)} %shard_map.107), channel_id=1, source_target_pairs={{0,2},{1,3},{4,0},{5,1},{8,4},{9,5},{12,8},{13,9},{14,12},{15,13},... | collective-permute-start | bytes 1376264 | tf_op jit(solution)/shard_map/ppermute | solution.py:94
  106.9 19.0 %collective-permute-start.13 = (bf16[64,3584]{1,0:T(8,128)(2,1)S(1)}, bf16[64,3584]{1,0:T(8,128)(2,1)S(1)}, u32[]{:S(2)}, u32[]{:S(2)}) collective-permute-start(bf16[64,3584]{1,0:T(8,128)(2,1)S(1)} %shard_map.100), channel_id=1, source_target_pairs={{0,4},{1,5},{4,8},{5,9},{8,12},{9,13},{12,14},{13,15},{14,10},{15,... | collective-permute-start | bytes 1376264 | tf_op jit(solution)/shard_map/ppermute | solution.py:94
  116.7 19.0 %collective-permute-start.20 = (bf16[64,3584]{1,0:T(8,128)(2,1)S(1)}, bf16[64,3584]{1,0:T(8,128)(2,1)S(1)}, u32[]{:S(2)}, u32[]{:S(2)}) collective-permute-start(bf16[64,3584]{1,0:T(8,128)(2,1)S(1)} %shard_map.105), channel_id=1, source_target_pairs={{0,4},{1,5},{4,8},{5,9},{8,12},{9,13},{12,14},{13,15},{14,10},{15,... | collective-permute-start | bytes 1376264 | tf_op jit(solution)/shard_map/ppermute | solution.py:94
  118.4 19.0 %collective-permute-start.17 = (bf16[64,3584]{1,0:T(8,128)(2,1)S(1)}, bf16[64,3584]{1,0:T(8,128)(2,1)S(1)}, u32[]{:S(2)}, u32[]{:S(2)}) collective-permute-start(bf16[64,3584]{1,0:T(8,128)(2,1)S(1)} %shard_map.103), channel_id=1, source_target_pairs={{0,2},{1,3},{4,0},{5,1},{8,4},{9,5},{12,8},{13,9},{14,12},{15,13},... | collective-permute-start | bytes 1376264 | tf_op jit(solution)/shard_map/ppermute | solution.py:94
  124.0 19.0 %collective-permute-start.24 = (bf16[64,3584]{1,0:T(8,128)(2,1)S(1)}, bf16[64,3584]{1,0:T(8,128)(2,1)S(1)}, u32[]{:S(2)}, u32[]{:S(2)}) collective-permute-start(bf16[64,3584]{1,0:T(8,128)(2,1)S(1)} %shard_map.108), channel_id=1, source_target_pairs={{0,2},{1,3},{4,0},{5,1},{8,4},{9,5},{12,8},{13,9},{14,12},{15,13},... | collective-permute-start | bytes 1376264 | tf_op jit(solution)/shard_map/ppermute | solution.py:94
  126.5 19.0 %collective-permute-start.14 = (bf16[64,3584]{1,0:T(8,128)(2,1)S(1)}, bf16[64,3584]{1,0:T(8,128)(2,1)S(1)}, u32[]{:S(2)}, u32[]{:S(2)}) collective-permute-start(bf16[64,3584]{1,0:T(8,128)(2,1)S(1)} %shard_map.101), channel_id=1, source_target_pairs={{0,4},{1,5},{4,8},{5,9},{8,12},{9,13},{12,14},{13,15},{14,10},{15,... | collective-permute-start | bytes 1376264 | tf_op jit(solution)/shard_map/ppermute | solution.py:94
  136.4 19.0 %collective-permute-start.21 = (bf16[64,3584]{1,0:T(8,128)(2,1)S(1)}, bf16[64,3584]{1,0:T(8,128)(2,1)S(1)}, u32[]{:S(2)}, u32[]{:S(2)}) collective-permute-start(bf16[64,3584]{1,0:T(8,128)(2,1)S(1)} %shard_map.106), channel_id=1, source_target_pairs={{0,4},{1,5},{4,8},{5,9},{8,12},{9,13},{12,14},{13,15},{14,10},{15,... | collective-permute-start | bytes 1376264 | tf_op jit(solution)/shard_map/ppermute | solution.py:94
  138.0 17.3 %collective-permute-start.18 = (bf16[64,3584]{1,0:T(8,128)(2,1)S(1)}, bf16[64,3584]{1,0:T(8,128)(2,1)S(1)}, u32[]{:S(2)}, u32[]{:S(2)}) collective-permute-start(bf16[64,3584]{1,0:T(8,128)(2,1)S(1)} %shard_map.104), channel_id=1, source_target_pairs={{0,2},{1,3},{4,0},{5,1},{8,4},{9,5},{12,8},{13,9},{14,12},{15,13},... | collective-permute-start | bytes 1376264 | tf_op jit(solution)/shard_map/ppermute | solution.py:94
  143.6 16.0 %collective-permute-start.25 = (bf16[64,3584]{1,0:T(8,128)(2,1)S(1)}, bf16[64,3584]{1,0:T(8,128)(2,1)S(1)}, u32[]{:S(2)}, u32[]{:S(2)}) collective-permute-start(bf16[64,3584]{1,0:T(8,128)(2,1)S(1)} %shard_map.109), channel_id=1, source_target_pairs={{0,2},{1,3},{4,0},{5,1},{8,4},{9,5},{12,8},{13,9},{14,12},{15,13},... | collective-permute-start | bytes 1376264 | tf_op jit(solution)/shard_map/ppermute | solution.py:94
  146.2 14.0 %collective-permute-start.15 = (bf16[64,3584]{1,0:T(8,128)(2,1)S(1)}, bf16[64,3584]{1,0:T(8,128)(2,1)S(1)}, u32[]{:S(2)}, u32[]{:S(2)}) collective-permute-start(bf16[64,3584]{1,0:T(8,128)(2,1)S(1)} %shard_map.102), channel_id=1, source_target_pairs={{0,4},{1,5},{4,8},{5,9},{8,12},{9,13},{12,14},{13,15},{14,10},{15,... | collective-permute-start | bytes 1376264 | tf_op jit(solution)/shard_map/ppermute | solution.py:94

commit v15 on v14

--- a/solution.py
+++ b/solution.py
@@ -123,14 +123,29 @@
     )(*operands)
 
 
-def first_blocks(stream, swapped, routes, route_gain, experts):
+def first_blocks(stream, swapped, routes, route_gain, experts, norm_gain, w_gate, w_up):
     chips, _, tok_here, feat_here = stream.shape
     width = 2 * feat_here
     tokens = chips * tok_here
     head = -(-3 * (experts + 1) // 16) * 16
 
-    def kernel(stream_ref, swapped_ref, routes_ref, gain_ref, out_ref):
+    hidden_here = w_gate.shape[1]
+
+    def kernel(stream_ref, swapped_ref, routes_ref, gain_ref, scale_ref, *refs):
+        gate_ref, up_ref, out_ref, early_ref, table_ref, sems = refs
+        chip = lax.div(lax.axis_index("ep"), 2)
+        row = pl.multiple_of(chip * width, width)
+        copies = [
+            pltpu.make_async_copy(ref.at[pl.ds(row, width), :], table_ref.at[k], sems.at[k])
+            for k, ref in enumerate((gate_ref, up_ref))
+        ]
         core = lax.rem(lax.axis_index("ep"), 2)
+
+        @pl.when(core == 1)
+        def _():
+            for copy in copies:
+                copy.start()
+
         square = (tok_here, tok_here)
         diagonal = lax.broadcasted_iota(jnp.int32, square, 0) == lax.broadcasted_iota(
             jnp.int32, square, 1
@@ -168,17 +183,41 @@
         if width > tokens:
             out_ref[:head, tokens:] = jnp.zeros((head, width - tokens), jnp.bfloat16)
 
+        @pl.when(core == 1)
+        def _():
+            for copy in copies:
+                copy.wait()
+            for k in range(2):
+                span = slice(k * tokens // 2, (k + 1) * tokens // 2)
+                at = head + k * tokens // 2
+                values = out_ref[at : at + tokens // 2, :].astype(jnp.float32)
+                scaled = (values * scale_ref[chip]).astype(jnp.bfloat16)
+                for which in range(2):
+                    cols = slice(which * hidden_here, (which + 1) * hidden_here)
+                    early_ref[span, cols] = jnp.dot(
+                        scaled, table_ref[which], preferred_element_type=jnp.float32
+                    )
+
+    operands = [stream, swapped, routes, route_gain, norm_gain, w_gate, w_up]
     return local_call(
         kernel,
-        jax.ShapeDtypeStruct((head + tokens, width), jnp.bfloat16),
-        [stream, swapped, routes, route_gain],
+        [
+            jax.ShapeDtypeStruct((head + tokens, width), jnp.bfloat16),
+            jax.ShapeDtypeStruct((tokens, 2 * hidden_here), jnp.float32),
+        ],
+        operands,
         flops=4 * tokens * width,
         bytes_accessed=4 * tokens * width,
+        scratch=[
+            pltpu.VMEM((2, width, hidden_here), jnp.bfloat16),
+            pltpu.SemaphoreType.DMA((2,)),
+        ],
+        far=[5, 6],
     )
 
 
 def accumulate(
-    where, positions, parts, norm_gain, tables, tok_here, carried, headers, ahead, leading
+    where, positions, parts, norm_gain, tables, tok_here, carried, headers, ahead, leading, early
 ):
     count = len(positions)
     width = parts[0][0].shape[1]
@@ -203,6 +242,7 @@
         scale_ref = refs.pop(0)
         stored = [refs.pop(0) for _ in tables]
         acc_in = None if first else refs.pop(0)
+        early_ref = refs.pop(0) if first else None
         tops = [refs.pop(0) for _ in headers] if last else []
         sources = [refs.pop(0) for _ in ahead[1]] if ahead else []
         product_ref = refs.pop(0) if leading else None
@@ -287,6 +327,20 @@
             for b in range(count):
                 if not last:
                     copies[which, b].wait()
+            if first and which < 2:
+                on_second = lax.rem(lax.axis_index("ep"), 2) == 1
+
+                @pl.when(on_second)
+                def _(cols=cols):
+                    acc_out[:, cols] = early_ref[:, cols]
+
+                @pl.when(jnp.logical_not(on_second))
+                def _(cols=cols, which=which):
+                    acc_out[:, cols] = jnp.dot(
+                        scaled[0], table_ref[which], preferred_element_type=jnp.float32
+                    )
+
+                continue
             for k, size in enumerate(sizes):
                 span = slice(starts[k], starts[k] + size)
                 total = None if first else acc_in[span, cols]
@@ -333,6 +387,8 @@
         if not last:
             aliases = {len(operands): count}
         operands.append(carried)
+    else:
+        operands.append(early)
     out_shape = [jax.ShapeDtypeStruct((tok_here, width), jnp.bfloat16)] * count
     if last:
         operands.extend(headers)
@@ -474,10 +530,13 @@
     by_core = stream_feat.reshape(chips, 2, tok_here, feat_here)
     swapped = swap_cores(lax.dynamic_index_in_dim(by_core, 1 - core, 1, keepdims=False))
 
-    blocks = {0: first_blocks(by_core, swapped, expert_routes, route_gain, experts)}
-
-    blocks[0], w_gate, w_up, w_down = lax.optimization_barrier((blocks[0], w_gate, w_up, w_down))
+    gain_rows = norm_gain.reshape(chips, 1, width)
+    swapped, w_gate, w_up, w_down = lax.optimization_barrier((swapped, w_gate, w_up, w_down))
     tables = [pltpu.with_memory_space_constraint(table, pltpu.HBM) for table in (w_gate, w_up)]
+    block, early = first_blocks(
+        by_core, swapped, expert_routes, route_gain, experts, gain_rows, *tables
+    )
+    blocks = {0: block}
     tables += [swap_cores(w_gate), swap_cores(w_up)]
     down = [pltpu.with_memory_space_constraint(w_down, pltpu.HBM), swap_cores(w_down)]
 
@@ -485,7 +544,6 @@
         for sign in (-1, 1):
             blocks[sign * distance] = ring_shift(blocks[sign * (distance - 1)], ring, -sign)
     groups = [[0]] + [[d, chips - d] for d in range(1, far)] + [[far]]
-    gain_rows = norm_gain.reshape(chips, 1, width)
     carried, owns, positions, headers, ahead, leading = None, [], [], None, None, None
     for group in groups:
         parts = [[blocks[d if d <= far else d - chips]] for d in group]
@@ -497,7 +555,7 @@
         if group == groups[-2]:
             ahead = (far, down)
         made, (carried, *rest) = accumulate(
-            where, group, parts, gain_rows, tables, tok_here, carried, headers, ahead, leading
+            where, group, parts, gain_rows, tables, tok_here, carried, headers, ahead, leading, early
         )
         owns.extend(made)
         positions.extend(group)

time: 162 us -> 170 us (1.049)
  waiting for transfers between devices: 89.3 us -> 92.2 us
  starting transfers between devices: 24.5 us -> 27 us
  local copies, waits for them, and re-layouts: 1.54 us -> 3.37 us
    ppermute x22, waiting for transfers between devices: 88 us -> 90.6 us  [ring_shift(): return lax.ppermute(value, 'ep', pairs)]
    ppermute x22, starting transfers between devices: 23 us -> 25.6 us  [ring_shift(): return lax.ppermute(value, 'ep', pairs)]
    unnamed x8 -> x12, local copies, waits for them, and re-layouts: 0.2 us -> 2.03 us
  transfers between devices with their start and end apart: 26 -> 26, of which waited for: 18 -> 16; matrix products, arithmetic and copies ran while one was open for 1% -> 1% of each run, Pallas kernels for 23% -> 23%
where the time goes in v15:
time: 170 us
  waiting for transfers between devices  92.2 us (54%)
  Pallas kernels  45.1 us (27%)
  starting transfers between devices  27 us (16%)
  local copies, waits for them, and re-layouts  3.37 us (2%)
  other arithmetic  1.83 us (1%)
    ppermute x22, waiting for transfers between devices, ring_shift(): return lax.ppermute(value, 'ep', pairs)  90.6 us
    pallas_call x20, Pallas kernels, local_call(): pl.pallas_call(kernel, out_shape=out_shape, in_specs=[IN_SMEM if value.nd...  45.1 us
    ppermute x22, starting transfers between devices, ring_shift(): return lax.ppermute(value, 'ep', pairs)  25.6 us
  transfers between devices with their start and end apart: 26, of which 16 were waited for; matrix products, arithmetic and copies ran while one was open for 1% of the time, Pallas kernels for 23%

profile of v15, /device:TPU:0, one launch (start us, length us, event | category | flops | bytes accessed | tf_op | source)
XLA Modules:
  0.0 169.7 jit_solution(17516777471657790002)
XLA Ops:
  0.0 1.8 %add_convert_fusion = bf16[1024,448]{0,1:T(8,128)(2,1)S(1)} fusion(bf16[1024,448]{0,1:T(8,128)(2,1)} %param.10, bf16[1024,448]{0,1:T(8,128)(2,1)} %param.9), kind=kLoop, calls=%fused_computation | loop fusion | flops 1835008 | bytes 2752512 | tf_op jit(solution)/shard_map/convert_element_type | solution.py:529
  1.8 0.5 copy.13
  2.4 0.5 collective-permute-start
  3.0 1.5 collective-permute-done.swapped_ref
  4.5 0.8 copy-done
  5.3 0.4 collective-permute-start.1
  5.7 0.1 collective-permute-start.2
  5.8 0.4 collective-permute-start.9
  6.2 0.1 copy.14.routes_ref
  6.3 0.1 copy.15.gain_ref
  6.4 1.0 copy-done.1
  7.4 0.7 shard_map.91
  8.2 2.8 %collective-permute-start.4 = (bf16[528,896]{1,0:T(8,128)(2,1)S(1)}, bf16[528,896]{1,0:T(8,128)(2,1)S(1)}, u32[]{:S(2)}, u32[]{:S(2)}) collective-permute-start(bf16[528,896]{1,0:T(8,128)(2,1)S(1)} %get-tuple-element.37.refs_0_.refs_5_), channel_id=1, source_target_pairs={{0,4},{1,5},{4,8},{5,9},{8,12},{9,13},{12,14},{13,15},{14,10},{15,... | collective-permute-start | bytes 2838536 | tf_op jit(solution)/shard_map/ppermute | solution.py:94
  10.9 20.9 %collective-permute-done.4.refs_1_.refs_12_ = bf16[528,896]{1,0:T(8,128)(2,1)S(1)} collective-permute-done((bf16[528,896]{1,0:T(8,128)(2,1)S(1)}, bf16[528,896]{1,0:T(8,128)(2,1)S(1)}, u32[]{:S(2)}, u32[]{:S(2)}) %collective-permute-start.4) | collective-permute-done | bytes 946208 | tf_op jit(solution)/shard_map/ppermute | solution.py:94
  31.8 2.4 %collective-permute-start.6 = (bf16[528,896]{1,0:T(8,128)(2,1)S(1)}, bf16[528,896]{1,0:T(8,128)(2,1)}, u32[]{:S(2)}, u32[]{:S(2)}) collective-permute-start(bf16[528,896]{1,0:T(8,128)(2,1)S(1)} %collective-permute-done.4.refs_1_.refs_12_), channel_id=1, source_target_pairs={{0,4},{1,5},{4,8},{5,9},{8,12},{9,13},{12,14},{13,15},{14,10},{15,... | collective-permute-start | bytes 2838536 | tf_op jit(solution)/shard_map/ppermute | solution.py:94
  34.2 0.3 collective-permute-done.3.refs_0_.refs_6_
  34.5 0.7 dynamic-slice_bitcast_fusion.1.where_ref
  35.2 20.6 %collective-permute-done.6.refs_1_.refs_11_ = bf16[528,896]{1,0:T(8,128)(2,1)} collective-permute-done((bf16[528,896]{1,0:T(8,128)(2,1)S(1)}, bf16[528,896]{1,0:T(8,128)(2,1)}, u32[]{:S(2)}, u32[]{:S(2)}) %collective-permute-start.6) | collective-permute-done | bytes 946208 | tf_op jit(solution)/shard_map/ppermute | solution.py:94
  55.9 2.1 %collective-permute-start.8 = (bf16[528,896]{1,0:T(8,128)(2,1)}, bf16[528,896]{1,0:T(8,128)(2,1)S(1)}, u32[]{:S(2)}, u32[]{:S(2)}) collective-permute-start(bf16[528,896]{1,0:T(8,128)(2,1)} %collective-permute-done.6.refs_1_.refs_11_), channel_id=1, source_target_pairs={{0,4},{1,5},{4,8},{5,9},{8,12},{9,13},{12,14},{13,15},{14,10},{15,... | collective-permute-start | bytes 2838536 | tf_op jit(solution)/shard_map/ppermute | solution.py:94
  58.0 0.2 collective-permute-start.7
  58.2 3.9 %shard_map.92 = (bf16[64,896]{1,0:T(8,128)(2,1)S(1)}, f32[512,1024]{1,0:T(8,128)S(1)}) custom-call(s32[9]{0:T(128)S(1)} %dynamic-slice_bitcast_fusion.1.where_ref, bf16[528,896]{1,0:T(8,128)(2,1)S(1)} %get-tuple-element.37.refs_0_.refs_5_, f32[8,1,896]{2,1,0:T(1,128)S(1)} %bitcast.9, bf16[7168,256]{1,0:T(8,128)(2,1)} %refs_3_.3, bf16[7168,256]{1,0:T(8,128)(2,1)} %refs_4_.2, ...), custom_call_target="tpu_custom_call" | custom-call | flops 2818572288 | bytes 6946816 | tf_op jit(solution)/shard_map/pallas_call | solution.py:107
  62.1 7.4 %shard_map.93 = (bf16[64,896]{1,0:T(8,128)(2,1)S(1)}, bf16[64,896]{1,0:T(8,128)(2,1)S(1)}, f32[512,1024]{1,0:T(8,128)S(1)}) custom-call(s32[9]{0:T(128)S(1)} %dynamic-slice_bitcast_fusion.1.where_ref, bf16[528,896]{1,0:T(8,128)(2,1)} %collective-permute-done.3.refs_0_.refs_6_, ...), custom_call_target="tpu_custom_call", output_to_operand_aliasing={{2}: (8, {})} | custom-call | flops 5637144576 | bytes 9699328 | tf_op jit(solution)/shard_map/pallas_call | solution.py:107
  69.5 7.7 %shard_map.94 = (bf16[64,896]{1,0:T(8,128)(2,1)S(1)}, bf16[64,896]{1,0:T(8,128)(2,1)S(1)}, f32[512,1024]{1,0:T(8,128)S(1)}) custom-call(s32[9]{0:T(128)S(1)} %dynamic-slice_bitcast_fusion.1.where_ref, bf16[528,896]{1,0:T(8,128)(2,1)} %collective-permute-done.5.refs_0_.refs_7_, ...), custom_call_target="tpu_custom_call", output_to_operand_aliasing={{2}: (8, {})} | custom-call | flops 5637144576 | bytes 9699328 | tf_op jit(solution)/shard_map/pallas_call | solution.py:107
  77.3 1.6 collective-permute-done.8.refs_1_.refs_10_
  78.9 1.8 %collective-permute-done.7.refs_0_.refs_8_ = bf16[528,896]{1,0:T(8,128)(2,1)S(1)} collective-permute-done((bf16[528,896]{1,0:T(8,128)(2,1)}, bf16[528,896]{1,0:T(8,128)(2,1)S(1)}, u32[]{:S(2)}, u32[]{:S(2)}) %collective-permute-start.7) | collective-permute-done | bytes 946208 | tf_op jit(solution)/shard_map/ppermute | solution.py:94
  80.7 0.3 collective-permute-start.11
  81.1 1.8 %collective-permute-start.10 = (bf16[272,896]{1,0:T(8,128)(2,1)S(1)}, bf16[272,896]{1,0:T(8,128)(2,1)S(1)}, u32[]{:S(2)}, u32[]{:S(2)}) collective-permute-start(bf16[272,896]{1,0:T(8,128)(2,1)S(1)} %slice.6), channel_id=1, source_target_pairs={{0,4},{1,5},{4,8},{5,9},{8,12},{9,13},{12,14},{13,15},{14,10},{15,... | collective-permute-start | bytes 1462280 | tf_op jit(solution)/shard_map/ppermute | solution.py:94
  82.9 6.8 %shard_map.95 = (bf16[64,896]{1,0:T(8,128)(2,1)S(1)}, bf16[64,896]{1,0:T(8,128)(2,1)S(1)}, f32[512,1024]{1,0:T(8,128)S(1)}, bf16[4,896,256]{2,1,0:T(8,128)(2,1)S(1)}, bf16[512,7168]{1,0:T(8,128)(2,1)S(1)}) custom-call(s32[9]{0:T(128)S(1)} %dynamic-slice_bitcast_fusion.1.where_ref, ...), custom_call_target="tpu_custom_call", output_to_operand_aliasing={{2}: (8, {})} | custom-call | flops 5637144576 | bytes 9699328 | tf_op jit(solution)/shard_map/pallas_call | solution.py:107
  89.7 2.2 %collective-permute-done.11.refs_1_ = bf16[256,896]{1,0:T(8,128)(2,1)S(1)} collective-permute-done((bf16[256,896]{1,0:T(8,128)(2,1)S(1)}, bf16[256,896]{1,0:T(8,128)(2,1)S(1)}, u32[]{:S(2)}, u32[]{:S(2)}) %collective-permute-start.11) | collective-permute-done | bytes 458784 | tf_op jit(solution)/shard_map/ppermute | solution.py:94
  91.9 0.8 collective-permute-done.10.refs_0_.refs_9_
  92.7 4.3 %shard_map.96 = (bf16[64,896]{1,0:T(8,128)(2,1)S(1)}, bf16[512,512]{1,0:T(8,128)(2,1)S(1)}, bf16[64,3584]{1,0:T(8,128)(2,1)S(1)}, bf16[64,3584]{1,0:T(8,128)(2,1...) custom-call(s32[9]{0:T(128)S(1)} %dynamic-slice_bitcast_fusion.1.where_ref, ...), custom_call_target="tpu_custom_call" | custom-call | flops 2818572288 | bytes 6946816 | tf_op jit(solution)/shard_map/pallas_call | solution.py:107
  97.0 1.8 %collective-permute-start.22 = (bf16[64,3584]{1,0:T(8,128)(2,1)S(1)}, bf16[64,3584]{1,0:T(8,128)(2,1)S(1)}, u32[]{:S(2)}, u32[]{:S(2)}) collective-permute-start(bf16[64,3584]{1,0:T(8,128)(2,1)S(1)} %get-tuple-element.62), channel_id=1, source_target_pairs={{0,2},{1,3},{4,0},{5,1},{8,4},{9,5},{12,8},{13,9},{14,12},{15,13},... | collective-permute-start | bytes 1376264 | tf_op jit(solution)/shard_map/ppermute | solution.py:94
  98.8 0.3 collective-permute-start.12
  99.1 1.7 collective-permute-start.19
  100.8 2.6 %shard_map.99.table_ref.refs_1_ = bf16[512,3584]{1,0:T(8,128)(2,1)S(1)} custom-call(s32[9]{0:T(128)S(1)} %dynamic-slice_bitcast_fusion.1.where_ref, bf16[512,512]{1,0:T(8,128)(2,1)S(1)} %get-tuple-element.58.hidden_ref, bf16[512,7168]{1,0:T(8,128)(2,1)S(1)} %get-tuple-element.56.refs_13_.down_ref), custom_call_target="tpu_custom_call" | custom-call | flops 1879048192 | bytes 7340032 | tf_op jit(solution)/shard_map/pallas_call | solution.py:107
  103.4 2.6 %shard_map.98.table_ref.refs_0_ = bf16[512,3584]{1,0:T(8,128)(2,1)S(1)} custom-call(s32[9]{0:T(128)S(1)} %dynamic-slice_bitcast_fusion.1.where_ref, bf16[512,512]{1,0:T(8,128)(2,1)S(1)} %get-tuple-element.58.hidden_ref, bf16[512,7168]{1,0:T(8,128)(2,1)S(1)} %get-tuple-element.56.refs_13_.down_ref), custom_call_target="tpu_custom_call" | custom-call | flops 1879048192 | bytes 7340032 | tf_op jit(solution)/shard_map/pallas_call | solution.py:107
  106.0 0.4 collective-permute-start.16
  106.4 3.2 %collective-permute-done.22.moved_ref = bf16[64,3584]{1,0:T(8,128)(2,1)S(1)} collective-permute-done((bf16[64,3584]{1,0:T(8,128)(2,1)S(1)}, bf16[64,3584]{1,0:T(8,128)(2,1)S(1)}, u32[]{:S(2)}, u32[]{:S(2)}) %collective-permute-start.22) | collective-permute-done | bytes 458784 | tf_op jit(solution)/shard_map/ppermute | solution.py:94
  109.6 0.6 shard_map.107
  110.3 2.5 %collective-permute-start.23 = (bf16[64,3584]{1,0:T(8,128)(2,1)S(1)}, bf16[64,3584]{1,0:T(8,128)(2,1)S(1)}, u32[]{:S(2)}, u32[]{:S(2)}) collective-permute-start(bf16[64,3584]{1,0:T(8,128)(2,1)S(1)} %shard_map.107), channel_id=1, source_target_pairs={{0,2},{1,3},{4,0},{5,1},{8,4},{9,5},{12,8},{13,9},{14,12},{15,13},... | collective-permute-start | bytes 1376264 | tf_op jit(solution)/shard_map/ppermute | solution.py:94
  112.8 0.6 shard_map.100
  113.5 8.6 %collective-permute-done.19.moved_ref = bf16[64,3584]{1,0:T(8,128)(2,1)S(1)} collective-permute-done((bf16[64,3584]{1,0:T(8,128)(2,1)S(1)}, bf16[64,3584]{1,0:T(8,128)(2,1)S(1)}, u32[]{:S(2)}, u32[]{:S(2)}) %collective-permute-start.19) | collective-permute-done | bytes 458784 | tf_op jit(solution)/shard_map/ppermute | solution.py:94
  122.1 0.6 shard_map.105
  122.8 0.3 collective-permute-start.20
  123.1 0.6 shard_map.103
  123.8 1.8 %collective-permute-start.17 = (bf16[64,3584]{1,0:T(8,128)(2,1)S(1)}, bf16[64,3584]{1,0:T(8,128)(2,1)S(1)}, u32[]{:S(2)}, u32[]{:S(2)}) collective-permute-start(bf16[64,3584]{1,0:T(8,128)(2,1)S(1)} %shard_map.103), channel_id=1, source_target_pairs={{0,2},{1,3},{4,0},{5,1},{8,4},{9,5},{12,8},{13,9},{14,12},{15,13},... | collective-permute-start | bytes 1376264 | tf_op jit(solution)/shard_map/ppermute | solution.py:94
  125.6 3.8 %collective-permute-done.23.moved_ref = bf16[64,3584]{1,0:T(8,128)(2,1)S(1)} collective-permute-done((bf16[64,3584]{1,0:T(8,128)(2,1)S(1)}, bf16[64,3584]{1,0:T(8,128)(2,1)S(1)}, u32[]{:S(2)}, u32[]{:S(2)}) %collective-permute-start.23) | collective-permute-done | bytes 458784 | tf_op jit(solution)/shard_map/ppermute | solution.py:94
  129.4 0.6 shard_map.108
  130.0 2.4 %collective-permute-start.24 = (bf16[64,3584]{1,0:T(8,128)(2,1)S(1)}, bf16[64,3584]{1,0:T(8,128)(2,1)S(1)}, u32[]{:S(2)}, u32[]{:S(2)}) collective-permute-start(bf16[64,3584]{1,0:T(8,128)(2,1)S(1)} %shard_map.108), channel_id=1, source_target_pairs={{0,2},{1,3},{4,0},{5,1},{8,4},{9,5},{12,8},{13,9},{14,12},{15,13},... | collective-permute-start | bytes 1376264 | tf_op jit(solution)/shard_map/ppermute | solution.py:94
  132.5 0.6 shard_map.101
  133.2 8.6 %collective-permute-done.20.moved_ref = bf16[64,3584]{1,0:T(8,128)(2,1)S(1)} collective-permute-done((bf16[64,3584]{1,0:T(8,128)(2,1)S(1)}, bf16[64,3584]{1,0:T(8,128)(2,1)S(1)}, u32[]{:S(2)}, u32[]{:S(2)}) %collective-permute-start.20) | collective-permute-done | bytes 458784 | tf_op jit(solution)/shard_map/ppermute | solution.py:94
  141.8 0.6 shard_map.106
  142.4 0.3 collective-permute-start.21
  142.8 0.6 shard_map.104
  143.4 1.8 %collective-permute-start.18 = (bf16[64,3584]{1,0:T(8,128)(2,1)S(1)}, bf16[64,3584]{1,0:T(8,128)(2,1)S(1)}, u32[]{:S(2)}, u32[]{:S(2)}) collective-permute-start(bf16[64,3584]{1,0:T(8,128)(2,1)S(1)} %shard_map.104), channel_id=1, source_target_pairs={{0,2},{1,3},{4,0},{5,1},{8,4},{9,5},{12,8},{13,9},{14,12},{15,13},... | collective-permute-start | bytes 1376264 | tf_op jit(solution)/shard_map/ppermute | solution.py:94
  145.2 3.8 %collective-permute-done.24.moved_ref = bf16[64,3584]{1,0:T(8,128)(2,1)S(1)} collective-permute-done((bf16[64,3584]{1,0:T(8,128)(2,1)S(1)}, bf16[64,3584]{1,0:T(8,128)(2,1)S(1)}, u32[]{:S(2)}, u32[]{:S(2)}) %collective-permute-start.24) | collective-permute-done | bytes 458784 | tf_op jit(solution)/shard_map/ppermute | solution.py:94
  149.0 0.6 shard_map.109
  149.7 2.4 %collective-permute-start.25 = (bf16[64,3584]{1,0:T(8,128)(2,1)S(1)}, bf16[64,3584]{1,0:T(8,128)(2,1)S(1)}, u32[]{:S(2)}, u32[]{:S(2)}) collective-permute-start(bf16[64,3584]{1,0:T(8,128)(2,1)S(1)} %shard_map.109), channel_id=1, source_target_pairs={{0,2},{1,3},{4,0},{5,1},{8,4},{9,5},{12,8},{13,9},{14,12},{15,13},... | collective-permute-start | bytes 1376264 | tf_op jit(solution)/shard_map/ppermute | solution.py:94
  152.1 0.6 shard_map.102
  152.8 0.6 shard_map.97.stream_ref
  153.5 8.0 %collective-permute-done.21.refs_4_ = bf16[64,3584]{1,0:T(8,128)(2,1)S(1)} collective-permute-done((bf16[64,3584]{1,0:T(8,128)(2,1)S(1)}, bf16[64,3584]{1,0:T(8,128)(2,1)S(1)}, u32[]{:S(2)}, u32[]{:S(2)}) %collective-permute-start.21) | collective-permute-done | bytes 458784 | tf_op jit(solution)/shard_map/ppermute | solution.py:94
  161.5 4.7 %collective-permute-done.25.refs_5_ = bf16[64,3584]{1,0:T(8,128)(2,1)S(1)} collective-permute-done((bf16[64,3584]{1,0:T(8,128)(2,1)S(1)}, bf16[64,3584]{1,0:T(8,128)(2,1)S(1)}, u32[]{:S(2)}, u32[]{:S(2)}) %collective-permute-start.25) | collective-permute-done | bytes 458784 | tf_op jit(solution)/shard_map/ppermute | solution.py:94
  166.1 1.7 collective-permute-done.15.refs_2_
  167.8 1.9 %shard_map.110 = bf16[64,7168]{1,0:T(8,128)(2,1)} custom-call(s32[9]{0:T(128)S(1)} %dynamic-slice_bitcast_fusion.1.where_ref, bf16[64,7168]{1,0:T(8,128)(2,1)S(1)} %shard_map.97.stream_ref, bf16[512,3584]{1,0:T(8,128)(2,1)S(1)} %shard_map.98.table_ref.refs_0_, bf16[512,3584]{1,0:T(8,128)(2,1)S(1)} %shard_map.99.table_ref.refs_1_, ...), custom_call_target="tpu_custom_call" | custom-call | flops 1376256 | bytes 4587520 | tf_op jit(solution)/shard_map/pallas_call | solution.py:107
  (26 shorter events, 0.3 us)
Async XLA Ops:
  0.0 6.2 %copy-start.3 = (s32[64,2]{0,1:T(2,128)S(1)}, s32[64,2]{0,1:T(2,128)}, u32[]{:S(2)}) copy-start(s32[64,2]{0,1:T(2,128)} %param.12) | copy-start | bytes 1540
  0.0 6.3 %copy-start.4 = (f32[64,2]{0,1:T(2,128)S(1)}, f32[64,2]{0,1:T(2,128)}, u32[]{:S(2)}) copy-start(f32[64,2]{0,1:T(2,128)} %param.13) | copy-start | bytes 1540
  0.0 6.4 %copy-start.2 = (f32[7168]{0:T(1024)S(1)}, f32[7168]{0:T(1024)}, u32[]{:S(2)}) copy-start(f32[7168]{0:T(1024)} %param.11) | copy-start | bytes 86020
  2.4 2.1 %collective-permute-start = (bf16[8,64,448]{2,1,0:T(8,128)(2,1)S(1)}, bf16[8,64,448]{2,1,0:T(8,128)(2,1)S(1)}, u32[]{:S(2)}, u32[]{:S(2)}) collective-permute-start(bf16[8,64,448]{2,1,0:T(8,128)(2,1)S(1)} %dynamic-slice_bitcast_fusion), channel_id=1, source_target_pairs={{0,1},{1,0},{2,3},{3,2},{4,5},{5,4},{6,7},{7,6},{8,9},{9,8},{10,11... | collective-permute-start | bytes 1376264 | tf_op jit(solution)/shard_map/ppermute | solution.py:84
  4.5 0.8 copy-start
  5.3 52.9 %collective-permute-start.1 = (bf16[7168,256]{1,0:T(8,128)(2,1)}, bf16[7168,256]{1,0:T(8,128)(2,1)}, u32[]{:S(2)}, u32[]{:S(2)}) collective-permute-start(bf16[7168,256]{1,0:T(8,128)(2,1)} %refs_3_.3), channel_id=1, source_target_pairs={{0,1},{1,0},{2,3},{3,2},{4,5},{5,4},{6,7},{7,6},{8,9},{9,8},{10,11... | collective-permute-start | bytes 11010056 | tf_op jit(solution)/shard_map/ppermute | solution.py:84
  5.7 52.5 %collective-permute-start.2 = (bf16[7168,256]{1,0:T(8,128)(2,1)}, bf16[7168,256]{1,0:T(8,128)(2,1)}, u32[]{:S(2)}, u32[]{:S(2)}) collective-permute-start(bf16[7168,256]{1,0:T(8,128)(2,1)} %refs_4_.2), channel_id=1, source_target_pairs={{0,1},{1,0},{2,3},{3,2},{4,5},{5,4},{6,7},{7,6},{8,9},{9,8},{10,11... | collective-permute-start | bytes 11010056 | tf_op jit(solution)/shard_map/ppermute | solution.py:84
  5.8 77.1 %collective-permute-start.9 = (bf16[256,7168]{1,0:T(8,128)(2,1)}, bf16[256,7168]{1,0:T(8,128)(2,1)}, u32[]{:S(2)}, u32[]{:S(2)}) collective-permute-start(bf16[256,7168]{1,0:T(8,128)(2,1)} %refs_8_), channel_id=1, source_target_pairs={{0,1},{1,0},{2,3},{3,2},{4,5},{5,4},{6,7},{7,6},{8,9},{9,8},{10,11... | collective-permute-start | bytes 11010056 | tf_op jit(solution)/shard_map/ppermute | solution.py:84
  6.4 1.0 copy-start.1
  8.2 23.7 %collective-permute-start.4 = (bf16[528,896]{1,0:T(8,128)(2,1)S(1)}, bf16[528,896]{1,0:T(8,128)(2,1)S(1)}, u32[]{:S(2)}, u32[]{:S(2)}) collective-permute-start(bf16[528,896]{1,0:T(8,128)(2,1)S(1)} %get-tuple-element.37.refs_0_.refs_5_), channel_id=1, source_target_pairs={{0,4},{1,5},{4,8},{5,9},{8,12},{9,13},{12,14},{13,15},{14,10},{15,... | collective-permute-start | bytes 2838536 | tf_op jit(solution)/shard_map/ppermute | solution.py:94
  10.9 23.6 %collective-permute-start.3 = (bf16[528,896]{1,0:T(8,128)(2,1)S(1)}, bf16[528,896]{1,0:T(8,128)(2,1)}, u32[]{:S(2)}, u32[]{:S(2)}) collective-permute-start(bf16[528,896]{1,0:T(8,128)(2,1)S(1)} %get-tuple-element.37.refs_0_.refs_5_), channel_id=1, source_target_pairs={{0,2},{1,3},{4,0},{5,1},{8,4},{9,5},{12,8},{13,9},{14,12},{15,13},... | collective-permute-start | bytes 2838536 | tf_op jit(solution)/shard_map/ppermute | solution.py:94
  31.8 24.1 %collective-permute-start.6 = (bf16[528,896]{1,0:T(8,128)(2,1)S(1)}, bf16[528,896]{1,0:T(8,128)(2,1)}, u32[]{:S(2)}, u32[]{:S(2)}) collective-permute-start(bf16[528,896]{1,0:T(8,128)(2,1)S(1)} %collective-permute-done.4.refs_1_.refs_12_), channel_id=1, source_target_pairs={{0,4},{1,5},{4,8},{5,9},{8,12},{9,13},{12,14},{13,15},{14,10},{15,... | collective-permute-start | bytes 2838536 | tf_op jit(solution)/shard_map/ppermute | solution.py:94
  34.5 23.4 %collective-permute-start.5 = (bf16[528,896]{1,0:T(8,128)(2,1)}, bf16[528,896]{1,0:T(8,128)(2,1)}, u32[]{:S(2)}, u32[]{:S(2)}) collective-permute-start(bf16[528,896]{1,0:T(8,128)(2,1)} %collective-permute-done.3.refs_0_.refs_6_), channel_id=1, source_target_pairs={{0,2},{1,3},{4,0},{5,1},{8,4},{9,5},{12,8},{13,9},{14,12},{15,13},... | collective-permute-start | bytes 2838536 | tf_op jit(solution)/shard_map/ppermute | solution.py:94
  55.9 23.0 %collective-permute-start.8 = (bf16[528,896]{1,0:T(8,128)(2,1)}, bf16[528,896]{1,0:T(8,128)(2,1)S(1)}, u32[]{:S(2)}, u32[]{:S(2)}) collective-permute-start(bf16[528,896]{1,0:T(8,128)(2,1)} %collective-permute-done.6.refs_1_.refs_11_), channel_id=1, source_target_pairs={{0,4},{1,5},{4,8},{5,9},{8,12},{9,13},{12,14},{13,15},{14,10},{15,... | collective-permute-start | bytes 2838536 | tf_op jit(solution)/shard_map/ppermute | solution.py:94
  58.0 22.7 %collective-permute-start.7 = (bf16[528,896]{1,0:T(8,128)(2,1)}, bf16[528,896]{1,0:T(8,128)(2,1)S(1)}, u32[]{:S(2)}, u32[]{:S(2)}) collective-permute-start(bf16[528,896]{1,0:T(8,128)(2,1)} %collective-permute-done.5.refs_0_.refs_7_), channel_id=1, source_target_pairs={{0,2},{1,3},{4,0},{5,1},{8,4},{9,5},{12,8},{13,9},{14,12},{15,13},... | collective-permute-start | bytes 2838536 | tf_op jit(solution)/shard_map/ppermute | solution.py:94
  80.7 11.2 %collective-permute-start.11 = (bf16[256,896]{1,0:T(8,128)(2,1)S(1)}, bf16[256,896]{1,0:T(8,128)(2,1)S(1)}, u32[]{:S(2)}, u32[]{:S(2)}) collective-permute-start(bf16[256,896]{1,0:T(8,128)(2,1)S(1)} %slice.7), channel_id=1, source_target_pairs={{0,2},{1,3},{4,0},{5,1},{8,4},{9,5},{12,8},{13,9},{14,12},{15,13},... | collective-permute-start | bytes 1376264 | tf_op jit(solution)/shard_map/ppermute | solution.py:94
  81.1 11.6 %collective-permute-start.10 = (bf16[272,896]{1,0:T(8,128)(2,1)S(1)}, bf16[272,896]{1,0:T(8,128)(2,1)S(1)}, u32[]{:S(2)}, u32[]{:S(2)}) collective-permute-start(bf16[272,896]{1,0:T(8,128)(2,1)S(1)} %slice.6), channel_id=1, source_target_pairs={{0,4},{1,5},{4,8},{5,9},{8,12},{9,13},{12,14},{13,15},{14,10},{15,... | collective-permute-start | bytes 1462280 | tf_op jit(solution)/shard_map/ppermute | solution.py:94
  97.0 12.5 %collective-permute-start.22 = (bf16[64,3584]{1,0:T(8,128)(2,1)S(1)}, bf16[64,3584]{1,0:T(8,128)(2,1)S(1)}, u32[]{:S(2)}, u32[]{:S(2)}) collective-permute-start(bf16[64,3584]{1,0:T(8,128)(2,1)S(1)} %get-tuple-element.62), channel_id=1, source_target_pairs={{0,2},{1,3},{4,0},{5,1},{8,4},{9,5},{12,8},{13,9},{14,12},{15,13},... | collective-permute-start | bytes 1376264 | tf_op jit(solution)/shard_map/ppermute | solution.py:94
  98.8 13.9 %collective-permute-start.12 = (bf16[64,3584]{1,0:T(8,128)(2,1)S(1)}, bf16[64,3584]{1,0:T(8,128)(2,1)S(1)}, u32[]{:S(2)}, u32[]{:S(2)}) collective-permute-start(bf16[64,3584]{1,0:T(8,128)(2,1)S(1)} %get-tuple-element.59), channel_id=1, source_target_pairs={{0,4},{1,5},{4,8},{5,9},{8,12},{9,13},{12,14},{13,15},{14,10},{15,... | collective-permute-start | bytes 1376264 | tf_op jit(solution)/shard_map/ppermute | solution.py:94
  99.1 23.0 %collective-permute-start.19 = (bf16[64,3584]{1,0:T(8,128)(2,1)S(1)}, bf16[64,3584]{1,0:T(8,128)(2,1)S(1)}, u32[]{:S(2)}, u32[]{:S(2)}) collective-permute-start(bf16[64,3584]{1,0:T(8,128)(2,1)S(1)} %get-tuple-element.61), channel_id=1, source_target_pairs={{0,4},{1,5},{4,8},{5,9},{8,12},{9,13},{12,14},{13,15},{14,10},{15,... | collective-permute-start | bytes 1376264 | tf_op jit(solution)/shard_map/ppermute | solution.py:94
  106.0 17.1 %collective-permute-start.16 = (bf16[64,3584]{1,0:T(8,128)(2,1)S(1)}, bf16[64,3584]{1,0:T(8,128)(2,1)S(1)}, u32[]{:S(2)}, u32[]{:S(2)}) collective-permute-start(bf16[64,3584]{1,0:T(8,128)(2,1)S(1)} %get-tuple-element.60), channel_id=1, source_target_pairs={{0,2},{1,3},{4,0},{5,1},{8,4},{9,5},{12,8},{13,9},{14,12},{15,13},... | collective-permute-start | bytes 1376264 | tf_op jit(solution)/shard_map/ppermute | solution.py:94
  110.3 19.1 %collective-permute-start.23 = (bf16[64,3584]{1,0:T(8,128)(2,1)S(1)}, bf16[64,3584]{1,0:T(8,128)(2,1)S(1)}, u32[]{:S(2)}, u32[]{:S(2)}) collective-permute-start(bf16[64,3584]{1,0:T(8,128)(2,1)S(1)} %shard_map.107), channel_id=1, source_target_pairs={{0,2},{1,3},{4,0},{5,1},{8,4},{9,5},{12,8},{13,9},{14,12},{15,13},... | collective-permute-start | bytes 1376264 | tf_op jit(solution)/shard_map/ppermute | solution.py:94
  113.4 19.0 %collective-permute-start.13 = (bf16[64,3584]{1,0:T(8,128)(2,1)S(1)}, bf16[64,3584]{1,0:T(8,128)(2,1)S(1)}, u32[]{:S(2)}, u32[]{:S(2)}) collective-permute-start(bf16[64,3584]{1,0:T(8,128)(2,1)S(1)} %shard_map.100), channel_id=1, source_target_pairs={{0,4},{1,5},{4,8},{5,9},{8,12},{9,13},{12,14},{13,15},{14,10},{15,... | collective-permute-start | bytes 1376264 | tf_op jit(solution)/shard_map/ppermute | solution.py:94
  122.8 19.0 %collective-permute-start.20 = (bf16[64,3584]{1,0:T(8,128)(2,1)S(1)}, bf16[64,3584]{1,0:T(8,128)(2,1)S(1)}, u32[]{:S(2)}, u32[]{:S(2)}) collective-permute-start(bf16[64,3584]{1,0:T(8,128)(2,1)S(1)} %shard_map.105), channel_id=1, source_target_pairs={{0,4},{1,5},{4,8},{5,9},{8,12},{9,13},{12,14},{13,15},{14,10},{15,... | collective-permute-start | bytes 1376264 | tf_op jit(solution)/shard_map/ppermute | solution.py:94
  123.8 19.0 %collective-permute-start.17 = (bf16[64,3584]{1,0:T(8,128)(2,1)S(1)}, bf16[64,3584]{1,0:T(8,128)(2,1)S(1)}, u32[]{:S(2)}, u32[]{:S(2)}) collective-permute-start(bf16[64,3584]{1,0:T(8,128)(2,1)S(1)} %shard_map.103), channel_id=1, source_target_pairs={{0,2},{1,3},{4,0},{5,1},{8,4},{9,5},{12,8},{13,9},{14,12},{15,13},... | collective-permute-start | bytes 1376264 | tf_op jit(solution)/shard_map/ppermute | solution.py:94
  130.0 19.0 %collective-permute-start.24 = (bf16[64,3584]{1,0:T(8,128)(2,1)S(1)}, bf16[64,3584]{1,0:T(8,128)(2,1)S(1)}, u32[]{:S(2)}, u32[]{:S(2)}) collective-permute-start(bf16[64,3584]{1,0:T(8,128)(2,1)S(1)} %shard_map.108), channel_id=1, source_target_pairs={{0,2},{1,3},{4,0},{5,1},{8,4},{9,5},{12,8},{13,9},{14,12},{15,13},... | collective-permute-start | bytes 1376264 | tf_op jit(solution)/shard_map/ppermute | solution.py:94
  133.1 19.0 %collective-permute-start.14 = (bf16[64,3584]{1,0:T(8,128)(2,1)S(1)}, bf16[64,3584]{1,0:T(8,128)(2,1)S(1)}, u32[]{:S(2)}, u32[]{:S(2)}) collective-permute-start(bf16[64,3584]{1,0:T(8,128)(2,1)S(1)} %shard_map.101), channel_id=1, source_target_pairs={{0,4},{1,5},{4,8},{5,9},{8,12},{9,13},{12,14},{13,15},{14,10},{15,... | collective-permute-start | bytes 1376264 | tf_op jit(solution)/shard_map/ppermute | solution.py:94
  142.4 19.0 %collective-permute-start.21 = (bf16[64,3584]{1,0:T(8,128)(2,1)S(1)}, bf16[64,3584]{1,0:T(8,128)(2,1)S(1)}, u32[]{:S(2)}, u32[]{:S(2)}) collective-permute-start(bf16[64,3584]{1,0:T(8,128)(2,1)S(1)} %shard_map.106), channel_id=1, source_target_pairs={{0,4},{1,5},{4,8},{5,9},{8,12},{9,13},{12,14},{13,15},{14,10},{15,... | collective-permute-start | bytes 1376264 | tf_op jit(solution)/shard_map/ppermute | solution.py:94
  143.4 18.0 %collective-permute-start.18 = (bf16[64,3584]{1,0:T(8,128)(2,1)S(1)}, bf16[64,3584]{1,0:T(8,128)(2,1)S(1)}, u32[]{:S(2)}, u32[]{:S(2)}) collective-permute-start(bf16[64,3584]{1,0:T(8,128)(2,1)S(1)} %shard_map.104), channel_id=1, source_target_pairs={{0,2},{1,3},{4,0},{5,1},{8,4},{9,5},{12,8},{13,9},{14,12},{15,13},... | collective-permute-start | bytes 1376264 | tf_op jit(solution)/shard_map/ppermute | solution.py:94
  149.7 16.4 %collective-permute-start.25 = (bf16[64,3584]{1,0:T(8,128)(2,1)S(1)}, bf16[64,3584]{1,0:T(8,128)(2,1)S(1)}, u32[]{:S(2)}, u32[]{:S(2)}) collective-permute-start(bf16[64,3584]{1,0:T(8,128)(2,1)S(1)} %shard_map.109), channel_id=1, source_target_pairs={{0,2},{1,3},{4,0},{5,1},{8,4},{9,5},{12,8},{13,9},{14,12},{15,13},... | collective-permute-start | bytes 1376264 | tf_op jit(solution)/shard_map/ppermute | solution.py:94
  152.8 15.0 %collective-permute-start.15 = (bf16[64,3584]{1,0:T(8,128)(2,1)S(1)}, bf16[64,3584]{1,0:T(8,128)(2,1)S(1)}, u32[]{:S(2)}, u32[]{:S(2)}) collective-permute-start(bf16[64,3584]{1,0:T(8,128)(2,1)S(1)} %shard_map.102), channel_id=1, source_target_pairs={{0,4},{1,5},{4,8},{5,9},{8,12},{9,13},{12,14},{13,15},{14,10},{15,... | collective-permute-start | bytes 1376264 | tf_op jit(solution)/shard_map/ppermute | solution.py:94

commit v16 on v12

--- a/solution.py
+++ b/solution.py
@@ -282,13 +282,15 @@
                 scale = scale_ref[where_ref[positions[b]]]
                 scaled.append((values * scale).astype(jnp.bfloat16))
         acts = {}
+        spans = [slice(at, at + size) for at, size in zip(starts, sizes)]
+        if last:
+            scaled, spans = [jnp.concatenate(scaled, axis=0)], [slice(0, tokens)]
         for which in range(4):
             cols = slice(which * hidden_here, (which + 1) * hidden_here)
             for b in range(count):
                 if not last:
                     copies[which, b].wait()
-            for k, size in enumerate(sizes):
-                span = slice(starts[k], starts[k] + size)
+            for k, span in enumerate(spans):
                 total = None if first else acc_in[span, cols]
                 for b in range(count):
                     if last:

time: 163 us -> 162 us (level)
  no operation moved by 1% of the time
where the time goes in v16:
time: 162 us
  waiting for transfers between devices  89.4 us (55%)
  Pallas kernels  44.7 us (28%)
  starting transfers between devices  24.6 us (15%)
  other arithmetic  1.82 us (1%)
    ppermute x22, waiting for transfers between devices, ring_shift(): return lax.ppermute(value, 'ep', pairs)  87.8 us
    pallas_call x20, Pallas kernels, local_call(): pl.pallas_call(kernel, out_shape=out_shape, in_specs=[IN_SMEM if value.nd...  44.7 us
    ppermute x22, starting transfers between devices, ring_shift(): return lax.ppermute(value, 'ep', pairs)  23.2 us
  transfers between devices with their start and end apart: 26, of which 18 were waited for; matrix products, arithmetic and copies ran while one was open for 1% of the time, Pallas kernels for 24%

profile of v16, /device:TPU:0, one launch (start us, length us, event | category | flops | bytes accessed | tf_op | source)
XLA Modules:
  0.0 162.2 jit_solution(10096142062845531298)
XLA Ops:
  0.0 1.8 %add_convert_fusion = bf16[1024,448]{0,1:T(8,128)(2,1)S(1)} fusion(bf16[1024,448]{0,1:T(8,128)(2,1)} %param.10, bf16[1024,448]{0,1:T(8,128)(2,1)} %param.9), kind=kLoop, calls=%fused_computation | loop fusion | flops 1835008 | bytes 2752512 | tf_op jit(solution)/shard_map/convert_element_type | solution.py:475
  1.8 0.5 copy.13
  2.4 0.5 collective-permute-start
  3.0 1.5 collective-permute-done.swapped_ref
  4.5 0.4 collective-permute-start.1
  5.0 0.4 collective-permute-start.9
  5.6 0.7 shard_map.91.refs_0_.refs_5_
  6.3 2.8 %collective-permute-start.4 = (bf16[528,896]{1,0:T(8,128)(2,1)S(1)}, bf16[528,896]{1,0:T(8,128)(2,1)S(1)}, u32[]{:S(2)}, u32[]{:S(2)}) collective-permute-start(bf16[528,896]{1,0:T(8,128)(2,1)S(1)} %shard_map.91.refs_0_.refs_5_), channel_id=1, source_target_pairs={{0,4},{1,5},{4,8},{5,9},{8,12},{9,13},{12,14},{13,15},{14,10},{15,... | collective-permute-start | bytes 2838536 | tf_op jit(solution)/shard_map/ppermute | solution.py:94
  9.1 21.4 %collective-permute-done.4.refs_1_.refs_12_ = bf16[528,896]{1,0:T(8,128)(2,1)S(1)} collective-permute-done((bf16[528,896]{1,0:T(8,128)(2,1)S(1)}, bf16[528,896]{1,0:T(8,128)(2,1)S(1)}, u32[]{:S(2)}, u32[]{:S(2)}) %collective-permute-start.4) | collective-permute-done | bytes 946208 | tf_op jit(solution)/shard_map/ppermute | solution.py:94
  30.5 1.8 %collective-permute-start.6 = (bf16[528,896]{1,0:T(8,128)(2,1)S(1)}, bf16[528,896]{1,0:T(8,128)(2,1)}, u32[]{:S(2)}, u32[]{:S(2)}) collective-permute-start(bf16[528,896]{1,0:T(8,128)(2,1)S(1)} %collective-permute-done.4.refs_1_.refs_12_), channel_id=1, source_target_pairs={{0,4},{1,5},{4,8},{5,9},{8,12},{9,13},{12,14},{13,15},{14,10},{15,... | collective-permute-start | bytes 2838536 | tf_op jit(solution)/shard_map/ppermute | solution.py:94
  32.3 0.2 collective-permute-start.5
  32.5 0.7 dynamic-slice_bitcast_fusion.1.where_ref
  33.2 20.1 %collective-permute-done.6.refs_1_.refs_11_ = bf16[528,896]{1,0:T(8,128)(2,1)} collective-permute-done((bf16[528,896]{1,0:T(8,128)(2,1)S(1)}, bf16[528,896]{1,0:T(8,128)(2,1)}, u32[]{:S(2)}, u32[]{:S(2)}) %collective-permute-start.6) | collective-permute-done | bytes 946208 | tf_op jit(solution)/shard_map/ppermute | solution.py:94
  53.3 1.6 collective-permute-start.8
  54.8 0.5 collective-permute-start.7
  55.3 4.4 %shard_map.92 = (bf16[64,896]{1,0:T(8,128)(2,1)S(1)}, f32[512,1024]{1,0:T(8,128)S(1)}) custom-call(s32[9]{0:T(128)S(1)} %dynamic-slice_bitcast_fusion.1.where_ref, bf16[528,896]{1,0:T(8,128)(2,1)S(1)} %shard_map.91.refs_0_.refs_5_, f32[8,1,896]{2,1,0:T(1,128)S(1)} %bitcast.8, bf16[7168,256]{1,0:T(8,128)(2,1)} %refs_3_.3, bf16[7168,256]{1,0:T(8,128)(2,1)} %refs_4_.2, ...), custom_call_target="tpu_custom_call" | custom-call | flops 2818572288 | bytes 6946816 | tf_op jit(solution)/shard_map/pallas_call | solution.py:107
  59.7 6.8 %shard_map.93 = (bf16[64,896]{1,0:T(8,128)(2,1)S(1)}, bf16[64,896]{1,0:T(8,128)(2,1)S(1)}, f32[512,1024]{1,0:T(8,128)S(1)}) custom-call(s32[9]{0:T(128)S(1)} %dynamic-slice_bitcast_fusion.1.where_ref, bf16[528,896]{1,0:T(8,128)(2,1)S(1)} %collective-permute-done.3.refs_0_.refs_6_, ...), custom_call_target="tpu_custom_call", output_to_operand_aliasing={{2}: (8, {})} | custom-call | flops 5637144576 | bytes 9699328 | tf_op jit(solution)/shard_map/pallas_call | solution.py:107
  66.5 7.7 %shard_map.94 = (bf16[64,896]{1,0:T(8,128)(2,1)S(1)}, bf16[64,896]{1,0:T(8,128)(2,1)S(1)}, f32[512,1024]{1,0:T(8,128)S(1)}) custom-call(s32[9]{0:T(128)S(1)} %dynamic-slice_bitcast_fusion.1.where_ref, bf16[528,896]{1,0:T(8,128)(2,1)} %collective-permute-done.5.refs_0_.refs_7_, ...), custom_call_target="tpu_custom_call", output_to_operand_aliasing={{2}: (8, {})} | custom-call | flops 5637144576 | bytes 9699328 | tf_op jit(solution)/shard_map/pallas_call | solution.py:107
  74.2 1.0 collective-permute-done.8.refs_1_.refs_10_
  75.3 1.0 collective-permute-done.7.refs_0_.refs_8_
  76.3 0.8 collective-permute-start.11
  77.2 1.3 collective-permute-start.10
  78.5 6.8 %shard_map.95 = (bf16[64,896]{1,0:T(8,128)(2,1)S(1)}, bf16[64,896]{1,0:T(8,128)(2,1)S(1)}, f32[512,1024]{1,0:T(8,128)S(1)}, bf16[4,896,256]{2,1,0:T(8,128)(2,1)S(1)}, bf16[512,7168]{1,0:T(8,128)(2,1)S(1)}) custom-call(s32[9]{0:T(128)S(1)} %dynamic-slice_bitcast_fusion.1.where_ref, ...), custom_call_target="tpu_custom_call", output_to_operand_aliasing={{2}: (8, {})} | custom-call | flops 5637144576 | bytes 9699328 | tf_op jit(solution)/shard_map/pallas_call | solution.py:107
  85.3 1.0 collective-permute-done.11.refs_1_
  86.2 1.4 collective-permute-done.10.refs_0_.refs_9_
  87.7 4.0 %shard_map.96 = (bf16[64,896]{1,0:T(8,128)(2,1)S(1)}, bf16[512,512]{1,0:T(8,128)(2,1)S(1)}, bf16[64,3584]{1,0:T(8,128)(2,1)S(1)}, bf16[64,3584]{1,0:T(8,128)(2,1...) custom-call(s32[9]{0:T(128)S(1)} %dynamic-slice_bitcast_fusion.1.where_ref, ...), custom_call_target="tpu_custom_call" | custom-call | flops 2818572288 | bytes 6946816 | tf_op jit(solution)/shard_map/pallas_call | solution.py:107
  91.7 1.1 collective-permute-start.22
  92.8 1.0 collective-permute-start.12
  93.8 0.6 shard_map.97.stream_ref
  94.4 1.1 collective-permute-start.19
  95.5 2.6 %shard_map.99.table_ref.refs_1_ = bf16[512,3584]{1,0:T(8,128)(2,1)S(1)} custom-call(s32[9]{0:T(128)S(1)} %dynamic-slice_bitcast_fusion.1.where_ref, bf16[512,512]{1,0:T(8,128)(2,1)S(1)} %get-tuple-element.56.hidden_ref, bf16[512,7168]{1,0:T(8,128)(2,1)S(1)} %get-tuple-element.52.refs_13_.down_ref), custom_call_target="tpu_custom_call" | custom-call | flops 1879048192 | bytes 7340032 | tf_op jit(solution)/shard_map/pallas_call | solution.py:107
  98.1 2.6 %shard_map.98.table_ref.refs_0_ = bf16[512,3584]{1,0:T(8,128)(2,1)S(1)} custom-call(s32[9]{0:T(128)S(1)} %dynamic-slice_bitcast_fusion.1.where_ref, bf16[512,512]{1,0:T(8,128)(2,1)S(1)} %get-tuple-element.56.hidden_ref, bf16[512,7168]{1,0:T(8,128)(2,1)S(1)} %get-tuple-element.52.refs_13_.down_ref), custom_call_target="tpu_custom_call" | custom-call | flops 1879048192 | bytes 7340032 | tf_op jit(solution)/shard_map/pallas_call | solution.py:107
  100.7 1.1 collective-permute-start.16
  101.8 0.8 collective-permute-done.22.moved_ref
  102.6 0.6 shard_map.107
  103.3 0.5 collective-permute-start.23
  103.8 2.5 %collective-permute-done.12.moved_ref = bf16[64,3584]{1,0:T(8,128)(2,1)S(1)} collective-permute-done((bf16[64,3584]{1,0:T(8,128)(2,1)S(1)}, bf16[64,3584]{1,0:T(8,128)(2,1)S(1)}, u32[]{:S(2)}, u32[]{:S(2)}) %collective-permute-start.12) | collective-permute-done | bytes 458784 | tf_op jit(solution)/shard_map/ppermute | solution.py:94
  106.3 0.6 shard_map.100
  106.9 1.0 collective-permute-start.13
  108.0 8.1 %collective-permute-done.19.moved_ref = bf16[64,3584]{1,0:T(8,128)(2,1)S(1)} collective-permute-done((bf16[64,3584]{1,0:T(8,128)(2,1)S(1)}, bf16[64,3584]{1,0:T(8,128)(2,1)S(1)}, u32[]{:S(2)}, u32[]{:S(2)}) %collective-permute-start.19) | collective-permute-done | bytes 458784 | tf_op jit(solution)/shard_map/ppermute | solution.py:94
  116.1 0.6 shard_map.105
  116.8 1.0 collective-permute-start.20
  117.8 0.6 shard_map.103
  118.5 1.1 collective-permute-start.17
  119.6 4.5 %collective-permute-done.23.moved_ref = bf16[64,3584]{1,0:T(8,128)(2,1)S(1)} collective-permute-done((bf16[64,3584]{1,0:T(8,128)(2,1)S(1)}, bf16[64,3584]{1,0:T(8,128)(2,1)S(1)}, u32[]{:S(2)}, u32[]{:S(2)}) %collective-permute-start.23) | collective-permute-done | bytes 458784 | tf_op jit(solution)/shard_map/ppermute | solution.py:94
  124.1 0.6 shard_map.108
  124.7 1.1 collective-permute-start.24
  125.8 0.2 collective-permute-done.13.moved_ref
  125.9 0.6 shard_map.101
  126.6 1.0 collective-permute-start.14
  127.6 8.1 %collective-permute-done.20.moved_ref = bf16[64,3584]{1,0:T(8,128)(2,1)S(1)} collective-permute-done((bf16[64,3584]{1,0:T(8,128)(2,1)S(1)}, bf16[64,3584]{1,0:T(8,128)(2,1)S(1)}, u32[]{:S(2)}, u32[]{:S(2)}) %collective-permute-start.20) | collective-permute-done | bytes 458784 | tf_op jit(solution)/shard_map/ppermute | solution.py:94
  135.8 0.6 shard_map.106
  136.4 1.0 collective-permute-start.21
  137.5 0.6 shard_map.104
  138.1 1.1 collective-permute-start.18
  139.2 4.5 %collective-permute-done.24.moved_ref = bf16[64,3584]{1,0:T(8,128)(2,1)S(1)} collective-permute-done((bf16[64,3584]{1,0:T(8,128)(2,1)S(1)}, bf16[64,3584]{1,0:T(8,128)(2,1)S(1)}, u32[]{:S(2)}, u32[]{:S(2)}) %collective-permute-start.24) | collective-permute-done | bytes 458784 | tf_op jit(solution)/shard_map/ppermute | solution.py:94
  143.7 0.6 shard_map.109
  144.4 1.1 collective-permute-start.25
  145.6 0.6 shard_map.102
  146.3 1.0 collective-permute-start.15
  147.3 8.1 %collective-permute-done.21.refs_4_ = bf16[64,3584]{1,0:T(8,128)(2,1)S(1)} collective-permute-done((bf16[64,3584]{1,0:T(8,128)(2,1)S(1)}, bf16[64,3584]{1,0:T(8,128)(2,1)S(1)}, u32[]{:S(2)}, u32[]{:S(2)}) %collective-permute-start.21) | collective-permute-done | bytes 458784 | tf_op jit(solution)/shard_map/ppermute | solution.py:94
  155.4 4.3 %collective-permute-done.25.refs_5_ = bf16[64,3584]{1,0:T(8,128)(2,1)S(1)} collective-permute-done((bf16[64,3584]{1,0:T(8,128)(2,1)S(1)}, bf16[64,3584]{1,0:T(8,128)(2,1)S(1)}, u32[]{:S(2)}, u32[]{:S(2)}) %collective-permute-start.25) | collective-permute-done | bytes 458784 | tf_op jit(solution)/shard_map/ppermute | solution.py:94
  159.7 0.6 collective-permute-done.15.refs_2_
  160.3 1.9 %shard_map.110 = bf16[64,7168]{1,0:T(8,128)(2,1)} custom-call(s32[9]{0:T(128)S(1)} %dynamic-slice_bitcast_fusion.1.where_ref, bf16[64,7168]{1,0:T(8,128)(2,1)S(1)} %shard_map.97.stream_ref, bf16[512,3584]{1,0:T(8,128)(2,1)S(1)} %shard_map.98.table_ref.refs_0_, bf16[512,3584]{1,0:T(8,128)(2,1)S(1)} %shard_map.99.table_ref.refs_1_, ...), custom_call_target="tpu_custom_call" | custom-call | flops 1376256 | bytes 4587520 | tf_op jit(solution)/shard_map/pallas_call | solution.py:107
  (22 shorter events, 0.6 us)
Async XLA Ops:
  0.0 5.4 %copy-start.1 = (s32[64,2]{0,1:T(2,128)S(1)}, s32[64,2]{0,1:T(2,128)}, u32[]{:S(2)}) copy-start(s32[64,2]{0,1:T(2,128)} %param.12) | copy-start | bytes 1540
  0.0 5.5 %copy-start.2 = (f32[64,2]{0,1:T(2,128)S(1)}, f32[64,2]{0,1:T(2,128)}, u32[]{:S(2)}) copy-start(f32[64,2]{0,1:T(2,128)} %param.13) | copy-start | bytes 1540
  0.0 55.3 %copy-start = (f32[7168]{0:T(1024)S(1)}, f32[7168]{0:T(1024)}, u32[]{:S(2)}) copy-start(f32[7168]{0:T(1024)} %param.11) | copy-start | bytes 86020
  2.4 2.1 %collective-permute-start = (bf16[8,64,448]{2,1,0:T(8,128)(2,1)S(1)}, bf16[8,64,448]{2,1,0:T(8,128)(2,1)S(1)}, u32[]{:S(2)}, u32[]{:S(2)}) collective-permute-start(bf16[8,64,448]{2,1,0:T(8,128)(2,1)S(1)} %dynamic-slice_bitcast_fusion), channel_id=1, source_target_pairs={{0,1},{1,0},{2,3},{3,2},{4,5},{5,4},{6,7},{7,6},{8,9},{9,8},{10,11... | collective-permute-start | bytes 1376264 | tf_op jit(solution)/shard_map/ppermute | solution.py:84
  4.5 50.8 %collective-permute-start.1 = (bf16[7168,256]{1,0:T(8,128)(2,1)}, bf16[7168,256]{1,0:T(8,128)(2,1)}, u32[]{:S(2)}, u32[]{:S(2)}) collective-permute-start(bf16[7168,256]{1,0:T(8,128)(2,1)} %refs_3_.3), channel_id=1, source_target_pairs={{0,1},{1,0},{2,3},{3,2},{4,5},{5,4},{6,7},{7,6},{8,9},{9,8},{10,11... | collective-permute-start | bytes 11010056 | tf_op jit(solution)/shard_map/ppermute | solution.py:84
  4.9 50.4 %collective-permute-start.2 = (bf16[7168,256]{1,0:T(8,128)(2,1)}, bf16[7168,256]{1,0:T(8,128)(2,1)}, u32[]{:S(2)}, u32[]{:S(2)}) collective-permute-start(bf16[7168,256]{1,0:T(8,128)(2,1)} %refs_4_.2), channel_id=1, source_target_pairs={{0,1},{1,0},{2,3},{3,2},{4,5},{5,4},{6,7},{7,6},{8,9},{9,8},{10,11... | collective-permute-start | bytes 11010056 | tf_op jit(solution)/shard_map/ppermute | solution.py:84
  5.0 73.5 %collective-permute-start.9 = (bf16[256,7168]{1,0:T(8,128)(2,1)}, bf16[256,7168]{1,0:T(8,128)(2,1)}, u32[]{:S(2)}, u32[]{:S(2)}) collective-permute-start(bf16[256,7168]{1,0:T(8,128)(2,1)} %refs_8_), channel_id=1, source_target_pairs={{0,1},{1,0},{2,3},{3,2},{4,5},{5,4},{6,7},{7,6},{8,9},{9,8},{10,11... | collective-permute-start | bytes 11010056 | tf_op jit(solution)/shard_map/ppermute | solution.py:84
  6.3 24.2 %collective-permute-start.4 = (bf16[528,896]{1,0:T(8,128)(2,1)S(1)}, bf16[528,896]{1,0:T(8,128)(2,1)S(1)}, u32[]{:S(2)}, u32[]{:S(2)}) collective-permute-start(bf16[528,896]{1,0:T(8,128)(2,1)S(1)} %shard_map.91.refs_0_.refs_5_), channel_id=1, source_target_pairs={{0,4},{1,5},{4,8},{5,9},{8,12},{9,13},{12,14},{13,15},{14,10},{15,... | collective-permute-start | bytes 2838536 | tf_op jit(solution)/shard_map/ppermute | solution.py:94
  9.1 23.2 %collective-permute-start.3 = (bf16[528,896]{1,0:T(8,128)(2,1)S(1)}, bf16[528,896]{1,0:T(8,128)(2,1)S(1)}, u32[]{:S(2)}, u32[]{:S(2)}) collective-permute-start(bf16[528,896]{1,0:T(8,128)(2,1)S(1)} %shard_map.91.refs_0_.refs_5_), channel_id=1, source_target_pairs={{0,2},{1,3},{4,0},{5,1},{8,4},{9,5},{12,8},{13,9},{14,12},{15,13},... | collective-permute-start | bytes 2838536 | tf_op jit(solution)/shard_map/ppermute | solution.py:94
  30.5 22.8 %collective-permute-start.6 = (bf16[528,896]{1,0:T(8,128)(2,1)S(1)}, bf16[528,896]{1,0:T(8,128)(2,1)}, u32[]{:S(2)}, u32[]{:S(2)}) collective-permute-start(bf16[528,896]{1,0:T(8,128)(2,1)S(1)} %collective-permute-done.4.refs_1_.refs_12_), channel_id=1, source_target_pairs={{0,4},{1,5},{4,8},{5,9},{8,12},{9,13},{12,14},{13,15},{14,10},{15,... | collective-permute-start | bytes 2838536 | tf_op jit(solution)/shard_map/ppermute | solution.py:94
  32.3 22.5 %collective-permute-start.5 = (bf16[528,896]{1,0:T(8,128)(2,1)S(1)}, bf16[528,896]{1,0:T(8,128)(2,1)}, u32[]{:S(2)}, u32[]{:S(2)}) collective-permute-start(bf16[528,896]{1,0:T(8,128)(2,1)S(1)} %collective-permute-done.3.refs_0_.refs_6_), channel_id=1, source_target_pairs={{0,2},{1,3},{4,0},{5,1},{8,4},{9,5},{12,8},{13,9},{14,12},{15,13},... | collective-permute-start | bytes 2838536 | tf_op jit(solution)/shard_map/ppermute | solution.py:94
  53.3 22.0 %collective-permute-start.8 = (bf16[528,896]{1,0:T(8,128)(2,1)}, bf16[528,896]{1,0:T(8,128)(2,1)S(1)}, u32[]{:S(2)}, u32[]{:S(2)}) collective-permute-start(bf16[528,896]{1,0:T(8,128)(2,1)} %collective-permute-done.6.refs_1_.refs_11_), channel_id=1, source_target_pairs={{0,4},{1,5},{4,8},{5,9},{8,12},{9,13},{12,14},{13,15},{14,10},{15,... | collective-permute-start | bytes 2838536 | tf_op jit(solution)/shard_map/ppermute | solution.py:94
  54.8 21.4 %collective-permute-start.7 = (bf16[528,896]{1,0:T(8,128)(2,1)}, bf16[528,896]{1,0:T(8,128)(2,1)S(1)}, u32[]{:S(2)}, u32[]{:S(2)}) collective-permute-start(bf16[528,896]{1,0:T(8,128)(2,1)} %collective-permute-done.5.refs_0_.refs_7_), channel_id=1, source_target_pairs={{0,2},{1,3},{4,0},{5,1},{8,4},{9,5},{12,8},{13,9},{14,12},{15,13},... | collective-permute-start | bytes 2838536 | tf_op jit(solution)/shard_map/ppermute | solution.py:94
  76.3 9.9 %collective-permute-start.11 = (bf16[256,896]{1,0:T(8,128)(2,1)S(1)}, bf16[256,896]{1,0:T(8,128)(2,1)S(1)}, u32[]{:S(2)}, u32[]{:S(2)}) collective-permute-start(bf16[256,896]{1,0:T(8,128)(2,1)S(1)} %slice.7), channel_id=1, source_target_pairs={{0,2},{1,3},{4,0},{5,1},{8,4},{9,5},{12,8},{13,9},{14,12},{15,13},... | collective-permute-start | bytes 1376264 | tf_op jit(solution)/shard_map/ppermute | solution.py:94
  77.2 10.5 %collective-permute-start.10 = (bf16[272,896]{1,0:T(8,128)(2,1)S(1)}, bf16[272,896]{1,0:T(8,128)(2,1)S(1)}, u32[]{:S(2)}, u32[]{:S(2)}) collective-permute-start(bf16[272,896]{1,0:T(8,128)(2,1)S(1)} %slice.6), channel_id=1, source_target_pairs={{0,4},{1,5},{4,8},{5,9},{8,12},{9,13},{12,14},{13,15},{14,10},{15,... | collective-permute-start | bytes 1462280 | tf_op jit(solution)/shard_map/ppermute | solution.py:94
  91.7 10.9 %collective-permute-start.22 = (bf16[64,3584]{1,0:T(8,128)(2,1)S(1)}, bf16[64,3584]{1,0:T(8,128)(2,1)S(1)}, u32[]{:S(2)}, u32[]{:S(2)}) collective-permute-start(bf16[64,3584]{1,0:T(8,128)(2,1)S(1)} %get-tuple-element.60), channel_id=1, source_target_pairs={{0,2},{1,3},{4,0},{5,1},{8,4},{9,5},{12,8},{13,9},{14,12},{15,13},... | collective-permute-start | bytes 1376264 | tf_op jit(solution)/shard_map/ppermute | solution.py:94
  92.8 13.5 %collective-permute-start.12 = (bf16[64,3584]{1,0:T(8,128)(2,1)S(1)}, bf16[64,3584]{1,0:T(8,128)(2,1)S(1)}, u32[]{:S(2)}, u32[]{:S(2)}) collective-permute-start(bf16[64,3584]{1,0:T(8,128)(2,1)S(1)} %get-tuple-element.57), channel_id=1, source_target_pairs={{0,4},{1,5},{4,8},{5,9},{8,12},{9,13},{12,14},{13,15},{14,10},{15,... | collective-permute-start | bytes 1376264 | tf_op jit(solution)/shard_map/ppermute | solution.py:94
  94.4 21.7 %collective-permute-start.19 = (bf16[64,3584]{1,0:T(8,128)(2,1)S(1)}, bf16[64,3584]{1,0:T(8,128)(2,1)S(1)}, u32[]{:S(2)}, u32[]{:S(2)}) collective-permute-start(bf16[64,3584]{1,0:T(8,128)(2,1)S(1)} %get-tuple-element.59), channel_id=1, source_target_pairs={{0,4},{1,5},{4,8},{5,9},{8,12},{9,13},{12,14},{13,15},{14,10},{15,... | collective-permute-start | bytes 1376264 | tf_op jit(solution)/shard_map/ppermute | solution.py:94
  100.7 17.1 %collective-permute-start.16 = (bf16[64,3584]{1,0:T(8,128)(2,1)S(1)}, bf16[64,3584]{1,0:T(8,128)(2,1)S(1)}, u32[]{:S(2)}, u32[]{:S(2)}) collective-permute-start(bf16[64,3584]{1,0:T(8,128)(2,1)S(1)} %get-tuple-element.58), channel_id=1, source_target_pairs={{0,2},{1,3},{4,0},{5,1},{8,4},{9,5},{12,8},{13,9},{14,12},{15,13},... | collective-permute-start | bytes 1376264 | tf_op jit(solution)/shard_map/ppermute | solution.py:94
  103.3 20.8 %collective-permute-start.23 = (bf16[64,3584]{1,0:T(8,128)(2,1)S(1)}, bf16[64,3584]{1,0:T(8,128)(2,1)S(1)}, u32[]{:S(2)}, u32[]{:S(2)}) collective-permute-start(bf16[64,3584]{1,0:T(8,128)(2,1)S(1)} %shard_map.107), channel_id=1, source_target_pairs={{0,2},{1,3},{4,0},{5,1},{8,4},{9,5},{12,8},{13,9},{14,12},{15,13},... | collective-permute-start | bytes 1376264 | tf_op jit(solution)/shard_map/ppermute | solution.py:94
  106.9 19.0 %collective-permute-start.13 = (bf16[64,3584]{1,0:T(8,128)(2,1)S(1)}, bf16[64,3584]{1,0:T(8,128)(2,1)S(1)}, u32[]{:S(2)}, u32[]{:S(2)}) collective-permute-start(bf16[64,3584]{1,0:T(8,128)(2,1)S(1)} %shard_map.100), channel_id=1, source_target_pairs={{0,4},{1,5},{4,8},{5,9},{8,12},{9,13},{12,14},{13,15},{14,10},{15,... | collective-permute-start | bytes 1376264 | tf_op jit(solution)/shard_map/ppermute | solution.py:94
  116.8 19.0 %collective-permute-start.20 = (bf16[64,3584]{1,0:T(8,128)(2,1)S(1)}, bf16[64,3584]{1,0:T(8,128)(2,1)S(1)}, u32[]{:S(2)}, u32[]{:S(2)}) collective-permute-start(bf16[64,3584]{1,0:T(8,128)(2,1)S(1)} %shard_map.105), channel_id=1, source_target_pairs={{0,4},{1,5},{4,8},{5,9},{8,12},{9,13},{12,14},{13,15},{14,10},{15,... | collective-permute-start | bytes 1376264 | tf_op jit(solution)/shard_map/ppermute | solution.py:94
  118.5 19.0 %collective-permute-start.17 = (bf16[64,3584]{1,0:T(8,128)(2,1)S(1)}, bf16[64,3584]{1,0:T(8,128)(2,1)S(1)}, u32[]{:S(2)}, u32[]{:S(2)}) collective-permute-start(bf16[64,3584]{1,0:T(8,128)(2,1)S(1)} %shard_map.103), channel_id=1, source_target_pairs={{0,2},{1,3},{4,0},{5,1},{8,4},{9,5},{12,8},{13,9},{14,12},{15,13},... | collective-permute-start | bytes 1376264 | tf_op jit(solution)/shard_map/ppermute | solution.py:94
  124.7 19.0 %collective-permute-start.24 = (bf16[64,3584]{1,0:T(8,128)(2,1)S(1)}, bf16[64,3584]{1,0:T(8,128)(2,1)S(1)}, u32[]{:S(2)}, u32[]{:S(2)}) collective-permute-start(bf16[64,3584]{1,0:T(8,128)(2,1)S(1)} %shard_map.108), channel_id=1, source_target_pairs={{0,2},{1,3},{4,0},{5,1},{8,4},{9,5},{12,8},{13,9},{14,12},{15,13},... | collective-permute-start | bytes 1376264 | tf_op jit(solution)/shard_map/ppermute | solution.py:94
  126.6 19.0 %collective-permute-start.14 = (bf16[64,3584]{1,0:T(8,128)(2,1)S(1)}, bf16[64,3584]{1,0:T(8,128)(2,1)S(1)}, u32[]{:S(2)}, u32[]{:S(2)}) collective-permute-start(bf16[64,3584]{1,0:T(8,128)(2,1)S(1)} %shard_map.101), channel_id=1, source_target_pairs={{0,4},{1,5},{4,8},{5,9},{8,12},{9,13},{12,14},{13,15},{14,10},{15,... | collective-permute-start | bytes 1376264 | tf_op jit(solution)/shard_map/ppermute | solution.py:94
  136.4 19.0 %collective-permute-start.21 = (bf16[64,3584]{1,0:T(8,128)(2,1)S(1)}, bf16[64,3584]{1,0:T(8,128)(2,1)S(1)}, u32[]{:S(2)}, u32[]{:S(2)}) collective-permute-start(bf16[64,3584]{1,0:T(8,128)(2,1)S(1)} %shard_map.106), channel_id=1, source_target_pairs={{0,4},{1,5},{4,8},{5,9},{8,12},{9,13},{12,14},{13,15},{14,10},{15,... | collective-permute-start | bytes 1376264 | tf_op jit(solution)/shard_map/ppermute | solution.py:94
  138.1 17.3 %collective-permute-start.18 = (bf16[64,3584]{1,0:T(8,128)(2,1)S(1)}, bf16[64,3584]{1,0:T(8,128)(2,1)S(1)}, u32[]{:S(2)}, u32[]{:S(2)}) collective-permute-start(bf16[64,3584]{1,0:T(8,128)(2,1)S(1)} %shard_map.104), channel_id=1, source_target_pairs={{0,2},{1,3},{4,0},{5,1},{8,4},{9,5},{12,8},{13,9},{14,12},{15,13},... | collective-permute-start | bytes 1376264 | tf_op jit(solution)/shard_map/ppermute | solution.py:94
  144.4 15.3 %collective-permute-start.25 = (bf16[64,3584]{1,0:T(8,128)(2,1)S(1)}, bf16[64,3584]{1,0:T(8,128)(2,1)S(1)}, u32[]{:S(2)}, u32[]{:S(2)}) collective-permute-start(bf16[64,3584]{1,0:T(8,128)(2,1)S(1)} %shard_map.109), channel_id=1, source_target_pairs={{0,2},{1,3},{4,0},{5,1},{8,4},{9,5},{12,8},{13,9},{14,12},{15,13},... | collective-permute-start | bytes 1376264 | tf_op jit(solution)/shard_map/ppermute | solution.py:94
  146.3 14.1 %collective-permute-start.15 = (bf16[64,3584]{1,0:T(8,128)(2,1)S(1)}, bf16[64,3584]{1,0:T(8,128)(2,1)S(1)}, u32[]{:S(2)}, u32[]{:S(2)}) collective-permute-start(bf16[64,3584]{1,0:T(8,128)(2,1)S(1)} %shard_map.102), channel_id=1, source_target_pairs={{0,4},{1,5},{4,8},{5,9},{8,12},{9,13},{12,14},{13,15},{14,10},{15,... | collective-permute-start | bytes 1376264 | tf_op jit(solution)/shard_map/ppermute | solution.py:94
